TPU v7x, 32 devices: a whole 2x2x4 slice. The times are simulated.
32 devices in a mesh: island: 8 (over y, x, core), seq: 4 (over z).
Axes of the slice: x: 2, y: 2, z: 4, core: 2. Of those that a mesh axis runs over, the one named last changes fastest.
Arguments:
- states: bfloat16 [8, 512, 5120], P('island', 'seq'), may hold values from -6 to 6
- key_vals: bfloat16 [8, 512, 2, 256], P('island', 'seq'), may hold values from -6 to 6
- cotangent: bfloat16 [8, 512, 256], P('island', 'seq'), may hold values from -6 to 6
- first_moment: bfloat16 [8, 5120, 256], P('island', 'seq'), may hold values from -0.75 to 0.75
- second_moment: bfloat16 [8, 5120, 256], P('island', 'seq'), may hold values from 0.00029945374 to 0.029907227
- anchor: float32 [5120, 256], P('seq', 'island'), may hold values from -6 to 6
- outer_momentum: float32 [5120, 256], P('seq', 'island'), may hold values from -1.5 to 1.5
Outputs:
- new_anchor: float32 [5120, 256], P('seq', 'island')
- new_momentum: float32 [5120, 256], P('seq', 'island')
- first_out: bfloat16 [8, 5120, 256], P('island', 'seq')
- second_out: bfloat16 [8, 5120, 256], P('island', 'seq')
All inputs are finite; a program needn't handle non-finite values.
Results may differ from a plain program's by a relative error of at most 0.01.
Values may be sent and summed in bfloat16 or wider, within the bound.
No kernel may reach another device: no remote copies, remote signals or barrier semaphores. Data moves between devices by JAX's collectives and lax.ppermute only.
A program may use at most 64 MiB of HBM per device.

v0:
```python
import jax
import jax.numpy as jnp
from jax import lax
from jax.sharding import PartitionSpec as P

D = 5120
HD = 64


inner_rate = 0.1
beta_one = 0.9
beta_two = 0.95
adam_eps = 1e-08
outer_rate = 0.7
outer_beta = 0.9


def head_update(query_head, key_head, value_head, cot_head):
    length = query_head.shape[0]
    rows_block = min(512, length)
    scale_factor = query_head.shape[1] ** (-0.5)
    col_ids = lax.broadcasted_iota(jnp.int32, (rows_block, length), 1)

    def one_block(block_index):
        first_row = block_index * rows_block
        query_rows = lax.dynamic_slice_in_dim(query_head, first_row, rows_block, 0)
        cot_rows = lax.dynamic_slice_in_dim(cot_head, first_row, rows_block, 0)
        scores = (
            lax.dot_general(
                query_rows, key_head, (((1,), (1,)), ((), ())), preferred_element_type=jnp.float32
            )
            * scale_factor
        )
        row_ids = lax.broadcasted_iota(jnp.int32, (rows_block, length), 0) + first_row
        scores = jnp.where(row_ids >= col_ids, scores, -1e30)
        peak_score = jnp.max(scores, axis=1, keepdims=True)
        expons = jnp.exp(scores - peak_score)
        attend = expons / jnp.sum(expons, axis=1, keepdims=True)
        attend_low = attend.astype(jnp.bfloat16)
        output = jnp.dot(attend_low, value_head, preferred_element_type=jnp.float32)
        dattend = lax.dot_general(
            cot_rows, value_head, (((1,), (1,)), ((), ())), preferred_element_type=jnp.float32
        )
        rowdot = jnp.sum(output * cot_rows.astype(jnp.float32), axis=1, keepdims=True)
        dscore = (attend * (dattend - rowdot)).astype(jnp.bfloat16)
        return (
            jnp.dot(dscore, key_head, preferred_element_type=jnp.float32) * scale_factor
        ).astype(jnp.bfloat16)

    blocks = lax.map(one_block, jnp.arange(length // rows_block, dtype=jnp.int32))
    return blocks.reshape(length, query_head.shape[1])


def query_grads(queries, key_rows, value_rows, cot_rows, head_size):
    length = queries.shape[0]
    head_count = queries.shape[1] // head_size

    def split_heads(matrix):
        return matrix.reshape(length, head_count, head_size).transpose(1, 0, 2)

    result = lax.map(
        lambda member: head_update(member[0], member[1], member[2], member[3]),
        (
            split_heads(queries),
            split_heads(key_rows),
            split_heads(value_rows),
            split_heads(cot_rows),
        ),
    )
    return result.transpose(1, 0, 2).reshape(length, head_count * head_size)


def adam_step(local_params, first_state, second_state, gradient):
    first_state = beta_one * first_state + (1.0 - beta_one) * gradient
    second_state = beta_two * second_state + (1.0 - beta_two) * gradient * gradient
    local_params = local_params - inner_rate * first_state / (jnp.sqrt(second_state) + adam_eps)
    return (local_params, first_state, second_state)


def on_device(states, key_vals, cotangent, first_moment, second_moment, anchor, outer_momentum):
    inverse = D ** (-0.5)
    features = lax.all_to_all(states[0], "seq", split_axis=1, concat_axis=0, tiled=True)
    cot_wide = cotangent[0][:, None, :]
    key_value, cot_heads = (
        lax.all_to_all(key_vals[0], "seq", split_axis=2, concat_axis=0, tiled=True),
        lax.all_to_all(cot_wide, "seq", split_axis=2, concat_axis=0, tiled=True),
    )
    key_rows = key_value[:, 0, :]
    value_rows = key_value[:, 1, :]
    cot_local = cot_heads[:, 0, :]
    local_params = lax.all_gather(anchor.astype(jnp.bfloat16), "island", axis=1, tiled=True).astype(
        anchor.dtype
    )
    start_params = local_params
    first_state = first_moment[0].astype(jnp.float32)
    second_state = second_moment[0].astype(jnp.float32)
    own_cols = local_params.shape[1] // lax.axis_size("seq")
    weight = local_params.astype(jnp.bfloat16)

    def column_term(first_col, col_count, weight=weight):
        return (
            lax.dot_general(
                weight, features, (((0,), (1,)), ((), ())), preferred_element_type=jnp.float32
            )
            * inverse
        )

    query_cols = lax.psum_scatter(
        column_term(jnp.int32(0), own_cols * lax.axis_size("seq")).astype(jnp.bfloat16),
        "seq",
        scatter_dimension=0,
        tiled=True,
    ).astype(jnp.float32)
    queries = query_cols.T.astype(jnp.bfloat16)
    dquery = query_grads(queries, key_rows, value_rows, cot_local, HD)
    weight_grad = (
        lax.dot_general(
            features,
            lax.all_gather(dquery, "seq", axis=1, tiled=True),
            (((0,), (0,)), ((), ())),
            preferred_element_type=jnp.float32,
        )
        * inverse
    )
    local_params, first_state, second_state = adam_step(
        local_params, first_state, second_state, weight_grad
    )
    pseudo_grad = start_params - local_params
    share_cols = anchor.shape[1]
    summed = lax.psum(pseudo_grad.astype(jnp.bfloat16), "island").astype(jnp.float32)
    own_slice = lax.dynamic_slice_in_dim(
        summed, lax.axis_index("island") * share_cols, share_cols, 1
    )
    average = own_slice / lax.axis_size("island")
    new_momentum = outer_beta * outer_momentum + average
    new_anchor = anchor - outer_rate * (average + outer_beta * new_momentum)
    return (
        new_anchor,
        new_momentum,
        first_state.astype(jnp.bfloat16)[None],
        second_state.astype(jnp.bfloat16)[None],
    )


def solution(mesh):
    return jax.shard_map(
        on_device,
        mesh=mesh,
        in_specs=(
            P("island", "seq", None),
            P("island", "seq", None, None),
            P("island", "seq", None),
            P("island", "seq", None),
            P("island", "seq", None),
            P("seq", "island"),
            P("seq", "island"),
        ),
        out_specs=(
            P("seq", "island"),
            P("seq", "island"),
            P("island", "seq", None),
            P("island", "seq", None),
        ),
        check_vma=False,
    )
```

profile of v0, /device:TPU:0, one launch (start us, length us, event | category | flops | bytes accessed | tf_op | source)
XLA Modules:
  0.0 156.2 jit_solution(5430936173904123920)
XLA Ops:
  7.2 2.4 %copy.47 = bf16[1,128,5120]{1,2,0:T(8,128)(2,1)} copy(bf16[1,128,5120]{2,1,0:T(8,128)(2,1)} %param.7) | data formatting | bytes 2621440 | tf_op args[0]
  9.6 0.0 copy-start.2
  9.6 6.4 %all-to-all-start = ((bf16[128,4,1280]{0,2,1:T(8,128)(2,1)}), bf16[128,4,1280]{0,2,1:T(8,128)(2,1)S(1)}, u32[]{:S(2)}, u32[]{:S(2)}) async-start(bf16[128,4,1280]{0,2,1:T(8,128)(2,1)} %bitcast.1), calls=%async_computation | async-start | bytes 2621440 | tf_op jit(solution)/shard_map/all_to_all | solution.py:82
  16.1 0.0 reduce-scatter.2.cloned.1.call-start
  16.1 0.0 copy-done.2
  16.1 10.1 %all_gather.6 = bf16[1280,256]{0,1:T(8,128)(2,1)S(1)} all-gather(bf16[1280,32]{0,1:T(8,128)(2,1)S(1)} %convert_element_type.53), channel_id=1, replica_groups=mesh['island'=8,'seq'=4] {'island'}, dimensions={1}, use_global_device_ids=true | all-gather | bytes 737280 | tf_op jit(solution)/shard_map/all_gather | solution.py:91
  26.2 21.2 %all-to-all-done = bf16[128,4,1280]{0,2,1:T(8,128)(2,1)S(1)} async-done(((bf16[128,4,1280]{0,2,1:T(8,128)(2,1)}), bf16[128,4,1280]{0,2,1:T(8,128)(2,1)S(1)}, u32[]{:S(2)}, u32[]{:S(2)}) %all-to-all-start) | async-done | bytes 1310752 | tf_op jit(solution)/shard_map/all_to_all | solution.py:82
  47.4 0.6 copy.48
  48.0 0.0 copy-start.4
  48.0 1.2 fusion.5
  49.2 0.0 copy-start
  49.3 0.0 reduce-scatter.2.cloned.1.call-update
  49.3 0.0 copy-start.1
  49.3 0.0 copy-done.4
  49.3 0.8 copy.52
  50.1 0.5 broadcast.47
  50.6 1.9 %reduce = bf16[256,128]{1,0:T(8,128)(2,1)S(1)} reduce(bf16[256,1,128]{2,1,0:T(2,128)(2,1)} %bitcast.77, bf16[]{:T(256)} %broadcast.47), dimensions={1}, to_apply=%bitcast.64.reduce_sub_computation | reduce | bytes 131074
  52.5 0.6 reshape.29
  53.1 3.3 %all-to-all-start.2 = ((bf16[4,2,4096]{2,1,0:T(2,128)(2,1)}), bf16[4,2,4096]{2,1,0:T(2,128)(2,1)S(1)}, u32[]{:S(2)}, u32[]{:S(2)}) async-start(bf16[4,2,4096]{2,1,0:T(2,128)(2,1)} %reshape.29), calls=%async_computation.3 | async-start | bytes 131072 | tf_op jit(solution)/shard_map/all_to_all | solution.py:86
  56.4 1.7 %copy.49 = bf16[1,128,2,256]{1,2,3,0:T(2,128)(2,1)} copy(bf16[1,128,2,256]{3,2,1,0:T(2,128)(2,1)} %param.8) | data formatting | bytes 262144 | tf_op args[1]
  58.2 4.7 %all-to-all-done.2 = bf16[4,2,4096]{2,1,0:T(2,128)(2,1)S(1)} async-done(((bf16[4,2,4096]{2,1,0:T(2,128)(2,1)}), bf16[4,2,4096]{2,1,0:T(2,128)(2,1)S(1)}, u32[]{:S(2)}, u32[]{:S(2)}) %all-to-all-start.2) | async-done | bytes 65568 | tf_op jit(solution)/shard_map/all_to_all | solution.py:86
  62.8 4.0 %all-to-all-start.1 = ((bf16[128,2,256]{0,1,2:T(2,128)(2,1)}), bf16[128,2,256]{0,1,2:T(2,128)(2,1)}, u32[]{:S(2)}, u32[]{:S(2)}) async-start(bf16[128,2,256]{0,1,2:T(2,128)(2,1)} %bitcast.79), calls=%async_computation.2 | async-start | bytes 262144 | tf_op jit(solution)/shard_map/all_to_all | solution.py:85
  66.8 0.0 all-reduce.2.cloned.1.call-start
  66.9 0.0 copy-done
  66.9 1.1 copy.46
  67.9 0.0 copy-done.1
  67.9 1.1 copy.55
  69.0 0.1 reshape.30
  69.1 0.1 copy.53
  69.2 3.6 %all-to-all-done.1 = bf16[128,2,256]{0,1,2:T(2,128)(2,1)} async-done(((bf16[128,2,256]{0,1,2:T(2,128)(2,1)}), bf16[128,2,256]{0,1,2:T(2,128)(2,1)}, u32[]{:S(2)}, u32[]{:S(2)}) %all-to-all-start.1) | async-done | bytes 131104 | tf_op jit(solution)/shard_map/all_to_all | solution.py:85
  72.8 0.9 copy.50
  73.7 0.0 reduce-scatter.2.cloned.1.call-done
  73.8 1.2 fusion.21
  75.0 0.2 fusion.10
  75.2 0.3 fusion.8
  75.5 0.5 fusion.7
  76.0 13.8 %all_gather.7 = bf16[512,256]{0,1:T(8,128)(2,1)S(1)} all-gather(bf16[512,64]{0,1:T(8,128)(2,1)S(1)} %fusion.7), channel_id=1, replica_groups=mesh['island'=8,'seq'=4] {'seq'}, dimensions={1}, use_global_device_ids=true | all-gather | bytes 327680 | tf_op jit(solution)/shard_map/all_gather | solution.py:119
  89.8 3.4 %convert_bitcast_fusion = (bf16[1,1280,256]{1,2,0:T(8,128)(2,1)S(1)}, bf16[1280,256]{0,1:T(8,128)(2,1)}, bf16[1,1280,256]{1,2,0:T(8,128)(2,1)S(1)}) fusion(bf16[1,1280,256]{1,2,0:T(8,128)(2,1)} %copy.55, bf16[1,1280,256]{1,2,0:T(8,128)(2,1)} %copy.46, bf16[1280,256]{0,1:T(8,128)(2,1)S(1)} %all_gather.6, bf16[512,256]{0,1:T(8,128)(2,1)S(1)} %all_gather.7, ...), kind=kOutput, calls=%fused_computation.22 | convolution fusion | flops 341770240 | bytes 5505024 | tf_op jit(solution)/shard_map/dot_general | solution.py:117
  93.2 0.0 all-reduce.2.cloned.1.call-update
  93.3 0.0 copy-start.3
  93.3 1.1 copy.56
  94.4 1.1 copy.57
  95.4 52.3 %all-reduce.2.cloned.1.call-done = bf16[1280,256]{0,1:T(8,128)(2,1)} async-done(((bf16[1280,256]{0,1:T(8,128)(2,1)}), bf16[1280,256]{0,1:T(8,128)(2,1)}) %all-reduce.2.cloned.1.call-update) | async-done | bytes 655376 | tf_op jit(solution)/shard_map/psum | solution.py:130
  147.7 0.0 copy-done.3
  147.7 1.6 %multiply_subtract_fusion = (f32[1280,32]{0,1:T(8,128)}, f32[1280,32]{0,1:T(8,128)}) fusion(f32[1280,32]{0,1:T(8,128)S(1)} %copy-done.2, bf16[1280,256]{0,1:T(8,128)(2,1)} %all-reduce.2.cloned.1.call-done, s32[]{:T(128)S(6)} %select_n.14, f32[1280,32]{0,1:T(8,128)S(1)} %copy-done.3), kind=kLoop, calls=%fused_computation.25 | loop fusion | flops 327680 | bytes 737284 | tf_op jit(solution)/shard_map/sub | solution.py:136
  (3 shorter events, 0.0 us)
Async XLA Ops:
  9.6 6.5 %copy-start.2 = (f32[1280,32]{0,1:T(8,128)S(1)}, f32[1280,32]{0,1:T(8,128)}, u32[]{:S(2)}) copy-start(f32[1280,32]{0,1:T(8,128)} %param.12) | copy-start | bytes 491524
  9.6 37.8 %all-to-all-start = ((bf16[128,4,1280]{0,2,1:T(8,128)(2,1)}), bf16[128,4,1280]{0,2,1:T(8,128)(2,1)S(1)}, u32[]{:S(2)}, u32[]{:S(2)}) async-start(bf16[128,4,1280]{0,2,1:T(8,128)(2,1)} %bitcast.1), calls=%async_computation | async-start | bytes 2621440 | tf_op jit(solution)/shard_map/all_to_all | solution.py:82
  16.1 57.7 %reduce-scatter.2.cloned.1.call-start = ((), (), s32[]{:S(2)}) async-start(), calls=%async_computation.4 | async-start | bytes 327680 | tf_op jit(solution)/shard_map/reduce_scatter | solution.py:108
  48.0 1.3 copy-start.4
  49.2 17.6 %copy-start = (bf16[1,1280,256]{2,1,0:T(8,128)(2,1)S(1)}, bf16[1,1280,256]{2,1,0:T(8,128)(2,1)}, u32[]{:S(2)}) copy-start(bf16[1,1280,256]{2,1,0:T(8,128)(2,1)} %param.10) | copy-start | bytes 1966084
  49.3 18.7 %copy-start.1 = (bf16[1,1280,256]{2,1,0:T(8,128)(2,1)S(1)}, bf16[1,1280,256]{2,1,0:T(8,128)(2,1)}, u32[]{:S(2)}) copy-start(bf16[1,1280,256]{2,1,0:T(8,128)(2,1)} %param.11) | copy-start | bytes 1966084
  53.1 9.7 %all-to-all-start.2 = ((bf16[4,2,4096]{2,1,0:T(2,128)(2,1)}), bf16[4,2,4096]{2,1,0:T(2,128)(2,1)S(1)}, u32[]{:S(2)}, u32[]{:S(2)}) async-start(bf16[4,2,4096]{2,1,0:T(2,128)(2,1)} %reshape.29), calls=%async_computation.3 | async-start | bytes 131072 | tf_op jit(solution)/shard_map/all_to_all | solution.py:86
  62.8 9.9 %all-to-all-start.1 = ((bf16[128,2,256]{0,1,2:T(2,128)(2,1)}), bf16[128,2,256]{0,1,2:T(2,128)(2,1)}, u32[]{:S(2)}, u32[]{:S(2)}) async-start(bf16[128,2,256]{0,1,2:T(2,128)(2,1)} %bitcast.79), calls=%async_computation.2 | async-start | bytes 262144 | tf_op jit(solution)/shard_map/all_to_all | solution.py:85
  66.8 80.9 %all-reduce.2.cloned.1.call-start = ((), (), s32[]{:S(2)}) async-start(), calls=%async_computation.5 | async-start | bytes 1310720 | tf_op jit(solution)/shard_map/psum | solution.py:130
  93.3 54.4 %copy-start.3 = (f32[1280,32]{0,1:T(8,128)S(1)}, f32[1280,32]{0,1:T(8,128)}, u32[]{:S(2)}) copy-start(f32[1280,32]{0,1:T(8,128)} %param.13) | copy-start | bytes 491524
Sparse Core Ops, SparseCore 0:
  49.4 18.9 reduce-scatter.1
  93.4 54.2 all-reduce.1
where the time goes:
time: 157 us; the launch traced here: 156 us
  waiting for transfers between devices  81.8 us (52%)
  blocking collectives  23.9 us (15%)
  between operations  14.2 us (9%)
  starting transfers between devices  13.7 us (9%)
  local copies, waits for them, and re-layouts  12.1 us (8%)
  matrix products  6.71 us (4%)
  other arithmetic  3.77 us (2%)
    psum x1, waiting for transfers between devices, on_device(): lax.psum(pseudo_grad.astype(jnp.bfloat16), 'island').astype(jnp.float32)  52.3 us
    all_to_all x1, waiting for transfers between devices, on_device(): lax.all_to_all(states[0], 'seq', split_axis=1, concat_axis=0, tiled=True)  21.2 us
    all_gather x1, blocking collectives, on_device(): lax.all_gather(dquery, 'seq', axis=1, tiled=True)  13.8 us
    all_gather x1, blocking collectives, on_device(): lax.all_gather(anchor.astype(jnp.bfloat16), 'island', axis=1, tiled=True)  10.1 us
    unnamed x20, local copies, waits for them, and re-layouts  9.73 us
    all_to_all x1, starting transfers between devices, on_device(): lax.all_to_all(states[0], 'seq', split_axis=1, concat_axis=0, tiled=True)  6.45 us
    all_to_all x1, waiting for transfers between devices, on_device(): lax.all_to_all(cot_wide, 'seq', split_axis=2, concat_axis=0, tiled=True)  4.67 us
    all_to_all x1, starting transfers between devices, on_device(): lax.all_to_all(key_vals[0], 'seq', split_axis=2, concat_axis=0, tiled=True)  3.95 us
  transfers between devices with their start and end apart: 5, of which 4 were waited for; matrix products, arithmetic and copies ran while one was open for 7% of the time, Pallas kernels for 0%

commit v1 on v0

v1 whole, which is shorter than its diff:
```python
import jax
import jax.numpy as jnp
from jax import lax
from jax.sharding import PartitionSpec as P

HD = 64

inner_rate = 0.1
beta_one = 0.9
beta_two = 0.95
adam_eps = 1e-08
outer_rate = 0.7
outer_beta = 0.9


def partner_perm(size, step, stride=1):
    pairs = []
    for group in range(size):
        other = group ^ step if size & (size - 1) == 0 else (group + step) % size
        for inner in range(stride):
            pairs.append((group * stride + inner, other * stride + inner))
    return pairs


def target_of(index, step, size):
    if size & (size - 1) == 0:
        return jnp.bitwise_xor(index, step)
    return lax.rem(index + step, size)


def source_of(index, step, size):
    if size & (size - 1) == 0:
        return jnp.bitwise_xor(index, step)
    return lax.rem(index - step + size, size)


def on_device(states, key_vals, cotangent, first_moment, second_moment, anchor, outer_momentum):
    n_seq = lax.axis_size("seq")
    n_island = lax.axis_size("island")
    n_chip = n_island // 2
    seq = lax.axis_index("seq")
    island = lax.axis_index("island")
    chip, core = island // 2, lax.rem(island, 2)
    tokens = states[0]
    rows, features = tokens.shape
    block = features // n_seq
    share = anchor.shape[1]
    cols = first_moment.shape[2]
    heads = cols // HD
    inverse = features ** (-0.5)
    scale = HD ** (-0.5)
    swap = [(i, i ^ 1) for i in range(n_island)]
    up_perm = [(i, i + 1) for i in range(n_seq - 1)]
    down_perm = [(i + 1, i) for i in range(n_seq - 1)]

    own_weight = anchor.T.astype(jnp.bfloat16)
    up, down = [own_weight], [own_weight]
    kv = [key_vals[0]]
    for step in range(1, n_seq):
        up.append(lax.ppermute(up[-1], "seq", up_perm))
        down.append(lax.ppermute(down[-1], "seq", down_perm))
    for step in range(1, n_seq):
        kv.append(lax.ppermute(kv[-1], "seq", up_perm))
    column = jnp.zeros((share, features), jnp.bfloat16)
    column = lax.dynamic_update_slice(column, own_weight, (0, seq * block))
    for step in range(1, n_seq):
        piece = jnp.where(step <= seq, up[step], down[n_seq - step])
        column = lax.dynamic_update_slice(
            column, piece, (0, lax.rem(seq - step + n_seq, n_seq) * block)
        )

    state_parts = [lax.dynamic_slice(tokens, (0, seq * block), (rows, block))]
    for step in range(1, n_seq):
        piece = lax.dynamic_slice(tokens, (0, target_of(seq, step, n_seq) * block), (rows, block))
        state_parts.append(lax.ppermute(piece, "seq", partner_perm(n_seq, step)))

    mine = [column]
    for step in range(1, n_chip):
        mine.append(lax.ppermute(column, "island", partner_perm(n_chip, step, 2)))
    query_parts = []
    for step in range(n_chip):
        theirs = lax.ppermute(mine[step], "island", swap)
        both = jnp.concatenate([mine[step], theirs], 0)
        query_parts.append(
            lax.dot_general(
                both, tokens, (((1,), (1,)), ((), ())), preferred_element_type=jnp.float32
            )
            * inverse
        )
    rel = jnp.stack(query_parts).reshape(n_chip, 2, share, rows)
    ordered = []
    for at in range(n_island):
        ordered.append(
            lax.dynamic_slice(
                rel,
                (source_of(chip, at // 2, n_chip), jnp.bitwise_xor(core, at % 2), 0, 0),
                (1, 1, share, rows),
            )[0, 0]
        )
    queries = jnp.concatenate(ordered, 0).astype(jnp.bfloat16).reshape(heads, HD, rows)

    kv_all = jnp.concatenate(kv, 0)
    length = kv_all.shape[0]
    keys = kv_all[:, 0, :].reshape(length, heads, HD)
    values = kv_all[:, 1, :].reshape(length, heads, HD)
    cot = cotangent[0].reshape(rows, heads, HD)
    where = lax.broadcasted_iota(jnp.int32, (rows, length), 1)
    key_at = lax.rem(where, rows) + (seq - where // rows) * rows
    query_at = lax.broadcasted_iota(jnp.int32, (rows, length), 0) + seq * rows
    seen = (query_at >= key_at) & (key_at >= 0)
    scores = (
        jnp.einsum("hdq,khd->hqk", queries, keys, preferred_element_type=jnp.float32) * scale
    )
    scores = jnp.where(seen[None], scores, -1e30)
    expons = jnp.exp(scores - jnp.max(scores, axis=2, keepdims=True))
    attend = expons / jnp.sum(expons, axis=2, keepdims=True)
    output = jnp.einsum(
        "hqk,khd->hqd", attend.astype(jnp.bfloat16), values, preferred_element_type=jnp.float32
    )
    dattend = jnp.einsum("qhd,khd->hqk", cot, values, preferred_element_type=jnp.float32)
    rowdot = jnp.sum(output * cot.transpose(1, 0, 2).astype(jnp.float32), axis=2, keepdims=True)
    dscore = (attend * (dattend - rowdot)).astype(jnp.bfloat16)
    dquery = (
        jnp.einsum("hqk,khd->qhd", dscore, keys, preferred_element_type=jnp.float32) * scale
    ).astype(jnp.bfloat16)
    dquery = dquery.reshape(rows, cols)

    dquery_parts = [dquery]
    for step in range(1, n_seq):
        dquery_parts.append(lax.ppermute(dquery, "seq", partner_perm(n_seq, step)))

    gradient = (
        lax.dot_general(
            jnp.concatenate(state_parts, 0),
            jnp.concatenate(dquery_parts, 0),
            (((0,), (0,)), ((), ())),
            preferred_element_type=jnp.float32,
        )
        * inverse
    )
    first = beta_one * first_moment[0].astype(jnp.float32) + (1.0 - beta_one) * gradient
    second = (
        beta_two * second_moment[0].astype(jnp.float32) + (1.0 - beta_two) * gradient * gradient
    )
    delta = (inner_rate * first / (jnp.sqrt(second) + adam_eps)).astype(jnp.bfloat16)

    parts = delta.T.reshape(n_chip, 2, share, block)
    other = lax.dynamic_index_in_dim(parts, 1 - core, 1, keepdims=False)
    same = lax.dynamic_index_in_dim(parts, core, 1, keepdims=False)
    paired = same.astype(jnp.float32) + lax.ppermute(other, "island", swap).astype(jnp.float32)
    total = lax.dynamic_index_in_dim(paired, chip, 0, keepdims=False)
    paired = paired.astype(jnp.bfloat16)
    for step in range(1, n_chip):
        piece = lax.dynamic_index_in_dim(paired, target_of(chip, step, n_chip), 0, keepdims=False)
        total = total + lax.ppermute(piece, "island", partner_perm(n_chip, step, 2)).astype(
            jnp.float32
        )
    average = total.T / n_island
    new_momentum = outer_beta * outer_momentum + average
    new_anchor = anchor - outer_rate * (average + outer_beta * new_momentum)
    return (
        new_anchor,
        new_momentum,
        first.astype(jnp.bfloat16)[None],
        second.astype(jnp.bfloat16)[None],
    )


def solution(mesh):
    return jax.shard_map(
        on_device,
        mesh=mesh,
        in_specs=(
            P("island", "seq", None),
            P("island", "seq", None, None),
            P("island", "seq", None),
            P("island", "seq", None),
            P("island", "seq", None),
            P("seq", "island"),
            P("seq", "island"),
        ),
        out_specs=(
            P("seq", "island"),
            P("seq", "island"),
            P("island", "seq", None),
            P("island", "seq", None),
        ),
        check_vma=False,
    )
```

time: 157 us -> 97.7 us (0.62)
  waiting for transfers between devices: 81.8 us -> 22.3 us
  starting transfers between devices: 13.7 us -> 56.8 us
  blocking collectives: 23.9 us -> 0 us
  between operations: 14.2 us -> 1.16 us
  local copies, waits for them, and re-layouts: 12.1 us -> 5.46 us
  matrix products: 6.71 us -> 9.42 us
  other arithmetic: 3.77 us -> 2.09 us
    ppermute x0 -> x26, starting transfers between devices: none -> 56.8 us  [the longest x3 21.1 us: on_device(): kv.append(lax.ppermute(kv[-1], 'seq', up_perm))]
    psum x1 -> x0, waiting for transfers between devices: 52.3 us -> none  [on_device(): lax.psum(pseudo_grad.astype(jnp.bfloat16), 'island').astype(jnp.float32)]
    all_to_all x3 -> x0, waiting for transfers between devices: 29.5 us -> none  [the longest x1 21.2 us: on_device(): lax.all_to_all(states[0], 'seq', split_axis=1, concat_axis=0, tiled=True)]
    all_gather x2 -> x0, blocking collectives: 23.9 us -> none  [the longest x1 13.8 us: on_device(): lax.all_gather(dquery, 'seq', axis=1, tiled=True)]
    ppermute x0 -> x26, waiting for transfers between devices: none -> 22.3 us  [the longest x3 6.63 us: on_device(): dquery_parts.append(lax.ppermute(dquery, 'seq', partner_perm(n_seq, step)))]
    all_to_all x3 -> x0, starting transfers between devices: 13.7 us -> none  [the longest x1 6.45 us: on_device(): lax.all_to_all(states[0], 'seq', split_axis=1, concat_axis=0, tiled=True)]
    unnamed x20 -> x25, local copies, waits for them, and re-layouts: 9.73 us -> 3.92 us
    unnamed x1 -> x0, other arithmetic: 1.91 us -> none
  transfers between devices with their start and end apart: 5 -> 26, of which waited for: 4 -> 12; matrix products, arithmetic and copies ran while one was open for 7% -> 13% of each run, Pallas kernels for 0% -> 0%
where the time goes in v1:
time: 97.7 us; the launch traced here: 97.3 us
  starting transfers between devices  56.8 us (58%)
  waiting for transfers between devices  22.3 us (23%)
  matrix products  9.42 us (10%)
  local copies, waits for them, and re-layouts  5.46 us (6%)
  other arithmetic  2.09 us (2%)
  between operations  1.16 us (1%)
    ppermute x3, starting transfers between devices, on_device(): kv.append(lax.ppermute(kv[-1], 'seq', up_perm))  21.1 us
    ppermute x3, starting transfers between devices, on_device(): up.append(lax.ppermute(up[-1], 'seq', up_perm))  13.4 us
    ppermute x3, waiting for transfers between devices, on_device(): dquery_parts.append(lax.ppermute(dquery, 'seq', partner_perm(n_seq, step)))  6.63 us
    ppermute x3, starting transfers between devices, on_device(): state_parts.append(lax.ppermute(piece, 'seq', partner_perm(n_seq, step)))  6.29 us
    ppermute x3, waiting for transfers between devices, on_device(): mine.append(lax.ppermute(column, 'island', partner_perm(n_chip, step, 2)))  5.4 us
    ppermute x3, starting transfers between devices, on_device(): dquery_parts.append(lax.ppermute(dquery, 'seq', partner_perm(n_seq, step)))  4.45 us
    unnamed x25, local copies, waits for them, and re-layouts  3.92 us
    ppermute x3, starting transfers between devices, on_device(): down.append(lax.ppermute(down[-1], 'seq', down_perm))  3.86 us
  transfers between devices with their start and end apart: 26, of which 12 were waited for; matrix products, arithmetic and copies ran while one was open for 13% of the time, Pallas kernels for 0%

profile of v1, /device:TPU:0, one launch (start us, length us, event | category | flops | bytes accessed | tf_op | source)
XLA Modules:
  0.0 97.3 jit_solution(1168404976660904505)
XLA Ops:
  0.7 0.9 constant_dynamic-update-slice_fusion.8
  1.6 4.9 %collective-permute-start.6 = (bf16[32,1280]{1,0:T(8,128)(2,1)S(1)}, bf16[32,1280]{1,0:T(8,128)(2,1)S(1)}, u32[]{:S(2)}, u32[]{:S(2)}) collective-permute-start(bf16[32,1280]{1,0:T(8,128)(2,1)S(1)} %get-tuple-element.17), channel_id=1, source_target_pairs={{0,1},{1,2},{2,3},{4,5},{5,6},{6,7},{8,9},{9,10},{10,11},{12,13},{... | collective-permute-start | bytes 245768 | tf_op jit(solution)/shard_map/ppermute | solution.py:60
  6.5 1.3 %collective-permute-start.7 = (bf16[32,1280]{1,0:T(8,128)(2,1)S(1)}, bf16[32,1280]{1,0:T(8,128)(2,1)S(1)}, u32[]{:S(2)}, u32[]{:S(2)}) collective-permute-start(bf16[32,1280]{1,0:T(8,128)(2,1)S(1)} %get-tuple-element.17), channel_id=1, source_target_pairs={{1,0},{2,1},{3,2},{5,4},{6,5},{7,6},{9,8},{10,9},{11,10},{13,12},{... | collective-permute-start | bytes 245768 | tf_op jit(solution)/shard_map/ppermute | solution.py:61
  7.8 1.0 %copy.17 = bf16[1,128,2,256]{1,3,2,0:T(8,128)(2,1)S(1)} copy(bf16[1,128,2,256]{3,2,1,0:T(2,128)(2,1)} %param.8) | data formatting | bytes 262144 | tf_op args[1]
  8.9 4.6 %collective-permute-start.3 = (bf16[128,2,256]{0,2,1:T(8,128)(2,1)S(1)}, bf16[128,2,256]{0,2,1:T(8,128)(2,1)S(1)}, u32[]{:S(2)}, u32[]{:S(2)}) collective-permute-start(bf16[128,2,256]{0,2,1:T(8,128)(2,1)S(1)} %bitcast.148), channel_id=1, source_target_pairs={{0,1},{1,2},{2,3},{4,5},{5,6},{6,7},{8,9},{9,10},{10,11},{12,13},{... | collective-permute-start | bytes 393224 | tf_op jit(solution)/shard_map/ppermute | solution.py:63
  13.5 1.4 %dynamic-slice_bitcast_fusion.4 = (bf16[128,1280]{1,0:T(8,128)(2,1)S(1)}, bf16[128,1280]{1,0:T(8,128)(2,1)S(1)}, bf16[128,1280]{1,0:T(8,128)(2,1)S(1)}, bf16[128,1280]{1,0:T(8,128)(2,1)S(1)}) fusion(bf16[1,128,5120]{2,1,0:T(8,128)(2,1)} %param.7, s32[]{:T(128)S(6)} %select_n.99, s32[]{:T(128)S(6)} %select_n.101, s32[]{:T(128)S(6)} %select_n.100, ...), kind=kLoop, calls=%fused_computation.61 | loop fusion | bytes 2621456 | tf_op jit(solution)/shard_map/dynamic_slice | solution.py:72
  14.9 2.7 %collective-permute-start.1 = (bf16[128,1280]{1,0:T(8,128)(2,1)S(1)}, bf16[128,1280]{1,0:T(8,128)(2,1)S(1)}, u32[]{:S(2)}, u32[]{:S(2)}) collective-permute-start(bf16[128,1280]{1,0:T(8,128)(2,1)S(1)} %get-tuple-element.22), channel_id=1, source_target_pairs={{0,2},{1,3},{2,0},{3,1},{4,6},{5,7},{6,4},{7,5},{8,10},{9,11},{10,... | collective-permute-start | bytes 983048 | tf_op jit(solution)/shard_map/ppermute | solution.py:75
  17.5 1.3 %collective-permute-start.8 = (bf16[32,1280]{1,0:T(8,128)(2,1)S(1)}, bf16[32,1280]{1,0:T(8,128)(2,1)S(1)}, u32[]{:S(2)}, u32[]{:S(2)}) collective-permute-start(bf16[32,1280]{1,0:T(8,128)(2,1)S(1)} %collective-permute-done.7), channel_id=1, source_target_pairs={{1,0},{2,1},{3,2},{5,4},{6,5},{7,6},{9,8},{10,9},{11,10},{13,12},{... | collective-permute-start | bytes 245768 | tf_op jit(solution)/shard_map/ppermute | solution.py:61
  19.1 4.6 %collective-permute-start.10 = (bf16[32,1280]{1,0:T(8,128)(2,1)S(1)}, bf16[32,1280]{1,0:T(8,128)(2,1)S(1)}, u32[]{:S(2)}, u32[]{:S(2)}) collective-permute-start(bf16[32,1280]{1,0:T(8,128)(2,1)S(1)} %collective-permute-done.6), channel_id=1, source_target_pairs={{0,1},{1,2},{2,3},{4,5},{5,6},{6,7},{8,9},{9,10},{10,11},{12,13},{... | collective-permute-start | bytes 245768 | tf_op jit(solution)/shard_map/ppermute | solution.py:60
  23.7 0.5 collective-permute-done.8
  24.1 1.3 %collective-permute-start.9 = (bf16[32,1280]{1,0:T(8,128)(2,1)S(1)}, bf16[32,1280]{1,0:T(8,128)(2,1)S(1)}, u32[]{:S(2)}, u32[]{:S(2)}) collective-permute-start(bf16[32,1280]{1,0:T(8,128)(2,1)S(1)} %collective-permute-done.8), channel_id=1, source_target_pairs={{1,0},{2,1},{3,2},{5,4},{6,5},{7,6},{9,8},{10,9},{11,10},{13,12},{... | collective-permute-start | bytes 245768 | tf_op jit(solution)/shard_map/ppermute | solution.py:61
  25.4 12.2 %collective-permute-start.4 = (bf16[128,2,256]{0,2,1:T(8,128)(2,1)S(1)}, bf16[128,2,256]{0,2,1:T(8,128)(2,1)S(1)}, u32[]{:S(2)}, u32[]{:S(2)}) collective-permute-start(bf16[128,2,256]{0,2,1:T(8,128)(2,1)S(1)} %collective-permute-done.3), channel_id=1, source_target_pairs={{0,1},{1,2},{2,3},{4,5},{5,6},{6,7},{8,9},{9,10},{10,11},{12,13},{... | collective-permute-start | bytes 393224 | tf_op jit(solution)/shard_map/ppermute | solution.py:63
  37.7 3.9 %collective-permute-start.11 = (bf16[32,1280]{1,0:T(8,128)(2,1)S(1)}, bf16[32,1280]{1,0:T(8,128)(2,1)S(1)}, u32[]{:S(2)}, u32[]{:S(2)}) collective-permute-start(bf16[32,1280]{1,0:T(8,128)(2,1)S(1)} %collective-permute-done.10), channel_id=1, source_target_pairs={{0,1},{1,2},{2,3},{4,5},{5,6},{6,7},{8,9},{9,10},{10,11},{12,13},{... | collective-permute-start | bytes 245768 | tf_op jit(solution)/shard_map/ppermute | solution.py:60
  41.7 1.9 %collective-permute-done.11 = bf16[32,1280]{1,0:T(8,128)(2,1)S(1)} collective-permute-done((bf16[32,1280]{1,0:T(8,128)(2,1)S(1)}, bf16[32,1280]{1,0:T(8,128)(2,1)S(1)}, u32[]{:S(2)}, u32[]{:S(2)}) %collective-permute-start.11) | collective-permute-done | bytes 81952 | tf_op jit(solution)/shard_map/ppermute | solution.py:60
  43.7 2.5 %collective-permute-start.17 = (bf16[32,5120]{1,0:T(8,128)(2,1)S(1)}, bf16[32,5120]{1,0:T(8,128)(2,1)S(1)}, u32[]{:S(2)}, u32[]{:S(2)}) collective-permute-start(bf16[32,5120]{1,0:T(8,128)(2,1)S(1)} %select_dynamic-update-slice_fusion), channel_id=1, source_target_pairs={{0,24},{4,28},{8,16},{12,20},{16,8},{20,12},{24,0},{28,4},{1,25},{... | collective-permute-start | bytes 983048 | tf_op jit(solution)/shard_map/ppermute | solution.py:79
  46.2 4.3 %collective-permute-start.5 = (bf16[128,2,256]{0,2,1:T(8,128)(2,1)S(1)}, bf16[128,2,256]{0,2,1:T(8,128)(2,1)S(1)}, u32[]{:S(2)}, u32[]{:S(2)}) collective-permute-start(bf16[128,2,256]{0,2,1:T(8,128)(2,1)S(1)} %collective-permute-done.4), channel_id=1, source_target_pairs={{0,1},{1,2},{2,3},{4,5},{5,6},{6,7},{8,9},{9,10},{10,11},{12,13},{... | collective-permute-start | bytes 393224 | tf_op jit(solution)/shard_map/ppermute | solution.py:63
  50.6 0.6 collective-permute-start.15
  51.2 0.5 collective-permute-start.13
  51.7 1.3 %collective-permute-done.5 = bf16[128,2,256]{0,2,1:T(8,128)(2,1)S(1)} collective-permute-done((bf16[128,2,256]{0,2,1:T(8,128)(2,1)S(1)}, bf16[128,2,256]{0,2,1:T(8,128)(2,1)S(1)}, u32[]{:S(2)}, u32[]{:S(2)}) %collective-permute-start.5) | collective-permute-done | bytes 131104 | tf_op jit(solution)/shard_map/ppermute | solution.py:63
  53.0 0.3 collective-permute-done.17
  53.3 0.3 collective-permute-start.18
  53.7 5.1 %collective-permute-done.15 = bf16[32,5120]{1,0:T(8,128)(2,1)S(1)} collective-permute-done((bf16[32,5120]{1,0:T(8,128)(2,1)S(1)}, bf16[32,5120]{1,0:T(8,128)(2,1)S(1)}, u32[]{:S(2)}, u32[]{:S(2)}) %collective-permute-start.15) | collective-permute-done | bytes 327712 | tf_op jit(solution)/shard_map/ppermute | solution.py:79
  58.7 2.2 %collective-permute-start = (bf16[128,1280]{1,0:T(8,128)(2,1)S(1)}, bf16[128,1280]{1,0:T(8,128)(2,1)}, u32[]{:S(2)}, u32[]{:S(2)}) collective-permute-start(bf16[128,1280]{1,0:T(8,128)(2,1)S(1)} %get-tuple-element.23), channel_id=1, source_target_pairs={{0,1},{1,0},{2,3},{3,2},{4,5},{5,4},{6,7},{7,6},{8,9},{9,8},{10,11... | collective-permute-start | bytes 983048 | tf_op jit(solution)/shard_map/ppermute | solution.py:75
  61.0 0.6 fusion.27
  61.6 1.4 %collective-permute-start.2 = (bf16[128,1280]{1,0:T(8,128)(2,1)S(1)}, bf16[128,1280]{1,0:T(8,128)(2,1)}, u32[]{:S(2)}, u32[]{:S(2)}) collective-permute-start(bf16[128,1280]{1,0:T(8,128)(2,1)S(1)} %get-tuple-element.24), channel_id=1, source_target_pairs={{0,3},{1,2},{2,1},{3,0},{4,7},{5,6},{6,5},{7,4},{8,11},{9,10},{10,... | collective-permute-start | bytes 983048 | tf_op jit(solution)/shard_map/ppermute | solution.py:75
  63.2 0.6 fusion.36
  63.8 0.6 fusion.33
  64.4 0.2 collective-permute-done.14
  64.6 0.6 fusion.30
  65.4 1.5 %fusion.90 = (f32[4,128]{1,0:T(4,128)S(1)}, f32[4,128,512]{2,1,0:T(8,128)}) fusion(bf16[4,64,128]{2,1,0:T(8,128)(2,1)S(1)} %bitcast.160, bf16[512,4,64]{0,2,1:T(8,128)(2,1)S(1)} %bitcast.152, pred[128,512]{1,0:T(8,128)(4,1)S(1)} %fusion.64), kind=kOutput, calls=%fused_computation.131 | convolution fusion | flops 34603520 | bytes 1443840 | tf_op jit(solution)/shard_map/sub | solution.py:115
  66.8 1.6 %fusion.26 = f32[4,128]{1,0:T(4,128)S(1)} fusion(bf16[512,4,64]{0,2,1:T(8,128)(2,1)S(1)} %bitcast.150, f32[4,128,512]{2,1,0:T(8,128)} %get-tuple-element.31, f32[4,128]{1,0:T(4,128)S(1)} %get-tuple-element.30, bf16[128,4,64]{0,2,1:T(8,128)(2,1)S(1)} %bitcast.154), kind=kOutput, calls=%fused_computation.32 | convolution fusion | flops 34176512 | bytes 1380352 | tf_op jit(solution)/shard_map/hqk,khd->hqd/dot_general | solution.py:117
  68.5 1.8 %fusion.25 = bf16[4,64,128]{2,1,0:T(8,128)(2,1)S(1)} fusion(bf16[512,4,64]{0,2,1:T(8,128)(2,1)S(1)} %bitcast.153, bf16[512,4,64]{0,2,1:T(8,128)(2,1)S(1)} %bitcast.151, bf16[128,4,64]{0,2,1:T(8,128)(2,1)S(1)} %bitcast.155, f32[4,128]{1,0:T(4,128)S(1)} %fusion.26, f32[4,128,512]{2,1,0:T(8,128)} %get-tuple-element.31, f32[4,128]{1,0:T(4,128)S(1)} %get-tuple-element.30), kind=kOutput, calls=%fused_computation.31 | convolution fusion | flops 68222976 | bytes 1708032 | tf_op jit(solution)/shard_map/hqk,khd->qhd/dot_general | solution.py:124
  70.3 2.6 %collective-permute-start.21 = (bf16[128,256]{0,1:T(8,128)(2,1)S(1)}, bf16[128,256]{0,1:T(8,128)(2,1)S(1)}, u32[]{:S(2)}, u32[]{:S(2)}) collective-permute-start(bf16[128,256]{0,1:T(8,128)(2,1)S(1)} %bitcast.161), channel_id=1, source_target_pairs={{0,3},{1,2},{2,1},{3,0},{4,7},{5,6},{6,5},{7,4},{8,11},{9,10},{10,... | collective-permute-start | bytes 196616 | tf_op jit(solution)/shard_map/ppermute | solution.py:130
  72.9 1.9 %collective-permute-start.19 = (bf16[128,256]{0,1:T(8,128)(2,1)S(1)}, bf16[128,256]{0,1:T(8,128)(2,1)S(1)}, u32[]{:S(2)}, u32[]{:S(2)}) collective-permute-start(bf16[128,256]{0,1:T(8,128)(2,1)S(1)} %bitcast.163), channel_id=1, source_target_pairs={{0,1},{1,0},{2,3},{3,2},{4,5},{5,4},{6,7},{7,6},{8,9},{9,8},{10,11... | collective-permute-start | bytes 196616 | tf_op jit(solution)/shard_map/ppermute | solution.py:130
  75.0 0.2 copy.19
  75.3 1.9 %collective-permute-done.2 = bf16[128,1280]{1,0:T(8,128)(2,1)} collective-permute-done((bf16[128,1280]{1,0:T(8,128)(2,1)S(1)}, bf16[128,1280]{1,0:T(8,128)(2,1)}, u32[]{:S(2)}, u32[]{:S(2)}) %collective-permute-start.2) | collective-permute-done | bytes 327712 | tf_op jit(solution)/shard_map/ppermute | solution.py:75
  77.2 1.2 %collective-permute-done.21 = bf16[128,256]{0,1:T(8,128)(2,1)S(1)} collective-permute-done((bf16[128,256]{0,1:T(8,128)(2,1)S(1)}, bf16[128,256]{0,1:T(8,128)(2,1)S(1)}, u32[]{:S(2)}, u32[]{:S(2)}) %collective-permute-start.21) | collective-permute-done | bytes 65568 | tf_op jit(solution)/shard_map/ppermute | solution.py:130
  78.5 5.4 %collective-permute-done.20 = bf16[128,256]{0,1:T(8,128)(2,1)S(1)} collective-permute-done((bf16[128,256]{0,1:T(8,128)(2,1)S(1)}, bf16[128,256]{0,1:T(8,128)(2,1)S(1)}, u32[]{:S(2)}, u32[]{:S(2)}) %collective-permute-start.20) | collective-permute-done | bytes 65568 | tf_op jit(solution)/shard_map/ppermute | solution.py:130
  83.8 2.2 %convert_bitcast_fusion = (bf16[1,1280,256]{1,2,0:T(8,128)(2,1)S(1)}, bf16[1280,256]{0,1:T(8,128)(2,1)S(1)}, bf16[1,1280,256]{1,2,0:T(8,128)(2,1)S(1)}) fusion(bf16[1,1280,256]{1,2,0:T(8,128)(2,1)S(1)} %copy.19, bf16[1,1280,256]{1,2,0:T(8,128)(2,1)S(1)} %copy.16, bf16[128,1280]{1,0:T(8,128)(2,1)} %collective-permute-done.2, ...), kind=kOutput, calls=%fused_computation.52 | convolution fusion | flops 347078656 | bytes 4849664 | tf_op jit(solution)/shard_map/dot_general | solution.py:133
  86.2 1.6 %collective-permute-done.22 = bf16[4,32,1280]{2,1,0:T(8,128)(2,1)S(1)} collective-permute-done((bf16[4,32,1280]{2,1,0:T(8,128)(2,1)S(1)}, bf16[4,32,1280]{2,1,0:T(8,128)(2,1)S(1)}, u32[]{:S(2)}, u32[]{:S(2)}) %collective-permute-start.22) | collective-permute-done | bytes 327712 | tf_op jit(solution)/shard_map/ppermute | solution.py:150
  88.0 1.5 %collective-permute-start.23 = (bf16[32,1280]{1,0:T(8,128)(2,1)S(1)}, bf16[32,1280]{1,0:T(8,128)(2,1)S(1)}, u32[]{:S(2)}, u32[]{:S(2)}) collective-permute-start(bf16[32,1280]{1,0:T(8,128)(2,1)S(1)} %get-tuple-element.27), channel_id=1, source_target_pairs={{0,8},{4,12},{8,0},{12,4},{16,24},{20,28},{24,16},{28,20},{1,9},{5... | collective-permute-start | bytes 245768 | tf_op jit(solution)/shard_map/ppermute | solution.py:155
  89.5 1.5 %collective-permute-start.25 = (bf16[32,1280]{1,0:T(8,128)(2,1)S(1)}, bf16[32,1280]{1,0:T(8,128)(2,1)S(1)}, u32[]{:S(2)}, u32[]{:S(2)}) collective-permute-start(bf16[32,1280]{1,0:T(8,128)(2,1)S(1)} %get-tuple-element.28), channel_id=1, source_target_pairs={{0,24},{4,28},{8,16},{12,20},{16,8},{20,12},{24,0},{28,4},{1,25},{... | collective-permute-start | bytes 245768 | tf_op jit(solution)/shard_map/ppermute | solution.py:155
  91.0 0.6 collective-permute-start.24
  91.5 1.1 %copy.21 = bf16[1,1280,256]{2,1,0:T(8,128)(2,1)} copy(bf16[1,1280,256]{1,2,0:T(8,128)(2,1)S(1)} %get-tuple-element.18) | data formatting | bytes 1310720
  92.6 1.1 %copy.20 = bf16[1,1280,256]{2,1,0:T(8,128)(2,1)} copy(bf16[1,1280,256]{1,2,0:T(8,128)(2,1)S(1)} %get-tuple-element.20) | data formatting | bytes 1310720
  93.7 1.6 %collective-permute-done.25 = bf16[32,1280]{1,0:T(8,128)(2,1)S(1)} collective-permute-done((bf16[32,1280]{1,0:T(8,128)(2,1)S(1)}, bf16[32,1280]{1,0:T(8,128)(2,1)S(1)}, u32[]{:S(2)}, u32[]{:S(2)}) %collective-permute-start.25) | collective-permute-done | bytes 81952 | tf_op jit(solution)/shard_map/ppermute | solution.py:155
  95.3 1.2 %collective-permute-done.24 = bf16[32,1280]{1,0:T(8,128)(2,1)S(1)} collective-permute-done((bf16[32,1280]{1,0:T(8,128)(2,1)S(1)}, bf16[32,1280]{1,0:T(8,128)(2,1)S(1)}, u32[]{:S(2)}, u32[]{:S(2)}) %collective-permute-start.24) | collective-permute-done | bytes 81952 | tf_op jit(solution)/shard_map/ppermute | solution.py:155
  96.5 0.8 fusion.66
  (56 shorter events, 1.3 us)
Async XLA Ops:
  1.6 17.5 %collective-permute-start.6 = (bf16[32,1280]{1,0:T(8,128)(2,1)S(1)}, bf16[32,1280]{1,0:T(8,128)(2,1)S(1)}, u32[]{:S(2)}, u32[]{:S(2)}) collective-permute-start(bf16[32,1280]{1,0:T(8,128)(2,1)S(1)} %get-tuple-element.17), channel_id=1, source_target_pairs={{0,1},{1,2},{2,3},{4,5},{5,6},{6,7},{8,9},{9,10},{10,11},{12,13},{... | collective-permute-start | bytes 245768 | tf_op jit(solution)/shard_map/ppermute | solution.py:60
  6.5 11.0 %collective-permute-start.7 = (bf16[32,1280]{1,0:T(8,128)(2,1)S(1)}, bf16[32,1280]{1,0:T(8,128)(2,1)S(1)}, u32[]{:S(2)}, u32[]{:S(2)}) collective-permute-start(bf16[32,1280]{1,0:T(8,128)(2,1)S(1)} %get-tuple-element.17), channel_id=1, source_target_pairs={{1,0},{2,1},{3,2},{5,4},{6,5},{7,6},{9,8},{10,9},{11,10},{13,12},{... | collective-permute-start | bytes 245768 | tf_op jit(solution)/shard_map/ppermute | solution.py:61
  8.9 16.5 %collective-permute-start.3 = (bf16[128,2,256]{0,2,1:T(8,128)(2,1)S(1)}, bf16[128,2,256]{0,2,1:T(8,128)(2,1)S(1)}, u32[]{:S(2)}, u32[]{:S(2)}) collective-permute-start(bf16[128,2,256]{0,2,1:T(8,128)(2,1)S(1)} %bitcast.148), channel_id=1, source_target_pairs={{0,1},{1,2},{2,3},{4,5},{5,6},{6,7},{8,9},{9,10},{10,11},{12,13},{... | collective-permute-start | bytes 393224 | tf_op jit(solution)/shard_map/ppermute | solution.py:63
  13.5 5.5 %copy-start.5 = (bf16[1,128,256]{2,1,0:T(8,128)(2,1)S(1)}, bf16[1,128,256]{2,1,0:T(8,128)(2,1)}, u32[]{:S(2)}) copy-start(bf16[1,128,256]{2,1,0:T(8,128)(2,1)} %param.9) | copy-start | bytes 196612
  14.9 58.0 %collective-permute-start.1 = (bf16[128,1280]{1,0:T(8,128)(2,1)S(1)}, bf16[128,1280]{1,0:T(8,128)(2,1)S(1)}, u32[]{:S(2)}, u32[]{:S(2)}) collective-permute-start(bf16[128,1280]{1,0:T(8,128)(2,1)S(1)} %get-tuple-element.22), channel_id=1, source_target_pairs={{0,2},{1,3},{2,0},{3,1},{4,6},{5,7},{6,4},{7,5},{8,10},{9,11},{10,... | collective-permute-start | bytes 983048 | tf_op jit(solution)/shard_map/ppermute | solution.py:75
  17.5 6.6 %collective-permute-start.8 = (bf16[32,1280]{1,0:T(8,128)(2,1)S(1)}, bf16[32,1280]{1,0:T(8,128)(2,1)S(1)}, u32[]{:S(2)}, u32[]{:S(2)}) collective-permute-start(bf16[32,1280]{1,0:T(8,128)(2,1)S(1)} %collective-permute-done.7), channel_id=1, source_target_pairs={{1,0},{2,1},{3,2},{5,4},{6,5},{7,6},{9,8},{10,9},{11,10},{13,12},{... | collective-permute-start | bytes 245768 | tf_op jit(solution)/shard_map/ppermute | solution.py:61
  19.1 18.6 %collective-permute-start.10 = (bf16[32,1280]{1,0:T(8,128)(2,1)S(1)}, bf16[32,1280]{1,0:T(8,128)(2,1)S(1)}, u32[]{:S(2)}, u32[]{:S(2)}) collective-permute-start(bf16[32,1280]{1,0:T(8,128)(2,1)S(1)} %collective-permute-done.6), channel_id=1, source_target_pairs={{0,1},{1,2},{2,3},{4,5},{5,6},{6,7},{8,9},{9,10},{10,11},{12,13},{... | collective-permute-start | bytes 245768 | tf_op jit(solution)/shard_map/ppermute | solution.py:60
  24.1 17.5 %collective-permute-start.9 = (bf16[32,1280]{1,0:T(8,128)(2,1)S(1)}, bf16[32,1280]{1,0:T(8,128)(2,1)S(1)}, u32[]{:S(2)}, u32[]{:S(2)}) collective-permute-start(bf16[32,1280]{1,0:T(8,128)(2,1)S(1)} %collective-permute-done.8), channel_id=1, source_target_pairs={{1,0},{2,1},{3,2},{5,4},{6,5},{7,6},{9,8},{10,9},{11,10},{13,12},{... | collective-permute-start | bytes 245768 | tf_op jit(solution)/shard_map/ppermute | solution.py:61
  25.4 20.7 %collective-permute-start.4 = (bf16[128,2,256]{0,2,1:T(8,128)(2,1)S(1)}, bf16[128,2,256]{0,2,1:T(8,128)(2,1)S(1)}, u32[]{:S(2)}, u32[]{:S(2)}) collective-permute-start(bf16[128,2,256]{0,2,1:T(8,128)(2,1)S(1)} %collective-permute-done.3), channel_id=1, source_target_pairs={{0,1},{1,2},{2,3},{4,5},{5,6},{6,7},{8,9},{9,10},{10,11},{12,13},{... | collective-permute-start | bytes 393224 | tf_op jit(solution)/shard_map/ppermute | solution.py:63
  37.7 6.0 %collective-permute-start.11 = (bf16[32,1280]{1,0:T(8,128)(2,1)S(1)}, bf16[32,1280]{1,0:T(8,128)(2,1)S(1)}, u32[]{:S(2)}, u32[]{:S(2)}) collective-permute-start(bf16[32,1280]{1,0:T(8,128)(2,1)S(1)} %collective-permute-done.10), channel_id=1, source_target_pairs={{0,1},{1,2},{2,3},{4,5},{5,6},{6,7},{8,9},{9,10},{10,11},{12,13},{... | collective-permute-start | bytes 245768 | tf_op jit(solution)/shard_map/ppermute | solution.py:60
  41.6 19.3 %copy-start = (bf16[1,128,5120]{2,1,0:T(8,128)(2,1)S(1)}, bf16[1,128,5120]{2,1,0:T(8,128)(2,1)}, u32[]{:S(2)}) copy-start(bf16[1,128,5120]{2,1,0:T(8,128)(2,1)} %param.7) | copy-start | bytes 3932164
  43.7 9.7 %collective-permute-start.17 = (bf16[32,5120]{1,0:T(8,128)(2,1)S(1)}, bf16[32,5120]{1,0:T(8,128)(2,1)S(1)}, u32[]{:S(2)}, u32[]{:S(2)}) collective-permute-start(bf16[32,5120]{1,0:T(8,128)(2,1)S(1)} %select_dynamic-update-slice_fusion), channel_id=1, source_target_pairs={{0,24},{4,28},{8,16},{12,20},{16,8},{20,12},{24,0},{28,4},{1,25},{... | collective-permute-start | bytes 983048 | tf_op jit(solution)/shard_map/ppermute | solution.py:79
  46.2 6.8 %collective-permute-start.5 = (bf16[128,2,256]{0,2,1:T(8,128)(2,1)S(1)}, bf16[128,2,256]{0,2,1:T(8,128)(2,1)S(1)}, u32[]{:S(2)}, u32[]{:S(2)}) collective-permute-start(bf16[128,2,256]{0,2,1:T(8,128)(2,1)S(1)} %collective-permute-done.4), channel_id=1, source_target_pairs={{0,1},{1,2},{2,3},{4,5},{5,6},{6,7},{8,9},{9,10},{10,11},{12,13},{... | collective-permute-start | bytes 393224 | tf_op jit(solution)/shard_map/ppermute | solution.py:63
  50.6 8.2 %collective-permute-start.15 = (bf16[32,5120]{1,0:T(8,128)(2,1)S(1)}, bf16[32,5120]{1,0:T(8,128)(2,1)S(1)}, u32[]{:S(2)}, u32[]{:S(2)}) collective-permute-start(bf16[32,5120]{1,0:T(8,128)(2,1)S(1)} %select_dynamic-update-slice_fusion), channel_id=1, source_target_pairs={{0,16},{4,20},{8,24},{12,28},{16,0},{20,4},{24,8},{28,12},{1,17},{... | collective-permute-start | bytes 983048 | tf_op jit(solution)/shard_map/ppermute | solution.py:79
  51.2 10.4 %collective-permute-start.13 = (bf16[32,5120]{1,0:T(8,128)(2,1)S(1)}, bf16[32,5120]{1,0:T(8,128)(2,1)S(1)}, u32[]{:S(2)}, u32[]{:S(2)}) collective-permute-start(bf16[32,5120]{1,0:T(8,128)(2,1)S(1)} %select_dynamic-update-slice_fusion), channel_id=1, source_target_pairs={{0,8},{4,12},{8,0},{12,4},{16,24},{20,28},{24,16},{28,20},{1,9},{5... | collective-permute-start | bytes 983048 | tf_op jit(solution)/shard_map/ppermute | solution.py:79
  53.0 8.0 %collective-permute-start.12 = (bf16[32,5120]{1,0:T(8,128)(2,1)S(1)}, bf16[32,5120]{1,0:T(8,128)(2,1)S(1)}, u32[]{:S(2)}, u32[]{:S(2)}) collective-permute-start(bf16[32,5120]{1,0:T(8,128)(2,1)S(1)} %select_dynamic-update-slice_fusion), channel_id=1, source_target_pairs={{0,4},{4,0},{8,12},{12,8},{16,20},{20,16},{24,28},{28,24},{1,5},{5... | collective-permute-start | bytes 983048 | tf_op jit(solution)/shard_map/ppermute | solution.py:82
  53.3 9.6 %collective-permute-start.18 = (bf16[32,5120]{1,0:T(8,128)(2,1)S(1)}, bf16[32,5120]{1,0:T(8,128)(2,1)S(1)}, u32[]{:S(2)}, u32[]{:S(2)}) collective-permute-start(bf16[32,5120]{1,0:T(8,128)(2,1)S(1)} %collective-permute-done.17), channel_id=1, source_target_pairs={{0,4},{4,0},{8,12},{12,8},{16,20},{20,16},{24,28},{28,24},{1,5},{5... | collective-permute-start | bytes 983048 | tf_op jit(solution)/shard_map/ppermute | solution.py:82
  58.7 16.5 %collective-permute-start = (bf16[128,1280]{1,0:T(8,128)(2,1)S(1)}, bf16[128,1280]{1,0:T(8,128)(2,1)}, u32[]{:S(2)}, u32[]{:S(2)}) collective-permute-start(bf16[128,1280]{1,0:T(8,128)(2,1)S(1)} %get-tuple-element.23), channel_id=1, source_target_pairs={{0,1},{1,0},{2,3},{3,2},{4,5},{5,4},{6,7},{7,6},{8,9},{9,8},{10,11... | collective-permute-start | bytes 983048 | tf_op jit(solution)/shard_map/ppermute | solution.py:75
  61.0 2.8 %collective-permute-start.16 = (bf16[32,5120]{1,0:T(8,128)(2,1)S(1)}, bf16[32,5120]{1,0:T(8,128)(2,1)S(1)}, u32[]{:S(2)}, u32[]{:S(2)}) collective-permute-start(bf16[32,5120]{1,0:T(8,128)(2,1)S(1)} %collective-permute-done.15), channel_id=1, source_target_pairs={{0,4},{4,0},{8,12},{12,8},{16,20},{20,16},{24,28},{28,24},{1,5},{5... | collective-permute-start | bytes 983048 | tf_op jit(solution)/shard_map/ppermute | solution.py:82
  61.6 15.6 %collective-permute-start.2 = (bf16[128,1280]{1,0:T(8,128)(2,1)S(1)}, bf16[128,1280]{1,0:T(8,128)(2,1)}, u32[]{:S(2)}, u32[]{:S(2)}) collective-permute-start(bf16[128,1280]{1,0:T(8,128)(2,1)S(1)} %get-tuple-element.24), channel_id=1, source_target_pairs={{0,3},{1,2},{2,1},{3,0},{4,7},{5,6},{6,5},{7,4},{8,11},{9,10},{10,... | collective-permute-start | bytes 983048 | tf_op jit(solution)/shard_map/ppermute | solution.py:75
  63.0 1.6 %collective-permute-start.14 = (bf16[32,5120]{1,0:T(8,128)(2,1)S(1)}, bf16[32,5120]{1,0:T(8,128)(2,1)S(1)}, u32[]{:S(2)}, u32[]{:S(2)}) collective-permute-start(bf16[32,5120]{1,0:T(8,128)(2,1)S(1)} %collective-permute-done.13), channel_id=1, source_target_pairs={{0,4},{4,0},{8,12},{12,8},{16,20},{20,16},{24,28},{28,24},{1,5},{5... | collective-permute-start | bytes 983048 | tf_op jit(solution)/shard_map/ppermute | solution.py:82
  68.4 6.3 %copy-start.1 = (bf16[1,1280,256]{2,1,0:T(8,128)(2,1)S(1)}, bf16[1,1280,256]{2,1,0:T(8,128)(2,1)}, u32[]{:S(2)}) copy-start(bf16[1,1280,256]{2,1,0:T(8,128)(2,1)} %param.10) | copy-start | bytes 1966084
  70.3 4.7 %copy-start.2 = (bf16[1,1280,256]{2,1,0:T(8,128)(2,1)S(1)}, bf16[1,1280,256]{2,1,0:T(8,128)(2,1)}, u32[]{:S(2)}) copy-start(bf16[1,1280,256]{2,1,0:T(8,128)(2,1)} %param.11) | copy-start | bytes 1966084
  70.3 8.1 %collective-permute-start.21 = (bf16[128,256]{0,1:T(8,128)(2,1)S(1)}, bf16[128,256]{0,1:T(8,128)(2,1)S(1)}, u32[]{:S(2)}, u32[]{:S(2)}) collective-permute-start(bf16[128,256]{0,1:T(8,128)(2,1)S(1)} %bitcast.161), channel_id=1, source_target_pairs={{0,3},{1,2},{2,1},{3,0},{4,7},{5,6},{6,5},{7,4},{8,11},{9,10},{10,... | collective-permute-start | bytes 196616 | tf_op jit(solution)/shard_map/ppermute | solution.py:130
  72.9 11.0 %collective-permute-start.20 = (bf16[128,256]{0,1:T(8,128)(2,1)S(1)}, bf16[128,256]{0,1:T(8,128)(2,1)S(1)}, u32[]{:S(2)}, u32[]{:S(2)}) collective-permute-start(bf16[128,256]{0,1:T(8,128)(2,1)S(1)} %bitcast.162), channel_id=1, source_target_pairs={{0,2},{1,3},{2,0},{3,1},{4,6},{5,7},{6,4},{7,5},{8,10},{9,11},{10,... | collective-permute-start | bytes 196616 | tf_op jit(solution)/shard_map/ppermute | solution.py:130
  72.9 11.0 %collective-permute-start.19 = (bf16[128,256]{0,1:T(8,128)(2,1)S(1)}, bf16[128,256]{0,1:T(8,128)(2,1)S(1)}, u32[]{:S(2)}, u32[]{:S(2)}) collective-permute-start(bf16[128,256]{0,1:T(8,128)(2,1)S(1)} %bitcast.163), channel_id=1, source_target_pairs={{0,1},{1,0},{2,3},{3,2},{4,5},{5,4},{6,7},{7,6},{8,9},{9,8},{10,11... | collective-permute-start | bytes 196616 | tf_op jit(solution)/shard_map/ppermute | solution.py:130
  86.1 1.7 %collective-permute-start.22 = (bf16[4,32,1280]{2,1,0:T(8,128)(2,1)S(1)}, bf16[4,32,1280]{2,1,0:T(8,128)(2,1)S(1)}, u32[]{:S(2)}, u32[]{:S(2)}) collective-permute-start(bf16[4,32,1280]{2,1,0:T(8,128)(2,1)S(1)} %dynamic-slice_bitcast_fusion), channel_id=1, source_target_pairs={{0,4},{4,0},{8,12},{12,8},{16,20},{20,16},{24,28},{28,24},{1,5},{5... | collective-permute-start | bytes 983048 | tf_op jit(solution)/shard_map/ppermute | solution.py:150
  88.0 5.7 %collective-permute-start.23 = (bf16[32,1280]{1,0:T(8,128)(2,1)S(1)}, bf16[32,1280]{1,0:T(8,128)(2,1)S(1)}, u32[]{:S(2)}, u32[]{:S(2)}) collective-permute-start(bf16[32,1280]{1,0:T(8,128)(2,1)S(1)} %get-tuple-element.27), channel_id=1, source_target_pairs={{0,8},{4,12},{8,0},{12,4},{16,24},{20,28},{24,16},{28,20},{1,9},{5... | collective-permute-start | bytes 245768 | tf_op jit(solution)/shard_map/ppermute | solution.py:155
  89.5 5.8 %collective-permute-start.25 = (bf16[32,1280]{1,0:T(8,128)(2,1)S(1)}, bf16[32,1280]{1,0:T(8,128)(2,1)S(1)}, u32[]{:S(2)}, u32[]{:S(2)}) collective-permute-start(bf16[32,1280]{1,0:T(8,128)(2,1)S(1)} %get-tuple-element.28), channel_id=1, source_target_pairs={{0,24},{4,28},{8,16},{12,20},{16,8},{20,12},{24,0},{28,4},{1,25},{... | collective-permute-start | bytes 245768 | tf_op jit(solution)/shard_map/ppermute | solution.py:155
  91.0 5.5 %collective-permute-start.24 = (bf16[32,1280]{1,0:T(8,128)(2,1)S(1)}, bf16[32,1280]{1,0:T(8,128)(2,1)S(1)}, u32[]{:S(2)}, u32[]{:S(2)}) collective-permute-start(bf16[32,1280]{1,0:T(8,128)(2,1)S(1)} %get-tuple-element.29), channel_id=1, source_target_pairs={{0,16},{4,20},{8,24},{12,28},{16,0},{20,4},{24,8},{28,12},{1,17},{... | collective-permute-start | bytes 245768 | tf_op jit(solution)/shard_map/ppermute | solution.py:155
  91.5 5.0 %copy-start.3 = (f32[1280,32]{0,1:T(8,128)S(1)}, f32[1280,32]{0,1:T(8,128)}, u32[]{:S(2)}) copy-start(f32[1280,32]{0,1:T(8,128)} %param.12) | copy-start | bytes 491524
  91.5 5.0 %copy-start.4 = (f32[1280,32]{0,1:T(8,128)S(1)}, f32[1280,32]{0,1:T(8,128)}, u32[]{:S(2)}) copy-start(f32[1280,32]{0,1:T(8,128)} %param.13) | copy-start | bytes 491524

commit v2 on v1

v2 whole, which is shorter than its diff:
```python
import functools

import jax
import jax.numpy as jnp
from jax import lax
from jax.experimental import pallas as pl
from jax.experimental.pallas import tpu as pltpu
from jax.sharding import PartitionSpec as P

HD = 64

inner_rate = 0.1
beta_one = 0.9
beta_two = 0.95
adam_eps = 1e-08
outer_rate = 0.7
outer_beta = 0.9


def pair_perm(size, step, stride=1):
    return [
        (group * stride + inner, (group ^ step) * stride + inner)
        for group in range(size)
        for inner in range(stride)
    ]


def exchange_gather(own, axis, size, stride=1):
    blocks = [own] + [None] * (size - 1)
    order = sorted(range(1, size), key=lambda k: (bin(k).count("1"), -k))
    for k in order:
        low = k & -k
        blocks[k] = lax.ppermute(blocks[k ^ low], axis, pair_perm(size, low, stride))
    return blocks


def attention_kernel(n_seq, rows, head_size, *refs):
    kv_refs, (query_ref, cot_ref, out_ref) = refs[: 2 * n_seq], refs[2 * n_seq :]
    seq = lax.axis_index("seq")
    cols = query_ref.shape[0]
    heads = cols // head_size
    wide = heads * rows
    scale = head_size**-0.5
    head_of_row = lax.broadcasted_iota(jnp.int32, (cols, wide), 0) // head_size
    head_of_col = lax.broadcasted_iota(jnp.int32, (cols, wide), 1) // rows
    diagonal = head_of_row == head_of_col

    def spread(matrix):
        tiled = jnp.concatenate([matrix] * heads, axis=1)
        return jnp.where(diagonal, tiled, 0.0).astype(jnp.bfloat16)

    query = spread(query_ref[...])
    cot = spread(cot_ref[...].astype(jnp.float32).T)
    key_row = lax.broadcasted_iota(jnp.int32, (rows, wide), 0)
    query_row = lax.rem(lax.broadcasted_iota(jnp.int32, (rows, wide), 1), rows) + seq * rows
    scores = []
    for k in range(n_seq):
        block = jnp.dot(kv_refs[2 * k][...], query, preferred_element_type=jnp.float32) * scale
        seen = query_row >= key_row + jnp.bitwise_xor(seq, k) * rows
        scores.append(jnp.where(seen, block, -1e30))
    peak = functools.reduce(jnp.maximum, [jnp.max(s, axis=0, keepdims=True) for s in scores])
    expons = [jnp.exp(s - peak) for s in scores]
    inverse = 1.0 / sum(jnp.sum(e, axis=0, keepdims=True) for e in expons)
    attend = [e * inverse for e in expons]
    dattend = [
        jnp.dot(kv_refs[2 * k + 1][...], cot, preferred_element_type=jnp.float32)
        for k in range(n_seq)
    ]
    rowdot = sum(
        jnp.sum(a.astype(jnp.bfloat16).astype(jnp.float32) * d, axis=0, keepdims=True)
        for a, d in zip(attend, dattend)
    )
    total = jnp.zeros((cols, wide), jnp.float32)
    for k in range(n_seq):
        dscore = (attend[k] * (dattend[k] - rowdot)).astype(jnp.bfloat16)
        total = total + lax.dot_general(
            kv_refs[2 * k][...],
            dscore,
            (((0,), (0,)), ((), ())),
            preferred_element_type=jnp.float32,
        )
    for h in range(heads):
        part = total[h * head_size : (h + 1) * head_size, h * rows : (h + 1) * rows] * scale
        out_ref[h * head_size : (h + 1) * head_size, :] = part.astype(jnp.bfloat16)


def attention(kv, queries, cot, cols):
    n_seq, rows = len(kv), cot.shape[0]
    group = min(cols, 4 * HD)
    groups = cols // group
    in_specs = []
    operands = []
    for block in kv:
        in_specs.append(pl.BlockSpec((rows, group), lambda g: (0, g)))
        in_specs.append(pl.BlockSpec((rows, group), lambda g: (0, g + groups)))
        operands += [block, block]
    in_specs.append(pl.BlockSpec((group, rows), lambda g: (g, 0)))
    in_specs.append(pl.BlockSpec((rows, group), lambda g: (0, g)))
    length = n_seq * rows
    return pl.pallas_call(
        functools.partial(attention_kernel, n_seq, rows, HD),
        grid=(groups,),
        in_specs=in_specs,
        out_specs=pl.BlockSpec((group, rows), lambda g: (g, 0)),
        out_shape=jax.ShapeDtypeStruct((cols, rows), jnp.bfloat16),
        compiler_params=pltpu.CompilerParams(vmem_limit_bytes=48 * 1024 * 1024),
        cost_estimate=pl.CostEstimate(
            flops=6 * length * cols * (group // HD) * rows,
            bytes_accessed=4 * length * cols + 8 * cols * rows,
            transcendentals=length * rows * (cols // HD),
        ),
    )(*operands, queries, cot)


def on_device(states, key_vals, cotangent, first_moment, second_moment, anchor, outer_momentum):
    n_seq = lax.axis_size("seq")
    n_island = lax.axis_size("island")
    n_chip = n_island // 2
    seq = lax.axis_index("seq")
    island = lax.axis_index("island")
    chip, core = island // 2, lax.rem(island, 2)
    tokens = states[0]
    rows, features = tokens.shape
    block = features // n_seq
    share = anchor.shape[1]
    cols = first_moment.shape[2]
    inverse = features ** (-0.5)
    swap = pair_perm(n_island, 1)

    own_weight = anchor.T.astype(jnp.bfloat16)
    weights = exchange_gather(own_weight, "seq", n_seq)
    kv = exchange_gather(key_vals[0].reshape(rows, 2 * cols), "seq", n_seq)
    column = jnp.zeros((share, features), jnp.bfloat16)
    for k in range(n_seq):
        column = lax.dynamic_update_slice(
            column, weights[k], (0, jnp.bitwise_xor(seq, k) * block)
        )

    sliced = tokens.reshape(rows, n_seq, block).transpose(1, 0, 2)
    if BARRIER:
        sliced, _ = lax.optimization_barrier((sliced, [weights[1 << j] for j in range(n_seq.bit_length() - 1)]))
    gathered = lax.all_to_all(sliced, "seq", split_axis=0, concat_axis=0, tiled=True)
    gathered = gathered.reshape(n_seq * rows, block)

    query_parts = []
    for step in range(n_chip):
        mine = (
            lax.ppermute(column, "island", pair_perm(n_chip, step, 2)) if step else column
        )
        theirs = lax.ppermute(mine, "island", swap)
        both = jnp.concatenate([mine, theirs], 0)
        query_parts.append(
            lax.dot_general(
                both, tokens, (((1,), (1,)), ((), ())), preferred_element_type=jnp.float32
            )
            * inverse
        )
    rel = jnp.stack(query_parts).reshape(n_chip, 2, share, rows)
    ordered = []
    for at in range(n_island):
        where = (jnp.bitwise_xor(chip, at // 2), jnp.bitwise_xor(core, at % 2), 0, 0)
        ordered.append(lax.dynamic_slice(rel, where, (1, 1, share, rows))[0, 0])
    queries = jnp.concatenate(ordered, 0)

    dquery = attention(kv, queries, cotangent[0], cols)
    dqueries = exchange_gather(dquery, "seq", n_seq)
    by_token = jnp.zeros((cols, n_seq * rows), jnp.bfloat16)
    for k in range(n_seq):
        by_token = lax.dynamic_update_slice(
            by_token, dqueries[k], (0, jnp.bitwise_xor(seq, k) * rows)
        )

    gradient = jnp.dot(by_token, gathered, preferred_element_type=jnp.float32) * inverse
    first = beta_one * first_moment[0].T.astype(jnp.float32) + (1.0 - beta_one) * gradient
    second = (
        beta_two * second_moment[0].T.astype(jnp.float32) + (1.0 - beta_two) * gradient * gradient
    )
    delta = (inner_rate * first / (jnp.sqrt(second) + adam_eps)).astype(jnp.bfloat16)

    parts = delta.reshape(n_chip, 2, share, block)
    other = lax.dynamic_index_in_dim(parts, 1 - core, 1, keepdims=False)
    same = lax.dynamic_index_in_dim(parts, core, 1, keepdims=False)
    paired = same.astype(jnp.float32) + lax.ppermute(other, "island", swap).astype(jnp.float32)
    total = lax.dynamic_index_in_dim(paired, chip, 0, keepdims=False)
    paired = paired.astype(jnp.bfloat16)
    for step in range(1, n_chip):
        piece = lax.dynamic_index_in_dim(paired, jnp.bitwise_xor(chip, step), 0, keepdims=False)
        total = total + lax.ppermute(piece, "island", pair_perm(n_chip, step, 2)).astype(
            jnp.float32
        )
    average = total.T / n_island
    new_momentum = outer_beta * outer_momentum + average
    new_anchor = anchor - outer_rate * (average + outer_beta * new_momentum)
    return (
        new_anchor,
        new_momentum,
        first.T.astype(jnp.bfloat16)[None],
        second.T.astype(jnp.bfloat16)[None],
    )


BARRIER = True


def solution(mesh):
    return jax.shard_map(
        on_device,
        mesh=mesh,
        in_specs=(
            P("island", "seq", None),
            P("island", "seq", None, None),
            P("island", "seq", None),
            P("island", "seq", None),
            P("island", "seq", None),
            P("seq", "island"),
            P("seq", "island"),
        ),
        out_specs=(
            P("seq", "island"),
            P("seq", "island"),
            P("island", "seq", None),
            P("island", "seq", None),
        ),
        check_vma=False,
    )
```

time: 97.7 us -> 94 us (0.962)
  starting transfers between devices: 56.8 us -> 29.5 us
  waiting for transfers between devices: 22.3 us -> 37.7 us
  local copies, waits for them, and re-layouts: 5.46 us -> 10.9 us
  other arithmetic: 2.09 us -> 3.98 us
  Pallas kernels: 0 us -> 1.23 us
    ppermute x25 -> x19, starting transfers between devices: 56.7 us -> 24.2 us  [the longest x9 16.7 us: exchange_gather(): lax.ppermute(blocks[k ^ low], axis, pair_perm(size, low, stride))]
    ppermute x25 -> x19, waiting for transfers between devices: 20.7 us -> 36.1 us  [the longest x9 28.7 us: exchange_gather(): lax.ppermute(blocks[k ^ low], axis, pair_perm(size, low, stride))]
    all_to_all x0 -> x1, starting transfers between devices: none -> 5.3 us  [on_device(): lax.all_to_all(sliced, 'seq', split_axis=0, concat_axis=0, tiled=True)]
    dot_general x4, matrix products: 2.27 us -> 6.84 us  [on_device(): lax.dot_general(both, tokens, (((1,), (1,)), ((), ())), preferred_element...]
    dot_general x3 -> x1, matrix products: 5.69 us -> 2.45 us  [on_device(): jnp.dot(by_token, gathered, preferred_element_type=jnp.float32) * inverse]
    unnamed x25 -> x27, local copies, waits for them, and re-layouts: 3.92 us -> 5.95 us
    dynamic_update_slice x0 -> x7, local copies, waits for them, and re-layouts: none -> 2.01 us  [the longest x3 1.92 us: on_device(): lax.dynamic_update_slice(column, weights[k], (0, jnp.bitwise_xor(seq, k)...]
    all_to_all x0 -> x1, local copies, waits for them, and re-layouts: none -> 1.48 us  [on_device(): lax.all_to_all(sliced, 'seq', split_axis=0, concat_axis=0, tiled=True)]
  transfers between devices with their start and end apart: 26 -> 21, of which waited for: 12 -> 11; matrix products, arithmetic and copies ran while one was open for 13% -> 15% of each run, Pallas kernels for 0% -> 1%
where the time goes in v2:
time: 94 us; the launch traced here: 93.6 us
  waiting for transfers between devices  37.7 us (40%)
  starting transfers between devices  29.5 us (31%)
  local copies, waits for them, and re-layouts  10.9 us (12%)
  matrix products  9.29 us (10%)
  other arithmetic  3.98 us (4%)
  Pallas kernels  1.23 us (1%)
    ppermute x9, waiting for transfers between devices, exchange_gather(): lax.ppermute(blocks[k ^ low], axis, pair_perm(size, low, stride))  28.7 us
    ppermute x9, starting transfers between devices, exchange_gather(): lax.ppermute(blocks[k ^ low], axis, pair_perm(size, low, stride))  16.7 us
    dot_general x4, matrix products, on_device(): lax.dot_general(both, tokens, (((1,), (1,)), ((), ())), preferred_element...  6.84 us
    unnamed x27, local copies, waits for them, and re-layouts  5.95 us
    all_to_all x1, starting transfers between devices, on_device(): lax.all_to_all(sliced, 'seq', split_axis=0, concat_axis=0, tiled=True)  5.3 us
    ppermute x3, waiting for transfers between devices, on_device(): lax.ppermute(column, 'island', pair_perm(n_chip, step, 2))  4.81 us
    ppermute x3, starting transfers between devices, on_device(): lax.ppermute(column, 'island', pair_perm(n_chip, step, 2))  3.49 us
    ppermute x3, starting transfers between devices, on_device(): lax.ppermute(piece, 'island', pair_perm(n_chip, step, 2))  3.49 us
  transfers between devices with their start and end apart: 21, of which 11 were waited for; matrix products, arithmetic and copies ran while one was open for 15% of the time, Pallas kernels for 1%

profile of v2, /device:TPU:0, one launch (start us, length us, event | category | flops | bytes accessed | tf_op | source)
XLA Modules:
  0.0 93.6 jit_solution(18003035065345723474)
XLA Ops:
  0.6 0.7 broadcast_in_dim.13
  1.4 1.6 %constant_dynamic-update-slice_fusion.15 = (bf16[32,5120]{1,0:T(8,128)(2,1)}, bf16[32,1280]{1,0:T(8,128)(2,1)S(1)}) fusion(bf16[32,5120]{1,0:T(8,128)(2,1)} %broadcast_in_dim.13, s32[]{:T(128)S(6)} %select_n.68, f32[1280,32]{0,1:T(8,128)} %param.12), kind=kLoop, calls=%fused_computation.70 | loop fusion | flops 40960 | bytes 327684 | tf_op jit(solution)/shard_map/dynamic_update_slice | solution.py:135
  3.0 4.0 %collective-permute-start.4 = (bf16[32,1280]{1,0:T(8,128)(2,1)S(1)}, bf16[32,1280]{1,0:T(8,128)(2,1)S(1)}, u32[]{:S(2)}, u32[]{:S(2)}) collective-permute-start(bf16[32,1280]{1,0:T(8,128)(2,1)S(1)} %get-tuple-element.23), channel_id=1, source_target_pairs={{0,2},{1,3},{2,0},{3,1},{4,6},{5,7},{6,4},{7,5},{8,10},{9,11},{10,... | collective-permute-start | bytes 245768 | tf_op jit(solution)/shard_map/ppermute | solution.py:33
  7.1 1.6 %collective-permute-start.3 = (bf16[32,1280]{1,0:T(8,128)(2,1)S(1)}, bf16[32,1280]{1,0:T(8,128)(2,1)S(1)}, u32[]{:S(2)}, u32[]{:S(2)}) collective-permute-start(bf16[32,1280]{1,0:T(8,128)(2,1)S(1)} %get-tuple-element.23), channel_id=1, source_target_pairs={{0,1},{1,0},{2,3},{3,2},{4,5},{5,4},{6,7},{7,6},{8,9},{9,8},{10,11... | collective-permute-start | bytes 245768 | tf_op jit(solution)/shard_map/ppermute | solution.py:33
  8.6 2.2 %collective-permute-done.4 = bf16[32,1280]{1,0:T(8,128)(2,1)S(1)} collective-permute-done((bf16[32,1280]{1,0:T(8,128)(2,1)S(1)}, bf16[32,1280]{1,0:T(8,128)(2,1)S(1)}, u32[]{:S(2)}, u32[]{:S(2)}) %collective-permute-start.4) | collective-permute-done | bytes 81952 | tf_op jit(solution)/shard_map/ppermute | solution.py:33
  10.8 1.2 %collective-permute-start.5 = (bf16[32,1280]{1,0:T(8,128)(2,1)S(1)}, bf16[32,1280]{1,0:T(8,128)(2,1)S(1)}, u32[]{:S(2)}, u32[]{:S(2)}) collective-permute-start(bf16[32,1280]{1,0:T(8,128)(2,1)S(1)} %collective-permute-done.4), channel_id=1, source_target_pairs={{0,1},{1,0},{2,3},{3,2},{4,5},{5,4},{6,7},{7,6},{8,9},{9,8},{10,11... | collective-permute-start | bytes 245768 | tf_op jit(solution)/shard_map/ppermute | solution.py:33
  12.0 0.6 constant_dynamic-update-slice_fusion.14
  12.7 0.6 constant_dynamic-update-slice_fusion.13
  13.3 1.9 %collective-permute-done.5 = bf16[32,1280]{1,0:T(8,128)(2,1)S(1)} collective-permute-done((bf16[32,1280]{1,0:T(8,128)(2,1)S(1)}, bf16[32,1280]{1,0:T(8,128)(2,1)S(1)}, u32[]{:S(2)}, u32[]{:S(2)}) %collective-permute-start.5) | collective-permute-done | bytes 81952 | tf_op jit(solution)/shard_map/ppermute | solution.py:33
  15.2 0.6 constant_dynamic-update-slice_fusion.12
  15.9 2.8 %collective-permute-start.11 = (bf16[32,5120]{1,0:T(8,128)(2,1)}, bf16[32,5120]{1,0:T(8,128)(2,1)}, u32[]{:S(2)}, u32[]{:S(2)}) collective-permute-start(bf16[32,5120]{1,0:T(8,128)(2,1)} %constant_dynamic-update-slice_fusion.12), channel_id=1, source_target_pairs={{0,24},{4,28},{8,16},{12,20},{16,8},{20,12},{24,0},{28,4},{1,25},{... | collective-permute-start | bytes 983048 | tf_op jit(solution)/shard_map/ppermute | solution.py:148
  18.7 0.5 collective-permute-start.9
  19.2 0.2 collective-permute-start.7
  19.4 0.9 copy.25
  20.3 2.7 %collective-permute-start.1 = (bf16[128,512]{1,0:T(8,128)(2,1)S(1)}, bf16[128,512]{1,0:T(8,128)(2,1)S(1)}, u32[]{:S(2)}, u32[]{:S(2)}) collective-permute-start(bf16[128,512]{1,0:T(8,128)(2,1)S(1)} %bitcast.128), channel_id=1, source_target_pairs={{0,2},{1,3},{2,0},{3,1},{4,6},{5,7},{6,4},{7,5},{8,10},{9,11},{10,... | collective-permute-start | bytes 393224 | tf_op jit(solution)/shard_map/ppermute | solution.py:33
  22.9 4.8 %collective-permute-done.11 = bf16[32,5120]{1,0:T(8,128)(2,1)} collective-permute-done((bf16[32,5120]{1,0:T(8,128)(2,1)}, bf16[32,5120]{1,0:T(8,128)(2,1)}, u32[]{:S(2)}, u32[]{:S(2)}) %collective-permute-start.11) | collective-permute-done | bytes 327712 | tf_op jit(solution)/shard_map/ppermute | solution.py:148
  27.8 0.2 copy.19
  28.0 0.2 copy.22
  28.3 0.8 copy-done.1
  29.1 1.5 %copy.20 = bf16[1,128,5120]{1,2,0:T(8,128)(2,1)} copy(bf16[1,128,5120]{2,1,0:T(8,128)(2,1)S(1)} %copy-done.1) | data formatting | bytes 2621440 | tf_op args[0]
  30.6 5.3 %all-to-all-start = ((bf16[4,128,1280]{1,2,0:T(8,128)(2,1)}), bf16[4,128,1280]{1,2,0:T(8,128)(2,1)S(1)}, u32[]{:S(2)}, u32[]{:S(2)}) async-start(bf16[4,128,1280]{1,2,0:T(8,128)(2,1)} %bitcast.18), calls=%async_computation | async-start | bytes 2621440 | tf_op jit(solution)/shard_map/all_to_all | solution.py:142
  35.9 2.0 %collective-permute-start = (bf16[128,512]{1,0:T(8,128)(2,1)S(1)}, bf16[128,512]{1,0:T(8,128)(2,1)S(1)}, u32[]{:S(2)}, u32[]{:S(2)}) collective-permute-start(bf16[128,512]{1,0:T(8,128)(2,1)S(1)} %bitcast.129), channel_id=1, source_target_pairs={{0,1},{1,0},{2,3},{3,2},{4,5},{5,4},{6,7},{7,6},{8,9},{9,8},{10,11... | collective-permute-start | bytes 393224 | tf_op jit(solution)/shard_map/ppermute | solution.py:33
  38.0 0.5 collective-permute-start.8
  38.5 2.1 %fusion.15 = f32[64,128]{1,0:T(8,128)S(1)} fusion(bf16[1,128,5120]{2,1,0:T(8,128)(2,1)} %param.7, bf16[32,5120]{1,0:T(8,128)(2,1)} %collective-permute-done.6, bf16[32,5120]{1,0:T(8,128)(2,1)} %constant_dynamic-update-slice_fusion.12), kind=kOutput, calls=%fused_computation.22 | convolution fusion | flops 85204992 | bytes 1998848 | tf_op jit(solution)/shard_map/dot_general | solution.py:153
  40.6 1.6 %fusion.24 = f32[64,128]{1,0:T(8,128)S(1)} fusion(bf16[1,128,5120]{2,1,0:T(8,128)(2,1)S(1)} %copy-done.2, bf16[32,5120]{1,0:T(8,128)(2,1)} %collective-permute-done.12, bf16[32,5120]{1,0:T(8,128)(2,1)} %collective-permute-done.11), kind=kOutput, calls=%fused_computation.25 | convolution fusion | flops 85204992 | bytes 1998848 | tf_op jit(solution)/shard_map/dot_general | solution.py:153
  42.3 1.5 %fusion.21 = f32[64,128]{1,0:T(8,128)S(1)} fusion(bf16[1,128,5120]{2,1,0:T(8,128)(2,1)S(1)} %copy-done.2, bf16[32,5120]{1,0:T(8,128)(2,1)S(1)} %collective-permute-done.10, bf16[32,5120]{1,0:T(8,128)(2,1)} %collective-permute-done.9), kind=kOutput, calls=%fused_computation.24 | convolution fusion | flops 85204992 | bytes 1998848 | tf_op jit(solution)/shard_map/dot_general | solution.py:153
  43.8 1.6 %fusion.18 = f32[64,128]{1,0:T(8,128)S(1)} fusion(bf16[1,128,5120]{2,1,0:T(8,128)(2,1)S(1)} %copy-done.2, bf16[32,5120]{1,0:T(8,128)(2,1)S(1)} %collective-permute-done.8, bf16[32,5120]{1,0:T(8,128)(2,1)} %collective-permute-done.7), kind=kOutput, calls=%fused_computation.23 | convolution fusion | flops 85204992 | bytes 1998848 | tf_op jit(solution)/shard_map/dot_general | solution.py:153
  45.6 15.4 %collective-permute-done.refs_2_.refs_3_ = bf16[128,512]{1,0:T(8,128)(2,1)S(1)} collective-permute-done((bf16[128,512]{1,0:T(8,128)(2,1)S(1)}, bf16[128,512]{1,0:T(8,128)(2,1)S(1)}, u32[]{:S(2)}, u32[]{:S(2)}) %collective-permute-start) | collective-permute-done | bytes 131104 | tf_op jit(solution)/shard_map/ppermute | solution.py:33
  61.0 2.4 %collective-permute-done.2.refs_6_.refs_7_ = bf16[128,512]{1,0:T(8,128)(2,1)S(1)} collective-permute-done((bf16[128,512]{1,0:T(8,128)(2,1)S(1)}, bf16[128,512]{1,0:T(8,128)(2,1)S(1)}, u32[]{:S(2)}, u32[]{:S(2)}) %collective-permute-start.2) | collective-permute-done | bytes 131104 | tf_op jit(solution)/shard_map/ppermute | solution.py:33
  63.4 1.2 %shard_map.102 = bf16[256,128]{1,0:T(8,128)(2,1)S(1)} custom-call(bf16[128,512]{1,0:T(8,128)(2,1)S(1)} %bitcast.130, bf16[128,512]{1,0:T(8,128)(2,1)S(1)} %bitcast.131, bf16[128,512]{1,0:T(8,128)(2,1)S(1)} %collective-permute-done.refs_2_.refs_3_, bf16[128,512]{1,0:T(8,128)(2,1)S(1)} %collective-permute-done.refs_2_.refs_3_, ...), custom_call_target="tpu_custom_call" | custom-call | flops 402653184 | bytes 786432 | tf_op jit(solution)/shard_map/pallas_call | solution.py:100
  64.6 4.7 %collective-permute-start.14 = (bf16[256,128]{1,0:T(8,128)(2,1)S(1)}, bf16[256,128]{1,0:T(8,128)(2,1)S(1)}, u32[]{:S(2)}, u32[]{:S(2)}) collective-permute-start(bf16[256,128]{1,0:T(8,128)(2,1)S(1)} %shard_map.102), channel_id=1, source_target_pairs={{0,2},{1,3},{2,0},{3,1},{4,6},{5,7},{6,4},{7,5},{8,10},{9,11},{10,... | collective-permute-start | bytes 196616 | tf_op jit(solution)/shard_map/ppermute | solution.py:33
  69.4 3.0 %collective-permute-done.14 = bf16[256,128]{1,0:T(8,128)(2,1)S(1)} collective-permute-done((bf16[256,128]{1,0:T(8,128)(2,1)S(1)}, bf16[256,128]{1,0:T(8,128)(2,1)S(1)}, u32[]{:S(2)}, u32[]{:S(2)}) %collective-permute-start.14) | collective-permute-done | bytes 65568 | tf_op jit(solution)/shard_map/ppermute | solution.py:33
  72.4 0.4 collective-permute-start.15
  72.8 0.8 collective-permute-done.13
  73.6 3.0 %collective-permute-done.15 = bf16[256,128]{1,0:T(8,128)(2,1)S(1)} collective-permute-done((bf16[256,128]{1,0:T(8,128)(2,1)S(1)}, bf16[256,128]{1,0:T(8,128)(2,1)S(1)}, u32[]{:S(2)}, u32[]{:S(2)}) %collective-permute-start.15) | collective-permute-done | bytes 65568 | tf_op jit(solution)/shard_map/ppermute | solution.py:33
  76.7 1.5 %copy.21 = bf16[4,128,1280]{2,1,0:T(8,128)(2,1)} copy(bf16[4,128,1280]{1,2,0:T(8,128)(2,1)S(1)} %all-to-all-done) | data formatting | bytes 2621440 | tf_op jit(solution)/shard_map/all_to_all | solution.py:142
  78.2 2.5 %fusion.14 = (bf16[256,1280]{1,0:T(8,128)(2,1)S(1)}, f32[256,1280]{1,0:T(8,128)S(1)}) fusion(bf16[1,1280,256]{1,2,0:T(8,128)(2,1)S(1)} %copy.22, bf16[1,1280,256]{1,2,0:T(8,128)(2,1)S(1)} %copy.19, bf16[256,512]{1,0:T(8,128)(2,1)S(1)} %constant_dynamic-update-slice_fusion.8, bf16[512,1280]{1,0:T(8,128)(2,1)} %bitcast.133), kind=kOutput, calls=%fused_computation.21 | convolution fusion | flops 340131840 | bytes 4849664 | tf_op jit(solution)/shard_map/dot_general | solution.py:173
  80.7 1.6 %collective-permute-done.16 = bf16[4,32,1280]{2,1,0:T(8,128)(2,1)S(1)} collective-permute-done((bf16[4,32,1280]{2,1,0:T(8,128)(2,1)S(1)}, bf16[4,32,1280]{2,1,0:T(8,128)(2,1)S(1)}, u32[]{:S(2)}, u32[]{:S(2)}) %collective-permute-start.16) | collective-permute-done | bytes 327712 | tf_op jit(solution)/shard_map/ppermute | solution.py:183
  82.4 0.7 dynamic-slice_bitcast_fusion.3
  83.1 1.4 %collective-permute-start.17 = (bf16[32,1280]{1,0:T(8,128)(2,1)}, bf16[32,1280]{1,0:T(8,128)(2,1)}, u32[]{:S(2)}, u32[]{:S(2)}) collective-permute-start(bf16[32,1280]{1,0:T(8,128)(2,1)} %get-tuple-element.26), channel_id=1, source_target_pairs={{0,8},{4,12},{8,0},{12,4},{16,24},{20,28},{24,16},{28,20},{1,9},{5... | collective-permute-start | bytes 245768 | tf_op jit(solution)/shard_map/ppermute | solution.py:188
  84.6 1.5 %collective-permute-start.19 = (bf16[32,1280]{1,0:T(8,128)(2,1)}, bf16[32,1280]{1,0:T(8,128)(2,1)}, u32[]{:S(2)}, u32[]{:S(2)}) collective-permute-start(bf16[32,1280]{1,0:T(8,128)(2,1)} %get-tuple-element.27), channel_id=1, source_target_pairs={{0,24},{4,28},{8,16},{12,20},{16,8},{20,12},{24,0},{28,4},{1,25},{... | collective-permute-start | bytes 245768 | tf_op jit(solution)/shard_map/ppermute | solution.py:188
  86.1 0.6 collective-permute-start.18
  86.6 0.5 fusion.28
  87.2 1.1 %copy.24 = bf16[1,1280,256]{2,1,0:T(8,128)(2,1)} copy(bf16[1,1280,256]{1,2,0:T(8,128)(2,1)S(1)} %get-tuple-element.24) | data formatting | bytes 1310720
  88.2 1.1 %copy.23 = bf16[1,1280,256]{2,1,0:T(8,128)(2,1)} copy(bf16[1,1280,256]{1,2,0:T(8,128)(2,1)S(1)} %get-tuple-element.25) | data formatting | bytes 1310720
  89.3 1.4 %collective-permute-done.19 = bf16[32,1280]{1,0:T(8,128)(2,1)} collective-permute-done((bf16[32,1280]{1,0:T(8,128)(2,1)}, bf16[32,1280]{1,0:T(8,128)(2,1)}, u32[]{:S(2)}, u32[]{:S(2)}) %collective-permute-start.19) | collective-permute-done | bytes 81952 | tf_op jit(solution)/shard_map/ppermute | solution.py:188
  90.7 1.1 %collective-permute-done.18 = bf16[32,1280]{1,0:T(8,128)(2,1)} collective-permute-done((bf16[32,1280]{1,0:T(8,128)(2,1)S(1)}, bf16[32,1280]{1,0:T(8,128)(2,1)}, u32[]{:S(2)}, u32[]{:S(2)}) %collective-permute-start.18) | collective-permute-done | bytes 81952 | tf_op jit(solution)/shard_map/ppermute | solution.py:188
  91.8 1.8 %fusion.42 = (f32[1280,32]{0,1:T(8,128)}, f32[1280,32]{0,1:T(8,128)}) fusion(f32[1280,32]{0,1:T(8,128)S(1)} %copy-done.5, bf16[32,1280]{1,0:T(8,128)(2,1)} %collective-permute-done.19, bf16[32,1280]{1,0:T(8,128)(2,1)} %collective-permute-done.18, bf16[32,1280]{1,0:T(8,128)(2,1)} %collective-permute-done.17, f32[4,32,1280]{2,1,0:T(8,128)S(1)} %get-tuple-element.21, ...), kind=kLoop, calls=%fused_computation.45 | loop fusion | flops 532480 | bytes 1064964 | tf_op jit(solution)/shard_map/sub | solution.py:193
  (45 shorter events, 0.5 us)
Async XLA Ops:
  0.6 27.1 %copy-start.3 = (bf16[1,1280,256]{2,1,0:T(8,128)(2,1)S(1)}, bf16[1,1280,256]{2,1,0:T(8,128)(2,1)}, u32[]{:S(2)}) copy-start(bf16[1,1280,256]{2,1,0:T(8,128)(2,1)} %param.10) | copy-start | bytes 1966084
  1.4 26.6 %copy-start.4 = (bf16[1,1280,256]{2,1,0:T(8,128)(2,1)S(1)}, bf16[1,1280,256]{2,1,0:T(8,128)(2,1)}, u32[]{:S(2)}) copy-start(bf16[1,1280,256]{2,1,0:T(8,128)(2,1)} %param.11) | copy-start | bytes 1966084
  3.0 7.8 %collective-permute-start.4 = (bf16[32,1280]{1,0:T(8,128)(2,1)S(1)}, bf16[32,1280]{1,0:T(8,128)(2,1)S(1)}, u32[]{:S(2)}, u32[]{:S(2)}) collective-permute-start(bf16[32,1280]{1,0:T(8,128)(2,1)S(1)} %get-tuple-element.23), channel_id=1, source_target_pairs={{0,2},{1,3},{2,0},{3,1},{4,6},{5,7},{6,4},{7,5},{8,10},{9,11},{10,... | collective-permute-start | bytes 245768 | tf_op jit(solution)/shard_map/ppermute | solution.py:33
  7.1 5.0 %collective-permute-start.3 = (bf16[32,1280]{1,0:T(8,128)(2,1)S(1)}, bf16[32,1280]{1,0:T(8,128)(2,1)S(1)}, u32[]{:S(2)}, u32[]{:S(2)}) collective-permute-start(bf16[32,1280]{1,0:T(8,128)(2,1)S(1)} %get-tuple-element.23), channel_id=1, source_target_pairs={{0,1},{1,0},{2,3},{3,2},{4,5},{5,4},{6,7},{7,6},{8,9},{9,8},{10,11... | collective-permute-start | bytes 245768 | tf_op jit(solution)/shard_map/ppermute | solution.py:33
  10.8 4.4 %collective-permute-start.5 = (bf16[32,1280]{1,0:T(8,128)(2,1)S(1)}, bf16[32,1280]{1,0:T(8,128)(2,1)S(1)}, u32[]{:S(2)}, u32[]{:S(2)}) collective-permute-start(bf16[32,1280]{1,0:T(8,128)(2,1)S(1)} %collective-permute-done.4), channel_id=1, source_target_pairs={{0,1},{1,0},{2,3},{3,2},{4,5},{5,4},{6,7},{7,6},{8,9},{9,8},{10,11... | collective-permute-start | bytes 245768 | tf_op jit(solution)/shard_map/ppermute | solution.py:33
  15.9 11.9 %collective-permute-start.11 = (bf16[32,5120]{1,0:T(8,128)(2,1)}, bf16[32,5120]{1,0:T(8,128)(2,1)}, u32[]{:S(2)}, u32[]{:S(2)}) collective-permute-start(bf16[32,5120]{1,0:T(8,128)(2,1)} %constant_dynamic-update-slice_fusion.12), channel_id=1, source_target_pairs={{0,24},{4,28},{8,16},{12,20},{16,8},{20,12},{24,0},{28,4},{1,25},{... | collective-permute-start | bytes 983048 | tf_op jit(solution)/shard_map/ppermute | solution.py:148
  18.7 19.2 %collective-permute-start.9 = (bf16[32,5120]{1,0:T(8,128)(2,1)}, bf16[32,5120]{1,0:T(8,128)(2,1)}, u32[]{:S(2)}, u32[]{:S(2)}) collective-permute-start(bf16[32,5120]{1,0:T(8,128)(2,1)} %constant_dynamic-update-slice_fusion.12), channel_id=1, source_target_pairs={{0,16},{4,20},{8,24},{12,28},{16,0},{20,4},{24,8},{28,12},{1,17},{... | collective-permute-start | bytes 983048 | tf_op jit(solution)/shard_map/ppermute | solution.py:148
  19.2 18.8 %collective-permute-start.7 = (bf16[32,5120]{1,0:T(8,128)(2,1)}, bf16[32,5120]{1,0:T(8,128)(2,1)}, u32[]{:S(2)}, u32[]{:S(2)}) collective-permute-start(bf16[32,5120]{1,0:T(8,128)(2,1)} %constant_dynamic-update-slice_fusion.12), channel_id=1, source_target_pairs={{0,8},{4,12},{8,0},{12,4},{16,24},{20,28},{24,16},{28,20},{1,9},{5... | collective-permute-start | bytes 983048 | tf_op jit(solution)/shard_map/ppermute | solution.py:148
  19.4 18.6 %collective-permute-start.6 = (bf16[32,5120]{1,0:T(8,128)(2,1)}, bf16[32,5120]{1,0:T(8,128)(2,1)}, u32[]{:S(2)}, u32[]{:S(2)}) collective-permute-start(bf16[32,5120]{1,0:T(8,128)(2,1)} %constant_dynamic-update-slice_fusion.12), channel_id=1, source_target_pairs={{0,4},{4,0},{8,12},{12,8},{16,20},{20,16},{24,28},{28,24},{1,5},{5... | collective-permute-start | bytes 983048 | tf_op jit(solution)/shard_map/ppermute | solution.py:150
  20.3 15.6 %collective-permute-start.1 = (bf16[128,512]{1,0:T(8,128)(2,1)S(1)}, bf16[128,512]{1,0:T(8,128)(2,1)S(1)}, u32[]{:S(2)}, u32[]{:S(2)}) collective-permute-start(bf16[128,512]{1,0:T(8,128)(2,1)S(1)} %bitcast.128), channel_id=1, source_target_pairs={{0,2},{1,3},{2,0},{3,1},{4,6},{5,7},{6,4},{7,5},{8,10},{9,11},{10,... | collective-permute-start | bytes 393224 | tf_op jit(solution)/shard_map/ppermute | solution.py:33
  27.8 12.8 %collective-permute-start.12 = (bf16[32,5120]{1,0:T(8,128)(2,1)}, bf16[32,5120]{1,0:T(8,128)(2,1)}, u32[]{:S(2)}, u32[]{:S(2)}) collective-permute-start(bf16[32,5120]{1,0:T(8,128)(2,1)} %collective-permute-done.11), channel_id=1, source_target_pairs={{0,4},{4,0},{8,12},{12,8},{16,20},{20,16},{24,28},{28,24},{1,5},{5... | collective-permute-start | bytes 983048 | tf_op jit(solution)/shard_map/ppermute | solution.py:150
  27.8 1.3 %copy-start.1 = (bf16[1,128,5120]{2,1,0:T(8,128)(2,1)S(1)}, bf16[1,128,5120]{2,1,0:T(8,128)(2,1)}, u32[]{:S(2)}) copy-start(bf16[1,128,5120]{2,1,0:T(8,128)(2,1)} %param.7) | copy-start | bytes 3932164
  30.6 46.1 %all-to-all-start = ((bf16[4,128,1280]{1,2,0:T(8,128)(2,1)}), bf16[4,128,1280]{1,2,0:T(8,128)(2,1)S(1)}, u32[]{:S(2)}, u32[]{:S(2)}) async-start(bf16[4,128,1280]{1,2,0:T(8,128)(2,1)} %bitcast.18), calls=%async_computation | async-start | bytes 2621440 | tf_op jit(solution)/shard_map/all_to_all | solution.py:142
  35.9 4.7 %copy-start.2 = (bf16[1,128,5120]{2,1,0:T(8,128)(2,1)S(1)}, bf16[1,128,5120]{2,1,0:T(8,128)(2,1)}, u32[]{:S(2)}) copy-start(bf16[1,128,5120]{2,1,0:T(8,128)(2,1)} %param.7) | copy-start | bytes 3932164
  35.9 25.1 %collective-permute-start = (bf16[128,512]{1,0:T(8,128)(2,1)S(1)}, bf16[128,512]{1,0:T(8,128)(2,1)S(1)}, u32[]{:S(2)}, u32[]{:S(2)}) collective-permute-start(bf16[128,512]{1,0:T(8,128)(2,1)S(1)} %bitcast.129), channel_id=1, source_target_pairs={{0,1},{1,0},{2,3},{3,2},{4,5},{5,4},{6,7},{7,6},{8,9},{9,8},{10,11... | collective-permute-start | bytes 393224 | tf_op jit(solution)/shard_map/ppermute | solution.py:33
  37.9 25.5 %collective-permute-start.2 = (bf16[128,512]{1,0:T(8,128)(2,1)S(1)}, bf16[128,512]{1,0:T(8,128)(2,1)S(1)}, u32[]{:S(2)}, u32[]{:S(2)}) collective-permute-start(bf16[128,512]{1,0:T(8,128)(2,1)S(1)} %collective-permute-done.1.refs_4_.refs_5_), channel_id=1, source_target_pairs={{0,1},{1,0},{2,3},{3,2},{4,5},{5,4},{6,7},{7,6},{8,9},{9,8},{10,11... | collective-permute-start | bytes 393224 | tf_op jit(solution)/shard_map/ppermute | solution.py:33
  38.0 4.3 %collective-permute-start.10 = (bf16[32,5120]{1,0:T(8,128)(2,1)}, bf16[32,5120]{1,0:T(8,128)(2,1)S(1)}, u32[]{:S(2)}, u32[]{:S(2)}) collective-permute-start(bf16[32,5120]{1,0:T(8,128)(2,1)} %collective-permute-done.9), channel_id=1, source_target_pairs={{0,4},{4,0},{8,12},{12,8},{16,20},{20,16},{24,28},{28,24},{1,5},{5... | collective-permute-start | bytes 983048 | tf_op jit(solution)/shard_map/ppermute | solution.py:150
  38.0 5.8 %collective-permute-start.8 = (bf16[32,5120]{1,0:T(8,128)(2,1)}, bf16[32,5120]{1,0:T(8,128)(2,1)S(1)}, u32[]{:S(2)}, u32[]{:S(2)}) collective-permute-start(bf16[32,5120]{1,0:T(8,128)(2,1)} %collective-permute-done.7), channel_id=1, source_target_pairs={{0,4},{4,0},{8,12},{12,8},{16,20},{20,16},{24,28},{28,24},{1,5},{5... | collective-permute-start | bytes 983048 | tf_op jit(solution)/shard_map/ppermute | solution.py:150
  43.8 19.6 %copy-start = (bf16[1,128,256]{2,1,0:T(8,128)(2,1)S(1)}, bf16[1,128,256]{2,1,0:T(8,128)(2,1)}, u32[]{:S(2)}) copy-start(bf16[1,128,256]{2,1,0:T(8,128)(2,1)} %param.9) | copy-start | bytes 196612
  64.6 7.7 %collective-permute-start.14 = (bf16[256,128]{1,0:T(8,128)(2,1)S(1)}, bf16[256,128]{1,0:T(8,128)(2,1)S(1)}, u32[]{:S(2)}, u32[]{:S(2)}) collective-permute-start(bf16[256,128]{1,0:T(8,128)(2,1)S(1)} %shard_map.102), channel_id=1, source_target_pairs={{0,2},{1,3},{2,0},{3,1},{4,6},{5,7},{6,4},{7,5},{8,10},{9,11},{10,... | collective-permute-start | bytes 196616 | tf_op jit(solution)/shard_map/ppermute | solution.py:33
  69.3 4.3 %collective-permute-start.13 = (bf16[256,128]{1,0:T(8,128)(2,1)S(1)}, bf16[256,128]{1,0:T(8,128)(2,1)S(1)}, u32[]{:S(2)}, u32[]{:S(2)}) collective-permute-start(bf16[256,128]{1,0:T(8,128)(2,1)S(1)} %shard_map.102), channel_id=1, source_target_pairs={{0,1},{1,0},{2,3},{3,2},{4,5},{5,4},{6,7},{7,6},{8,9},{9,8},{10,11... | collective-permute-start | bytes 196616 | tf_op jit(solution)/shard_map/ppermute | solution.py:33
  72.4 4.3 %collective-permute-start.15 = (bf16[256,128]{1,0:T(8,128)(2,1)S(1)}, bf16[256,128]{1,0:T(8,128)(2,1)S(1)}, u32[]{:S(2)}, u32[]{:S(2)}) collective-permute-start(bf16[256,128]{1,0:T(8,128)(2,1)S(1)} %collective-permute-done.14), channel_id=1, source_target_pairs={{0,1},{1,0},{2,3},{3,2},{4,5},{5,4},{6,7},{7,6},{8,9},{9,8},{10,11... | collective-permute-start | bytes 196616 | tf_op jit(solution)/shard_map/ppermute | solution.py:33
  80.7 1.7 %collective-permute-start.16 = (bf16[4,32,1280]{2,1,0:T(8,128)(2,1)S(1)}, bf16[4,32,1280]{2,1,0:T(8,128)(2,1)S(1)}, u32[]{:S(2)}, u32[]{:S(2)}) collective-permute-start(bf16[4,32,1280]{2,1,0:T(8,128)(2,1)S(1)} %dynamic-slice_bitcast_fusion), channel_id=1, source_target_pairs={{0,4},{4,0},{8,12},{12,8},{16,20},{20,16},{24,28},{28,24},{1,5},{5... | collective-permute-start | bytes 983048 | tf_op jit(solution)/shard_map/ppermute | solution.py:183
  83.1 6.2 %collective-permute-start.17 = (bf16[32,1280]{1,0:T(8,128)(2,1)}, bf16[32,1280]{1,0:T(8,128)(2,1)}, u32[]{:S(2)}, u32[]{:S(2)}) collective-permute-start(bf16[32,1280]{1,0:T(8,128)(2,1)} %get-tuple-element.26), channel_id=1, source_target_pairs={{0,8},{4,12},{8,0},{12,4},{16,24},{20,28},{24,16},{28,20},{1,9},{5... | collective-permute-start | bytes 245768 | tf_op jit(solution)/shard_map/ppermute | solution.py:188
  84.6 6.1 %collective-permute-start.19 = (bf16[32,1280]{1,0:T(8,128)(2,1)}, bf16[32,1280]{1,0:T(8,128)(2,1)}, u32[]{:S(2)}, u32[]{:S(2)}) collective-permute-start(bf16[32,1280]{1,0:T(8,128)(2,1)} %get-tuple-element.27), channel_id=1, source_target_pairs={{0,24},{4,28},{8,16},{12,20},{16,8},{20,12},{24,0},{28,4},{1,25},{... | collective-permute-start | bytes 245768 | tf_op jit(solution)/shard_map/ppermute | solution.py:188
  86.1 5.7 %collective-permute-start.18 = (bf16[32,1280]{1,0:T(8,128)(2,1)S(1)}, bf16[32,1280]{1,0:T(8,128)(2,1)}, u32[]{:S(2)}, u32[]{:S(2)}) collective-permute-start(bf16[32,1280]{1,0:T(8,128)(2,1)S(1)} %get-tuple-element.28), channel_id=1, source_target_pairs={{0,16},{4,20},{8,24},{12,28},{16,0},{20,4},{24,8},{28,12},{1,17},{... | collective-permute-start | bytes 245768 | tf_op jit(solution)/shard_map/ppermute | solution.py:188
  87.1 4.7 %copy-start.5 = (f32[1280,32]{0,1:T(8,128)S(1)}, f32[1280,32]{0,1:T(8,128)}, u32[]{:S(2)}) copy-start(f32[1280,32]{0,1:T(8,128)} %param.12) | copy-start | bytes 491524
  87.1 4.7 %copy-start.6 = (f32[1280,32]{0,1:T(8,128)S(1)}, f32[1280,32]{0,1:T(8,128)}, u32[]{:S(2)}) copy-start(f32[1280,32]{0,1:T(8,128)} %param.13) | copy-start | bytes 491524

commit v3 on v2

v3 whole, which is shorter than its diff:
```python
import functools

import jax
import jax.numpy as jnp
from jax import lax
from jax.experimental import pallas as pl
from jax.experimental.pallas import tpu as pltpu
from jax.sharding import PartitionSpec as P

HD = 64

inner_rate = 0.1
beta_one = 0.9
beta_two = 0.95
adam_eps = 1e-08
outer_rate = 0.7
outer_beta = 0.9

NT = (((1,), (1,)), ((), ()))
TN = (((0,), (0,)), ((), ()))
PARAMS = pltpu.CompilerParams(vmem_limit_bytes=48 * 1024 * 1024)


def cost(flops, elements, transcendentals=0):
    return pl.CostEstimate(
        flops=flops, bytes_accessed=2 * elements, transcendentals=transcendentals
    )


def pair_perm(size, step, stride=1):
    return [
        (group * stride + inner, (group ^ step) * stride + inner)
        for group in range(size)
        for inner in range(stride)
    ]


def exchange_gather(own, axis, size):
    blocks = [own] + [None] * (size - 1)
    for k in sorted(range(1, size), key=lambda k: (bin(k).count("1"), -k)):
        low = k & -k
        blocks[k] = lax.ppermute(blocks[k ^ low], axis, pair_perm(size, low))
    return blocks


def query_kernel(rounds, n_chip, inverse, *refs):
    n_seq = sum(len(r) for r in rounds)
    weights = refs[: len(rounds) * n_chip]
    own, partner = refs[len(weights) : len(weights) + n_seq], refs[len(weights) + n_seq :][:n_seq]
    own_out, partner_out = refs[-2:]
    share = own_out.shape[1]
    rows = own_out.shape[2]
    total = jnp.zeros((n_chip * share, 2 * rows), jnp.float32)
    for at, ks in enumerate(rounds):
        group = weights[at * n_chip : (at + 1) * n_chip]
        for place, k in enumerate(ks):
            left = jnp.concatenate(
                [ref[place * share : (place + 1) * share, :] for ref in group], axis=0
            )
            right = jnp.concatenate([own[k][...], partner[k][...]], axis=0)
            total = total + lax.dot_general(left, right, NT, preferred_element_type=jnp.float32)
    total = (total * inverse).astype(jnp.bfloat16)
    for j in range(n_chip):
        own_out[j] = total[j * share : (j + 1) * share, :rows]
        partner_out[j] = total[j * share : (j + 1) * share, rows:]


def half_queries(rounds, weights, own, partner, share, inverse):
    n_chip = len(weights[0])
    rows, block = own[0].shape
    shape = jax.ShapeDtypeStruct((n_chip, share, rows), jnp.bfloat16)
    operands = [w for group in weights for w in group] + own + partner
    macs = n_chip * share * 2 * rows * block * len(own)
    return pl.pallas_call(
        functools.partial(query_kernel, rounds, n_chip, inverse),
        out_shape=(shape, shape),
        compiler_params=PARAMS,
        cost_estimate=cost(2 * macs, sum(o.size for o in operands)),
    )(*operands)


def attention_kernel(n_seq, n_chip, rows, head_size, *refs):
    kv_refs, (mine_ref, other_ref, cot_ref, out_ref) = refs[: 2 * n_seq], refs[2 * n_seq :]
    seq = lax.axis_index("seq")
    chip, core = lax.axis_index("island") // 2, lax.rem(lax.axis_index("island"), 2)
    cols = out_ref.shape[0]
    share = mine_ref.shape[1]
    first_chip = pl.program_id(0) * (cols // (2 * share))
    heads = cols // head_size
    wide = heads * rows
    scale = head_size**-0.5
    head_of_row = lax.broadcasted_iota(jnp.int32, (cols, wide), 0) // head_size
    head_of_col = lax.broadcasted_iota(jnp.int32, (cols, wide), 1) // rows
    diagonal = head_of_row == head_of_col

    def spread(matrix):
        tiled = jnp.concatenate([matrix] * heads, axis=1)
        return jnp.where(diagonal, tiled, 0.0).astype(jnp.bfloat16)

    pieces = []
    for at in range(cols // (2 * share)):
        place = jnp.bitwise_xor(chip, first_chip + at)
        mine, other = mine_ref[place].astype(jnp.float32), other_ref[place].astype(jnp.float32)
        pieces.append(jnp.where(core == 0, mine, other))
        pieces.append(jnp.where(core == 0, other, mine))
    query = spread(jnp.concatenate(pieces, axis=0))
    cot = spread(cot_ref[...].astype(jnp.float32).T)
    key_row = lax.broadcasted_iota(jnp.int32, (rows, wide), 0)
    query_row = lax.rem(lax.broadcasted_iota(jnp.int32, (rows, wide), 1), rows) + seq * rows
    scores = []
    for k in range(n_seq):
        block = jnp.dot(kv_refs[2 * k][...], query, preferred_element_type=jnp.float32) * scale
        seen = query_row >= key_row + jnp.bitwise_xor(seq, k) * rows
        scores.append(jnp.where(seen, block, -1e30))
    peak = functools.reduce(jnp.maximum, [jnp.max(s, axis=0, keepdims=True) for s in scores])
    expons = [jnp.exp(s - peak) for s in scores]
    inverse = 1.0 / sum(jnp.sum(e, axis=0, keepdims=True) for e in expons)
    attend = [e * inverse for e in expons]
    dattend = [
        jnp.dot(kv_refs[2 * k + 1][...], cot, preferred_element_type=jnp.float32)
        for k in range(n_seq)
    ]
    rowdot = sum(
        jnp.sum(a.astype(jnp.bfloat16).astype(jnp.float32) * d, axis=0, keepdims=True)
        for a, d in zip(attend, dattend)
    )
    total = jnp.zeros((cols, wide), jnp.float32)
    for k in range(n_seq):
        dscore = (attend[k] * (dattend[k] - rowdot)).astype(jnp.bfloat16)
        total = total + lax.dot_general(
            kv_refs[2 * k][...], dscore, TN, preferred_element_type=jnp.float32
        )
    for h in range(heads):
        part = total[h * head_size : (h + 1) * head_size, h * rows : (h + 1) * rows] * scale
        out_ref[h * head_size : (h + 1) * head_size, :] = part.astype(jnp.bfloat16)


def attention(kv, mine, other, cot):
    n_seq, (rows, cols) = len(kv), cot.shape
    n_chip = mine.shape[0]
    group = min(cols, 4 * HD)
    groups = cols // group
    in_specs = []
    operands = []
    for block in kv:
        in_specs.append(pl.BlockSpec((rows, group), lambda g: (0, g)))
        in_specs.append(pl.BlockSpec((rows, group), lambda g: (0, g + groups)))
        operands += [block, block]
    in_specs.append(pl.BlockSpec(mine.shape, lambda g: (0, 0, 0)))
    in_specs.append(pl.BlockSpec(mine.shape, lambda g: (0, 0, 0)))
    in_specs.append(pl.BlockSpec((rows, group), lambda g: (0, g)))
    length = n_seq * rows
    return pl.pallas_call(
        functools.partial(attention_kernel, n_seq, n_chip, rows, HD),
        grid=(groups,),
        in_specs=in_specs,
        out_specs=pl.BlockSpec((group, rows), lambda g: (g, 0)),
        out_shape=jax.ShapeDtypeStruct((cols, rows), jnp.bfloat16),
        compiler_params=PARAMS,
        cost_estimate=cost(
            6 * length * cols * (group // HD) * rows,
            2 * length * cols + 4 * cols * rows,
            length * rows * (cols // HD),
        ),
    )(*operands, mine, other, cot)


def adam_kernel(n_seq, n_chip, own_half, inverse, *refs):
    dq_refs, state_refs = refs[:n_seq], refs[n_seq : 2 * n_seq]
    first_ref, second_ref, first_out, second_out, delta_out = refs[2 * n_seq :]
    share = first_ref.shape[2]
    core = lax.rem(lax.axis_index("island"), 2)
    half = core if own_half else 1 - core
    left = []
    for ref in dq_refs:
        pieces = []
        for j in range(n_chip):
            start = pl.multiple_of((2 * j + half) * share, share)
            pieces.append(ref[pl.ds(start, share), :])
        left.append(jnp.concatenate(pieces, axis=0))
    left = jnp.concatenate(left, axis=1)
    states = jnp.concatenate([ref[...] for ref in state_refs], axis=0)
    gradient = jnp.dot(left, states, preferred_element_type=jnp.float32) * inverse
    for j in range(n_chip):
        grad = gradient[j * share : (j + 1) * share]
        first = beta_one * first_ref[j, half].astype(jnp.float32) + (1.0 - beta_one) * grad
        second = (
            beta_two * second_ref[j, half].astype(jnp.float32) + (1.0 - beta_two) * grad * grad
        )
        first_out[j] = first.astype(jnp.bfloat16)
        second_out[j] = second.astype(jnp.bfloat16)
        delta = inner_rate * first / (jnp.sqrt(second) + adam_eps)
        delta_out[j] = delta.astype(jnp.bfloat16)


def gradient_adam(dqueries, states, first, second, own_half, inverse):
    n_seq = len(states)
    n_chip, _, share, block = first.shape
    shape = jax.ShapeDtypeStruct((n_chip, share, block), jnp.bfloat16)
    operands = list(dqueries) + list(states) + [first, second]
    half = n_chip * share * block
    return pl.pallas_call(
        functools.partial(adam_kernel, n_seq, n_chip, own_half, inverse),
        out_shape=(shape, shape, shape),
        compiler_params=PARAMS,
        cost_estimate=cost(
            2 * half * n_seq * states[0].shape[0], sum(o.size for o in operands) + 3 * half, 2 * half
        ),
    )(*operands)


def pair_kernel(n_chip, same_ref, got_ref, *outs):
    chip = lax.axis_index("island") // 2
    for step in range(n_chip):
        place = jnp.bitwise_xor(chip, step)
        total = same_ref[place].astype(jnp.float32) + got_ref[place].astype(jnp.float32)
        outs[step][...] = total.astype(outs[step].dtype)


def pair_sum(same, got):
    n_chip, share, block = same.shape
    shapes = [
        jax.ShapeDtypeStruct((share, block), jnp.bfloat16 if step else jnp.float32)
        for step in range(n_chip)
    ]
    return pl.pallas_call(
        functools.partial(pair_kernel, n_chip),
        out_shape=tuple(shapes),
        compiler_params=PARAMS,
        cost_estimate=cost(same.size, 3 * same.size),
    )(same, got)


def on_device(states, key_vals, cotangent, first_moment, second_moment, anchor, outer_momentum):
    n_seq = lax.axis_size("seq")
    n_island = lax.axis_size("island")
    n_chip = n_island // 2
    seq = lax.axis_index("seq")
    core = lax.rem(lax.axis_index("island"), 2)
    tokens = states[0]
    rows, features = tokens.shape
    block = features // n_seq
    share = anchor.shape[1]
    cols = first_moment.shape[2]
    inverse = features ** (-0.5)
    swap = pair_perm(n_island, 1)

    def feature_blocks(matrix):
        return [
            lax.dynamic_slice(matrix, (0, jnp.bitwise_xor(seq, k) * block), (rows, block))
            for k in range(n_seq)
        ]

    weights = exchange_gather(anchor.T.astype(jnp.bfloat16), "seq", n_seq)
    rounds = [[0], [k for k in range(1, n_seq) if k & (k - 1) == 0]]
    rounds.append([k for k in range(n_seq) if k not in rounds[0] + rounds[1]])
    rounds = [r for r in rounds if r]
    spread = []
    for ks in rounds:
        held = jnp.concatenate([weights[k] for k in ks], axis=0)
        spread.append(
            [held]
            + [
                lax.ppermute(held, "island", pair_perm(n_chip, step, 2))
                for step in range(1, n_chip)
            ]
        )

    partner_tokens = lax.ppermute(tokens, "island", swap)
    kv = exchange_gather(key_vals[0].reshape(rows, 2 * cols), "seq", n_seq)

    own_blocks = feature_blocks(tokens)
    gathered = [own_blocks[0]] + [
        lax.ppermute(own_blocks[k], "seq", pair_perm(n_seq, k)) for k in range(1, n_seq)
    ]

    mine, for_partner = half_queries(
        rounds, spread, own_blocks, feature_blocks(partner_tokens), share, inverse
    )
    other = lax.ppermute(for_partner, "island", swap)
    dquery = attention(kv, mine, other, cotangent[0])
    dqueries = [dquery] + [
        lax.ppermute(dquery, "seq", pair_perm(n_seq, k)) for k in range(1, n_seq)
    ]

    first = first_moment[0].T.reshape(n_chip, 2, share, block)
    second = second_moment[0].T.reshape(n_chip, 2, share, block)
    first_other, second_other, delta_other = gradient_adam(
        dqueries, gathered, first, second, False, inverse
    )
    got = lax.ppermute(delta_other, "island", swap)
    first_own, second_own, delta_own = gradient_adam(
        dqueries, gathered, first, second, True, inverse
    )

    def whole(own, other):
        lower = jnp.where(core == 0, own, other)
        upper = jnp.where(core == 0, other, own)
        return jnp.stack([lower, upper], axis=1).reshape(cols, block).T[None]

    parts = pair_sum(delta_own, got)
    total = parts[0]
    for step in range(1, n_chip):
        total = total + lax.ppermute(
            parts[step], "island", pair_perm(n_chip, step, 2)
        ).astype(jnp.float32)
    average = total.T / n_island
    new_momentum = outer_beta * outer_momentum + average
    new_anchor = anchor - outer_rate * (average + outer_beta * new_momentum)
    return (
        new_anchor,
        new_momentum,
        whole(first_own, first_other),
        whole(second_own, second_other),
    )


def solution(mesh):
    return jax.shard_map(
        on_device,
        mesh=mesh,
        in_specs=(
            P("island", "seq", None),
            P("island", "seq", None, None),
            P("island", "seq", None),
            P("island", "seq", None),
            P("island", "seq", None),
            P("seq", "island"),
            P("seq", "island"),
        ),
        out_specs=(
            P("seq", "island"),
            P("seq", "island"),
            P("island", "seq", None),
            P("island", "seq", None),
        ),
        check_vma=False,
    )
```

time: 94 us -> 77.8 us (0.83)
  waiting for transfers between devices: 37.7 us -> 26.9 us
  matrix products: 9.29 us -> 0 us
  starting transfers between devices: 29.5 us -> 35.7 us
  Pallas kernels: 1.23 us -> 3.61 us
  local copies, waits for them, and re-layouts: 10.9 us -> 8.56 us
  other arithmetic: 3.98 us -> 1.94 us
    ppermute x20 -> x27, starting transfers between devices: 24.2 us -> 35.7 us  [the longest x9 11.3 us: on_device(): lax.ppermute(held, 'island', pair_perm(n_chip, step, 2))]
    ppermute x20 -> x27, waiting for transfers between devices: 37.7 us -> 26.9 us  [the longest x6 21 us: exchange_gather(): blocks[k] = lax.ppermute(blocks[k ^ low], axis, pair_perm(size, low))]
    dot_general x5 -> x0, matrix products: 9.29 us -> none  [the longest x4 6.84 us: on_device(): lax.dot_general(both, tokens, (((1,), (1,)), ((), ())), preferred_element...]
    all_to_all x1 -> x0, starting transfers between devices: 5.3 us -> none  [on_device(): lax.all_to_all(sliced, 'seq', split_axis=0, concat_axis=0, tiled=True)]
    unnamed x27 -> x10, local copies, waits for them, and re-layouts: 5.95 us -> 3.09 us
    dynamic_slice x0 -> x2, local copies, waits for them, and re-layouts: none -> 2.71 us  [feature_blocks(): lax.dynamic_slice(matrix, (0, jnp.bitwise_xor(seq, k) * block), (rows, bl...]
    transpose x0 -> x2, local copies, waits for them, and re-layouts: none -> 2.66 us  [the longest x1 1.33 us: on_device(): first = first_moment[0].T.reshape(n_chip, 2, share, block)]
    pallas_call x1 -> x5, Pallas kernels: 1.23 us -> 3.61 us  [the longest x2 1.32 us: gradient_adam(): pl.pallas_call(functools.partial(adam_kernel, n_seq, n_chip, own_half, in...]
  transfers between devices with their start and end apart: 21 -> 27, of which waited for: 11 -> 7; matrix products, arithmetic and copies ran while one was open for 15% -> 13% of each run, Pallas kernels for 1% -> 4%
where the time goes in v3:
time: 77.8 us; the launch traced here: 77.5 us
  starting transfers between devices  35.7 us (46%)
  waiting for transfers between devices  26.9 us (35%)
  local copies, waits for them, and re-layouts  8.56 us (11%)
  Pallas kernels  3.61 us (5%)
  other arithmetic  1.94 us (2%)
  between operations  0.82 us (1%)
    ppermute x6, waiting for transfers between devices, exchange_gather(): blocks[k] = lax.ppermute(blocks[k ^ low], axis, pair_perm(size, low))  21 us
    ppermute x9, starting transfers between devices, on_device(): lax.ppermute(held, 'island', pair_perm(n_chip, step, 2))  11.3 us
    ppermute x6, starting transfers between devices, exchange_gather(): blocks[k] = lax.ppermute(blocks[k ^ low], axis, pair_perm(size, low))  9.08 us
    ppermute x3, starting transfers between devices, on_device(): lax.ppermute(dquery, 'seq', pair_perm(n_seq, k))  6.1 us
    ppermute x3, starting transfers between devices, on_device(): lax.ppermute(own_blocks[k], 'seq', pair_perm(n_seq, k))  5.05 us
    ppermute x3, starting transfers between devices, on_device(): lax.ppermute(parts[step], 'island', pair_perm(n_chip, step, 2))  3.55 us
    ppermute x3, waiting for transfers between devices, on_device(): lax.ppermute(dquery, 'seq', pair_perm(n_seq, k))  3.36 us
    unnamed x10, local copies, waits for them, and re-layouts  3.09 us
  transfers between devices with their start and end apart: 27, of which 7 were waited for; matrix products, arithmetic and copies ran while one was open for 13% of the time, Pallas kernels for 4%

profile of v3, /device:TPU:0, one launch (start us, length us, event | category | flops | bytes accessed | tf_op | source)
XLA Modules:
  0.0 77.5 jit_solution(10707372386013737379)
XLA Ops:
  0.6 0.5 collective-permute-start.15
  1.1 0.9 %convert_bitcast_fusion.refs_0_ = bf16[32,1280]{1,0:T(8,128)(2,1)S(1)} fusion(f32[1280,32]{0,1:T(8,128)} %param.12), kind=kLoop, calls=%fused_computation.15 | loop fusion | flops 40960 | bytes 245760 | tf_op jit(solution)/shard_map/convert_element_type | solution.py:254
  2.1 2.7 %collective-permute-start.6 = (bf16[32,1280]{1,0:T(8,128)(2,1)S(1)}, bf16[32,1280]{1,0:T(8,128)(2,1)S(1)}, u32[]{:S(2)}, u32[]{:S(2)}) collective-permute-start(bf16[32,1280]{1,0:T(8,128)(2,1)S(1)} %convert_bitcast_fusion.refs_0_), channel_id=1, source_target_pairs={{0,1},{1,0},{2,3},{3,2},{4,5},{5,4},{6,7},{7,6},{8,9},{9,8},{10,11... | collective-permute-start | bytes 245768 | tf_op jit(solution)/shard_map/ppermute | solution.py:42
  4.7 2.6 %collective-permute-start.7 = (bf16[32,1280]{1,0:T(8,128)(2,1)S(1)}, bf16[32,1280]{1,0:T(8,128)(2,1)S(1)}, u32[]{:S(2)}, u32[]{:S(2)}) collective-permute-start(bf16[32,1280]{1,0:T(8,128)(2,1)S(1)} %convert_bitcast_fusion.refs_0_), channel_id=1, source_target_pairs={{0,2},{1,3},{2,0},{3,1},{4,6},{5,7},{6,4},{7,5},{8,10},{9,11},{10,... | collective-permute-start | bytes 245768 | tf_op jit(solution)/shard_map/ppermute | solution.py:42
  7.3 1.5 %collective-permute-start.3 = (bf16[32,1280]{1,0:T(8,128)(2,1)S(1)}, bf16[32,1280]{1,0:T(8,128)(2,1)S(1)}, u32[]{:S(2)}, u32[]{:S(2)}) collective-permute-start(bf16[32,1280]{1,0:T(8,128)(2,1)S(1)} %convert_bitcast_fusion.refs_0_), channel_id=1, source_target_pairs={{0,8},{4,12},{8,0},{12,4},{16,24},{20,28},{24,16},{28,20},{1,9},{5... | collective-permute-start | bytes 245768 | tf_op jit(solution)/shard_map/ppermute | solution.py:264
  8.8 1.5 %collective-permute-start.4 = (bf16[32,1280]{1,0:T(8,128)(2,1)S(1)}, bf16[32,1280]{1,0:T(8,128)(2,1)S(1)}, u32[]{:S(2)}, u32[]{:S(2)}) collective-permute-start(bf16[32,1280]{1,0:T(8,128)(2,1)S(1)} %convert_bitcast_fusion.refs_0_), channel_id=1, source_target_pairs={{0,16},{4,20},{8,24},{12,28},{16,0},{20,4},{24,8},{28,12},{1,17},{... | collective-permute-start | bytes 245768 | tf_op jit(solution)/shard_map/ppermute | solution.py:264
  10.3 0.5 collective-permute-start.5
  10.8 1.1 %collective-permute-done.7 = bf16[32,1280]{1,0:T(8,128)(2,1)S(1)} collective-permute-done((bf16[32,1280]{1,0:T(8,128)(2,1)S(1)}, bf16[32,1280]{1,0:T(8,128)(2,1)S(1)}, u32[]{:S(2)}, u32[]{:S(2)}) %collective-permute-start.7) | collective-permute-done | bytes 81952 | tf_op jit(solution)/shard_map/ppermute | solution.py:42
  12.0 2.4 %collective-permute-start.10 = (bf16[64,1280]{1,0:T(8,128)(2,1)S(1)}, bf16[64,1280]{1,0:T(8,128)(2,1)S(1)}, u32[]{:S(2)}, u32[]{:S(2)}) collective-permute-start(bf16[64,1280]{1,0:T(8,128)(2,1)S(1)} %constant_dynamic-update-slice_fusion.refs_4_), channel_id=1, source_target_pairs={{0,24},{4,28},{8,16},{12,20},{16,8},{20,12},{24,0},{28,4},{1,25},{... | collective-permute-start | bytes 491528 | tf_op jit(solution)/shard_map/ppermute | solution.py:264
  14.4 0.5 collective-permute-start.8
  14.9 0.9 %copy.19 = bf16[16,8,2,256]{3,1,2,0:T(8,128)(2,1)S(1)} copy(bf16[16,8,2,256]{3,2,1,0:T(2,128)(2,1)} %bitcast.63) | data formatting | bytes 262144
  15.9 1.0 %collective-permute-start.1 = (bf16[128,512]{1,0:T(8,128)(2,1)S(1)}, bf16[128,512]{1,0:T(8,128)(2,1)S(1)}, u32[]{:S(2)}, u32[]{:S(2)}) collective-permute-start(bf16[128,512]{1,0:T(8,128)(2,1)S(1)} %bitcast.53), channel_id=1, source_target_pairs={{0,2},{1,3},{2,0},{3,1},{4,6},{5,7},{6,4},{7,5},{8,10},{9,11},{10,... | collective-permute-start | bytes 393224 | tf_op jit(solution)/shard_map/ppermute | solution.py:42
  16.9 2.1 %collective-permute-start.11 = (bf16[32,1280]{1,0:T(8,128)(2,1)S(1)}, bf16[32,1280]{1,0:T(8,128)(2,1)S(1)}, u32[]{:S(2)}, u32[]{:S(2)}) collective-permute-start(bf16[32,1280]{1,0:T(8,128)(2,1)S(1)} %collective-permute-done.7), channel_id=1, source_target_pairs={{0,1},{1,0},{2,3},{3,2},{4,5},{5,4},{6,7},{7,6},{8,9},{9,8},{10,11... | collective-permute-start | bytes 245768 | tf_op jit(solution)/shard_map/ppermute | solution.py:42
  19.0 4.2 %collective-permute-done.1.refs_4_.refs_5_ = bf16[128,512]{1,0:T(8,128)(2,1)S(1)} collective-permute-done((bf16[128,512]{1,0:T(8,128)(2,1)S(1)}, bf16[128,512]{1,0:T(8,128)(2,1)S(1)}, u32[]{:S(2)}, u32[]{:S(2)}) %collective-permute-start.1) | collective-permute-done | bytes 131104 | tf_op jit(solution)/shard_map/ppermute | solution.py:42
  23.2 1.3 %collective-permute-start.9 = (bf16[64,1280]{1,0:T(8,128)(2,1)S(1)}, bf16[64,1280]{1,0:T(8,128)(2,1)S(1)}, u32[]{:S(2)}, u32[]{:S(2)}) collective-permute-start(bf16[64,1280]{1,0:T(8,128)(2,1)S(1)} %constant_dynamic-update-slice_fusion.refs_4_), channel_id=1, source_target_pairs={{0,16},{4,20},{8,24},{12,28},{16,0},{20,4},{24,8},{28,12},{1,17},{... | collective-permute-start | bytes 491528 | tf_op jit(solution)/shard_map/ppermute | solution.py:264
  24.5 1.0 %collective-permute-start.12 = (bf16[32,1280]{1,0:T(8,128)(2,1)S(1)}, bf16[32,1280]{1,0:T(8,128)(2,1)S(1)}, u32[]{:S(2)}, u32[]{:S(2)}) collective-permute-start(bf16[32,1280]{1,0:T(8,128)(2,1)S(1)} %collective-permute-done.11.refs_8_), channel_id=1, source_target_pairs={{0,8},{4,12},{8,0},{12,4},{16,24},{20,28},{24,16},{28,20},{1,9},{5... | collective-permute-start | bytes 245768 | tf_op jit(solution)/shard_map/ppermute | solution.py:264
  25.5 1.2 %collective-permute-start.13 = (bf16[32,1280]{1,0:T(8,128)(2,1)S(1)}, bf16[32,1280]{1,0:T(8,128)(2,1)S(1)}, u32[]{:S(2)}, u32[]{:S(2)}) collective-permute-start(bf16[32,1280]{1,0:T(8,128)(2,1)S(1)} %collective-permute-done.11.refs_8_), channel_id=1, source_target_pairs={{0,16},{4,20},{8,24},{12,28},{16,0},{20,4},{24,8},{28,12},{1,17},{... | collective-permute-start | bytes 245768 | tf_op jit(solution)/shard_map/ppermute | solution.py:264
  26.7 1.3 %collective-permute-start.14 = (bf16[32,1280]{1,0:T(8,128)(2,1)S(1)}, bf16[32,1280]{1,0:T(8,128)(2,1)S(1)}, u32[]{:S(2)}, u32[]{:S(2)}) collective-permute-start(bf16[32,1280]{1,0:T(8,128)(2,1)S(1)} %collective-permute-done.11.refs_8_), channel_id=1, source_target_pairs={{0,24},{4,28},{8,16},{12,20},{16,8},{20,12},{24,0},{28,4},{1,25},{... | collective-permute-start | bytes 245768 | tf_op jit(solution)/shard_map/ppermute | solution.py:264
  28.0 1.4 %dynamic-slice_bitcast_fusion = (bf16[128,1280]{1,0:T(8,128)(2,1)S(1)}, bf16[128,1280]{1,0:T(8,128)(2,1)S(1)}, bf16[128,1280]{1,0:T(8,128)(2,1)S(1)}, bf16[128,1280]{1,0:T(8,128)(2,1)S(1)}) fusion(bf16[1,128,5120]{2,1,0:T(8,128)(2,1)} %param.7, s32[]{:T(128)S(6)} %select_n.39, s32[]{:T(128)S(6)} %select_n.38, s32[]{:T(128)S(6)} %select_n.37, s32[]{:T(128)S(6)} %select_n.36), kind=kLoop, calls=%fused_computation.6 | loop fusion | bytes 2621456 | tf_op jit(solution)/shard_map/dynamic_slice | solution.py:250
  29.4 0.1 collective-permute-start
  29.5 2.0 %collective-permute-start.20 = (bf16[128,1280]{1,0:T(8,128)(2,1)S(1)}, bf16[128,1280]{1,0:T(8,128)(2,1)S(1)}, u32[]{:S(2)}, u32[]{:S(2)}) collective-permute-start(bf16[128,1280]{1,0:T(8,128)(2,1)S(1)} %get-tuple-element.40.refs_13_), channel_id=1, source_target_pairs={{0,1},{1,0},{2,3},{3,2},{4,5},{5,4},{6,7},{7,6},{8,9},{9,8},{10,11... | collective-permute-start | bytes 983048 | tf_op jit(solution)/shard_map/ppermute | solution.py:274
  31.5 1.6 %collective-permute-start.21 = (bf16[128,1280]{1,0:T(8,128)(2,1)S(1)}, bf16[128,1280]{1,0:T(8,128)(2,1)S(1)}, u32[]{:S(2)}, u32[]{:S(2)}) collective-permute-start(bf16[128,1280]{1,0:T(8,128)(2,1)S(1)} %get-tuple-element.39.refs_14_), channel_id=1, source_target_pairs={{0,2},{1,3},{2,0},{3,1},{4,6},{5,7},{6,4},{7,5},{8,10},{9,11},{10,... | collective-permute-start | bytes 983048 | tf_op jit(solution)/shard_map/ppermute | solution.py:274
  33.1 1.5 %collective-permute-start.22 = (bf16[128,1280]{1,0:T(8,128)(2,1)S(1)}, bf16[128,1280]{1,0:T(8,128)(2,1)S(1)}, u32[]{:S(2)}, u32[]{:S(2)}) collective-permute-start(bf16[128,1280]{1,0:T(8,128)(2,1)S(1)} %get-tuple-element.38.refs_15_), channel_id=1, source_target_pairs={{0,3},{1,2},{2,1},{3,0},{4,7},{5,6},{6,5},{7,4},{8,11},{9,10},{10,... | collective-permute-start | bytes 983048 | tf_op jit(solution)/shard_map/ppermute | solution.py:274
  34.6 0.6 collective-permute-start.2
  35.1 1.4 %constant_dynamic-slice_fusion = (bf16[128,1280]{1,0:T(8,128)(2,1)S(1)}, bf16[128,1280]{1,0:T(8,128)(2,1)S(1)}, bf16[128,1280]{1,0:T(8,128)(2,1)S(1)}, bf16[128,1280]{1,0:T(8,128)(2,1)S(1)}) fusion(bf16[128,5120]{1,0:T(8,128)(2,1)} %collective-permute-done.15, s32[]{:T(128)S(6)} %select_n.39, s32[]{:T(128)S(6)} %select_n.38, s32[]{:T(128)S(6)} %select_n.37, ...), kind=kLoop, calls=%fused_computation.18 | loop fusion | bytes 2621456 | tf_op jit(solution)/shard_map/dynamic_slice | solution.py:250
  36.5 1.0 %shard_map.102 = (bf16[4,32,128]{2,1,0:T(8,128)(2,1)S(1)}, bf16[4,32,128]{2,1,0:T(8,128)(2,1)S(1)}) custom-call(bf16[32,1280]{1,0:T(8,128)(2,1)S(1)} %convert_bitcast_fusion.refs_0_, bf16[32,1280]{1,0:T(8,128)(2,1)S(1)} %collective-permute-done.3.refs_1_, bf16[32,1280]{1,0:T(8,128)(2,1)S(1)} %collective-permute-done.4.refs_2_, ...), custom_call_target="tpu_custom_call" | custom-call | flops 335544320 | bytes 3932160 | tf_op jit(solution)/shard_map/pallas_call | solution.py:74
  37.5 0.1 collective-permute-start.16
  37.6 15.7 %collective-permute-done.2.refs_6_.refs_7_ = bf16[128,512]{1,0:T(8,128)(2,1)S(1)} collective-permute-done((bf16[128,512]{1,0:T(8,128)(2,1)S(1)}, bf16[128,512]{1,0:T(8,128)(2,1)S(1)}, u32[]{:S(2)}, u32[]{:S(2)}) %collective-permute-start.2) | collective-permute-done | bytes 131104 | tf_op jit(solution)/shard_map/ppermute | solution.py:42
  53.3 1.2 %shard_map.103.refs_0_ = bf16[256,128]{1,0:T(8,128)(2,1)S(1)} custom-call(bf16[128,512]{1,0:T(8,128)(2,1)S(1)} %bitcast.55, bf16[128,512]{1,0:T(8,128)(2,1)S(1)} %bitcast.56, bf16[128,512]{1,0:T(8,128)(2,1)S(1)} %collective-permute-done.refs_2_.refs_3_, bf16[128,512]{1,0:T(8,128)(2,1)S(1)} %collective-permute-done.refs_2_.refs_3_, ...), custom_call_target="tpu_custom_call" | custom-call | flops 402653184 | bytes 786432 | tf_op jit(solution)/shard_map/pallas_call | solution.py:153
  54.5 2.5 %collective-permute-start.17 = (bf16[256,128]{1,0:T(8,128)(2,1)S(1)}, bf16[256,128]{1,0:T(8,128)(2,1)S(1)}, u32[]{:S(2)}, u32[]{:S(2)}) collective-permute-start(bf16[256,128]{1,0:T(8,128)(2,1)S(1)} %shard_map.103.refs_0_), channel_id=1, source_target_pairs={{0,1},{1,0},{2,3},{3,2},{4,5},{5,4},{6,7},{7,6},{8,9},{9,8},{10,11... | collective-permute-start | bytes 196616 | tf_op jit(solution)/shard_map/ppermute | solution.py:283
  57.1 3.5 %collective-permute-start.18 = (bf16[256,128]{1,0:T(8,128)(2,1)S(1)}, bf16[256,128]{1,0:T(8,128)(2,1)S(1)}, u32[]{:S(2)}, u32[]{:S(2)}) collective-permute-start(bf16[256,128]{1,0:T(8,128)(2,1)S(1)} %shard_map.103.refs_0_), channel_id=1, source_target_pairs={{0,2},{1,3},{2,0},{3,1},{4,6},{5,7},{6,4},{7,5},{8,10},{9,11},{10,... | collective-permute-start | bytes 196616 | tf_op jit(solution)/shard_map/ppermute | solution.py:283
  60.6 1.3 %copy.14 = bf16[256,1280]{1,0:T(8,128)(2,1)S(1)} copy(bf16[256,1280]{0,1:T(8,128)(2,1)} %bitcast.61) | data formatting | bytes 1310720 | tf_op jit(solution)/shard_map/transpose | solution.py:287
  62.0 1.3 %copy.13 = bf16[256,1280]{1,0:T(8,128)(2,1)S(1)} copy(bf16[256,1280]{0,1:T(8,128)(2,1)} %bitcast.62) | data formatting | bytes 1310720 | tf_op jit(solution)/shard_map/transpose | solution.py:286
  63.4 0.2 collective-permute-done.18.refs_2_
  63.6 3.1 %collective-permute-done.19.refs_3_ = bf16[256,128]{1,0:T(8,128)(2,1)S(1)} collective-permute-done((bf16[256,128]{1,0:T(8,128)(2,1)S(1)}, bf16[256,128]{1,0:T(8,128)(2,1)S(1)}, u32[]{:S(2)}, u32[]{:S(2)}) %collective-permute-start.19) | collective-permute-done | bytes 65568 | tf_op jit(solution)/shard_map/ppermute | solution.py:283
  66.7 0.7 shard_map.105
  67.4 0.1 collective-permute-start.23
  67.5 0.7 shard_map.104
  68.1 0.1 select_bitcast_fusion.1
  68.3 0.8 %collective-permute-done.23.got_ref = bf16[4,32,1280]{2,1,0:T(8,128)(2,1)S(1)} collective-permute-done((bf16[4,32,1280]{2,1,0:T(8,128)(2,1)S(1)}, bf16[4,32,1280]{2,1,0:T(8,128)(2,1)S(1)}, u32[]{:S(2)}, u32[]{:S(2)}) %collective-permute-start.23) | collective-permute-done | bytes 327712 | tf_op jit(solution)/shard_map/ppermute | solution.py:291
  69.1 0.1 shard_map.106
  69.2 1.4 %collective-permute-start.24 = (bf16[32,1280]{1,0:T(8,128)(2,1)S(1)}, bf16[32,1280]{1,0:T(8,128)(2,1)S(1)}, u32[]{:S(2)}, u32[]{:S(2)}) collective-permute-start(bf16[32,1280]{1,0:T(8,128)(2,1)S(1)} %get-tuple-element.21), channel_id=1, source_target_pairs={{0,8},{4,12},{8,0},{12,4},{16,24},{20,28},{24,16},{28,20},{1,9},{5... | collective-permute-start | bytes 245768 | tf_op jit(solution)/shard_map/ppermute | solution.py:304
  70.5 0.7 collective-permute-start.25
  71.2 1.5 %collective-permute-start.26 = (bf16[32,1280]{1,0:T(8,128)(2,1)S(1)}, bf16[32,1280]{1,0:T(8,128)(2,1)S(1)}, u32[]{:S(2)}, u32[]{:S(2)}) collective-permute-start(bf16[32,1280]{1,0:T(8,128)(2,1)S(1)} %get-tuple-element.23), channel_id=1, source_target_pairs={{0,24},{4,28},{8,16},{12,20},{16,8},{20,12},{24,0},{28,4},{1,25},{... | collective-permute-start | bytes 245768 | tf_op jit(solution)/shard_map/ppermute | solution.py:304
  72.8 1.1 %copy.18 = bf16[1,1280,256]{2,1,0:T(8,128)(2,1)} copy(bf16[1,1280,256]{1,2,0:T(8,128)(2,1)S(1)} %bitcast.58) | data formatting | bytes 1310720
  74.0 1.1 %copy.17 = bf16[1,1280,256]{2,1,0:T(8,128)(2,1)} copy(bf16[1,1280,256]{1,2,0:T(8,128)(2,1)S(1)} %bitcast.59) | data formatting | bytes 1310720
  75.0 1.7 %collective-permute-done.25 = bf16[32,1280]{1,0:T(8,128)(2,1)S(1)} collective-permute-done((bf16[32,1280]{1,0:T(8,128)(2,1)S(1)}, bf16[32,1280]{1,0:T(8,128)(2,1)S(1)}, u32[]{:S(2)}, u32[]{:S(2)}) %collective-permute-start.25) | collective-permute-done | bytes 81952 | tf_op jit(solution)/shard_map/ppermute | solution.py:304
  76.8 0.8 %fusion.1 = (f32[1280,32]{0,1:T(8,128)}, f32[1280,32]{0,1:T(8,128)}) fusion(f32[1280,32]{0,1:T(8,128)S(1)} %copy-done.1, bf16[32,1280]{1,0:T(8,128)(2,1)S(1)} %collective-permute-done.26, bf16[32,1280]{1,0:T(8,128)(2,1)S(1)} %collective-permute-done.25, f32[32,1280]{1,0:T(8,128)S(1)} %get-tuple-element.20, bf16[32,1280]{1,0:T(8,128)(2,1)S(1)} %collective-permute-done.24, ...), kind=kLoop, calls=%fused_computation.13 | loop fusion | flops 532480 | bytes 1064960 | tf_op jit(solution)/shard_map/sub | solution.py:309
  (33 shorter events, 0.3 us)
Async XLA Ops:
  0.6 34.0 %collective-permute-start.15 = (bf16[128,5120]{1,0:T(8,128)(2,1)}, bf16[128,5120]{1,0:T(8,128)(2,1)}, u32[]{:S(2)}, u32[]{:S(2)}) collective-permute-start(bf16[128,5120]{1,0:T(8,128)(2,1)} %bitcast.60), channel_id=1, source_target_pairs={{0,4},{4,0},{8,12},{12,8},{16,20},{20,16},{24,28},{28,24},{1,5},{5... | collective-permute-start | bytes 3932168 | tf_op jit(solution)/shard_map/ppermute | solution.py:269
  2.1 8.3 %collective-permute-start.6 = (bf16[32,1280]{1,0:T(8,128)(2,1)S(1)}, bf16[32,1280]{1,0:T(8,128)(2,1)S(1)}, u32[]{:S(2)}, u32[]{:S(2)}) collective-permute-start(bf16[32,1280]{1,0:T(8,128)(2,1)S(1)} %convert_bitcast_fusion.refs_0_), channel_id=1, source_target_pairs={{0,1},{1,0},{2,3},{3,2},{4,5},{5,4},{6,7},{7,6},{8,9},{9,8},{10,11... | collective-permute-start | bytes 245768 | tf_op jit(solution)/shard_map/ppermute | solution.py:42
  4.7 7.2 %collective-permute-start.7 = (bf16[32,1280]{1,0:T(8,128)(2,1)S(1)}, bf16[32,1280]{1,0:T(8,128)(2,1)S(1)}, u32[]{:S(2)}, u32[]{:S(2)}) collective-permute-start(bf16[32,1280]{1,0:T(8,128)(2,1)S(1)} %convert_bitcast_fusion.refs_0_), channel_id=1, source_target_pairs={{0,2},{1,3},{2,0},{3,1},{4,6},{5,7},{6,4},{7,5},{8,10},{9,11},{10,... | collective-permute-start | bytes 245768 | tf_op jit(solution)/shard_map/ppermute | solution.py:42
  7.3 7.1 %collective-permute-start.3 = (bf16[32,1280]{1,0:T(8,128)(2,1)S(1)}, bf16[32,1280]{1,0:T(8,128)(2,1)S(1)}, u32[]{:S(2)}, u32[]{:S(2)}) collective-permute-start(bf16[32,1280]{1,0:T(8,128)(2,1)S(1)} %convert_bitcast_fusion.refs_0_), channel_id=1, source_target_pairs={{0,8},{4,12},{8,0},{12,4},{16,24},{20,28},{24,16},{28,20},{1,9},{5... | collective-permute-start | bytes 245768 | tf_op jit(solution)/shard_map/ppermute | solution.py:264
  8.8 7.1 %collective-permute-start.4 = (bf16[32,1280]{1,0:T(8,128)(2,1)S(1)}, bf16[32,1280]{1,0:T(8,128)(2,1)S(1)}, u32[]{:S(2)}, u32[]{:S(2)}) collective-permute-start(bf16[32,1280]{1,0:T(8,128)(2,1)S(1)} %convert_bitcast_fusion.refs_0_), channel_id=1, source_target_pairs={{0,16},{4,20},{8,24},{12,28},{16,0},{20,4},{24,8},{28,12},{1,17},{... | collective-permute-start | bytes 245768 | tf_op jit(solution)/shard_map/ppermute | solution.py:264
  10.3 6.5 %collective-permute-start.5 = (bf16[32,1280]{1,0:T(8,128)(2,1)S(1)}, bf16[32,1280]{1,0:T(8,128)(2,1)S(1)}, u32[]{:S(2)}, u32[]{:S(2)}) collective-permute-start(bf16[32,1280]{1,0:T(8,128)(2,1)S(1)} %convert_bitcast_fusion.refs_0_), channel_id=1, source_target_pairs={{0,24},{4,28},{8,16},{12,20},{16,8},{20,12},{24,0},{28,4},{1,25},{... | collective-permute-start | bytes 245768 | tf_op jit(solution)/shard_map/ppermute | solution.py:264
  12.0 13.6 %collective-permute-start.10 = (bf16[64,1280]{1,0:T(8,128)(2,1)S(1)}, bf16[64,1280]{1,0:T(8,128)(2,1)S(1)}, u32[]{:S(2)}, u32[]{:S(2)}) collective-permute-start(bf16[64,1280]{1,0:T(8,128)(2,1)S(1)} %constant_dynamic-update-slice_fusion.refs_4_), channel_id=1, source_target_pairs={{0,24},{4,28},{8,16},{12,20},{16,8},{20,12},{24,0},{28,4},{1,25},{... | collective-permute-start | bytes 491528 | tf_op jit(solution)/shard_map/ppermute | solution.py:264
  14.4 12.3 %collective-permute-start.8 = (bf16[64,1280]{1,0:T(8,128)(2,1)S(1)}, bf16[64,1280]{1,0:T(8,128)(2,1)S(1)}, u32[]{:S(2)}, u32[]{:S(2)}) collective-permute-start(bf16[64,1280]{1,0:T(8,128)(2,1)S(1)} %constant_dynamic-update-slice_fusion.refs_4_), channel_id=1, source_target_pairs={{0,8},{4,12},{8,0},{12,4},{16,24},{20,28},{24,16},{28,20},{1,9},{5... | collective-permute-start | bytes 491528 | tf_op jit(solution)/shard_map/ppermute | solution.py:264
  15.9 7.3 %collective-permute-start.1 = (bf16[128,512]{1,0:T(8,128)(2,1)S(1)}, bf16[128,512]{1,0:T(8,128)(2,1)S(1)}, u32[]{:S(2)}, u32[]{:S(2)}) collective-permute-start(bf16[128,512]{1,0:T(8,128)(2,1)S(1)} %bitcast.53), channel_id=1, source_target_pairs={{0,2},{1,3},{2,0},{3,1},{4,6},{5,7},{6,4},{7,5},{8,10},{9,11},{10,... | collective-permute-start | bytes 393224 | tf_op jit(solution)/shard_map/ppermute | solution.py:42
  16.9 7.6 %collective-permute-start.11 = (bf16[32,1280]{1,0:T(8,128)(2,1)S(1)}, bf16[32,1280]{1,0:T(8,128)(2,1)S(1)}, u32[]{:S(2)}, u32[]{:S(2)}) collective-permute-start(bf16[32,1280]{1,0:T(8,128)(2,1)S(1)} %collective-permute-done.7), channel_id=1, source_target_pairs={{0,1},{1,0},{2,3},{3,2},{4,5},{5,4},{6,7},{7,6},{8,9},{9,8},{10,11... | collective-permute-start | bytes 245768 | tf_op jit(solution)/shard_map/ppermute | solution.py:42
  23.2 6.2 %collective-permute-start.9 = (bf16[64,1280]{1,0:T(8,128)(2,1)S(1)}, bf16[64,1280]{1,0:T(8,128)(2,1)S(1)}, u32[]{:S(2)}, u32[]{:S(2)}) collective-permute-start(bf16[64,1280]{1,0:T(8,128)(2,1)S(1)} %constant_dynamic-update-slice_fusion.refs_4_), channel_id=1, source_target_pairs={{0,16},{4,20},{8,24},{12,28},{16,0},{20,4},{24,8},{28,12},{1,17},{... | collective-permute-start | bytes 491528 | tf_op jit(solution)/shard_map/ppermute | solution.py:264
  24.5 5.0 %collective-permute-start.12 = (bf16[32,1280]{1,0:T(8,128)(2,1)S(1)}, bf16[32,1280]{1,0:T(8,128)(2,1)S(1)}, u32[]{:S(2)}, u32[]{:S(2)}) collective-permute-start(bf16[32,1280]{1,0:T(8,128)(2,1)S(1)} %collective-permute-done.11.refs_8_), channel_id=1, source_target_pairs={{0,8},{4,12},{8,0},{12,4},{16,24},{20,28},{24,16},{28,20},{1,9},{5... | collective-permute-start | bytes 245768 | tf_op jit(solution)/shard_map/ppermute | solution.py:264
  25.5 6.0 %collective-permute-start.13 = (bf16[32,1280]{1,0:T(8,128)(2,1)S(1)}, bf16[32,1280]{1,0:T(8,128)(2,1)S(1)}, u32[]{:S(2)}, u32[]{:S(2)}) collective-permute-start(bf16[32,1280]{1,0:T(8,128)(2,1)S(1)} %collective-permute-done.11.refs_8_), channel_id=1, source_target_pairs={{0,16},{4,20},{8,24},{12,28},{16,0},{20,4},{24,8},{28,12},{1,17},{... | collective-permute-start | bytes 245768 | tf_op jit(solution)/shard_map/ppermute | solution.py:264
  26.7 6.4 %collective-permute-start.14 = (bf16[32,1280]{1,0:T(8,128)(2,1)S(1)}, bf16[32,1280]{1,0:T(8,128)(2,1)S(1)}, u32[]{:S(2)}, u32[]{:S(2)}) collective-permute-start(bf16[32,1280]{1,0:T(8,128)(2,1)S(1)} %collective-permute-done.11.refs_8_), channel_id=1, source_target_pairs={{0,24},{4,28},{8,16},{12,20},{16,8},{20,12},{24,0},{28,4},{1,25},{... | collective-permute-start | bytes 245768 | tf_op jit(solution)/shard_map/ppermute | solution.py:264
  29.4 8.1 %collective-permute-start = (bf16[128,512]{1,0:T(8,128)(2,1)S(1)}, bf16[128,512]{1,0:T(8,128)(2,1)S(1)}, u32[]{:S(2)}, u32[]{:S(2)}) collective-permute-start(bf16[128,512]{1,0:T(8,128)(2,1)S(1)} %bitcast.54), channel_id=1, source_target_pairs={{0,1},{1,0},{2,3},{3,2},{4,5},{5,4},{6,7},{7,6},{8,9},{9,8},{10,11... | collective-permute-start | bytes 393224 | tf_op jit(solution)/shard_map/ppermute | solution.py:42
  29.5 31.1 %collective-permute-start.20 = (bf16[128,1280]{1,0:T(8,128)(2,1)S(1)}, bf16[128,1280]{1,0:T(8,128)(2,1)S(1)}, u32[]{:S(2)}, u32[]{:S(2)}) collective-permute-start(bf16[128,1280]{1,0:T(8,128)(2,1)S(1)} %get-tuple-element.40.refs_13_), channel_id=1, source_target_pairs={{0,1},{1,0},{2,3},{3,2},{4,5},{5,4},{6,7},{7,6},{8,9},{9,8},{10,11... | collective-permute-start | bytes 983048 | tf_op jit(solution)/shard_map/ppermute | solution.py:274
  31.5 31.8 %collective-permute-start.21 = (bf16[128,1280]{1,0:T(8,128)(2,1)S(1)}, bf16[128,1280]{1,0:T(8,128)(2,1)S(1)}, u32[]{:S(2)}, u32[]{:S(2)}) collective-permute-start(bf16[128,1280]{1,0:T(8,128)(2,1)S(1)} %get-tuple-element.39.refs_14_), channel_id=1, source_target_pairs={{0,2},{1,3},{2,0},{3,1},{4,6},{5,7},{6,4},{7,5},{8,10},{9,11},{10,... | collective-permute-start | bytes 983048 | tf_op jit(solution)/shard_map/ppermute | solution.py:274
  33.1 30.2 %collective-permute-start.22 = (bf16[128,1280]{1,0:T(8,128)(2,1)S(1)}, bf16[128,1280]{1,0:T(8,128)(2,1)S(1)}, u32[]{:S(2)}, u32[]{:S(2)}) collective-permute-start(bf16[128,1280]{1,0:T(8,128)(2,1)S(1)} %get-tuple-element.38.refs_15_), channel_id=1, source_target_pairs={{0,3},{1,2},{2,1},{3,0},{4,7},{5,6},{6,5},{7,4},{8,11},{9,10},{10,... | collective-permute-start | bytes 983048 | tf_op jit(solution)/shard_map/ppermute | solution.py:274
  34.6 18.7 %collective-permute-start.2 = (bf16[128,512]{1,0:T(8,128)(2,1)S(1)}, bf16[128,512]{1,0:T(8,128)(2,1)S(1)}, u32[]{:S(2)}, u32[]{:S(2)}) collective-permute-start(bf16[128,512]{1,0:T(8,128)(2,1)S(1)} %collective-permute-done.1.refs_4_.refs_5_), channel_id=1, source_target_pairs={{0,1},{1,0},{2,3},{3,2},{4,5},{5,4},{6,7},{7,6},{8,9},{9,8},{10,11... | collective-permute-start | bytes 393224 | tf_op jit(solution)/shard_map/ppermute | solution.py:42
  36.5 16.8 %copy-start = (bf16[1,128,256]{2,1,0:T(8,128)(2,1)S(1)}, bf16[1,128,256]{2,1,0:T(8,128)(2,1)}, u32[]{:S(2)}) copy-start(bf16[1,128,256]{2,1,0:T(8,128)(2,1)} %param.9) | copy-start | bytes 196612
  37.5 15.8 %collective-permute-start.16 = (bf16[4,32,128]{2,1,0:T(8,128)(2,1)S(1)}, bf16[4,32,128]{2,1,0:T(8,128)(2,1)S(1)}, u32[]{:S(2)}, u32[]{:S(2)}) collective-permute-start(bf16[4,32,128]{2,1,0:T(8,128)(2,1)S(1)} %get-tuple-element.17), channel_id=1, source_target_pairs={{0,4},{4,0},{8,12},{12,8},{16,20},{20,16},{24,28},{28,24},{1,5},{5... | collective-permute-start | bytes 98312 | tf_op jit(solution)/shard_map/ppermute | solution.py:280
  54.5 8.8 %collective-permute-start.17 = (bf16[256,128]{1,0:T(8,128)(2,1)S(1)}, bf16[256,128]{1,0:T(8,128)(2,1)S(1)}, u32[]{:S(2)}, u32[]{:S(2)}) collective-permute-start(bf16[256,128]{1,0:T(8,128)(2,1)S(1)} %shard_map.103.refs_0_), channel_id=1, source_target_pairs={{0,1},{1,0},{2,3},{3,2},{4,5},{5,4},{6,7},{7,6},{8,9},{9,8},{10,11... | collective-permute-start | bytes 196616 | tf_op jit(solution)/shard_map/ppermute | solution.py:283
  57.1 6.5 %collective-permute-start.18 = (bf16[256,128]{1,0:T(8,128)(2,1)S(1)}, bf16[256,128]{1,0:T(8,128)(2,1)S(1)}, u32[]{:S(2)}, u32[]{:S(2)}) collective-permute-start(bf16[256,128]{1,0:T(8,128)(2,1)S(1)} %shard_map.103.refs_0_), channel_id=1, source_target_pairs={{0,2},{1,3},{2,0},{3,1},{4,6},{5,7},{6,4},{7,5},{8,10},{9,11},{10,... | collective-permute-start | bytes 196616 | tf_op jit(solution)/shard_map/ppermute | solution.py:283
  60.6 6.1 %collective-permute-start.19 = (bf16[256,128]{1,0:T(8,128)(2,1)S(1)}, bf16[256,128]{1,0:T(8,128)(2,1)S(1)}, u32[]{:S(2)}, u32[]{:S(2)}) collective-permute-start(bf16[256,128]{1,0:T(8,128)(2,1)S(1)} %shard_map.103.refs_0_), channel_id=1, source_target_pairs={{0,3},{1,2},{2,1},{3,0},{4,7},{5,6},{6,5},{7,4},{8,11},{9,10},{10,... | collective-permute-start | bytes 196616 | tf_op jit(solution)/shard_map/ppermute | solution.py:283
  67.4 1.7 %collective-permute-start.23 = (bf16[4,32,1280]{2,1,0:T(8,128)(2,1)S(1)}, bf16[4,32,1280]{2,1,0:T(8,128)(2,1)S(1)}, u32[]{:S(2)}, u32[]{:S(2)}) collective-permute-start(bf16[4,32,1280]{2,1,0:T(8,128)(2,1)S(1)} %get-tuple-element.19), channel_id=1, source_target_pairs={{0,4},{4,0},{8,12},{12,8},{16,20},{20,16},{24,28},{28,24},{1,5},{5... | collective-permute-start | bytes 983048 | tf_op jit(solution)/shard_map/ppermute | solution.py:291
  69.2 5.9 %collective-permute-start.24 = (bf16[32,1280]{1,0:T(8,128)(2,1)S(1)}, bf16[32,1280]{1,0:T(8,128)(2,1)S(1)}, u32[]{:S(2)}, u32[]{:S(2)}) collective-permute-start(bf16[32,1280]{1,0:T(8,128)(2,1)S(1)} %get-tuple-element.21), channel_id=1, source_target_pairs={{0,8},{4,12},{8,0},{12,4},{16,24},{20,28},{24,16},{28,20},{1,9},{5... | collective-permute-start | bytes 245768 | tf_op jit(solution)/shard_map/ppermute | solution.py:304
  70.5 6.2 %collective-permute-start.25 = (bf16[32,1280]{1,0:T(8,128)(2,1)S(1)}, bf16[32,1280]{1,0:T(8,128)(2,1)S(1)}, u32[]{:S(2)}, u32[]{:S(2)}) collective-permute-start(bf16[32,1280]{1,0:T(8,128)(2,1)S(1)} %get-tuple-element.22), channel_id=1, source_target_pairs={{0,16},{4,20},{8,24},{12,28},{16,0},{20,4},{24,8},{28,12},{1,17},{... | collective-permute-start | bytes 245768 | tf_op jit(solution)/shard_map/ppermute | solution.py:304
  71.2 5.5 %collective-permute-start.26 = (bf16[32,1280]{1,0:T(8,128)(2,1)S(1)}, bf16[32,1280]{1,0:T(8,128)(2,1)S(1)}, u32[]{:S(2)}, u32[]{:S(2)}) collective-permute-start(bf16[32,1280]{1,0:T(8,128)(2,1)S(1)} %get-tuple-element.23), channel_id=1, source_target_pairs={{0,24},{4,28},{8,16},{12,20},{16,8},{20,12},{24,0},{28,4},{1,25},{... | collective-permute-start | bytes 245768 | tf_op jit(solution)/shard_map/ppermute | solution.py:304
  73.9 2.8 %copy-start.1 = (f32[1280,32]{0,1:T(8,128)S(1)}, f32[1280,32]{0,1:T(8,128)}, u32[]{:S(2)}) copy-start(f32[1280,32]{0,1:T(8,128)} %param.12) | copy-start | bytes 491524
  73.9 2.8 %copy-start.2 = (f32[1280,32]{0,1:T(8,128)S(1)}, f32[1280,32]{0,1:T(8,128)}, u32[]{:S(2)}) copy-start(f32[1280,32]{0,1:T(8,128)} %param.13) | copy-start | bytes 491524

commit v4 on v3

--- a/solution.py
+++ b/solution.py
@@ -35,11 +35,19 @@
     ]
 
 
-def exchange_gather(own, axis, size):
+def exchange_start(own, axis, size):
     blocks = [own] + [None] * (size - 1)
-    for k in sorted(range(1, size), key=lambda k: (bin(k).count("1"), -k)):
-        low = k & -k
-        blocks[k] = lax.ppermute(blocks[k ^ low], axis, pair_perm(size, low))
+    for bit in reversed(range(size.bit_length() - 1)):
+        blocks[1 << bit] = lax.ppermute(own, axis, pair_perm(size, 1 << bit))
+    return blocks
+
+
+def exchange_finish(blocks, axis, size):
+    blocks = list(blocks)
+    for k in sorted(range(1, size), key=lambda k: (bin(k).count("1"), k)):
+        if blocks[k] is None:
+            low = k & -k
+            blocks[k] = lax.ppermute(blocks[k ^ low], axis, pair_perm(size, low))
     return blocks
 
 
@@ -251,31 +259,33 @@
             for k in range(n_seq)
         ]
 
-    weights = exchange_gather(anchor.T.astype(jnp.bfloat16), "seq", n_seq)
-    rounds = [[0], [k for k in range(1, n_seq) if k & (k - 1) == 0]]
-    rounds.append([k for k in range(n_seq) if k not in rounds[0] + rounds[1]])
-    rounds = [r for r in rounds if r]
-    spread = []
-    for ks in rounds:
-        held = jnp.concatenate([weights[k] for k in ks], axis=0)
-        spread.append(
-            [held]
-            + [
-                lax.ppermute(held, "island", pair_perm(n_chip, step, 2))
-                for step in range(1, n_chip)
-            ]
-        )
-
     partner_tokens = lax.ppermute(tokens, "island", swap)
-    kv = exchange_gather(key_vals[0].reshape(rows, 2 * cols), "seq", n_seq)
+    singles = [1 << j for j in range(n_seq.bit_length() - 1)]
+    weights = exchange_start(anchor.T.astype(jnp.bfloat16), "seq", n_seq)
+    own_kv = key_vals[0].reshape(rows, 2 * cols)
+    (weights_ready, own_kv, partner_tokens) = lax.optimization_barrier(
+        ([weights[k] for k in singles], own_kv, partner_tokens)
+    )
+    for k, value in zip(singles, weights_ready):
+        weights[k] = value
+    weights = exchange_finish(weights, "seq", n_seq)
+    kv = exchange_finish(exchange_start(own_kv, "seq", n_seq), "seq", n_seq)
+
+    rounds = [list(range(n_seq))]
+    held = jnp.concatenate(weights, axis=0)
+    spread = [held] + [
+        lax.ppermute(held, "island", pair_perm(n_chip, step, 2)) for step in range(1, n_chip)
+    ]
 
     own_blocks = feature_blocks(tokens)
-    gathered = [own_blocks[0]] + [
-        lax.ppermute(own_blocks[k], "seq", pair_perm(n_seq, k)) for k in range(1, n_seq)
+    far, kv = lax.optimization_barrier((own_blocks[2:], kv))
+    near, spread[1] = lax.optimization_barrier((own_blocks[1], spread[1]))
+    gathered = [own_blocks[0], lax.ppermute(near, "seq", pair_perm(n_seq, 1))] + [
+        lax.ppermute(piece, "seq", pair_perm(n_seq, k)) for k, piece in enumerate(far, 2)
     ]
 
     mine, for_partner = half_queries(
-        rounds, spread, own_blocks, feature_blocks(partner_tokens), share, inverse
+        rounds, [spread], own_blocks, feature_blocks(partner_tokens), share, inverse
     )
     other = lax.ppermute(for_partner, "island", swap)
     dquery = attention(kv, mine, other, cotangent[0])

time: 77.8 us -> 73.9 us (0.950)
  starting transfers between devices: 35.7 us -> 27.5 us
  waiting for transfers between devices: 26.9 us -> 30.4 us
  Pallas kernels: 3.61 us -> 5.57 us
  local copies, waits for them, and re-layouts: 8.56 us -> 7.33 us
    ppermute x3, waiting for transfers between devices: 3.36 us -> 18.5 us  [on_device(): lax.ppermute(dquery, 'seq', pair_perm(n_seq, k))]
    ppermute x9, waiting for transfers between devices: 21 us -> 8.05 us  [the longest x2 4.29 us: exchange_finish(): blocks[k] = lax.ppermute(blocks[k ^ low], axis, pair_perm(size, low))]
    ppermute x9 -> x3, starting transfers between devices: 11.3 us -> 3.67 us  [on_device(): lax.ppermute(held, 'island', pair_perm(n_chip, step, 2))]
    ppermute x3, starting transfers between devices: 6.1 us -> 3.73 us  [on_device(): lax.ppermute(dquery, 'seq', pair_perm(n_seq, k))]
    pallas_call x2, Pallas kernels: 1.32 us -> 3.27 us  [gradient_adam(): pl.pallas_call(functools.partial(adam_kernel, n_seq, n_chip, own_half, in...]
    ppermute x9, starting transfers between devices: 14.1 us -> 15.8 us  [the longest x4 8.86 us: exchange_start(): blocks[1 << bit] = lax.ppermute(own, axis, pair_perm(size, 1 << bit))]
    dynamic_slice x2, local copies, waits for them, and re-layouts: 2.71 us -> 1.49 us  [feature_blocks(): lax.dynamic_slice(matrix, (0, jnp.bitwise_xor(seq, k) * block), (rows, bl...]
    ppermute x1, waiting for transfers between devices: 0.01 us -> 1.19 us  [on_device(): other = lax.ppermute(for_partner, 'island', swap)]
  transfers between devices with their start and end apart: 27 -> 21, of which waited for: 7 -> 10; matrix products, arithmetic and copies ran while one was open for 13% -> 12% of each run, Pallas kernels for 4% -> 5%
where the time goes in v4:
time: 73.9 us; the launch traced here: 73.5 us
  waiting for transfers between devices  30.4 us (41%)
  starting transfers between devices  27.5 us (37%)
  local copies, waits for them, and re-layouts  7.33 us (10%)
  Pallas kernels  5.57 us (8%)
  other arithmetic  1.96 us (3%)
  between operations  0.79 us (1%)
    ppermute x3, waiting for transfers between devices, on_device(): lax.ppermute(dquery, 'seq', pair_perm(n_seq, k))  18.5 us
    ppermute x4, starting transfers between devices, exchange_start(): blocks[1 << bit] = lax.ppermute(own, axis, pair_perm(size, 1 << bit))  8.86 us
    ppermute x2, starting transfers between devices, on_device(): lax.ppermute(piece, 'seq', pair_perm(n_seq, k))  5.04 us
    ppermute x2, waiting for transfers between devices, exchange_finish(): blocks[k] = lax.ppermute(blocks[k ^ low], axis, pair_perm(size, low))  4.29 us
    ppermute x4, waiting for transfers between devices, exchange_start(): blocks[1 << bit] = lax.ppermute(own, axis, pair_perm(size, 1 << bit))  3.75 us
    ppermute x3, starting transfers between devices, on_device(): lax.ppermute(dquery, 'seq', pair_perm(n_seq, k))  3.73 us
    ppermute x3, starting transfers between devices, on_device(): lax.ppermute(held, 'island', pair_perm(n_chip, step, 2))  3.67 us
    ppermute x3, starting transfers between devices, on_device(): lax.ppermute(parts[step], 'island', pair_perm(n_chip, step, 2))  3.55 us
  transfers between devices with their start and end apart: 21, of which 10 were waited for; matrix products, arithmetic and copies ran while one was open for 12% of the time, Pallas kernels for 5%

profile of v4, /device:TPU:0, one launch (start us, length us, event | category | flops | bytes accessed | tf_op | source)
XLA Modules:
  0.0 73.5 jit_solution(12311177792010035345)
XLA Ops:
  0.6 0.5 collective-permute-start.2
  1.1 0.9 %convert_bitcast_fusion = bf16[32,1280]{1,0:T(8,128)(2,1)S(1)} fusion(f32[1280,32]{0,1:T(8,128)} %param.12), kind=kLoop, calls=%fused_computation.16 | loop fusion | flops 40960 | bytes 245760 | tf_op jit(solution)/shard_map/convert_element_type | solution.py:264
  2.1 2.7 %collective-permute-start = (bf16[32,1280]{1,0:T(8,128)(2,1)S(1)}, bf16[32,1280]{1,0:T(8,128)(2,1)S(1)}, u32[]{:S(2)}, u32[]{:S(2)}) collective-permute-start(bf16[32,1280]{1,0:T(8,128)(2,1)S(1)} %convert_bitcast_fusion), channel_id=1, source_target_pairs={{0,1},{1,0},{2,3},{3,2},{4,5},{5,4},{6,7},{7,6},{8,9},{9,8},{10,11... | collective-permute-start | bytes 245768 | tf_op jit(solution)/shard_map/ppermute | solution.py:41
  4.7 2.6 %collective-permute-start.1 = (bf16[32,1280]{1,0:T(8,128)(2,1)S(1)}, bf16[32,1280]{1,0:T(8,128)(2,1)S(1)}, u32[]{:S(2)}, u32[]{:S(2)}) collective-permute-start(bf16[32,1280]{1,0:T(8,128)(2,1)S(1)} %convert_bitcast_fusion), channel_id=1, source_target_pairs={{0,2},{1,3},{2,0},{3,1},{4,6},{5,7},{6,4},{7,5},{8,10},{9,11},{10,... | collective-permute-start | bytes 245768 | tf_op jit(solution)/shard_map/ppermute | solution.py:41
  7.3 0.9 %copy.19 = bf16[16,8,2,256]{3,1,2,0:T(8,128)(2,1)S(1)} copy(bf16[16,8,2,256]{3,2,1,0:T(2,128)(2,1)} %bitcast.63) | data formatting | bytes 262144
  8.3 3.7 %collective-permute-done.1 = bf16[32,1280]{1,0:T(8,128)(2,1)S(1)} collective-permute-done((bf16[32,1280]{1,0:T(8,128)(2,1)S(1)}, bf16[32,1280]{1,0:T(8,128)(2,1)S(1)}, u32[]{:S(2)}, u32[]{:S(2)}) %collective-permute-start.1) | collective-permute-done | bytes 81952 | tf_op jit(solution)/shard_map/ppermute | solution.py:41
  11.9 0.0 collective-permute-done.2
  12.0 0.5 collective-permute-start.6
  12.4 2.6 %collective-permute-start.4 = (bf16[128,512]{1,0:T(8,128)(2,1)S(1)}, bf16[128,512]{1,0:T(8,128)(2,1)S(1)}, u32[]{:S(2)}, u32[]{:S(2)}) collective-permute-start(bf16[128,512]{1,0:T(8,128)(2,1)S(1)} %bitcast.53), channel_id=1, source_target_pairs={{0,2},{1,3},{2,0},{3,1},{4,6},{5,7},{6,4},{7,5},{8,10},{9,11},{10,... | collective-permute-start | bytes 393224 | tf_op jit(solution)/shard_map/ppermute | solution.py:41
  15.0 1.6 %collective-permute-done.6 = bf16[32,1280]{1,0:T(8,128)(2,1)S(1)} collective-permute-done((bf16[32,1280]{1,0:T(8,128)(2,1)S(1)}, bf16[32,1280]{1,0:T(8,128)(2,1)S(1)}, u32[]{:S(2)}, u32[]{:S(2)}) %collective-permute-start.6) | collective-permute-done | bytes 81952 | tf_op jit(solution)/shard_map/ppermute | solution.py:50
  16.7 1.7 %collective-permute-start.7 = (bf16[128,1280]{1,0:T(8,128)(2,1)S(1)}, bf16[128,1280]{1,0:T(8,128)(2,1)S(1)}, u32[]{:S(2)}, u32[]{:S(2)}) collective-permute-start(bf16[128,1280]{1,0:T(8,128)(2,1)S(1)} %pad_maximum_fusion.2.refs_0_), channel_id=1, source_target_pairs={{0,8},{4,12},{8,0},{12,4},{16,24},{20,28},{24,16},{28,20},{1,9},{5... | collective-permute-start | bytes 983048 | tf_op jit(solution)/shard_map/ppermute | solution.py:277
  18.4 1.0 %collective-permute-start.3 = (bf16[128,512]{1,0:T(8,128)(2,1)S(1)}, bf16[128,512]{1,0:T(8,128)(2,1)S(1)}, u32[]{:S(2)}, u32[]{:S(2)}) collective-permute-start(bf16[128,512]{1,0:T(8,128)(2,1)S(1)} %bitcast.54), channel_id=1, source_target_pairs={{0,1},{1,0},{2,3},{3,2},{4,5},{5,4},{6,7},{7,6},{8,9},{9,8},{10,11... | collective-permute-start | bytes 393224 | tf_op jit(solution)/shard_map/ppermute | solution.py:41
  19.4 1.5 %collective-permute-start.8 = (bf16[128,1280]{1,0:T(8,128)(2,1)S(1)}, bf16[128,1280]{1,0:T(8,128)(2,1)S(1)}, u32[]{:S(2)}, u32[]{:S(2)}) collective-permute-start(bf16[128,1280]{1,0:T(8,128)(2,1)S(1)} %pad_maximum_fusion.2.refs_0_), channel_id=1, source_target_pairs={{0,16},{4,20},{8,24},{12,28},{16,0},{20,4},{24,8},{28,12},{1,17},{... | collective-permute-start | bytes 983048 | tf_op jit(solution)/shard_map/ppermute | solution.py:277
  20.9 0.5 collective-permute-start.9
  21.4 0.9 %collective-permute-start.5 = (bf16[128,512]{1,0:T(8,128)(2,1)S(1)}, bf16[128,512]{1,0:T(8,128)(2,1)S(1)}, u32[]{:S(2)}, u32[]{:S(2)}) collective-permute-start(bf16[128,512]{1,0:T(8,128)(2,1)S(1)} %collective-permute-done.4.refs_4_.refs_5_), channel_id=1, source_target_pairs={{0,1},{1,0},{2,3},{3,2},{4,5},{5,4},{6,7},{7,6},{8,9},{9,8},{10,11... | collective-permute-start | bytes 393224 | tf_op jit(solution)/shard_map/ppermute | solution.py:50
  22.3 1.4 %dynamic-slice_bitcast_fusion = (bf16[128,1280]{1,0:T(8,128)(2,1)S(1)}, bf16[128,1280]{1,0:T(8,128)(2,1)S(1)}, bf16[128,1280]{1,0:T(8,128)(2,1)S(1)}, bf16[128,1280]{1,0:T(8,128)(2,1)S(1)}) fusion(bf16[1,128,5120]{2,1,0:T(8,128)(2,1)} %param.7, s32[]{:T(128)S(6)} %select_n.39, s32[]{:T(128)S(6)} %select_n.37, s32[]{:T(128)S(6)} %select_n.36, s32[]{:T(128)S(6)} %select_n.38), kind=kLoop, calls=%fused_computation.7 | loop fusion | bytes 2621456 | tf_op jit(solution)/shard_map/dynamic_slice | solution.py:258
  23.6 0.1 collective-permute-done.3.refs_2_.refs_3_
  23.7 2.7 %collective-permute-done.5.refs_6_.refs_7_ = bf16[128,512]{1,0:T(8,128)(2,1)S(1)} collective-permute-done((bf16[128,512]{1,0:T(8,128)(2,1)S(1)}, bf16[128,512]{1,0:T(8,128)(2,1)S(1)}, u32[]{:S(2)}, u32[]{:S(2)}) %collective-permute-start.5) | collective-permute-done | bytes 131104 | tf_op jit(solution)/shard_map/ppermute | solution.py:50
  26.4 5.0 %collective-permute-start.15 = (bf16[128,1280]{1,0:T(8,128)(2,1)S(1)}, bf16[128,1280]{1,0:T(8,128)(2,1)S(1)}, u32[]{:S(2)}, u32[]{:S(2)}) collective-permute-start(bf16[128,1280]{1,0:T(8,128)(2,1)S(1)} %get-tuple-element.40.refs_6_), channel_id=1, source_target_pairs={{0,2},{1,3},{2,0},{3,1},{4,6},{5,7},{6,4},{7,5},{8,10},{9,11},{10,... | collective-permute-start | bytes 983048 | tf_op jit(solution)/shard_map/ppermute | solution.py:284
  31.4 0.6 collective-permute-start.14
  32.0 0.1 constant_dynamic-slice_fusion
  32.1 0.9 %collective-permute-done.8.refs_2_ = bf16[128,1280]{1,0:T(8,128)(2,1)S(1)} collective-permute-done((bf16[128,1280]{1,0:T(8,128)(2,1)S(1)}, bf16[128,1280]{1,0:T(8,128)(2,1)S(1)}, u32[]{:S(2)}, u32[]{:S(2)}) %collective-permute-start.8) | collective-permute-done | bytes 327712 | tf_op jit(solution)/shard_map/ppermute | solution.py:277
  33.0 1.0 %shard_map.102 = (bf16[4,32,128]{2,1,0:T(8,128)(2,1)S(1)}, bf16[4,32,128]{2,1,0:T(8,128)(2,1)S(1)}) custom-call(bf16[128,1280]{1,0:T(8,128)(2,1)S(1)} %pad_maximum_fusion.2.refs_0_, bf16[128,1280]{1,0:T(8,128)(2,1)S(1)} %collective-permute-done.7.refs_1_, bf16[128,1280]{1,0:T(8,128)(2,1)S(1)} %collective-permute-done.8.refs_2_, ...), custom_call_target="tpu_custom_call" | custom-call | flops 335544320 | bytes 3932160 | tf_op jit(solution)/shard_map/pallas_call | solution.py:82
  34.0 0.1 collective-permute-start.10
  34.1 1.2 %collective-permute-done.10.refs_9_ = bf16[4,32,128]{2,1,0:T(8,128)(2,1)S(1)} collective-permute-done((bf16[4,32,128]{2,1,0:T(8,128)(2,1)S(1)}, bf16[4,32,128]{2,1,0:T(8,128)(2,1)S(1)}, u32[]{:S(2)}, u32[]{:S(2)}) %collective-permute-start.10) | collective-permute-done | bytes 32800 | tf_op jit(solution)/shard_map/ppermute | solution.py:290
  35.3 1.2 %shard_map.103.refs_0_ = bf16[256,128]{1,0:T(8,128)(2,1)S(1)} custom-call(bf16[128,512]{1,0:T(8,128)(2,1)S(1)} %bitcast.55, bf16[128,512]{1,0:T(8,128)(2,1)S(1)} %bitcast.56, bf16[128,512]{1,0:T(8,128)(2,1)S(1)} %collective-permute-done.3.refs_2_.refs_3_, bf16[128,512]{1,0:T(8,128)(2,1)S(1)} %collective-permute-done.3.refs_2_.refs_3_, ...), custom_call_target="tpu_custom_call" | custom-call | flops 402653184 | bytes 786432 | tf_op jit(solution)/shard_map/pallas_call | solution.py:161
  36.5 0.8 %collective-permute-start.11 = (bf16[256,128]{1,0:T(8,128)(2,1)S(1)}, bf16[256,128]{1,0:T(8,128)(2,1)S(1)}, u32[]{:S(2)}, u32[]{:S(2)}) collective-permute-start(bf16[256,128]{1,0:T(8,128)(2,1)S(1)} %shard_map.103.refs_0_), channel_id=1, source_target_pairs={{0,1},{1,0},{2,3},{3,2},{4,5},{5,4},{6,7},{7,6},{8,9},{9,8},{10,11... | collective-permute-start | bytes 196616 | tf_op jit(solution)/shard_map/ppermute | solution.py:293
  37.3 2.3 %collective-permute-start.12 = (bf16[256,128]{1,0:T(8,128)(2,1)S(1)}, bf16[256,128]{1,0:T(8,128)(2,1)S(1)}, u32[]{:S(2)}, u32[]{:S(2)}) collective-permute-start(bf16[256,128]{1,0:T(8,128)(2,1)S(1)} %shard_map.103.refs_0_), channel_id=1, source_target_pairs={{0,2},{1,3},{2,0},{3,1},{4,6},{5,7},{6,4},{7,5},{8,10},{9,11},{10,... | collective-permute-start | bytes 196616 | tf_op jit(solution)/shard_map/ppermute | solution.py:293
  39.6 12.7 %collective-permute-done.11.refs_1_ = bf16[256,128]{1,0:T(8,128)(2,1)S(1)} collective-permute-done((bf16[256,128]{1,0:T(8,128)(2,1)S(1)}, bf16[256,128]{1,0:T(8,128)(2,1)S(1)}, u32[]{:S(2)}, u32[]{:S(2)}) %collective-permute-start.11) | collective-permute-done | bytes 65568 | tf_op jit(solution)/shard_map/ppermute | solution.py:293
  52.3 0.6 collective-permute-start.13
  52.9 1.3 %copy.14 = bf16[256,1280]{1,0:T(8,128)(2,1)S(1)} copy(bf16[256,1280]{0,1:T(8,128)(2,1)} %bitcast.61) | data formatting | bytes 1310720 | tf_op jit(solution)/shard_map/transpose | solution.py:297
  54.3 1.3 %copy.13 = bf16[256,1280]{1,0:T(8,128)(2,1)S(1)} copy(bf16[256,1280]{0,1:T(8,128)(2,1)} %bitcast.62) | data formatting | bytes 1310720 | tf_op jit(solution)/shard_map/transpose | solution.py:296
  55.6 5.8 %collective-permute-done.12.refs_2_ = bf16[256,128]{1,0:T(8,128)(2,1)S(1)} collective-permute-done((bf16[256,128]{1,0:T(8,128)(2,1)S(1)}, bf16[256,128]{1,0:T(8,128)(2,1)S(1)}, u32[]{:S(2)}, u32[]{:S(2)}) %collective-permute-start.12) | collective-permute-done | bytes 65568 | tf_op jit(solution)/shard_map/ppermute | solution.py:293
  61.4 1.6 %shard_map.105 = (bf16[4,32,1280]{2,1,0:T(8,128)(2,1)S(1)}, bf16[4,32,1280]{2,1,0:T(8,128)(2,1)S(1)}, bf16[4,32,1280]{2,1,0:T(8,128)(2,1)S(1)}) custom-call(bf16[256,128]{1,0:T(8,128)(2,1)S(1)} %shard_map.103.refs_0_, bf16[256,128]{1,0:T(8,128)(2,1)S(1)} %collective-permute-done.11.refs_1_, bf16[256,128]{1,0:T(8,128)(2,1)S(1)} %collective-permute-done.12.refs_2_, ...), custom_call_target="tpu_custom_call" | custom-call | flops 167772160 | bytes 3866624 | tf_op jit(solution)/shard_map/pallas_call | solution.py:210
  63.1 0.1 collective-permute-start.17
  63.2 1.6 %shard_map.104 = (bf16[4,32,1280]{2,1,0:T(8,128)(2,1)S(1)}, bf16[4,32,1280]{2,1,0:T(8,128)(2,1)S(1)}, bf16[4,32,1280]{2,1,0:T(8,128)(2,1)S(1)}) custom-call(bf16[256,128]{1,0:T(8,128)(2,1)S(1)} %shard_map.103.refs_0_, bf16[256,128]{1,0:T(8,128)(2,1)S(1)} %collective-permute-done.11.refs_1_, bf16[256,128]{1,0:T(8,128)(2,1)S(1)} %collective-permute-done.12.refs_2_, ...), custom_call_target="tpu_custom_call" | custom-call | flops 167772160 | bytes 3866624 | tf_op jit(solution)/shard_map/pallas_call | solution.py:210
  64.8 0.1 select_bitcast_fusion.1
  64.9 0.1 pad_maximum_fusion.1
  65.0 0.1 shard_map.106
  65.1 0.8 %collective-permute-start.18 = (bf16[32,1280]{1,0:T(8,128)(2,1)S(1)}, bf16[32,1280]{1,0:T(8,128)(2,1)S(1)}, u32[]{:S(2)}, u32[]{:S(2)}) collective-permute-start(bf16[32,1280]{1,0:T(8,128)(2,1)S(1)} %get-tuple-element.45), channel_id=1, source_target_pairs={{0,8},{4,12},{8,0},{12,4},{16,24},{20,28},{24,16},{28,20},{1,9},{5... | collective-permute-start | bytes 245768 | tf_op jit(solution)/shard_map/ppermute | solution.py:314
  65.8 1.5 %collective-permute-start.19 = (bf16[32,1280]{1,0:T(8,128)(2,1)S(1)}, bf16[32,1280]{1,0:T(8,128)(2,1)S(1)}, u32[]{:S(2)}, u32[]{:S(2)}) collective-permute-start(bf16[32,1280]{1,0:T(8,128)(2,1)S(1)} %get-tuple-element.46), channel_id=1, source_target_pairs={{0,16},{4,20},{8,24},{12,28},{16,0},{20,4},{24,8},{28,12},{1,17},{... | collective-permute-start | bytes 245768 | tf_op jit(solution)/shard_map/ppermute | solution.py:314
  67.4 1.3 %collective-permute-start.20 = (bf16[32,1280]{1,0:T(8,128)(2,1)S(1)}, bf16[32,1280]{1,0:T(8,128)(2,1)S(1)}, u32[]{:S(2)}, u32[]{:S(2)}) collective-permute-start(bf16[32,1280]{1,0:T(8,128)(2,1)S(1)} %get-tuple-element.47), channel_id=1, source_target_pairs={{0,24},{4,28},{8,16},{12,20},{16,8},{20,12},{24,0},{28,4},{1,25},{... | collective-permute-start | bytes 245768 | tf_op jit(solution)/shard_map/ppermute | solution.py:314
  68.6 0.1 pad_maximum_fusion
  68.7 1.1 %copy.18 = bf16[1,1280,256]{2,1,0:T(8,128)(2,1)} copy(bf16[1,1280,256]{1,2,0:T(8,128)(2,1)S(1)} %bitcast.58) | data formatting | bytes 1310720
  69.9 1.1 %copy.17 = bf16[1,1280,256]{2,1,0:T(8,128)(2,1)} copy(bf16[1,1280,256]{1,2,0:T(8,128)(2,1)S(1)} %bitcast.59) | data formatting | bytes 1310720
  71.0 0.3 collective-permute-done.19
  71.2 1.5 %collective-permute-done.20 = bf16[32,1280]{1,0:T(8,128)(2,1)S(1)} collective-permute-done((bf16[32,1280]{1,0:T(8,128)(2,1)S(1)}, bf16[32,1280]{1,0:T(8,128)(2,1)S(1)}, u32[]{:S(2)}, u32[]{:S(2)}) %collective-permute-start.20) | collective-permute-done | bytes 81952 | tf_op jit(solution)/shard_map/ppermute | solution.py:314
  72.7 0.8 %fusion.1 = (f32[1280,32]{0,1:T(8,128)}, f32[1280,32]{0,1:T(8,128)}) fusion(f32[1280,32]{0,1:T(8,128)S(1)} %copy-done.3, bf16[32,1280]{1,0:T(8,128)(2,1)S(1)} %collective-permute-done.20, bf16[32,1280]{1,0:T(8,128)(2,1)S(1)} %collective-permute-done.19, f32[32,1280]{1,0:T(8,128)S(1)} %get-tuple-element.44, bf16[32,1280]{1,0:T(8,128)(2,1)S(1)} %collective-permute-done.18, ...), kind=kLoop, calls=%fused_computation.14 | loop fusion | flops 532480 | bytes 1064960 | tf_op jit(solution)/shard_map/sub | solution.py:319
  (24 shorter events, 0.2 us)
Async XLA Ops:
  0.6 11.3 %collective-permute-start.2 = (bf16[128,5120]{1,0:T(8,128)(2,1)}, bf16[128,5120]{1,0:T(8,128)(2,1)S(1)}, u32[]{:S(2)}, u32[]{:S(2)}) collective-permute-start(bf16[128,5120]{1,0:T(8,128)(2,1)} %bitcast.60), channel_id=1, source_target_pairs={{0,4},{4,0},{8,12},{12,8},{16,20},{20,16},{24,28},{28,24},{1,5},{5... | collective-permute-start | bytes 3932168 | tf_op jit(solution)/shard_map/ppermute | solution.py:262
  2.1 6.2 %collective-permute-start = (bf16[32,1280]{1,0:T(8,128)(2,1)S(1)}, bf16[32,1280]{1,0:T(8,128)(2,1)S(1)}, u32[]{:S(2)}, u32[]{:S(2)}) collective-permute-start(bf16[32,1280]{1,0:T(8,128)(2,1)S(1)} %convert_bitcast_fusion), channel_id=1, source_target_pairs={{0,1},{1,0},{2,3},{3,2},{4,5},{5,4},{6,7},{7,6},{8,9},{9,8},{10,11... | collective-permute-start | bytes 245768 | tf_op jit(solution)/shard_map/ppermute | solution.py:41
  4.7 7.2 %collective-permute-start.1 = (bf16[32,1280]{1,0:T(8,128)(2,1)S(1)}, bf16[32,1280]{1,0:T(8,128)(2,1)S(1)}, u32[]{:S(2)}, u32[]{:S(2)}) collective-permute-start(bf16[32,1280]{1,0:T(8,128)(2,1)S(1)} %convert_bitcast_fusion), channel_id=1, source_target_pairs={{0,2},{1,3},{2,0},{3,1},{4,6},{5,7},{6,4},{7,5},{8,10},{9,11},{10,... | collective-permute-start | bytes 245768 | tf_op jit(solution)/shard_map/ppermute | solution.py:41
  12.0 3.1 %copy-start.1 = (bf16[128,5120]{1,0:T(8,128)(2,1)}, bf16[128,5120]{1,0:T(8,128)(2,1)S(1)}, u32[]{:S(2)}) copy-start(bf16[128,5120]{1,0:T(8,128)(2,1)S(1)} %collective-permute-done.2) | copy-start | bytes 3932164
  12.0 4.7 %collective-permute-start.6 = (bf16[32,1280]{1,0:T(8,128)(2,1)S(1)}, bf16[32,1280]{1,0:T(8,128)(2,1)S(1)}, u32[]{:S(2)}, u32[]{:S(2)}) collective-permute-start(bf16[32,1280]{1,0:T(8,128)(2,1)S(1)} %collective-permute-done.1), channel_id=1, source_target_pairs={{0,1},{1,0},{2,3},{3,2},{4,5},{5,4},{6,7},{7,6},{8,9},{9,8},{10,11... | collective-permute-start | bytes 245768 | tf_op jit(solution)/shard_map/ppermute | solution.py:50
  12.4 8.9 %collective-permute-start.4 = (bf16[128,512]{1,0:T(8,128)(2,1)S(1)}, bf16[128,512]{1,0:T(8,128)(2,1)S(1)}, u32[]{:S(2)}, u32[]{:S(2)}) collective-permute-start(bf16[128,512]{1,0:T(8,128)(2,1)S(1)} %bitcast.53), channel_id=1, source_target_pairs={{0,2},{1,3},{2,0},{3,1},{4,6},{5,7},{6,4},{7,5},{8,10},{9,11},{10,... | collective-permute-start | bytes 393224 | tf_op jit(solution)/shard_map/ppermute | solution.py:41
  16.7 14.7 %collective-permute-start.7 = (bf16[128,1280]{1,0:T(8,128)(2,1)S(1)}, bf16[128,1280]{1,0:T(8,128)(2,1)S(1)}, u32[]{:S(2)}, u32[]{:S(2)}) collective-permute-start(bf16[128,1280]{1,0:T(8,128)(2,1)S(1)} %pad_maximum_fusion.2.refs_0_), channel_id=1, source_target_pairs={{0,8},{4,12},{8,0},{12,4},{16,24},{20,28},{24,16},{28,20},{1,9},{5... | collective-permute-start | bytes 983048 | tf_op jit(solution)/shard_map/ppermute | solution.py:277
  18.4 13.6 %copy-start.2 = (bf16[128,5120]{1,0:T(8,128)(2,1)S(1)}, bf16[128,5120]{1,0:T(8,128)(2,1)}, u32[]{:S(2)}) copy-start(bf16[128,5120]{1,0:T(8,128)(2,1)} %copy-done.1) | copy-start | bytes 3932164
  18.4 5.3 %collective-permute-start.3 = (bf16[128,512]{1,0:T(8,128)(2,1)S(1)}, bf16[128,512]{1,0:T(8,128)(2,1)S(1)}, u32[]{:S(2)}, u32[]{:S(2)}) collective-permute-start(bf16[128,512]{1,0:T(8,128)(2,1)S(1)} %bitcast.54), channel_id=1, source_target_pairs={{0,1},{1,0},{2,3},{3,2},{4,5},{5,4},{6,7},{7,6},{8,9},{9,8},{10,11... | collective-permute-start | bytes 393224 | tf_op jit(solution)/shard_map/ppermute | solution.py:41
  19.4 13.6 %collective-permute-start.8 = (bf16[128,1280]{1,0:T(8,128)(2,1)S(1)}, bf16[128,1280]{1,0:T(8,128)(2,1)S(1)}, u32[]{:S(2)}, u32[]{:S(2)}) collective-permute-start(bf16[128,1280]{1,0:T(8,128)(2,1)S(1)} %pad_maximum_fusion.2.refs_0_), channel_id=1, source_target_pairs={{0,16},{4,20},{8,24},{12,28},{16,0},{20,4},{24,8},{28,12},{1,17},{... | collective-permute-start | bytes 983048 | tf_op jit(solution)/shard_map/ppermute | solution.py:277
  20.9 12.1 %collective-permute-start.9 = (bf16[128,1280]{1,0:T(8,128)(2,1)S(1)}, bf16[128,1280]{1,0:T(8,128)(2,1)S(1)}, u32[]{:S(2)}, u32[]{:S(2)}) collective-permute-start(bf16[128,1280]{1,0:T(8,128)(2,1)S(1)} %pad_maximum_fusion.2.refs_0_), channel_id=1, source_target_pairs={{0,24},{4,28},{8,16},{12,20},{16,8},{20,12},{24,0},{28,4},{1,25},{... | collective-permute-start | bytes 983048 | tf_op jit(solution)/shard_map/ppermute | solution.py:277
  21.4 5.0 %collective-permute-start.5 = (bf16[128,512]{1,0:T(8,128)(2,1)S(1)}, bf16[128,512]{1,0:T(8,128)(2,1)S(1)}, u32[]{:S(2)}, u32[]{:S(2)}) collective-permute-start(bf16[128,512]{1,0:T(8,128)(2,1)S(1)} %collective-permute-done.4.refs_4_.refs_5_), channel_id=1, source_target_pairs={{0,1},{1,0},{2,3},{3,2},{4,5},{5,4},{6,7},{7,6},{8,9},{9,8},{10,11... | collective-permute-start | bytes 393224 | tf_op jit(solution)/shard_map/ppermute | solution.py:50
  26.4 35.0 %collective-permute-start.15 = (bf16[128,1280]{1,0:T(8,128)(2,1)S(1)}, bf16[128,1280]{1,0:T(8,128)(2,1)S(1)}, u32[]{:S(2)}, u32[]{:S(2)}) collective-permute-start(bf16[128,1280]{1,0:T(8,128)(2,1)S(1)} %get-tuple-element.40.refs_6_), channel_id=1, source_target_pairs={{0,2},{1,3},{2,0},{3,1},{4,6},{5,7},{6,4},{7,5},{8,10},{9,11},{10,... | collective-permute-start | bytes 983048 | tf_op jit(solution)/shard_map/ppermute | solution.py:284
  31.4 30.0 %collective-permute-start.16 = (bf16[128,1280]{1,0:T(8,128)(2,1)S(1)}, bf16[128,1280]{1,0:T(8,128)(2,1)S(1)}, u32[]{:S(2)}, u32[]{:S(2)}) collective-permute-start(bf16[128,1280]{1,0:T(8,128)(2,1)S(1)} %get-tuple-element.41.refs_7_), channel_id=1, source_target_pairs={{0,3},{1,2},{2,1},{3,0},{4,7},{5,6},{6,5},{7,4},{8,11},{9,10},{10,... | collective-permute-start | bytes 983048 | tf_op jit(solution)/shard_map/ppermute | solution.py:284
  31.4 30.0 %collective-permute-start.14 = (bf16[128,1280]{1,0:T(8,128)(2,1)S(1)}, bf16[128,1280]{1,0:T(8,128)(2,1)}, u32[]{:S(2)}, u32[]{:S(2)}) collective-permute-start(bf16[128,1280]{1,0:T(8,128)(2,1)S(1)} %get-tuple-element.39.refs_5_), channel_id=1, source_target_pairs={{0,1},{1,0},{2,3},{3,2},{4,5},{5,4},{6,7},{7,6},{8,9},{9,8},{10,11... | collective-permute-start | bytes 983048 | tf_op jit(solution)/shard_map/ppermute | solution.py:283
  33.0 2.3 %copy-start = (bf16[1,128,256]{2,1,0:T(8,128)(2,1)S(1)}, bf16[1,128,256]{2,1,0:T(8,128)(2,1)}, u32[]{:S(2)}) copy-start(bf16[1,128,256]{2,1,0:T(8,128)(2,1)} %param.9) | copy-start | bytes 196612
  34.0 1.3 %collective-permute-start.10 = (bf16[4,32,128]{2,1,0:T(8,128)(2,1)S(1)}, bf16[4,32,128]{2,1,0:T(8,128)(2,1)S(1)}, u32[]{:S(2)}, u32[]{:S(2)}) collective-permute-start(bf16[4,32,128]{2,1,0:T(8,128)(2,1)S(1)} %get-tuple-element.38), channel_id=1, source_target_pairs={{0,4},{4,0},{8,12},{12,8},{16,20},{20,16},{24,28},{28,24},{1,5},{5... | collective-permute-start | bytes 98312 | tf_op jit(solution)/shard_map/ppermute | solution.py:290
  36.5 15.8 %collective-permute-start.11 = (bf16[256,128]{1,0:T(8,128)(2,1)S(1)}, bf16[256,128]{1,0:T(8,128)(2,1)S(1)}, u32[]{:S(2)}, u32[]{:S(2)}) collective-permute-start(bf16[256,128]{1,0:T(8,128)(2,1)S(1)} %shard_map.103.refs_0_), channel_id=1, source_target_pairs={{0,1},{1,0},{2,3},{3,2},{4,5},{5,4},{6,7},{7,6},{8,9},{9,8},{10,11... | collective-permute-start | bytes 196616 | tf_op jit(solution)/shard_map/ppermute | solution.py:293
  37.3 24.1 %collective-permute-start.12 = (bf16[256,128]{1,0:T(8,128)(2,1)S(1)}, bf16[256,128]{1,0:T(8,128)(2,1)S(1)}, u32[]{:S(2)}, u32[]{:S(2)}) collective-permute-start(bf16[256,128]{1,0:T(8,128)(2,1)S(1)} %shard_map.103.refs_0_), channel_id=1, source_target_pairs={{0,2},{1,3},{2,0},{3,1},{4,6},{5,7},{6,4},{7,5},{8,10},{9,11},{10,... | collective-permute-start | bytes 196616 | tf_op jit(solution)/shard_map/ppermute | solution.py:293
  52.3 9.1 %collective-permute-start.13 = (bf16[256,128]{1,0:T(8,128)(2,1)S(1)}, bf16[256,128]{1,0:T(8,128)(2,1)S(1)}, u32[]{:S(2)}, u32[]{:S(2)}) collective-permute-start(bf16[256,128]{1,0:T(8,128)(2,1)S(1)} %shard_map.103.refs_0_), channel_id=1, source_target_pairs={{0,3},{1,2},{2,1},{3,0},{4,7},{5,6},{6,5},{7,4},{8,11},{9,10},{10,... | collective-permute-start | bytes 196616 | tf_op jit(solution)/shard_map/ppermute | solution.py:293
  63.1 1.9 %collective-permute-start.17 = (bf16[4,32,1280]{2,1,0:T(8,128)(2,1)S(1)}, bf16[4,32,1280]{2,1,0:T(8,128)(2,1)S(1)}, u32[]{:S(2)}, u32[]{:S(2)}) collective-permute-start(bf16[4,32,1280]{2,1,0:T(8,128)(2,1)S(1)} %get-tuple-element.43), channel_id=1, source_target_pairs={{0,4},{4,0},{8,12},{12,8},{16,20},{20,16},{24,28},{28,24},{1,5},{5... | collective-permute-start | bytes 983048 | tf_op jit(solution)/shard_map/ppermute | solution.py:301
  65.1 5.9 %collective-permute-start.18 = (bf16[32,1280]{1,0:T(8,128)(2,1)S(1)}, bf16[32,1280]{1,0:T(8,128)(2,1)S(1)}, u32[]{:S(2)}, u32[]{:S(2)}) collective-permute-start(bf16[32,1280]{1,0:T(8,128)(2,1)S(1)} %get-tuple-element.45), channel_id=1, source_target_pairs={{0,8},{4,12},{8,0},{12,4},{16,24},{20,28},{24,16},{28,20},{1,9},{5... | collective-permute-start | bytes 245768 | tf_op jit(solution)/shard_map/ppermute | solution.py:314
  65.8 5.4 %collective-permute-start.19 = (bf16[32,1280]{1,0:T(8,128)(2,1)S(1)}, bf16[32,1280]{1,0:T(8,128)(2,1)S(1)}, u32[]{:S(2)}, u32[]{:S(2)}) collective-permute-start(bf16[32,1280]{1,0:T(8,128)(2,1)S(1)} %get-tuple-element.46), channel_id=1, source_target_pairs={{0,16},{4,20},{8,24},{12,28},{16,0},{20,4},{24,8},{28,12},{1,17},{... | collective-permute-start | bytes 245768 | tf_op jit(solution)/shard_map/ppermute | solution.py:314
  67.4 5.3 %collective-permute-start.20 = (bf16[32,1280]{1,0:T(8,128)(2,1)S(1)}, bf16[32,1280]{1,0:T(8,128)(2,1)S(1)}, u32[]{:S(2)}, u32[]{:S(2)}) collective-permute-start(bf16[32,1280]{1,0:T(8,128)(2,1)S(1)} %get-tuple-element.47), channel_id=1, source_target_pairs={{0,24},{4,28},{8,16},{12,20},{16,8},{20,12},{24,0},{28,4},{1,25},{... | collective-permute-start | bytes 245768 | tf_op jit(solution)/shard_map/ppermute | solution.py:314
  69.8 2.9 %copy-start.3 = (f32[1280,32]{0,1:T(8,128)S(1)}, f32[1280,32]{0,1:T(8,128)}, u32[]{:S(2)}) copy-start(f32[1280,32]{0,1:T(8,128)} %param.12) | copy-start | bytes 491524
  69.8 2.9 %copy-start.4 = (f32[1280,32]{0,1:T(8,128)S(1)}, f32[1280,32]{0,1:T(8,128)}, u32[]{:S(2)}) copy-start(f32[1280,32]{0,1:T(8,128)} %param.13) | copy-start | bytes 491524

commit v5 on v4

--- a/solution.py
+++ b/solution.py
@@ -35,20 +35,11 @@
     ]
 
 
-def exchange_start(own, axis, size):
-    blocks = [own] + [None] * (size - 1)
+def gather_order(size):
+    order = [0]
     for bit in reversed(range(size.bit_length() - 1)):
-        blocks[1 << bit] = lax.ppermute(own, axis, pair_perm(size, 1 << bit))
-    return blocks
-
-
-def exchange_finish(blocks, axis, size):
-    blocks = list(blocks)
-    for k in sorted(range(1, size), key=lambda k: (bin(k).count("1"), k)):
-        if blocks[k] is None:
-            low = k & -k
-            blocks[k] = lax.ppermute(blocks[k ^ low], axis, pair_perm(size, low))
-    return blocks
+        order += [k ^ (1 << bit) for k in order]
+    return order
 
 
 def query_kernel(rounds, n_chip, inverse, *refs):
@@ -87,8 +78,13 @@
     )(*operands)
 
 
-def attention_kernel(n_seq, n_chip, rows, head_size, *refs):
-    kv_refs, (mine_ref, other_ref, cot_ref, out_ref) = refs[: 2 * n_seq], refs[2 * n_seq :]
+def attention_kernel(order, stacks, rows, head_size, *refs):
+    mine_ref, other_ref, cot_ref, out_ref = refs[2 * stacks :]
+    key_blocks, value_blocks = [], []
+    for stack in range(stacks):
+        for at in range(refs[2 * stack].shape[0] // rows):
+            key_blocks.append(refs[2 * stack][at * rows : (at + 1) * rows, :])
+            value_blocks.append(refs[2 * stack + 1][at * rows : (at + 1) * rows, :])
     seq = lax.axis_index("seq")
     chip, core = lax.axis_index("island") // 2, lax.rem(lax.axis_index("island"), 2)
     cols = out_ref.shape[0]
@@ -116,8 +112,8 @@
     key_row = lax.broadcasted_iota(jnp.int32, (rows, wide), 0)
     query_row = lax.rem(lax.broadcasted_iota(jnp.int32, (rows, wide), 1), rows) + seq * rows
     scores = []
-    for k in range(n_seq):
-        block = jnp.dot(kv_refs[2 * k][...], query, preferred_element_type=jnp.float32) * scale
+    for k, keys in zip(order, key_blocks):
+        block = jnp.dot(keys, query, preferred_element_type=jnp.float32) * scale
         seen = query_row >= key_row + jnp.bitwise_xor(seq, k) * rows
         scores.append(jnp.where(seen, block, -1e30))
     peak = functools.reduce(jnp.maximum, [jnp.max(s, axis=0, keepdims=True) for s in scores])
@@ -125,41 +121,37 @@
     inverse = 1.0 / sum(jnp.sum(e, axis=0, keepdims=True) for e in expons)
     attend = [e * inverse for e in expons]
     dattend = [
-        jnp.dot(kv_refs[2 * k + 1][...], cot, preferred_element_type=jnp.float32)
-        for k in range(n_seq)
+        jnp.dot(values, cot, preferred_element_type=jnp.float32) for values in value_blocks
     ]
     rowdot = sum(
         jnp.sum(a.astype(jnp.bfloat16).astype(jnp.float32) * d, axis=0, keepdims=True)
         for a, d in zip(attend, dattend)
     )
     total = jnp.zeros((cols, wide), jnp.float32)
-    for k in range(n_seq):
-        dscore = (attend[k] * (dattend[k] - rowdot)).astype(jnp.bfloat16)
-        total = total + lax.dot_general(
-            kv_refs[2 * k][...], dscore, TN, preferred_element_type=jnp.float32
-        )
+    for weights, slopes, keys in zip(attend, dattend, key_blocks):
+        dscore = (weights * (slopes - rowdot)).astype(jnp.bfloat16)
+        total = total + lax.dot_general(keys, dscore, TN, preferred_element_type=jnp.float32)
     for h in range(heads):
         part = total[h * head_size : (h + 1) * head_size, h * rows : (h + 1) * rows] * scale
         out_ref[h * head_size : (h + 1) * head_size, :] = part.astype(jnp.bfloat16)
 
 
-def attention(kv, mine, other, cot):
-    n_seq, (rows, cols) = len(kv), cot.shape
-    n_chip = mine.shape[0]
+def attention(kv, order, mine, other, cot):
+    rows, cols = cot.shape
     group = min(cols, 4 * HD)
     groups = cols // group
     in_specs = []
     operands = []
     for block in kv:
-        in_specs.append(pl.BlockSpec((rows, group), lambda g: (0, g)))
-        in_specs.append(pl.BlockSpec((rows, group), lambda g: (0, g + groups)))
+        in_specs.append(pl.BlockSpec((block.shape[0], group), lambda g: (0, g)))
+        in_specs.append(pl.BlockSpec((block.shape[0], group), lambda g: (0, g + groups)))
         operands += [block, block]
     in_specs.append(pl.BlockSpec(mine.shape, lambda g: (0, 0, 0)))
     in_specs.append(pl.BlockSpec(mine.shape, lambda g: (0, 0, 0)))
     in_specs.append(pl.BlockSpec((rows, group), lambda g: (0, g)))
-    length = n_seq * rows
+    length = len(order) * rows
     return pl.pallas_call(
-        functools.partial(attention_kernel, n_seq, n_chip, rows, HD),
+        functools.partial(attention_kernel, order, len(kv), rows, HD),
         grid=(groups,),
         in_specs=in_specs,
         out_specs=pl.BlockSpec((group, rows), lambda g: (g, 0)),
@@ -259,36 +251,42 @@
             for k in range(n_seq)
         ]
 
+    order = gather_order(n_seq)
+    bits = [1 << bit for bit in reversed(range(n_seq.bit_length() - 1))]
     partner_tokens = lax.ppermute(tokens, "island", swap)
-    singles = [1 << j for j in range(n_seq.bit_length() - 1)]
-    weights = exchange_start(anchor.T.astype(jnp.bfloat16), "seq", n_seq)
+    weight = anchor.T.astype(jnp.bfloat16)
     own_kv = key_vals[0].reshape(rows, 2 * cols)
-    (weights_ready, own_kv, partner_tokens) = lax.optimization_barrier(
-        ([weights[k] for k in singles], own_kv, partner_tokens)
-    )
-    for k, value in zip(singles, weights_ready):
-        weights[k] = value
-    weights = exchange_finish(weights, "seq", n_seq)
-    kv = exchange_finish(exchange_start(own_kv, "seq", n_seq), "seq", n_seq)
-
-    rounds = [list(range(n_seq))]
-    held = jnp.concatenate(weights, axis=0)
-    spread = [held] + [
-        lax.ppermute(held, "island", pair_perm(n_chip, step, 2)) for step in range(1, n_chip)
-    ]
+    held = jnp.concatenate([weight, lax.ppermute(weight, "seq", pair_perm(n_seq, bits[0]))], 0)
+    own_kv, partner_tokens = lax.optimization_barrier((own_kv, partner_tokens))
+    kv = [own_kv, lax.ppermute(own_kv, "seq", pair_perm(n_seq, bits[0]))]
 
     own_blocks = feature_blocks(tokens)
-    far, kv = lax.optimization_barrier((own_blocks[2:], kv))
+    far, held = lax.optimization_barrier((own_blocks[2:], held))
+    gathered = [own_blocks[0], None] + [
+        lax.ppermute(piece, "seq", pair_perm(n_seq, k)) for k, piece in enumerate(far, 2)
+    ]
+    for bit in bits[1:]:
+        held = jnp.concatenate([held, lax.ppermute(held, "seq", pair_perm(n_seq, bit))], 0)
+        kv.append(
+            lax.ppermute(jnp.concatenate(kv, axis=0), "seq", pair_perm(n_seq, bit))
+        )
+
+    rounds = [order]
+    held, kv[1], partner_tokens = lax.optimization_barrier((held, kv[1], partner_tokens))
+    spread = [held] + [None] * (n_chip - 1)
+    for step in range(1, n_chip):
+        if step & (step - 1):
+            held, spread[1] = lax.optimization_barrier((held, spread[1]))
+        spread[step] = lax.ppermute(held, "island", pair_perm(n_chip, step, 2))
     near, spread[1] = lax.optimization_barrier((own_blocks[1], spread[1]))
-    gathered = [own_blocks[0], lax.ppermute(near, "seq", pair_perm(n_seq, 1))] + [
-        lax.ppermute(piece, "seq", pair_perm(n_seq, k)) for k, piece in enumerate(far, 2)
-    ]
-
+    gathered[1] = lax.ppermute(near, "seq", pair_perm(n_seq, 1))
+
+    (spread, gathered[2]) = lax.optimization_barrier((spread, gathered[2]))
     mine, for_partner = half_queries(
         rounds, [spread], own_blocks, feature_blocks(partner_tokens), share, inverse
     )
     other = lax.ppermute(for_partner, "island", swap)
-    dquery = attention(kv, mine, other, cotangent[0])
+    dquery = attention(kv, order, mine, other, cotangent[0])
     dqueries = [dquery] + [
         lax.ppermute(dquery, "seq", pair_perm(n_seq, k)) for k in range(1, n_seq)
     ]

time: 73.9 us -> 72 us (0.974)
  starting transfers between devices: 27.5 us -> 30.1 us
  Pallas kernels: 5.57 us -> 3.6 us
  local copies, waits for them, and re-layouts: 7.33 us -> 5.38 us
    ppermute x3, waiting for transfers between devices: 18.5 us -> 4.04 us  [on_device(): lax.ppermute(dquery, 'seq', pair_perm(n_seq, k))]
    ppermute x2, waiting for transfers between devices: 0.01 us -> 12.9 us  [on_device(): lax.ppermute(piece, 'seq', pair_perm(n_seq, k))]
    ppermute x10 -> x8, starting transfers between devices: 14.5 us -> 16.5 us  [the longest x3 4.61 us: on_device(): spread[step] = lax.ppermute(held, 'island', pair_perm(n_chip, step, 2))]
    pallas_call x2, Pallas kernels: 3.27 us -> 1.32 us  [gradient_adam(): pl.pallas_call(functools.partial(adam_kernel, n_seq, n_chip, own_half, in...]
    ppermute x10 -> x8, waiting for transfers between devices: 8.95 us -> 10.5 us  [the longest x1 4.62 us: on_device(): lax.ppermute(held, 'seq', pair_perm(n_seq, bit))]
    ppermute x1, waiting for transfers between devices: 1.19 us -> 0.01 us  [on_device(): other = lax.ppermute(for_partner, 'island', swap)]
    transpose x1, local copies, waits for them, and re-layouts: 1.33 us -> 0.24 us  [on_device(): second = second_moment[0].T.reshape(n_chip, 2, share, block)]
    unnamed x13, local copies, waits for them, and re-layouts: 3.09 us -> 2.19 us
  transfers between devices with their start and end apart: 21 -> 19, of which waited for: 10 -> 11; matrix products, arithmetic and copies ran while one was open for 12% -> 9% of each run, Pallas kernels for 5% -> 4%
where the time goes in v5:
time: 72 us; the launch traced here: 71.8 us
  starting transfers between devices  30.1 us (42%)
  waiting for transfers between devices  29.8 us (41%)
  local copies, waits for them, and re-layouts  5.38 us (7%)
  Pallas kernels  3.6 us (5%)
  other arithmetic  1.99 us (3%)
  between operations  0.82 us (1%)
    ppermute x2, waiting for transfers between devices, on_device(): lax.ppermute(piece, 'seq', pair_perm(n_seq, k))  12.9 us
    ppermute x2, starting transfers between devices, on_device(): lax.ppermute(piece, 'seq', pair_perm(n_seq, k))  4.93 us
    ppermute x1, waiting for transfers between devices, on_device(): lax.ppermute(held, 'seq', pair_perm(n_seq, bit))  4.62 us
    ppermute x3, starting transfers between devices, on_device(): spread[step] = lax.ppermute(held, 'island', pair_perm(n_chip, step, 2))  4.61 us
    ppermute x3, starting transfers between devices, on_device(): lax.ppermute(dquery, 'seq', pair_perm(n_seq, k))  4.45 us
    ppermute x3, waiting for transfers between devices, on_device(): lax.ppermute(dquery, 'seq', pair_perm(n_seq, k))  4.04 us
    ppermute x1, starting transfers between devices, on_device(): lax.ppermute(jnp.concatenate(kv, axis=0), 'seq', pair_perm(n_seq, bit))  4.03 us
    ppermute x1, starting transfers between devices, on_device(): lax.ppermute(weight, 'seq', pair_perm(n_seq, bits[0]))  3.67 us
  transfers between devices with their start and end apart: 19, of which 11 were waited for; matrix products, arithmetic and copies ran while one was open for 9% of the time, Pallas kernels for 4%

profile of v5, /device:TPU:0, one launch (start us, length us, event | category | flops | bytes accessed | tf_op | source)
XLA Modules:
  0.0 71.8 jit_solution(1091411666205899338)
XLA Ops:
  0.6 0.5 collective-permute-start
  1.1 0.9 %convert_bitcast_fusion = bf16[32,1280]{1,0:T(8,128)(2,1)S(1)} fusion(f32[1280,32]{0,1:T(8,128)} %param.12), kind=kLoop, calls=%fused_computation.18 | loop fusion | flops 40960 | bytes 245760 | tf_op jit(solution)/shard_map/convert_element_type | solution.py:257
  2.1 3.7 %collective-permute-start.1 = (bf16[32,1280]{1,0:T(8,128)(2,1)S(1)}, bf16[32,1280]{1,0:T(8,128)(2,1)S(1)}, u32[]{:S(2)}, u32[]{:S(2)}) collective-permute-start(bf16[32,1280]{1,0:T(8,128)(2,1)S(1)} %convert_bitcast_fusion), channel_id=1, source_target_pairs={{0,2},{1,3},{2,0},{3,1},{4,6},{5,7},{6,4},{7,5},{8,10},{9,11},{10,... | collective-permute-start | bytes 245768 | tf_op jit(solution)/shard_map/ppermute | solution.py:259
  5.7 1.4 %dynamic-slice_bitcast_fusion = (bf16[128,1280]{1,0:T(8,128)(2,1)S(1)}, bf16[128,1280]{1,0:T(8,128)(2,1)S(1)}, bf16[128,1280]{1,0:T(8,128)(2,1)S(1)}, bf16[128,1280]{1,0:T(8,128)(2,1)S(1)}) fusion(bf16[1,128,5120]{2,1,0:T(8,128)(2,1)} %param.7, s32[]{:T(128)S(6)} %select_n.39, s32[]{:T(128)S(6)} %select_n.37, s32[]{:T(128)S(6)} %select_n.36, s32[]{:T(128)S(6)} %select_n.38), kind=kLoop, calls=%fused_computation.7 | loop fusion | bytes 2621456 | tf_op jit(solution)/shard_map/dynamic_slice | solution.py:250
  7.1 3.5 %collective-permute-done.1 = bf16[32,1280]{1,0:T(8,128)(2,1)S(1)} collective-permute-done((bf16[32,1280]{1,0:T(8,128)(2,1)S(1)}, bf16[32,1280]{1,0:T(8,128)(2,1)S(1)}, u32[]{:S(2)}, u32[]{:S(2)}) %collective-permute-start.1) | collective-permute-done | bytes 81952 | tf_op jit(solution)/shard_map/ppermute | solution.py:259
  10.6 0.8 %collective-permute-start.2 = (bf16[64,1280]{1,0:T(8,128)(2,1)S(1)}, bf16[64,1280]{1,0:T(8,128)(2,1)S(1)}, u32[]{:S(2)}, u32[]{:S(2)}) collective-permute-start(bf16[64,1280]{1,0:T(8,128)(2,1)S(1)} %pad_maximum_fusion.4), channel_id=1, source_target_pairs={{0,1},{1,0},{2,3},{3,2},{4,5},{5,4},{6,7},{7,6},{8,9},{9,8},{10,11... | collective-permute-start | bytes 491528 | tf_op jit(solution)/shard_map/ppermute | solution.py:269
  11.5 3.4 %collective-permute-start.3 = (bf16[128,512]{1,0:T(8,128)(2,1)S(1)}, bf16[128,512]{1,0:T(8,128)(2,1)S(1)}, u32[]{:S(2)}, u32[]{:S(2)}) collective-permute-start(bf16[128,512]{1,0:T(8,128)(2,1)S(1)} %bitcast.53), channel_id=1, source_target_pairs={{0,2},{1,3},{2,0},{3,1},{4,6},{5,7},{6,4},{7,5},{8,10},{9,11},{10,... | collective-permute-start | bytes 393224 | tf_op jit(solution)/shard_map/ppermute | solution.py:261
  14.9 4.6 %collective-permute-done.2 = bf16[64,1280]{1,0:T(8,128)(2,1)S(1)} collective-permute-done((bf16[64,1280]{1,0:T(8,128)(2,1)S(1)}, bf16[64,1280]{1,0:T(8,128)(2,1)S(1)}, u32[]{:S(2)}, u32[]{:S(2)}) %collective-permute-start.2) | collective-permute-done | bytes 163872 | tf_op jit(solution)/shard_map/ppermute | solution.py:269
  19.5 1.4 %collective-permute-start.5 = (bf16[128,1280]{1,0:T(8,128)(2,1)S(1)}, bf16[128,1280]{1,0:T(8,128)(2,1)S(1)}, u32[]{:S(2)}, u32[]{:S(2)}) collective-permute-start(bf16[128,1280]{1,0:T(8,128)(2,1)S(1)} %pad_maximum_fusion.2.refs_0_), channel_id=1, source_target_pairs={{0,8},{4,12},{8,0},{12,4},{16,24},{20,28},{24,16},{28,20},{1,9},{5... | collective-permute-start | bytes 983048 | tf_op jit(solution)/shard_map/ppermute | solution.py:280
  20.9 1.9 %collective-permute-start.8 = (bf16[128,1280]{1,0:T(8,128)(2,1)S(1)}, bf16[128,1280]{1,0:T(8,128)(2,1)S(1)}, u32[]{:S(2)}, u32[]{:S(2)}) collective-permute-start(bf16[128,1280]{1,0:T(8,128)(2,1)S(1)} %get-tuple-element.41.refs_6_), channel_id=1, source_target_pairs={{0,2},{1,3},{2,0},{3,1},{4,6},{5,7},{6,4},{7,5},{8,10},{9,11},{10,... | collective-permute-start | bytes 983048 | tf_op jit(solution)/shard_map/ppermute | solution.py:266
  22.9 3.0 %collective-permute-start.14 = (bf16[128,1280]{1,0:T(8,128)(2,1)S(1)}, bf16[128,1280]{1,0:T(8,128)(2,1)S(1)}, u32[]{:S(2)}, u32[]{:S(2)}) collective-permute-start(bf16[128,1280]{1,0:T(8,128)(2,1)S(1)} %get-tuple-element.51.refs_7_), channel_id=1, source_target_pairs={{0,3},{1,2},{2,1},{3,0},{4,7},{5,6},{6,5},{7,4},{8,11},{9,10},{10,... | collective-permute-start | bytes 983048 | tf_op jit(solution)/shard_map/ppermute | solution.py:266
  25.9 1.5 %collective-permute-start.6 = (bf16[128,1280]{1,0:T(8,128)(2,1)S(1)}, bf16[128,1280]{1,0:T(8,128)(2,1)S(1)}, u32[]{:S(2)}, u32[]{:S(2)}) collective-permute-start(bf16[128,1280]{1,0:T(8,128)(2,1)S(1)} %pad_maximum_fusion.2.refs_0_), channel_id=1, source_target_pairs={{0,16},{4,20},{8,24},{12,28},{16,0},{20,4},{24,8},{28,12},{1,17},{... | collective-permute-start | bytes 983048 | tf_op jit(solution)/shard_map/ppermute | solution.py:280
  27.4 0.6 collective-permute-done.5.refs_1_
  28.0 1.7 %collective-permute-start.7 = (bf16[128,1280]{1,0:T(8,128)(2,1)S(1)}, bf16[128,1280]{1,0:T(8,128)(2,1)S(1)}, u32[]{:S(2)}, u32[]{:S(2)}) collective-permute-start(bf16[128,1280]{1,0:T(8,128)(2,1)S(1)} %pad_maximum_fusion.2.refs_0_), channel_id=1, source_target_pairs={{0,24},{4,28},{8,16},{12,20},{16,8},{20,12},{24,0},{28,4},{1,25},{... | collective-permute-start | bytes 983048 | tf_op jit(solution)/shard_map/ppermute | solution.py:280
  29.7 4.0 %collective-permute-start.4 = (bf16[256,512]{1,0:T(8,128)(2,1)S(1)}, bf16[256,512]{1,0:T(8,128)(2,1)S(1)}, u32[]{:S(2)}, u32[]{:S(2)}) collective-permute-start(bf16[256,512]{1,0:T(8,128)(2,1)S(1)} %pad_maximum_fusion.3), channel_id=1, source_target_pairs={{0,1},{1,0},{2,3},{3,2},{4,5},{5,4},{6,7},{7,6},{8,9},{9,8},{10,11... | collective-permute-start | bytes 786440 | tf_op jit(solution)/shard_map/ppermute | solution.py:271
  33.7 12.9 %collective-permute-done.8.refs_6_ = bf16[128,1280]{1,0:T(8,128)(2,1)S(1)} collective-permute-done((bf16[128,1280]{1,0:T(8,128)(2,1)S(1)}, bf16[128,1280]{1,0:T(8,128)(2,1)S(1)}, u32[]{:S(2)}, u32[]{:S(2)}) %collective-permute-start.8) | collective-permute-done | bytes 327712 | tf_op jit(solution)/shard_map/ppermute | solution.py:266
  46.6 0.1 constant_dynamic-slice_fusion
  46.8 0.0 copy-start
  46.8 1.0 %shard_map.102 = (bf16[4,32,128]{2,1,0:T(8,128)(2,1)S(1)}, bf16[4,32,128]{2,1,0:T(8,128)(2,1)S(1)}) custom-call(bf16[128,1280]{1,0:T(8,128)(2,1)S(1)} %pad_maximum_fusion.2.refs_0_, bf16[128,1280]{1,0:T(8,128)(2,1)S(1)} %collective-permute-done.5.refs_1_, bf16[128,1280]{1,0:T(8,128)(2,1)S(1)} %collective-permute-done.6.refs_2_, ...), custom_call_target="tpu_custom_call" | custom-call | flops 335544320 | bytes 3932160 | tf_op jit(solution)/shard_map/pallas_call | solution.py:73
  47.7 0.0 copy-start.1
  47.8 0.1 collective-permute-start.9
  47.8 1.6 %collective-permute-done.4.refs_4_.refs_5_ = bf16[256,512]{1,0:T(8,128)(2,1)S(1)} collective-permute-done((bf16[256,512]{1,0:T(8,128)(2,1)S(1)}, bf16[256,512]{1,0:T(8,128)(2,1)S(1)}, u32[]{:S(2)}, u32[]{:S(2)}) %collective-permute-start.4) | collective-permute-done | bytes 262176 | tf_op jit(solution)/shard_map/ppermute | solution.py:271
  49.5 1.2 %shard_map.103.refs_0_ = bf16[256,128]{1,0:T(8,128)(2,1)S(1)} custom-call(bf16[128,512]{1,0:T(8,128)(2,1)S(1)} %bitcast.55, bf16[128,512]{1,0:T(8,128)(2,1)S(1)} %bitcast.56, bf16[128,512]{1,0:T(8,128)(2,1)S(1)} %collective-permute-done.3.refs_2_.refs_3_, bf16[128,512]{1,0:T(8,128)(2,1)S(1)} %collective-permute-done.3.refs_2_.refs_3_, ...), custom_call_target="tpu_custom_call" | custom-call | flops 402653184 | bytes 786432 | tf_op jit(solution)/shard_map/pallas_call | solution.py:153
  50.7 1.6 %collective-permute-start.10 = (bf16[256,128]{1,0:T(8,128)(2,1)S(1)}, bf16[256,128]{1,0:T(8,128)(2,1)S(1)}, u32[]{:S(2)}, u32[]{:S(2)}) collective-permute-start(bf16[256,128]{1,0:T(8,128)(2,1)S(1)} %shard_map.103.refs_0_), channel_id=1, source_target_pairs={{0,1},{1,0},{2,3},{3,2},{4,5},{5,4},{6,7},{7,6},{8,9},{9,8},{10,11... | collective-permute-start | bytes 196616 | tf_op jit(solution)/shard_map/ppermute | solution.py:291
  52.3 2.5 %collective-permute-start.11 = (bf16[256,128]{1,0:T(8,128)(2,1)S(1)}, bf16[256,128]{1,0:T(8,128)(2,1)S(1)}, u32[]{:S(2)}, u32[]{:S(2)}) collective-permute-start(bf16[256,128]{1,0:T(8,128)(2,1)S(1)} %shard_map.103.refs_0_), channel_id=1, source_target_pairs={{0,2},{1,3},{2,0},{3,1},{4,6},{5,7},{6,4},{7,5},{8,10},{9,11},{10,... | collective-permute-start | bytes 196616 | tf_op jit(solution)/shard_map/ppermute | solution.py:291
  54.8 0.3 collective-permute-start.12
  55.2 0.2 copy.14
  55.4 1.3 %copy.13 = bf16[256,1280]{1,0:T(8,128)(2,1)S(1)} copy(bf16[256,1280]{0,1:T(8,128)(2,1)} %bitcast.62) | data formatting | bytes 1310720 | tf_op jit(solution)/shard_map/transpose | solution.py:294
  56.8 0.2 collective-permute-done.13.refs_5_
  57.0 0.8 %collective-permute-done.10.refs_1_ = bf16[256,128]{1,0:T(8,128)(2,1)S(1)} collective-permute-done((bf16[256,128]{1,0:T(8,128)(2,1)S(1)}, bf16[256,128]{1,0:T(8,128)(2,1)S(1)}, u32[]{:S(2)}, u32[]{:S(2)}) %collective-permute-start.10) | collective-permute-done | bytes 65568 | tf_op jit(solution)/shard_map/ppermute | solution.py:291
  57.8 2.1 %collective-permute-done.11.refs_2_ = bf16[256,128]{1,0:T(8,128)(2,1)S(1)} collective-permute-done((bf16[256,128]{1,0:T(8,128)(2,1)S(1)}, bf16[256,128]{1,0:T(8,128)(2,1)S(1)}, u32[]{:S(2)}, u32[]{:S(2)}) %collective-permute-start.11) | collective-permute-done | bytes 65568 | tf_op jit(solution)/shard_map/ppermute | solution.py:291
  59.9 1.1 %collective-permute-done.12.refs_3_ = bf16[256,128]{1,0:T(8,128)(2,1)S(1)} collective-permute-done((bf16[256,128]{1,0:T(8,128)(2,1)S(1)}, bf16[256,128]{1,0:T(8,128)(2,1)S(1)}, u32[]{:S(2)}, u32[]{:S(2)}) %collective-permute-start.12) | collective-permute-done | bytes 65568 | tf_op jit(solution)/shard_map/ppermute | solution.py:291
  61.0 0.7 shard_map.105
  61.7 0.1 collective-permute-start.15
  61.7 0.7 shard_map.104
  62.4 0.1 select_bitcast_fusion.1
  62.5 0.1 pad_maximum_fusion.1
  62.6 0.8 %collective-permute-done.15.got_ref = bf16[4,32,1280]{2,1,0:T(8,128)(2,1)S(1)} collective-permute-done((bf16[4,32,1280]{2,1,0:T(8,128)(2,1)S(1)}, bf16[4,32,1280]{2,1,0:T(8,128)(2,1)S(1)}, u32[]{:S(2)}, u32[]{:S(2)}) %collective-permute-start.15) | collective-permute-done | bytes 327712 | tf_op jit(solution)/shard_map/ppermute | solution.py:299
  63.4 0.1 shard_map.106
  63.4 0.6 collective-permute-start.16
  64.0 1.6 %collective-permute-start.17 = (bf16[32,1280]{1,0:T(8,128)(2,1)S(1)}, bf16[32,1280]{1,0:T(8,128)(2,1)S(1)}, u32[]{:S(2)}, u32[]{:S(2)}) collective-permute-start(bf16[32,1280]{1,0:T(8,128)(2,1)S(1)} %get-tuple-element.56), channel_id=1, source_target_pairs={{0,16},{4,20},{8,24},{12,28},{16,0},{20,4},{24,8},{28,12},{1,17},{... | collective-permute-start | bytes 245768 | tf_op jit(solution)/shard_map/ppermute | solution.py:312
  65.6 1.4 %collective-permute-start.18 = (bf16[32,1280]{1,0:T(8,128)(2,1)S(1)}, bf16[32,1280]{1,0:T(8,128)(2,1)S(1)}, u32[]{:S(2)}, u32[]{:S(2)}) collective-permute-start(bf16[32,1280]{1,0:T(8,128)(2,1)S(1)} %get-tuple-element.57), channel_id=1, source_target_pairs={{0,24},{4,28},{8,16},{12,20},{16,8},{20,12},{24,0},{28,4},{1,25},{... | collective-permute-start | bytes 245768 | tf_op jit(solution)/shard_map/ppermute | solution.py:312
  67.0 0.1 pad_maximum_fusion
  67.1 1.1 %copy.18 = bf16[1,1280,256]{2,1,0:T(8,128)(2,1)} copy(bf16[1,1280,256]{1,2,0:T(8,128)(2,1)S(1)} %bitcast.58) | data formatting | bytes 1310720
  68.2 1.1 %copy.17 = bf16[1,1280,256]{2,1,0:T(8,128)(2,1)} copy(bf16[1,1280,256]{1,2,0:T(8,128)(2,1)S(1)} %bitcast.59) | data formatting | bytes 1310720
  69.3 0.0 collective-permute-done.17
  69.3 1.6 %collective-permute-done.18 = bf16[32,1280]{1,0:T(8,128)(2,1)S(1)} collective-permute-done((bf16[32,1280]{1,0:T(8,128)(2,1)S(1)}, bf16[32,1280]{1,0:T(8,128)(2,1)S(1)}, u32[]{:S(2)}, u32[]{:S(2)}) %collective-permute-start.18) | collective-permute-done | bytes 81952 | tf_op jit(solution)/shard_map/ppermute | solution.py:312
  71.0 0.8 %fusion.1 = (f32[1280,32]{0,1:T(8,128)}, f32[1280,32]{0,1:T(8,128)}) fusion(f32[1280,32]{0,1:T(8,128)S(1)} %copy-done.2, bf16[32,1280]{1,0:T(8,128)(2,1)S(1)} %collective-permute-done.18, bf16[32,1280]{1,0:T(8,128)(2,1)S(1)} %collective-permute-done.17, f32[32,1280]{1,0:T(8,128)S(1)} %get-tuple-element.54, bf16[32,1280]{1,0:T(8,128)(2,1)S(1)} %collective-permute-done.16, ...), kind=kLoop, calls=%fused_computation.16 | loop fusion | flops 532480 | bytes 1064960 | tf_op jit(solution)/shard_map/sub | solution.py:317
  (22 shorter events, 0.2 us)
Async XLA Ops:
  0.6 10.8 %collective-permute-start = (bf16[128,5120]{1,0:T(8,128)(2,1)}, bf16[128,5120]{1,0:T(8,128)(2,1)S(1)}, u32[]{:S(2)}, u32[]{:S(2)}) collective-permute-start(bf16[128,5120]{1,0:T(8,128)(2,1)} %bitcast.60), channel_id=1, source_target_pairs={{0,4},{4,0},{8,12},{12,8},{16,20},{20,16},{24,28},{28,24},{1,5},{5... | collective-permute-start | bytes 3932168 | tf_op jit(solution)/shard_map/ppermute | solution.py:256
  2.1 8.5 %collective-permute-start.1 = (bf16[32,1280]{1,0:T(8,128)(2,1)S(1)}, bf16[32,1280]{1,0:T(8,128)(2,1)S(1)}, u32[]{:S(2)}, u32[]{:S(2)}) collective-permute-start(bf16[32,1280]{1,0:T(8,128)(2,1)S(1)} %convert_bitcast_fusion), channel_id=1, source_target_pairs={{0,2},{1,3},{2,0},{3,1},{4,6},{5,7},{6,4},{7,5},{8,10},{9,11},{10,... | collective-permute-start | bytes 245768 | tf_op jit(solution)/shard_map/ppermute | solution.py:259
  5.7 5.7 %copy-start.4 = (bf16[1,128,2,256]{3,2,1,0:T(2,128)(2,1)S(1)}, bf16[1,128,2,256]{3,2,1,0:T(2,128)(2,1)}, u32[]{:S(2)}) copy-start(bf16[1,128,2,256]{3,2,1,0:T(2,128)(2,1)} %param.8) | copy-start | bytes 393220
  10.6 8.9 %collective-permute-start.2 = (bf16[64,1280]{1,0:T(8,128)(2,1)S(1)}, bf16[64,1280]{1,0:T(8,128)(2,1)S(1)}, u32[]{:S(2)}, u32[]{:S(2)}) collective-permute-start(bf16[64,1280]{1,0:T(8,128)(2,1)S(1)} %pad_maximum_fusion.4), channel_id=1, source_target_pairs={{0,1},{1,0},{2,3},{3,2},{4,5},{5,4},{6,7},{7,6},{8,9},{9,8},{10,11... | collective-permute-start | bytes 491528 | tf_op jit(solution)/shard_map/ppermute | solution.py:269
  11.5 8.1 %collective-permute-start.3 = (bf16[128,512]{1,0:T(8,128)(2,1)S(1)}, bf16[128,512]{1,0:T(8,128)(2,1)S(1)}, u32[]{:S(2)}, u32[]{:S(2)}) collective-permute-start(bf16[128,512]{1,0:T(8,128)(2,1)S(1)} %bitcast.53), channel_id=1, source_target_pairs={{0,2},{1,3},{2,0},{3,1},{4,6},{5,7},{6,4},{7,5},{8,10},{9,11},{10,... | collective-permute-start | bytes 393224 | tf_op jit(solution)/shard_map/ppermute | solution.py:261
  19.5 8.4 %collective-permute-start.5 = (bf16[128,1280]{1,0:T(8,128)(2,1)S(1)}, bf16[128,1280]{1,0:T(8,128)(2,1)S(1)}, u32[]{:S(2)}, u32[]{:S(2)}) collective-permute-start(bf16[128,1280]{1,0:T(8,128)(2,1)S(1)} %pad_maximum_fusion.2.refs_0_), channel_id=1, source_target_pairs={{0,8},{4,12},{8,0},{12,4},{16,24},{20,28},{24,16},{28,20},{1,9},{5... | collective-permute-start | bytes 983048 | tf_op jit(solution)/shard_map/ppermute | solution.py:280
  20.9 25.6 %collective-permute-start.8 = (bf16[128,1280]{1,0:T(8,128)(2,1)S(1)}, bf16[128,1280]{1,0:T(8,128)(2,1)S(1)}, u32[]{:S(2)}, u32[]{:S(2)}) collective-permute-start(bf16[128,1280]{1,0:T(8,128)(2,1)S(1)} %get-tuple-element.41.refs_6_), channel_id=1, source_target_pairs={{0,2},{1,3},{2,0},{3,1},{4,6},{5,7},{6,4},{7,5},{8,10},{9,11},{10,... | collective-permute-start | bytes 983048 | tf_op jit(solution)/shard_map/ppermute | solution.py:266
  22.9 33.9 %collective-permute-start.14 = (bf16[128,1280]{1,0:T(8,128)(2,1)S(1)}, bf16[128,1280]{1,0:T(8,128)(2,1)S(1)}, u32[]{:S(2)}, u32[]{:S(2)}) collective-permute-start(bf16[128,1280]{1,0:T(8,128)(2,1)S(1)} %get-tuple-element.51.refs_7_), channel_id=1, source_target_pairs={{0,3},{1,2},{2,1},{3,0},{4,7},{5,6},{6,5},{7,4},{8,11},{9,10},{10,... | collective-permute-start | bytes 983048 | tf_op jit(solution)/shard_map/ppermute | solution.py:266
  25.9 20.9 %collective-permute-start.6 = (bf16[128,1280]{1,0:T(8,128)(2,1)S(1)}, bf16[128,1280]{1,0:T(8,128)(2,1)S(1)}, u32[]{:S(2)}, u32[]{:S(2)}) collective-permute-start(bf16[128,1280]{1,0:T(8,128)(2,1)S(1)} %pad_maximum_fusion.2.refs_0_), channel_id=1, source_target_pairs={{0,16},{4,20},{8,24},{12,28},{16,0},{20,4},{24,8},{28,12},{1,17},{... | collective-permute-start | bytes 983048 | tf_op jit(solution)/shard_map/ppermute | solution.py:280
  28.0 18.8 %collective-permute-start.7 = (bf16[128,1280]{1,0:T(8,128)(2,1)S(1)}, bf16[128,1280]{1,0:T(8,128)(2,1)S(1)}, u32[]{:S(2)}, u32[]{:S(2)}) collective-permute-start(bf16[128,1280]{1,0:T(8,128)(2,1)S(1)} %pad_maximum_fusion.2.refs_0_), channel_id=1, source_target_pairs={{0,24},{4,28},{8,16},{12,20},{16,8},{20,12},{24,0},{28,4},{1,25},{... | collective-permute-start | bytes 983048 | tf_op jit(solution)/shard_map/ppermute | solution.py:280
  29.7 19.8 %collective-permute-start.4 = (bf16[256,512]{1,0:T(8,128)(2,1)S(1)}, bf16[256,512]{1,0:T(8,128)(2,1)S(1)}, u32[]{:S(2)}, u32[]{:S(2)}) collective-permute-start(bf16[256,512]{1,0:T(8,128)(2,1)S(1)} %pad_maximum_fusion.3), channel_id=1, source_target_pairs={{0,1},{1,0},{2,3},{3,2},{4,5},{5,4},{6,7},{7,6},{8,9},{9,8},{10,11... | collective-permute-start | bytes 786440 | tf_op jit(solution)/shard_map/ppermute | solution.py:271
  46.6 10.4 %collective-permute-start.13 = (bf16[128,1280]{1,0:T(8,128)(2,1)S(1)}, bf16[128,1280]{1,0:T(8,128)(2,1)S(1)}, u32[]{:S(2)}, u32[]{:S(2)}) collective-permute-start(bf16[128,1280]{1,0:T(8,128)(2,1)S(1)} %get-tuple-element.49.refs_5_), channel_id=1, source_target_pairs={{0,1},{1,0},{2,3},{3,2},{4,5},{5,4},{6,7},{7,6},{8,9},{9,8},{10,11... | collective-permute-start | bytes 983048 | tf_op jit(solution)/shard_map/ppermute | solution.py:282
  46.8 2.7 %copy-start = (bf16[1,128,256]{2,1,0:T(8,128)(2,1)S(1)}, bf16[1,128,256]{2,1,0:T(8,128)(2,1)}, u32[]{:S(2)}) copy-start(bf16[1,128,256]{2,1,0:T(8,128)(2,1)} %param.9) | copy-start | bytes 196612
  47.7 7.4 %copy-start.1 = (bf16[1,1280,256]{2,1,0:T(8,128)(2,1)S(1)}, bf16[1,1280,256]{2,1,0:T(8,128)(2,1)}, u32[]{:S(2)}) copy-start(bf16[1,1280,256]{2,1,0:T(8,128)(2,1)} %param.11) | copy-start | bytes 1966084
  47.8 1.7 %collective-permute-start.9 = (bf16[4,32,128]{2,1,0:T(8,128)(2,1)S(1)}, bf16[4,32,128]{2,1,0:T(8,128)(2,1)S(1)}, u32[]{:S(2)}, u32[]{:S(2)}) collective-permute-start(bf16[4,32,128]{2,1,0:T(8,128)(2,1)S(1)} %get-tuple-element.48), channel_id=1, source_target_pairs={{0,4},{4,0},{8,12},{12,8},{16,20},{20,16},{24,28},{28,24},{1,5},{5... | collective-permute-start | bytes 98312 | tf_op jit(solution)/shard_map/ppermute | solution.py:288
  50.7 7.0 %collective-permute-start.10 = (bf16[256,128]{1,0:T(8,128)(2,1)S(1)}, bf16[256,128]{1,0:T(8,128)(2,1)S(1)}, u32[]{:S(2)}, u32[]{:S(2)}) collective-permute-start(bf16[256,128]{1,0:T(8,128)(2,1)S(1)} %shard_map.103.refs_0_), channel_id=1, source_target_pairs={{0,1},{1,0},{2,3},{3,2},{4,5},{5,4},{6,7},{7,6},{8,9},{9,8},{10,11... | collective-permute-start | bytes 196616 | tf_op jit(solution)/shard_map/ppermute | solution.py:291
  52.3 7.6 %collective-permute-start.11 = (bf16[256,128]{1,0:T(8,128)(2,1)S(1)}, bf16[256,128]{1,0:T(8,128)(2,1)S(1)}, u32[]{:S(2)}, u32[]{:S(2)}) collective-permute-start(bf16[256,128]{1,0:T(8,128)(2,1)S(1)} %shard_map.103.refs_0_), channel_id=1, source_target_pairs={{0,2},{1,3},{2,0},{3,1},{4,6},{5,7},{6,4},{7,5},{8,10},{9,11},{10,... | collective-permute-start | bytes 196616 | tf_op jit(solution)/shard_map/ppermute | solution.py:291
  54.8 6.2 %collective-permute-start.12 = (bf16[256,128]{1,0:T(8,128)(2,1)S(1)}, bf16[256,128]{1,0:T(8,128)(2,1)S(1)}, u32[]{:S(2)}, u32[]{:S(2)}) collective-permute-start(bf16[256,128]{1,0:T(8,128)(2,1)S(1)} %shard_map.103.refs_0_), channel_id=1, source_target_pairs={{0,3},{1,2},{2,1},{3,0},{4,7},{5,6},{6,5},{7,4},{8,11},{9,10},{10,... | collective-permute-start | bytes 196616 | tf_op jit(solution)/shard_map/ppermute | solution.py:291
  61.7 1.7 %collective-permute-start.15 = (bf16[4,32,1280]{2,1,0:T(8,128)(2,1)S(1)}, bf16[4,32,1280]{2,1,0:T(8,128)(2,1)S(1)}, u32[]{:S(2)}, u32[]{:S(2)}) collective-permute-start(bf16[4,32,1280]{2,1,0:T(8,128)(2,1)S(1)} %get-tuple-element.53), channel_id=1, source_target_pairs={{0,4},{4,0},{8,12},{12,8},{16,20},{20,16},{24,28},{28,24},{1,5},{5... | collective-permute-start | bytes 983048 | tf_op jit(solution)/shard_map/ppermute | solution.py:299
  63.4 5.9 %collective-permute-start.16 = (bf16[32,1280]{1,0:T(8,128)(2,1)S(1)}, bf16[32,1280]{1,0:T(8,128)(2,1)S(1)}, u32[]{:S(2)}, u32[]{:S(2)}) collective-permute-start(bf16[32,1280]{1,0:T(8,128)(2,1)S(1)} %get-tuple-element.55), channel_id=1, source_target_pairs={{0,8},{4,12},{8,0},{12,4},{16,24},{20,28},{24,16},{28,20},{1,9},{5... | collective-permute-start | bytes 245768 | tf_op jit(solution)/shard_map/ppermute | solution.py:312
  64.0 5.3 %collective-permute-start.17 = (bf16[32,1280]{1,0:T(8,128)(2,1)S(1)}, bf16[32,1280]{1,0:T(8,128)(2,1)S(1)}, u32[]{:S(2)}, u32[]{:S(2)}) collective-permute-start(bf16[32,1280]{1,0:T(8,128)(2,1)S(1)} %get-tuple-element.56), channel_id=1, source_target_pairs={{0,16},{4,20},{8,24},{12,28},{16,0},{20,4},{24,8},{28,12},{1,17},{... | collective-permute-start | bytes 245768 | tf_op jit(solution)/shard_map/ppermute | solution.py:312
  65.6 5.3 %collective-permute-start.18 = (bf16[32,1280]{1,0:T(8,128)(2,1)S(1)}, bf16[32,1280]{1,0:T(8,128)(2,1)S(1)}, u32[]{:S(2)}, u32[]{:S(2)}) collective-permute-start(bf16[32,1280]{1,0:T(8,128)(2,1)S(1)} %get-tuple-element.57), channel_id=1, source_target_pairs={{0,24},{4,28},{8,16},{12,20},{16,8},{20,12},{24,0},{28,4},{1,25},{... | collective-permute-start | bytes 245768 | tf_op jit(solution)/shard_map/ppermute | solution.py:312
  68.2 2.8 %copy-start.2 = (f32[1280,32]{0,1:T(8,128)S(1)}, f32[1280,32]{0,1:T(8,128)}, u32[]{:S(2)}) copy-start(f32[1280,32]{0,1:T(8,128)} %param.12) | copy-start | bytes 491524
  68.2 2.8 %copy-start.3 = (f32[1280,32]{0,1:T(8,128)S(1)}, f32[1280,32]{0,1:T(8,128)}, u32[]{:S(2)}) copy-start(f32[1280,32]{0,1:T(8,128)} %param.13) | copy-start | bytes 491524

commit v6 on v5

--- a/solution.py
+++ b/solution.py
@@ -32,6 +32,14 @@
         (group * stride + inner, (group ^ step) * stride + inner)
         for group in range(size)
         for inner in range(stride)
+    ]
+
+
+def far_pairs(n_island, n_seq, step):
+    return [
+        (i * n_seq + s, i * n_seq + (s ^ (step + i % 2)))
+        for i in range(n_island)
+        for s in range(n_seq)
     ]
 
 
@@ -177,8 +185,11 @@
         for j in range(n_chip):
             start = pl.multiple_of((2 * j + half) * share, share)
             pieces.append(ref[pl.ds(start, share), :])
-        left.append(jnp.concatenate(pieces, axis=0))
-    left = jnp.concatenate(left, axis=1)
+        left.append(jnp.concatenate(pieces, axis=0).astype(jnp.float32))
+    for k in range(2, n_seq, 2):
+        even, odd = left[k], left[k + 1]
+        left[k], left[k + 1] = jnp.where(core == 0, even, odd), jnp.where(core == 0, odd, even)
+    left = jnp.concatenate(left, axis=1).astype(jnp.bfloat16)
     states = jnp.concatenate([ref[...] for ref in state_refs], axis=0)
     gradient = jnp.dot(left, states, preferred_element_type=jnp.float32) * inverse
     for j in range(n_chip):
@@ -245,47 +256,45 @@
     inverse = features ** (-0.5)
     swap = pair_perm(n_island, 1)
 
-    def feature_blocks(matrix):
-        return [
-            lax.dynamic_slice(matrix, (0, jnp.bitwise_xor(seq, k) * block), (rows, block))
-            for k in range(n_seq)
-        ]
-
     order = gather_order(n_seq)
     bits = [1 << bit for bit in reversed(range(n_seq.bit_length() - 1))]
+    far_perm = pair_perm(n_seq, bits[0])
     partner_tokens = lax.ppermute(tokens, "island", swap)
     weight = anchor.T.astype(jnp.bfloat16)
-    own_kv = key_vals[0].reshape(rows, 2 * cols)
-    held = jnp.concatenate([weight, lax.ppermute(weight, "seq", pair_perm(n_seq, bits[0]))], 0)
-    own_kv, partner_tokens = lax.optimization_barrier((own_kv, partner_tokens))
-    kv = [own_kv, lax.ppermute(own_kv, "seq", pair_perm(n_seq, bits[0]))]
-
-    own_blocks = feature_blocks(tokens)
-    far, held = lax.optimization_barrier((own_blocks[2:], held))
-    gathered = [own_blocks[0], None] + [
-        lax.ppermute(piece, "seq", pair_perm(n_seq, k)) for k, piece in enumerate(far, 2)
-    ]
+    held = jnp.concatenate([weight, lax.ppermute(weight, "seq", far_perm)], 0)
+    kv = [key_vals[0].reshape(rows, 2 * cols)]
+    kv.append(lax.ppermute(kv[0], "seq", far_perm))
+    held, kv, partner_tokens = lax.optimization_barrier((held, kv, partner_tokens))
+
+    def feature_block(matrix, k):
+        return lax.dynamic_slice(matrix, (0, jnp.bitwise_xor(seq, k) * block), (rows, block))
+
+    far = []
+    for k in range(2, n_seq, 2):
+        both = jnp.concatenate([feature_block(m, k + core) for m in (tokens, partner_tokens)], 0)
+        far.append(lax.ppermute(both, ("island", "seq"), far_pairs(n_island, n_seq, k)))
+    own_blocks = [feature_block(tokens, k) for k in range(n_seq)]
+    partner_blocks = [feature_block(partner_tokens, k) for k in range(n_seq)]
     for bit in bits[1:]:
         held = jnp.concatenate([held, lax.ppermute(held, "seq", pair_perm(n_seq, bit))], 0)
-        kv.append(
-            lax.ppermute(jnp.concatenate(kv, axis=0), "seq", pair_perm(n_seq, bit))
-        )
+        kv.append(lax.ppermute(jnp.concatenate(kv, axis=0), "seq", pair_perm(n_seq, bit)))
 
     rounds = [order]
-    held, kv[1], partner_tokens = lax.optimization_barrier((held, kv[1], partner_tokens))
     spread = [held] + [None] * (n_chip - 1)
     for step in range(1, n_chip):
         if step & (step - 1):
             held, spread[1] = lax.optimization_barrier((held, spread[1]))
         spread[step] = lax.ppermute(held, "island", pair_perm(n_chip, step, 2))
-    near, spread[1] = lax.optimization_barrier((own_blocks[1], spread[1]))
-    gathered[1] = lax.ppermute(near, "seq", pair_perm(n_seq, 1))
-
-    (spread, gathered[2]) = lax.optimization_barrier((spread, gathered[2]))
+
     mine, for_partner = half_queries(
-        rounds, [spread], own_blocks, feature_blocks(partner_tokens), share, inverse
-    )
+        rounds, [spread], own_blocks, partner_blocks, share, inverse
+    )
+    near, for_partner = lax.optimization_barrier((own_blocks[1], for_partner))
     other = lax.ppermute(for_partner, "island", swap)
+    gathered = [own_blocks[0], lax.ppermute(near, "seq", pair_perm(n_seq, 1))]
+    _, far = lax.optimization_barrier((for_partner, far))
+    for got in far:
+        gathered += [got[:rows], lax.ppermute(got[rows:], "island", swap)]
     dquery = attention(kv, order, mine, other, cotangent[0])
     dqueries = [dquery] + [
         lax.ppermute(dquery, "seq", pair_perm(n_seq, k)) for k in range(1, n_seq)

time: 72 us -> 80.9 us (1.12)
  waiting for transfers between devices: 29.8 us -> 43.2 us
  starting transfers between devices: 30.1 us -> 23.9 us
  local copies, waits for them, and re-layouts: 5.38 us -> 7.18 us
    ppermute x3, waiting for transfers between devices: 0.59 us -> 10.6 us  [on_device(): spread[step] = lax.ppermute(held, 'island', pair_perm(n_chip, step, 2))]
    ppermute x5, starting transfers between devices: 12 us -> 6.62 us  [the longest x1 3.67 us: on_device(): held = jnp.concatenate([weight, lax.ppermute(weight, 'seq', far_perm)], 0)]
    ppermute x1, starting transfers between devices: 4.03 us -> 1.75 us  [on_device(): lax.ppermute(jnp.concatenate(kv, axis=0), 'seq', pair_perm(n_seq, bit))]
    ppermute x5, waiting for transfers between devices: 16.5 us -> 18.7 us  [the longest x1 10.7 us: on_device(): lax.ppermute(both, ('island', 'seq'), far_pairs(n_island, n_seq, k))]
    ppermute x3, waiting for transfers between devices: 4.04 us -> 5.84 us  [on_device(): lax.ppermute(dquery, 'seq', pair_perm(n_seq, k))]
    ppermute x1, waiting for transfers between devices: 1.64 us -> 0.01 us  [on_device(): lax.ppermute(jnp.concatenate(kv, axis=0), 'seq', pair_perm(n_seq, bit))]
    ppermute x3, starting transfers between devices: 4.61 us -> 5.78 us  [on_device(): spread[step] = lax.ppermute(held, 'island', pair_perm(n_chip, step, 2))]
    transpose x1, local copies, waits for them, and re-layouts: 0.24 us -> 1.33 us  [on_device(): second = second_moment[0].T.reshape(n_chip, 2, share, block)]
  transfers between devices with their start and end apart: 19 -> 19, of which waited for: 11 -> 12; matrix products, arithmetic and copies ran while one was open for 9% -> 10% of each run, Pallas kernels for 4% -> 4%
where the time goes in v6:
time: 80.9 us; the launch traced here: 80.7 us
  waiting for transfers between devices  43.2 us (53%)
  starting transfers between devices  23.9 us (30%)
  local copies, waits for them, and re-layouts  7.18 us (9%)
  Pallas kernels  3.59 us (4%)
  other arithmetic  2.01 us (2%)
  between operations  0.81 us (1%)
    ppermute x1, waiting for transfers between devices, on_device(): lax.ppermute(both, ('island', 'seq'), far_pairs(n_island, n_seq, k))  10.7 us
    ppermute x3, waiting for transfers between devices, on_device(): spread[step] = lax.ppermute(held, 'island', pair_perm(n_chip, step, 2))  10.6 us
    ppermute x3, waiting for transfers between devices, on_device(): lax.ppermute(dquery, 'seq', pair_perm(n_seq, k))  5.84 us
    ppermute x3, starting transfers between devices, on_device(): spread[step] = lax.ppermute(held, 'island', pair_perm(n_chip, step, 2))  5.78 us
    ppermute x1, waiting for transfers between devices, on_device(): kv.append(lax.ppermute(kv[0], 'seq', far_perm))  5.51 us
    ppermute x1, waiting for transfers between devices, on_device(): lax.ppermute(held, 'seq', pair_perm(n_seq, bit))  4.89 us
    ppermute x3, starting transfers between devices, on_device(): lax.ppermute(dquery, 'seq', pair_perm(n_seq, k))  4.29 us
    ppermute x1, starting transfers between devices, on_device(): held = jnp.concatenate([weight, lax.ppermute(weight, 'seq', far_perm)], 0)  3.67 us
  transfers between devices with their start and end apart: 19, of which 12 were waited for; matrix products, arithmetic and copies ran while one was open for 10% of the time, Pallas kernels for 4%

profile of v6, /device:TPU:0, one launch (start us, length us, event | category | flops | bytes accessed | tf_op | source)
XLA Modules:
  0.0 80.7 jit_solution(16810198169559236657)
XLA Ops:
  0.6 0.5 collective-permute-start.2
  1.1 0.9 %convert_bitcast_fusion = bf16[32,1280]{1,0:T(8,128)(2,1)S(1)} fusion(f32[1280,32]{0,1:T(8,128)} %param.12), kind=kLoop, calls=%fused_computation.19 | loop fusion | flops 40960 | bytes 245760 | tf_op jit(solution)/shard_map/convert_element_type | solution.py:263
  2.1 3.7 %collective-permute-start = (bf16[32,1280]{1,0:T(8,128)(2,1)S(1)}, bf16[32,1280]{1,0:T(8,128)(2,1)S(1)}, u32[]{:S(2)}, u32[]{:S(2)}) collective-permute-start(bf16[32,1280]{1,0:T(8,128)(2,1)S(1)} %convert_bitcast_fusion), channel_id=1, source_target_pairs={{0,2},{1,3},{2,0},{3,1},{4,6},{5,7},{6,4},{7,5},{8,10},{9,11},{10,... | collective-permute-start | bytes 245768 | tf_op jit(solution)/shard_map/ppermute | solution.py:264
  5.7 0.9 %copy.19 = bf16[16,8,2,256]{3,1,2,0:T(8,128)(2,1)S(1)} copy(bf16[16,8,2,256]{3,2,1,0:T(2,128)(2,1)} %bitcast.65) | data formatting | bytes 262144
  6.7 0.1 collective-permute-start.1
  6.8 1.5 %dynamic-slice_bitcast_fusion = (bf16[128,1280]{1,0:T(8,128)(2,1)S(1)}, bf16[128,1280]{1,0:T(8,128)(2,1)S(1)}, bf16[128,1280]{1,0:T(8,128)(2,1)S(1)}, bf16[128,1280]{1,0:T(8,128)(2,1)S(1)}, bf16[128,1280]{1,0:T(8,128)(2,1)S(1)}) fusion(bf16[1,128,5120]{2,1,0:T(8,128)(2,1)} %param.7, s32[]{:T(128)S(6)} %select_n.44, s32[]{:T(128)S(6)} %select_n.42, ...), kind=kLoop, calls=%fused_computation.7 | loop fusion | bytes 3276820 | tf_op jit(solution)/shard_map/dynamic_slice | solution.py:270
  8.3 2.4 %collective-permute-done = bf16[32,1280]{1,0:T(8,128)(2,1)S(1)} collective-permute-done((bf16[32,1280]{1,0:T(8,128)(2,1)S(1)}, bf16[32,1280]{1,0:T(8,128)(2,1)S(1)}, u32[]{:S(2)}, u32[]{:S(2)}) %collective-permute-start) | collective-permute-done | bytes 81952 | tf_op jit(solution)/shard_map/ppermute | solution.py:264
  10.7 5.5 %collective-permute-done.1.refs_2_.refs_3_ = bf16[128,512]{1,0:T(8,128)(2,1)S(1)} collective-permute-done((bf16[128,512]{1,0:T(8,128)(2,1)S(1)}, bf16[128,512]{1,0:T(8,128)(2,1)S(1)}, u32[]{:S(2)}, u32[]{:S(2)}) %collective-permute-start.1) | collective-permute-done | bytes 131104 | tf_op jit(solution)/shard_map/ppermute | solution.py:266
  16.2 0.1 constant_dynamic-slice_fusion
  16.4 0.8 %collective-permute-start.4 = (bf16[64,1280]{1,0:T(8,128)(2,1)S(1)}, bf16[64,1280]{1,0:T(8,128)(2,1)S(1)}, u32[]{:S(2)}, u32[]{:S(2)}) collective-permute-start(bf16[64,1280]{1,0:T(8,128)(2,1)S(1)} %pad_maximum_fusion.4), channel_id=1, source_target_pairs={{0,1},{1,0},{2,3},{3,2},{4,5},{5,4},{6,7},{7,6},{8,9},{9,8},{10,11... | collective-permute-start | bytes 491528 | tf_op jit(solution)/shard_map/ppermute | solution.py:279
  17.2 4.9 %collective-permute-done.4 = bf16[64,1280]{1,0:T(8,128)(2,1)S(1)} collective-permute-done((bf16[64,1280]{1,0:T(8,128)(2,1)S(1)}, bf16[64,1280]{1,0:T(8,128)(2,1)S(1)}, u32[]{:S(2)}, u32[]{:S(2)}) %collective-permute-start.4) | collective-permute-done | bytes 163872 | tf_op jit(solution)/shard_map/ppermute | solution.py:279
  22.1 1.7 %collective-permute-start.5 = (bf16[128,1280]{1,0:T(8,128)(2,1)S(1)}, bf16[128,1280]{1,0:T(8,128)(2,1)S(1)}, u32[]{:S(2)}, u32[]{:S(2)}) collective-permute-start(bf16[128,1280]{1,0:T(8,128)(2,1)S(1)} %constant_dynamic-update-slice_fusion.refs_0_), channel_id=1, source_target_pairs={{0,8},{4,12},{8,0},{12,4},{16,24},{20,28},{24,16},{28,20},{1,9},{5... | collective-permute-start | bytes 983048 | tf_op jit(solution)/shard_map/ppermute | solution.py:287
  23.8 2.9 %collective-permute-start.13 = (bf16[256,1280]{1,0:T(8,128)(2,1)S(1)}, bf16[256,1280]{1,0:T(8,128)(2,1)S(1)}, u32[]{:S(2)}, u32[]{:S(2)}) collective-permute-start(bf16[256,1280]{1,0:T(8,128)(2,1)S(1)} %pad_maximum_fusion), channel_id=1, source_target_pairs={{0,2},{1,3},{2,0},{3,1},{4,7},{5,6},{6,5},{7,4},{8,10},{9,11},{10,... | collective-permute-start | bytes 1966088 | tf_op jit(solution)/shard_map/ppermute | solution.py:275
  26.7 1.5 %collective-permute-start.6 = (bf16[128,1280]{1,0:T(8,128)(2,1)S(1)}, bf16[128,1280]{1,0:T(8,128)(2,1)S(1)}, u32[]{:S(2)}, u32[]{:S(2)}) collective-permute-start(bf16[128,1280]{1,0:T(8,128)(2,1)S(1)} %constant_dynamic-update-slice_fusion.refs_0_), channel_id=1, source_target_pairs={{0,16},{4,20},{8,24},{12,28},{16,0},{20,4},{24,8},{28,12},{1,17},{... | collective-permute-start | bytes 983048 | tf_op jit(solution)/shard_map/ppermute | solution.py:287
  28.2 2.2 %collective-permute-done.5.refs_1_ = bf16[128,1280]{1,0:T(8,128)(2,1)S(1)} collective-permute-done((bf16[128,1280]{1,0:T(8,128)(2,1)S(1)}, bf16[128,1280]{1,0:T(8,128)(2,1)S(1)}, u32[]{:S(2)}, u32[]{:S(2)}) %collective-permute-start.5) | collective-permute-done | bytes 327712 | tf_op jit(solution)/shard_map/ppermute | solution.py:287
  30.4 2.6 %collective-permute-start.7 = (bf16[128,1280]{1,0:T(8,128)(2,1)S(1)}, bf16[128,1280]{1,0:T(8,128)(2,1)S(1)}, u32[]{:S(2)}, u32[]{:S(2)}) collective-permute-start(bf16[128,1280]{1,0:T(8,128)(2,1)S(1)} %constant_dynamic-update-slice_fusion.refs_0_), channel_id=1, source_target_pairs={{0,24},{4,28},{8,16},{12,20},{16,8},{20,12},{24,0},{28,4},{1,25},{... | collective-permute-start | bytes 983048 | tf_op jit(solution)/shard_map/ppermute | solution.py:287
  33.0 1.8 %collective-permute-start.3 = (bf16[256,512]{1,0:T(8,128)(2,1)S(1)}, bf16[256,512]{1,0:T(8,128)(2,1)S(1)}, u32[]{:S(2)}, u32[]{:S(2)}) collective-permute-start(bf16[256,512]{1,0:T(8,128)(2,1)S(1)} %pad_maximum_fusion.3), channel_id=1, source_target_pairs={{0,1},{1,0},{2,3},{3,2},{4,5},{5,4},{6,7},{7,6},{8,9},{9,8},{10,11... | collective-permute-start | bytes 786440 | tf_op jit(solution)/shard_map/ppermute | solution.py:280
  34.8 8.4 %collective-permute-done.6.refs_2_ = bf16[128,1280]{1,0:T(8,128)(2,1)S(1)} collective-permute-done((bf16[128,1280]{1,0:T(8,128)(2,1)S(1)}, bf16[128,1280]{1,0:T(8,128)(2,1)S(1)}, u32[]{:S(2)}, u32[]{:S(2)}) %collective-permute-start.6) | collective-permute-done | bytes 327712 | tf_op jit(solution)/shard_map/ppermute | solution.py:287
  43.2 1.0 %shard_map.102 = (bf16[4,32,128]{2,1,0:T(8,128)(2,1)S(1)}, bf16[4,32,128]{2,1,0:T(8,128)(2,1)S(1)}) custom-call(bf16[128,1280]{1,0:T(8,128)(2,1)S(1)} %constant_dynamic-update-slice_fusion.refs_0_, bf16[128,1280]{1,0:T(8,128)(2,1)S(1)} %collective-permute-done.5.refs_1_, bf16[128,1280]{1,0:T(8,128)(2,1)S(1)} %collective-permute-done.6.refs_2_, ...), custom_call_target="tpu_custom_call" | custom-call | flops 335544320 | bytes 3932160 | tf_op jit(solution)/shard_map/pallas_call | solution.py:81
  44.1 0.0 copy-start
  44.2 0.0 copy-start.1
  44.2 10.7 %collective-permute-done.13 = bf16[256,1280]{1,0:T(8,128)(2,1)S(1)} collective-permute-done((bf16[256,1280]{1,0:T(8,128)(2,1)S(1)}, bf16[256,1280]{1,0:T(8,128)(2,1)S(1)}, u32[]{:S(2)}, u32[]{:S(2)}) %collective-permute-start.13) | collective-permute-done | bytes 655392 | tf_op jit(solution)/shard_map/ppermute | solution.py:275
  54.9 0.8 fusion.2
  55.7 0.5 collective-permute-start.8
  56.2 0.9 %collective-permute-done.8.refs_7_ = bf16[4,32,128]{2,1,0:T(8,128)(2,1)S(1)} collective-permute-done((bf16[4,32,128]{2,1,0:T(8,128)(2,1)S(1)}, bf16[4,32,128]{2,1,0:T(8,128)(2,1)S(1)}, u32[]{:S(2)}, u32[]{:S(2)}) %collective-permute-start.8) | collective-permute-done | bytes 32800 | tf_op jit(solution)/shard_map/ppermute | solution.py:293
  57.0 1.2 %shard_map.103.refs_0_ = bf16[256,128]{1,0:T(8,128)(2,1)S(1)} custom-call(bf16[128,512]{1,0:T(8,128)(2,1)S(1)} %bitcast.57, bf16[128,512]{1,0:T(8,128)(2,1)S(1)} %bitcast.58, bf16[128,512]{1,0:T(8,128)(2,1)S(1)} %collective-permute-done.1.refs_2_.refs_3_, bf16[128,512]{1,0:T(8,128)(2,1)S(1)} %collective-permute-done.1.refs_2_.refs_3_, ...), custom_call_target="tpu_custom_call" | custom-call | flops 402653184 | bytes 786432 | tf_op jit(solution)/shard_map/pallas_call | solution.py:161
  58.3 3.1 %collective-permute-start.10 = (bf16[256,128]{1,0:T(8,128)(2,1)S(1)}, bf16[256,128]{1,0:T(8,128)(2,1)S(1)}, u32[]{:S(2)}, u32[]{:S(2)}) collective-permute-start(bf16[256,128]{1,0:T(8,128)(2,1)S(1)} %shard_map.103.refs_0_), channel_id=1, source_target_pairs={{0,2},{1,3},{2,0},{3,1},{4,6},{5,7},{6,4},{7,5},{8,10},{9,11},{10,... | collective-permute-start | bytes 196616 | tf_op jit(solution)/shard_map/ppermute | solution.py:300
  61.4 1.2 %collective-permute-start.11 = (bf16[256,128]{1,0:T(8,128)(2,1)S(1)}, bf16[256,128]{1,0:T(8,128)(2,1)S(1)}, u32[]{:S(2)}, u32[]{:S(2)}) collective-permute-start(bf16[256,128]{1,0:T(8,128)(2,1)S(1)} %shard_map.103.refs_0_), channel_id=1, source_target_pairs={{0,3},{1,2},{2,1},{3,0},{4,7},{5,6},{6,5},{7,4},{8,11},{9,10},{10,... | collective-permute-start | bytes 196616 | tf_op jit(solution)/shard_map/ppermute | solution.py:300
  62.6 0.2 copy.13
  62.8 1.3 %copy.14 = bf16[256,1280]{1,0:T(8,128)(2,1)S(1)} copy(bf16[256,1280]{0,1:T(8,128)(2,1)} %bitcast.64) | data formatting | bytes 1310720 | tf_op jit(solution)/shard_map/transpose | solution.py:304
  64.2 1.0 %collective-permute-done.10.refs_2_ = bf16[256,128]{1,0:T(8,128)(2,1)S(1)} collective-permute-done((bf16[256,128]{1,0:T(8,128)(2,1)S(1)}, bf16[256,128]{1,0:T(8,128)(2,1)S(1)}, u32[]{:S(2)}, u32[]{:S(2)}) %collective-permute-start.10) | collective-permute-done | bytes 65568 | tf_op jit(solution)/shard_map/ppermute | solution.py:300
  65.2 4.5 %collective-permute-done.11.refs_3_ = bf16[256,128]{1,0:T(8,128)(2,1)S(1)} collective-permute-done((bf16[256,128]{1,0:T(8,128)(2,1)S(1)}, bf16[256,128]{1,0:T(8,128)(2,1)S(1)}, u32[]{:S(2)}, u32[]{:S(2)}) %collective-permute-start.11) | collective-permute-done | bytes 65568 | tf_op jit(solution)/shard_map/ppermute | solution.py:300
  69.7 0.3 collective-permute-done.9.refs_1_
  70.0 0.7 shard_map.105
  70.7 0.1 collective-permute-start.15
  70.8 0.7 shard_map.104
  71.4 0.1 select_bitcast_fusion.1
  71.5 0.1 pad_maximum_fusion.2
  71.6 0.8 collective-permute-done.15.got_ref
  72.4 0.1 shard_map.106
  72.4 0.6 collective-permute-start.16
  73.0 1.5 %collective-permute-start.17 = (bf16[32,1280]{1,0:T(8,128)(2,1)S(1)}, bf16[32,1280]{1,0:T(8,128)(2,1)S(1)}, u32[]{:S(2)}, u32[]{:S(2)}) collective-permute-start(bf16[32,1280]{1,0:T(8,128)(2,1)S(1)} %get-tuple-element.40), channel_id=1, source_target_pairs={{0,16},{4,20},{8,24},{12,28},{16,0},{20,4},{24,8},{28,12},{1,17},{... | collective-permute-start | bytes 245768 | tf_op jit(solution)/shard_map/ppermute | solution.py:321
  74.6 1.4 %collective-permute-start.18 = (bf16[32,1280]{1,0:T(8,128)(2,1)S(1)}, bf16[32,1280]{1,0:T(8,128)(2,1)S(1)}, u32[]{:S(2)}, u32[]{:S(2)}) collective-permute-start(bf16[32,1280]{1,0:T(8,128)(2,1)S(1)} %get-tuple-element.41), channel_id=1, source_target_pairs={{0,24},{4,28},{8,16},{12,20},{16,8},{20,12},{24,0},{28,4},{1,25},{... | collective-permute-start | bytes 245768 | tf_op jit(solution)/shard_map/ppermute | solution.py:321
  76.0 0.1 pad_maximum_fusion.1
  76.1 1.1 %copy.18 = bf16[1,1280,256]{2,1,0:T(8,128)(2,1)} copy(bf16[1,1280,256]{1,2,0:T(8,128)(2,1)S(1)} %bitcast.60) | data formatting | bytes 1310720
  77.2 1.1 %copy.17 = bf16[1,1280,256]{2,1,0:T(8,128)(2,1)} copy(bf16[1,1280,256]{1,2,0:T(8,128)(2,1)S(1)} %bitcast.61) | data formatting | bytes 1310720
  78.3 1.6 %collective-permute-done.18 = bf16[32,1280]{1,0:T(8,128)(2,1)S(1)} collective-permute-done((bf16[32,1280]{1,0:T(8,128)(2,1)S(1)}, bf16[32,1280]{1,0:T(8,128)(2,1)S(1)}, u32[]{:S(2)}, u32[]{:S(2)}) %collective-permute-start.18) | collective-permute-done | bytes 81952 | tf_op jit(solution)/shard_map/ppermute | solution.py:321
  79.9 0.8 fusion.1
  (23 shorter events, 0.2 us)
Async XLA Ops:
  0.6 15.6 %collective-permute-start.2 = (bf16[128,5120]{1,0:T(8,128)(2,1)}, bf16[128,5120]{1,0:T(8,128)(2,1)S(1)}, u32[]{:S(2)}, u32[]{:S(2)}) collective-permute-start(bf16[128,5120]{1,0:T(8,128)(2,1)} %bitcast.62), channel_id=1, source_target_pairs={{0,4},{4,0},{8,12},{12,8},{16,20},{20,16},{24,28},{28,24},{1,5},{5... | collective-permute-start | bytes 3932168 | tf_op jit(solution)/shard_map/ppermute | solution.py:262
  2.1 8.6 %collective-permute-start = (bf16[32,1280]{1,0:T(8,128)(2,1)S(1)}, bf16[32,1280]{1,0:T(8,128)(2,1)S(1)}, u32[]{:S(2)}, u32[]{:S(2)}) collective-permute-start(bf16[32,1280]{1,0:T(8,128)(2,1)S(1)} %convert_bitcast_fusion), channel_id=1, source_target_pairs={{0,2},{1,3},{2,0},{3,1},{4,6},{5,7},{6,4},{7,5},{8,10},{9,11},{10,... | collective-permute-start | bytes 245768 | tf_op jit(solution)/shard_map/ppermute | solution.py:264
  6.7 9.6 %collective-permute-start.1 = (bf16[128,512]{1,0:T(8,128)(2,1)S(1)}, bf16[128,512]{1,0:T(8,128)(2,1)S(1)}, u32[]{:S(2)}, u32[]{:S(2)}) collective-permute-start(bf16[128,512]{1,0:T(8,128)(2,1)S(1)} %bitcast.55), channel_id=1, source_target_pairs={{0,2},{1,3},{2,0},{3,1},{4,6},{5,7},{6,4},{7,5},{8,10},{9,11},{10,... | collective-permute-start | bytes 393224 | tf_op jit(solution)/shard_map/ppermute | solution.py:266
  16.4 5.7 %collective-permute-start.4 = (bf16[64,1280]{1,0:T(8,128)(2,1)S(1)}, bf16[64,1280]{1,0:T(8,128)(2,1)S(1)}, u32[]{:S(2)}, u32[]{:S(2)}) collective-permute-start(bf16[64,1280]{1,0:T(8,128)(2,1)S(1)} %pad_maximum_fusion.4), channel_id=1, source_target_pairs={{0,1},{1,0},{2,3},{3,2},{4,5},{5,4},{6,7},{7,6},{8,9},{9,8},{10,11... | collective-permute-start | bytes 491528 | tf_op jit(solution)/shard_map/ppermute | solution.py:279
  22.1 8.3 %collective-permute-start.5 = (bf16[128,1280]{1,0:T(8,128)(2,1)S(1)}, bf16[128,1280]{1,0:T(8,128)(2,1)S(1)}, u32[]{:S(2)}, u32[]{:S(2)}) collective-permute-start(bf16[128,1280]{1,0:T(8,128)(2,1)S(1)} %constant_dynamic-update-slice_fusion.refs_0_), channel_id=1, source_target_pairs={{0,8},{4,12},{8,0},{12,4},{16,24},{20,28},{24,16},{28,20},{1,9},{5... | collective-permute-start | bytes 983048 | tf_op jit(solution)/shard_map/ppermute | solution.py:287
  23.8 31.1 %collective-permute-start.13 = (bf16[256,1280]{1,0:T(8,128)(2,1)S(1)}, bf16[256,1280]{1,0:T(8,128)(2,1)S(1)}, u32[]{:S(2)}, u32[]{:S(2)}) collective-permute-start(bf16[256,1280]{1,0:T(8,128)(2,1)S(1)} %pad_maximum_fusion), channel_id=1, source_target_pairs={{0,2},{1,3},{2,0},{3,1},{4,7},{5,6},{6,5},{7,4},{8,10},{9,11},{10,... | collective-permute-start | bytes 1966088 | tf_op jit(solution)/shard_map/ppermute | solution.py:275
  26.7 16.5 %collective-permute-start.6 = (bf16[128,1280]{1,0:T(8,128)(2,1)S(1)}, bf16[128,1280]{1,0:T(8,128)(2,1)S(1)}, u32[]{:S(2)}, u32[]{:S(2)}) collective-permute-start(bf16[128,1280]{1,0:T(8,128)(2,1)S(1)} %constant_dynamic-update-slice_fusion.refs_0_), channel_id=1, source_target_pairs={{0,16},{4,20},{8,24},{12,28},{16,0},{20,4},{24,8},{28,12},{1,17},{... | collective-permute-start | bytes 983048 | tf_op jit(solution)/shard_map/ppermute | solution.py:287
  30.4 12.8 %collective-permute-start.7 = (bf16[128,1280]{1,0:T(8,128)(2,1)S(1)}, bf16[128,1280]{1,0:T(8,128)(2,1)S(1)}, u32[]{:S(2)}, u32[]{:S(2)}) collective-permute-start(bf16[128,1280]{1,0:T(8,128)(2,1)S(1)} %constant_dynamic-update-slice_fusion.refs_0_), channel_id=1, source_target_pairs={{0,24},{4,28},{8,16},{12,20},{16,8},{20,12},{24,0},{28,4},{1,25},{... | collective-permute-start | bytes 983048 | tf_op jit(solution)/shard_map/ppermute | solution.py:287
  33.0 23.1 %collective-permute-start.3 = (bf16[256,512]{1,0:T(8,128)(2,1)S(1)}, bf16[256,512]{1,0:T(8,128)(2,1)S(1)}, u32[]{:S(2)}, u32[]{:S(2)}) collective-permute-start(bf16[256,512]{1,0:T(8,128)(2,1)S(1)} %pad_maximum_fusion.3), channel_id=1, source_target_pairs={{0,1},{1,0},{2,3},{3,2},{4,5},{5,4},{6,7},{7,6},{8,9},{9,8},{10,11... | collective-permute-start | bytes 786440 | tf_op jit(solution)/shard_map/ppermute | solution.py:280
  44.1 12.9 %copy-start = (bf16[1,128,256]{2,1,0:T(8,128)(2,1)S(1)}, bf16[1,128,256]{2,1,0:T(8,128)(2,1)}, u32[]{:S(2)}) copy-start(bf16[1,128,256]{2,1,0:T(8,128)(2,1)} %param.9) | copy-start | bytes 196612
  44.2 18.4 %copy-start.1 = (bf16[1,1280,256]{2,1,0:T(8,128)(2,1)S(1)}, bf16[1,1280,256]{2,1,0:T(8,128)(2,1)}, u32[]{:S(2)}) copy-start(bf16[1,1280,256]{2,1,0:T(8,128)(2,1)} %param.10) | copy-start | bytes 1966084
  55.7 14.3 %collective-permute-start.14 = (bf16[128,1280]{1,0:T(8,128)(2,1)}, bf16[128,1280]{1,0:T(8,128)(2,1)S(1)}, u32[]{:S(2)}, u32[]{:S(2)}) collective-permute-start(bf16[128,1280]{1,0:T(8,128)(2,1)} %get-tuple-element.66), channel_id=1, source_target_pairs={{0,4},{4,0},{8,12},{12,8},{16,20},{20,16},{24,28},{28,24},{1,5},{5... | collective-permute-start | bytes 983048 | tf_op jit(solution)/shard_map/ppermute | solution.py:297
  55.7 14.3 %collective-permute-start.12 = (bf16[128,1280]{1,0:T(8,128)(2,1)S(1)}, bf16[128,1280]{1,0:T(8,128)(2,1)S(1)}, u32[]{:S(2)}, u32[]{:S(2)}) collective-permute-start(bf16[128,1280]{1,0:T(8,128)(2,1)S(1)} %get-tuple-element.34.refs_5_), channel_id=1, source_target_pairs={{0,1},{1,0},{2,3},{3,2},{4,5},{5,4},{6,7},{7,6},{8,9},{9,8},{10,11... | collective-permute-start | bytes 983048 | tf_op jit(solution)/shard_map/ppermute | solution.py:294
  55.7 1.4 %collective-permute-start.8 = (bf16[4,32,128]{2,1,0:T(8,128)(2,1)S(1)}, bf16[4,32,128]{2,1,0:T(8,128)(2,1)S(1)}, u32[]{:S(2)}, u32[]{:S(2)}) collective-permute-start(bf16[4,32,128]{2,1,0:T(8,128)(2,1)S(1)} %get-tuple-element.33), channel_id=1, source_target_pairs={{0,4},{4,0},{8,12},{12,8},{16,20},{20,16},{24,28},{28,24},{1,5},{5... | collective-permute-start | bytes 98312 | tf_op jit(solution)/shard_map/ppermute | solution.py:293
  58.3 6.9 %collective-permute-start.10 = (bf16[256,128]{1,0:T(8,128)(2,1)S(1)}, bf16[256,128]{1,0:T(8,128)(2,1)S(1)}, u32[]{:S(2)}, u32[]{:S(2)}) collective-permute-start(bf16[256,128]{1,0:T(8,128)(2,1)S(1)} %shard_map.103.refs_0_), channel_id=1, source_target_pairs={{0,2},{1,3},{2,0},{3,1},{4,6},{5,7},{6,4},{7,5},{8,10},{9,11},{10,... | collective-permute-start | bytes 196616 | tf_op jit(solution)/shard_map/ppermute | solution.py:300
  61.4 8.3 %collective-permute-start.11 = (bf16[256,128]{1,0:T(8,128)(2,1)S(1)}, bf16[256,128]{1,0:T(8,128)(2,1)S(1)}, u32[]{:S(2)}, u32[]{:S(2)}) collective-permute-start(bf16[256,128]{1,0:T(8,128)(2,1)S(1)} %shard_map.103.refs_0_), channel_id=1, source_target_pairs={{0,3},{1,2},{2,1},{3,0},{4,7},{5,6},{6,5},{7,4},{8,11},{9,10},{10,... | collective-permute-start | bytes 196616 | tf_op jit(solution)/shard_map/ppermute | solution.py:300
  62.6 7.4 %collective-permute-start.9 = (bf16[256,128]{1,0:T(8,128)(2,1)S(1)}, bf16[256,128]{1,0:T(8,128)(2,1)S(1)}, u32[]{:S(2)}, u32[]{:S(2)}) collective-permute-start(bf16[256,128]{1,0:T(8,128)(2,1)S(1)} %shard_map.103.refs_0_), channel_id=1, source_target_pairs={{0,1},{1,0},{2,3},{3,2},{4,5},{5,4},{6,7},{7,6},{8,9},{9,8},{10,11... | collective-permute-start | bytes 196616 | tf_op jit(solution)/shard_map/ppermute | solution.py:300
  70.7 1.7 %collective-permute-start.15 = (bf16[4,32,1280]{2,1,0:T(8,128)(2,1)S(1)}, bf16[4,32,1280]{2,1,0:T(8,128)(2,1)S(1)}, u32[]{:S(2)}, u32[]{:S(2)}) collective-permute-start(bf16[4,32,1280]{2,1,0:T(8,128)(2,1)S(1)} %get-tuple-element.37), channel_id=1, source_target_pairs={{0,4},{4,0},{8,12},{12,8},{16,20},{20,16},{24,28},{28,24},{1,5},{5... | collective-permute-start | bytes 983048 | tf_op jit(solution)/shard_map/ppermute | solution.py:308
  72.4 5.9 %collective-permute-start.16 = (bf16[32,1280]{1,0:T(8,128)(2,1)S(1)}, bf16[32,1280]{1,0:T(8,128)(2,1)S(1)}, u32[]{:S(2)}, u32[]{:S(2)}) collective-permute-start(bf16[32,1280]{1,0:T(8,128)(2,1)S(1)} %get-tuple-element.39), channel_id=1, source_target_pairs={{0,8},{4,12},{8,0},{12,4},{16,24},{20,28},{24,16},{28,20},{1,9},{5... | collective-permute-start | bytes 245768 | tf_op jit(solution)/shard_map/ppermute | solution.py:321
  73.0 5.3 %collective-permute-start.17 = (bf16[32,1280]{1,0:T(8,128)(2,1)S(1)}, bf16[32,1280]{1,0:T(8,128)(2,1)S(1)}, u32[]{:S(2)}, u32[]{:S(2)}) collective-permute-start(bf16[32,1280]{1,0:T(8,128)(2,1)S(1)} %get-tuple-element.40), channel_id=1, source_target_pairs={{0,16},{4,20},{8,24},{12,28},{16,0},{20,4},{24,8},{28,12},{1,17},{... | collective-permute-start | bytes 245768 | tf_op jit(solution)/shard_map/ppermute | solution.py:321
  74.6 5.3 %collective-permute-start.18 = (bf16[32,1280]{1,0:T(8,128)(2,1)S(1)}, bf16[32,1280]{1,0:T(8,128)(2,1)S(1)}, u32[]{:S(2)}, u32[]{:S(2)}) collective-permute-start(bf16[32,1280]{1,0:T(8,128)(2,1)S(1)} %get-tuple-element.41), channel_id=1, source_target_pairs={{0,24},{4,28},{8,16},{12,20},{16,8},{20,12},{24,0},{28,4},{1,25},{... | collective-permute-start | bytes 245768 | tf_op jit(solution)/shard_map/ppermute | solution.py:321
  77.2 2.7 %copy-start.2 = (f32[1280,32]{0,1:T(8,128)S(1)}, f32[1280,32]{0,1:T(8,128)}, u32[]{:S(2)}) copy-start(f32[1280,32]{0,1:T(8,128)} %param.12) | copy-start | bytes 491524
  77.2 2.7 %copy-start.3 = (f32[1280,32]{0,1:T(8,128)S(1)}, f32[1280,32]{0,1:T(8,128)}, u32[]{:S(2)}) copy-start(f32[1280,32]{0,1:T(8,128)} %param.13) | copy-start | bytes 491524

commit v7 on v6

--- a/solution.py
+++ b/solution.py
@@ -264,7 +264,7 @@
     held = jnp.concatenate([weight, lax.ppermute(weight, "seq", far_perm)], 0)
     kv = [key_vals[0].reshape(rows, 2 * cols)]
     kv.append(lax.ppermute(kv[0], "seq", far_perm))
-    held, kv, partner_tokens = lax.optimization_barrier((held, kv, partner_tokens))
+    held, partner_tokens = lax.optimization_barrier((held, partner_tokens))
 
     def feature_block(matrix, k):
         return lax.dynamic_slice(matrix, (0, jnp.bitwise_xor(seq, k) * block), (rows, block))
@@ -282,8 +282,6 @@
     rounds = [order]
     spread = [held] + [None] * (n_chip - 1)
     for step in range(1, n_chip):
-        if step & (step - 1):
-            held, spread[1] = lax.optimization_barrier((held, spread[1]))
         spread[step] = lax.ppermute(held, "island", pair_perm(n_chip, step, 2))
 
     mine, for_partner = half_queries(
@@ -292,10 +290,10 @@
     near, for_partner = lax.optimization_barrier((own_blocks[1], for_partner))
     other = lax.ppermute(for_partner, "island", swap)
     gathered = [own_blocks[0], lax.ppermute(near, "seq", pair_perm(n_seq, 1))]
-    _, far = lax.optimization_barrier((for_partner, far))
+    dquery = attention(kv, order, mine, other, cotangent[0])
+    _, far = lax.optimization_barrier((dquery, far))
     for got in far:
         gathered += [got[:rows], lax.ppermute(got[rows:], "island", swap)]
-    dquery = attention(kv, order, mine, other, cotangent[0])
     dqueries = [dquery] + [
         lax.ppermute(dquery, "seq", pair_perm(n_seq, k)) for k in range(1, n_seq)
     ]

time: 80.9 us -> 68.9 us (0.85)
  waiting for transfers between devices: 43.2 us -> 31.9 us
    ppermute x1, waiting for transfers between devices: 10.7 us -> 5.15 us  [on_device(): lax.ppermute(both, ('island', 'seq'), far_pairs(n_island, n_seq, k))]
    ppermute x1, waiting for transfers between devices: 5.51 us -> 0.01 us  [on_device(): kv.append(lax.ppermute(kv[0], 'seq', far_perm))]
    ppermute x1, waiting for transfers between devices: 4.89 us -> 2.07 us  [on_device(): lax.ppermute(held, 'seq', pair_perm(n_seq, bit))]
    ppermute x1, starting transfers between devices: 0.81 us -> 3.54 us  [on_device(): lax.ppermute(held, 'seq', pair_perm(n_seq, bit))]
    ppermute x3, waiting for transfers between devices: 10.6 us -> 13.3 us  [on_device(): spread[step] = lax.ppermute(held, 'island', pair_perm(n_chip, step, 2))]
    ppermute x3, starting transfers between devices: 5.78 us -> 3.55 us  [on_device(): spread[step] = lax.ppermute(held, 'island', pair_perm(n_chip, step, 2))]
    ppermute x3, waiting for transfers between devices: 5.84 us -> 4.36 us  [on_device(): lax.ppermute(dquery, 'seq', pair_perm(n_seq, k))]
    ppermute x3, waiting for transfers between devices: 1.58 us -> 2.66 us  [on_device(): lax.ppermute(parts[step], 'island', pair_perm(n_chip, step, 2))]
  transfers between devices with their start and end apart: 19 -> 19, of which waited for: 12 -> 11; matrix products, arithmetic and copies ran while one was open for 10% -> 12% of each run, Pallas kernels for 4% -> 4%
where the time goes in v7:
time: 68.9 us; the launch traced here: 68.7 us
  waiting for transfers between devices  31.9 us (46%)
  starting transfers between devices  23.2 us (34%)
  local copies, waits for them, and re-layouts  7.19 us (10%)
  Pallas kernels  3.59 us (5%)
  other arithmetic  2.01 us (3%)
  between operations  0.83 us (1%)
    ppermute x3, waiting for transfers between devices, on_device(): spread[step] = lax.ppermute(held, 'island', pair_perm(n_chip, step, 2))  13.3 us
    ppermute x1, waiting for transfers between devices, on_device(): lax.ppermute(both, ('island', 'seq'), far_pairs(n_island, n_seq, k))  5.15 us
    ppermute x3, waiting for transfers between devices, on_device(): lax.ppermute(dquery, 'seq', pair_perm(n_seq, k))  4.36 us
    ppermute x1, starting transfers between devices, on_device(): held = jnp.concatenate([weight, lax.ppermute(weight, 'seq', far_perm)], 0)  3.67 us
    ppermute x3, starting transfers between devices, on_device(): spread[step] = lax.ppermute(held, 'island', pair_perm(n_chip, step, 2))  3.55 us
    ppermute x3, starting transfers between devices, on_device(): lax.ppermute(parts[step], 'island', pair_perm(n_chip, step, 2))  3.55 us
    ppermute x1, starting transfers between devices, on_device(): lax.ppermute(held, 'seq', pair_perm(n_seq, bit))  3.54 us
    ppermute x3, starting transfers between devices, on_device(): lax.ppermute(dquery, 'seq', pair_perm(n_seq, k))  3.49 us
  transfers between devices with their start and end apart: 19, of which 11 were waited for; matrix products, arithmetic and copies ran while one was open for 12% of the time, Pallas kernels for 4%

profile of v7, /device:TPU:0, one launch (start us, length us, event | category | flops | bytes accessed | tf_op | source)
XLA Modules:
  0.0 68.7 jit_solution(12936273236245901654)
XLA Ops:
  0.6 0.5 collective-permute-start.3
  1.1 0.9 %convert_bitcast_fusion = bf16[32,1280]{1,0:T(8,128)(2,1)S(1)} fusion(f32[1280,32]{0,1:T(8,128)} %param.12), kind=kLoop, calls=%fused_computation.19 | loop fusion | flops 40960 | bytes 245760 | tf_op jit(solution)/shard_map/convert_element_type | solution.py:263
  2.1 3.7 %collective-permute-start.2 = (bf16[32,1280]{1,0:T(8,128)(2,1)S(1)}, bf16[32,1280]{1,0:T(8,128)(2,1)S(1)}, u32[]{:S(2)}, u32[]{:S(2)}) collective-permute-start(bf16[32,1280]{1,0:T(8,128)(2,1)S(1)} %convert_bitcast_fusion), channel_id=1, source_target_pairs={{0,2},{1,3},{2,0},{3,1},{4,6},{5,7},{6,4},{7,5},{8,10},{9,11},{10,... | collective-permute-start | bytes 245768 | tf_op jit(solution)/shard_map/ppermute | solution.py:264
  5.7 0.9 %copy.19 = bf16[16,8,2,256]{3,1,2,0:T(8,128)(2,1)S(1)} copy(bf16[16,8,2,256]{3,2,1,0:T(2,128)(2,1)} %bitcast.65) | data formatting | bytes 262144
  6.7 0.1 collective-permute-start
  6.8 1.5 %dynamic-slice_bitcast_fusion = (bf16[128,1280]{1,0:T(8,128)(2,1)S(1)}, bf16[128,1280]{1,0:T(8,128)(2,1)S(1)}, bf16[128,1280]{1,0:T(8,128)(2,1)S(1)}, bf16[128,1280]{1,0:T(8,128)(2,1)S(1)}, bf16[128,1280]{1,0:T(8,128)(2,1)S(1)}) fusion(bf16[1,128,5120]{2,1,0:T(8,128)(2,1)} %param.7, s32[]{:T(128)S(6)} %select_n.44, s32[]{:T(128)S(6)} %select_n.42, ...), kind=kLoop, calls=%fused_computation.7 | loop fusion | bytes 3276820 | tf_op jit(solution)/shard_map/dynamic_slice | solution.py:270
  8.3 2.4 %collective-permute-done.2 = bf16[32,1280]{1,0:T(8,128)(2,1)S(1)} collective-permute-done((bf16[32,1280]{1,0:T(8,128)(2,1)S(1)}, bf16[32,1280]{1,0:T(8,128)(2,1)S(1)}, u32[]{:S(2)}, u32[]{:S(2)}) %collective-permute-start.2) | collective-permute-done | bytes 81952 | tf_op jit(solution)/shard_map/ppermute | solution.py:264
  10.7 0.2 constant_dynamic-slice_fusion
  10.9 3.5 %collective-permute-start.4 = (bf16[64,1280]{1,0:T(8,128)(2,1)S(1)}, bf16[64,1280]{1,0:T(8,128)(2,1)S(1)}, u32[]{:S(2)}, u32[]{:S(2)}) collective-permute-start(bf16[64,1280]{1,0:T(8,128)(2,1)S(1)} %pad_maximum_fusion.4), channel_id=1, source_target_pairs={{0,1},{1,0},{2,3},{3,2},{4,5},{5,4},{6,7},{7,6},{8,9},{9,8},{10,11... | collective-permute-start | bytes 491528 | tf_op jit(solution)/shard_map/ppermute | solution.py:279
  14.5 3.4 %collective-permute-start.13 = (bf16[256,1280]{1,0:T(8,128)(2,1)S(1)}, bf16[256,1280]{1,0:T(8,128)(2,1)S(1)}, u32[]{:S(2)}, u32[]{:S(2)}) collective-permute-start(bf16[256,1280]{1,0:T(8,128)(2,1)S(1)} %pad_maximum_fusion), channel_id=1, source_target_pairs={{0,2},{1,3},{2,0},{3,1},{4,7},{5,6},{6,5},{7,4},{8,10},{9,11},{10,... | collective-permute-start | bytes 1966088 | tf_op jit(solution)/shard_map/ppermute | solution.py:275
  17.9 2.1 %collective-permute-done.4 = bf16[64,1280]{1,0:T(8,128)(2,1)S(1)} collective-permute-done((bf16[64,1280]{1,0:T(8,128)(2,1)S(1)}, bf16[64,1280]{1,0:T(8,128)(2,1)S(1)}, u32[]{:S(2)}, u32[]{:S(2)}) %collective-permute-start.4) | collective-permute-done | bytes 163872 | tf_op jit(solution)/shard_map/ppermute | solution.py:279
  20.0 1.7 %collective-permute-start.5 = (bf16[128,1280]{1,0:T(8,128)(2,1)S(1)}, bf16[128,1280]{1,0:T(8,128)(2,1)S(1)}, u32[]{:S(2)}, u32[]{:S(2)}) collective-permute-start(bf16[128,1280]{1,0:T(8,128)(2,1)S(1)} %constant_dynamic-update-slice_fusion.refs_0_), channel_id=1, source_target_pairs={{0,8},{4,12},{8,0},{12,4},{16,24},{20,28},{24,16},{28,20},{1,9},{5... | collective-permute-start | bytes 983048 | tf_op jit(solution)/shard_map/ppermute | solution.py:285
  21.7 1.5 %collective-permute-start.6 = (bf16[128,1280]{1,0:T(8,128)(2,1)S(1)}, bf16[128,1280]{1,0:T(8,128)(2,1)S(1)}, u32[]{:S(2)}, u32[]{:S(2)}) collective-permute-start(bf16[128,1280]{1,0:T(8,128)(2,1)S(1)} %constant_dynamic-update-slice_fusion.refs_0_), channel_id=1, source_target_pairs={{0,16},{4,20},{8,24},{12,28},{16,0},{20,4},{24,8},{28,12},{1,17},{... | collective-permute-start | bytes 983048 | tf_op jit(solution)/shard_map/ppermute | solution.py:285
  23.2 0.4 collective-permute-start.7
  23.6 0.0 collective-permute-done.refs_2_.refs_3_
  23.6 1.1 %collective-permute-start.1 = (bf16[256,512]{1,0:T(8,128)(2,1)S(1)}, bf16[256,512]{1,0:T(8,128)(2,1)S(1)}, u32[]{:S(2)}, u32[]{:S(2)}) collective-permute-start(bf16[256,512]{1,0:T(8,128)(2,1)S(1)} %pad_maximum_fusion.3), channel_id=1, source_target_pairs={{0,1},{1,0},{2,3},{3,2},{4,5},{5,4},{6,7},{7,6},{8,9},{9,8},{10,11... | collective-permute-start | bytes 786440 | tf_op jit(solution)/shard_map/ppermute | solution.py:280
  24.7 5.9 %collective-permute-done.5.refs_1_ = bf16[128,1280]{1,0:T(8,128)(2,1)S(1)} collective-permute-done((bf16[128,1280]{1,0:T(8,128)(2,1)S(1)}, bf16[128,1280]{1,0:T(8,128)(2,1)S(1)}, u32[]{:S(2)}, u32[]{:S(2)}) %collective-permute-start.5) | collective-permute-done | bytes 327712 | tf_op jit(solution)/shard_map/ppermute | solution.py:285
  30.7 7.4 %collective-permute-done.6.refs_2_ = bf16[128,1280]{1,0:T(8,128)(2,1)S(1)} collective-permute-done((bf16[128,1280]{1,0:T(8,128)(2,1)S(1)}, bf16[128,1280]{1,0:T(8,128)(2,1)S(1)}, u32[]{:S(2)}, u32[]{:S(2)}) %collective-permute-start.6) | collective-permute-done | bytes 327712 | tf_op jit(solution)/shard_map/ppermute | solution.py:285
  38.0 1.0 %shard_map.102 = (bf16[4,32,128]{2,1,0:T(8,128)(2,1)S(1)}, bf16[4,32,128]{2,1,0:T(8,128)(2,1)S(1)}) custom-call(bf16[128,1280]{1,0:T(8,128)(2,1)S(1)} %constant_dynamic-update-slice_fusion.refs_0_, bf16[128,1280]{1,0:T(8,128)(2,1)S(1)} %collective-permute-done.5.refs_1_, bf16[128,1280]{1,0:T(8,128)(2,1)S(1)} %collective-permute-done.6.refs_2_, ...), custom_call_target="tpu_custom_call" | custom-call | flops 335544320 | bytes 3932160 | tf_op jit(solution)/shard_map/pallas_call | solution.py:81
  39.0 0.1 collective-permute-start.8
  39.1 0.1 collective-permute-start.12
  39.2 1.1 %collective-permute-done.8.refs_7_ = bf16[4,32,128]{2,1,0:T(8,128)(2,1)S(1)} collective-permute-done((bf16[4,32,128]{2,1,0:T(8,128)(2,1)S(1)}, bf16[4,32,128]{2,1,0:T(8,128)(2,1)S(1)}, u32[]{:S(2)}, u32[]{:S(2)}) %collective-permute-start.8) | collective-permute-done | bytes 32800 | tf_op jit(solution)/shard_map/ppermute | solution.py:291
  40.3 1.2 %shard_map.103.refs_0_ = bf16[256,128]{1,0:T(8,128)(2,1)S(1)} custom-call(bf16[128,512]{1,0:T(8,128)(2,1)S(1)} %bitcast.57, bf16[128,512]{1,0:T(8,128)(2,1)S(1)} %bitcast.58, bf16[128,512]{1,0:T(8,128)(2,1)S(1)} %collective-permute-done.refs_2_.refs_3_, bf16[128,512]{1,0:T(8,128)(2,1)S(1)} %collective-permute-done.refs_2_.refs_3_, ...), custom_call_target="tpu_custom_call" | custom-call | flops 402653184 | bytes 786432 | tf_op jit(solution)/shard_map/pallas_call | solution.py:161
  41.5 5.2 %collective-permute-done.13 = bf16[256,1280]{1,0:T(8,128)(2,1)S(1)} collective-permute-done((bf16[256,1280]{1,0:T(8,128)(2,1)S(1)}, bf16[256,1280]{1,0:T(8,128)(2,1)S(1)}, u32[]{:S(2)}, u32[]{:S(2)}) %collective-permute-start.13) | collective-permute-done | bytes 655392 | tf_op jit(solution)/shard_map/ppermute | solution.py:275
  46.7 0.8 %fusion.2 = (bf16[128,1280]{1,0:T(8,128)(2,1)}, bf16[128,1280]{1,0:T(8,128)(2,1)S(1)}) fusion(bf16[256,1280]{1,0:T(8,128)(2,1)S(1)} %collective-permute-done.13), kind=kLoop, calls=%fused_computation.27 | loop fusion | bytes 1310720 | tf_op jit(solution)/shard_map/slice | solution.py:296
  47.5 1.2 %collective-permute-start.10 = (bf16[256,128]{1,0:T(8,128)(2,1)S(1)}, bf16[256,128]{1,0:T(8,128)(2,1)S(1)}, u32[]{:S(2)}, u32[]{:S(2)}) collective-permute-start(bf16[256,128]{1,0:T(8,128)(2,1)S(1)} %shard_map.103.refs_0_), channel_id=1, source_target_pairs={{0,2},{1,3},{2,0},{3,1},{4,6},{5,7},{6,4},{7,5},{8,10},{9,11},{10,... | collective-permute-start | bytes 196616 | tf_op jit(solution)/shard_map/ppermute | solution.py:298
  48.6 1.5 %collective-permute-start.11 = (bf16[256,128]{1,0:T(8,128)(2,1)S(1)}, bf16[256,128]{1,0:T(8,128)(2,1)S(1)}, u32[]{:S(2)}, u32[]{:S(2)}) collective-permute-start(bf16[256,128]{1,0:T(8,128)(2,1)S(1)} %shard_map.103.refs_0_), channel_id=1, source_target_pairs={{0,3},{1,2},{2,1},{3,0},{4,7},{5,6},{6,5},{7,4},{8,11},{9,10},{10,... | collective-permute-start | bytes 196616 | tf_op jit(solution)/shard_map/ppermute | solution.py:298
  50.1 0.8 %collective-permute-start.9 = (bf16[256,128]{1,0:T(8,128)(2,1)S(1)}, bf16[256,128]{1,0:T(8,128)(2,1)S(1)}, u32[]{:S(2)}, u32[]{:S(2)}) collective-permute-start(bf16[256,128]{1,0:T(8,128)(2,1)S(1)} %shard_map.103.refs_0_), channel_id=1, source_target_pairs={{0,1},{1,0},{2,3},{3,2},{4,5},{5,4},{6,7},{7,6},{8,9},{9,8},{10,11... | collective-permute-start | bytes 196616 | tf_op jit(solution)/shard_map/ppermute | solution.py:298
  50.9 0.2 copy.13
  51.2 1.3 %copy.14 = bf16[256,1280]{1,0:T(8,128)(2,1)S(1)} copy(bf16[256,1280]{0,1:T(8,128)(2,1)} %bitcast.64) | data formatting | bytes 1310720 | tf_op jit(solution)/shard_map/transpose | solution.py:302
  52.5 3.4 %collective-permute-done.10.refs_2_ = bf16[256,128]{1,0:T(8,128)(2,1)S(1)} collective-permute-done((bf16[256,128]{1,0:T(8,128)(2,1)S(1)}, bf16[256,128]{1,0:T(8,128)(2,1)S(1)}, u32[]{:S(2)}, u32[]{:S(2)}) %collective-permute-start.10) | collective-permute-done | bytes 65568 | tf_op jit(solution)/shard_map/ppermute | solution.py:298
  56.0 0.9 %collective-permute-done.9.refs_1_ = bf16[256,128]{1,0:T(8,128)(2,1)S(1)} collective-permute-done((bf16[256,128]{1,0:T(8,128)(2,1)S(1)}, bf16[256,128]{1,0:T(8,128)(2,1)S(1)}, u32[]{:S(2)}, u32[]{:S(2)}) %collective-permute-start.9) | collective-permute-done | bytes 65568 | tf_op jit(solution)/shard_map/ppermute | solution.py:298
  56.9 0.7 shard_map.105
  57.6 0.1 collective-permute-start.15
  57.6 0.7 shard_map.104
  58.3 0.1 select_bitcast_fusion.1
  58.4 0.1 pad_maximum_fusion.2
  58.5 0.8 %collective-permute-done.15.got_ref = bf16[4,32,1280]{2,1,0:T(8,128)(2,1)S(1)} collective-permute-done((bf16[4,32,1280]{2,1,0:T(8,128)(2,1)S(1)}, bf16[4,32,1280]{2,1,0:T(8,128)(2,1)S(1)}, u32[]{:S(2)}, u32[]{:S(2)}) %collective-permute-start.15) | collective-permute-done | bytes 327712 | tf_op jit(solution)/shard_map/ppermute | solution.py:306
  59.3 0.1 shard_map.106
  59.3 1.7 %collective-permute-start.16 = (bf16[32,1280]{1,0:T(8,128)(2,1)S(1)}, bf16[32,1280]{1,0:T(8,128)(2,1)S(1)}, u32[]{:S(2)}, u32[]{:S(2)}) collective-permute-start(bf16[32,1280]{1,0:T(8,128)(2,1)S(1)} %get-tuple-element.31), channel_id=1, source_target_pairs={{0,8},{4,12},{8,0},{12,4},{16,24},{20,28},{24,16},{28,20},{1,9},{5... | collective-permute-start | bytes 245768 | tf_op jit(solution)/shard_map/ppermute | solution.py:319
  61.0 1.5 %collective-permute-start.17 = (bf16[32,1280]{1,0:T(8,128)(2,1)S(1)}, bf16[32,1280]{1,0:T(8,128)(2,1)S(1)}, u32[]{:S(2)}, u32[]{:S(2)}) collective-permute-start(bf16[32,1280]{1,0:T(8,128)(2,1)S(1)} %get-tuple-element.32), channel_id=1, source_target_pairs={{0,16},{4,20},{8,24},{12,28},{16,0},{20,4},{24,8},{28,12},{1,17},{... | collective-permute-start | bytes 245768 | tf_op jit(solution)/shard_map/ppermute | solution.py:319
  62.5 0.4 collective-permute-start.18
  62.9 0.1 pad_maximum_fusion.1
  63.0 1.1 %copy.18 = bf16[1,1280,256]{2,1,0:T(8,128)(2,1)} copy(bf16[1,1280,256]{1,2,0:T(8,128)(2,1)S(1)} %bitcast.60) | data formatting | bytes 1310720
  64.1 1.1 %copy.17 = bf16[1,1280,256]{2,1,0:T(8,128)(2,1)} copy(bf16[1,1280,256]{1,2,0:T(8,128)(2,1)S(1)} %bitcast.61) | data formatting | bytes 1310720
  65.2 1.1 %collective-permute-done.17 = bf16[32,1280]{1,0:T(8,128)(2,1)S(1)} collective-permute-done((bf16[32,1280]{1,0:T(8,128)(2,1)S(1)}, bf16[32,1280]{1,0:T(8,128)(2,1)S(1)}, u32[]{:S(2)}, u32[]{:S(2)}) %collective-permute-start.17) | collective-permute-done | bytes 81952 | tf_op jit(solution)/shard_map/ppermute | solution.py:319
  66.3 1.6 %collective-permute-done.18 = bf16[32,1280]{1,0:T(8,128)(2,1)S(1)} collective-permute-done((bf16[32,1280]{1,0:T(8,128)(2,1)S(1)}, bf16[32,1280]{1,0:T(8,128)(2,1)S(1)}, u32[]{:S(2)}, u32[]{:S(2)}) %collective-permute-start.18) | collective-permute-done | bytes 81952 | tf_op jit(solution)/shard_map/ppermute | solution.py:319
  67.9 0.8 %fusion.1 = (f32[1280,32]{0,1:T(8,128)}, f32[1280,32]{0,1:T(8,128)}) fusion(f32[1280,32]{0,1:T(8,128)S(1)} %copy-done.2, bf16[32,1280]{1,0:T(8,128)(2,1)S(1)} %collective-permute-done.18, bf16[32,1280]{1,0:T(8,128)(2,1)S(1)} %collective-permute-done.17, f32[32,1280]{1,0:T(8,128)S(1)} %get-tuple-element.30, bf16[32,1280]{1,0:T(8,128)(2,1)S(1)} %collective-permute-done.16, ...), kind=kLoop, calls=%fused_computation.17 | loop fusion | flops 532480 | bytes 1064960 | tf_op jit(solution)/shard_map/sub | solution.py:324
  (23 shorter events, 0.2 us)
Async XLA Ops:
  0.6 10.1 %collective-permute-start.3 = (bf16[128,5120]{1,0:T(8,128)(2,1)}, bf16[128,5120]{1,0:T(8,128)(2,1)S(1)}, u32[]{:S(2)}, u32[]{:S(2)}) collective-permute-start(bf16[128,5120]{1,0:T(8,128)(2,1)} %bitcast.62), channel_id=1, source_target_pairs={{0,4},{4,0},{8,12},{12,8},{16,20},{20,16},{24,28},{28,24},{1,5},{5... | collective-permute-start | bytes 3932168 | tf_op jit(solution)/shard_map/ppermute | solution.py:262
  2.1 8.6 %collective-permute-start.2 = (bf16[32,1280]{1,0:T(8,128)(2,1)S(1)}, bf16[32,1280]{1,0:T(8,128)(2,1)S(1)}, u32[]{:S(2)}, u32[]{:S(2)}) collective-permute-start(bf16[32,1280]{1,0:T(8,128)(2,1)S(1)} %convert_bitcast_fusion), channel_id=1, source_target_pairs={{0,2},{1,3},{2,0},{3,1},{4,6},{5,7},{6,4},{7,5},{8,10},{9,11},{10,... | collective-permute-start | bytes 245768 | tf_op jit(solution)/shard_map/ppermute | solution.py:264
  6.7 16.9 %collective-permute-start = (bf16[128,512]{1,0:T(8,128)(2,1)S(1)}, bf16[128,512]{1,0:T(8,128)(2,1)S(1)}, u32[]{:S(2)}, u32[]{:S(2)}) collective-permute-start(bf16[128,512]{1,0:T(8,128)(2,1)S(1)} %bitcast.55), channel_id=1, source_target_pairs={{0,2},{1,3},{2,0},{3,1},{4,6},{5,7},{6,4},{7,5},{8,10},{9,11},{10,... | collective-permute-start | bytes 393224 | tf_op jit(solution)/shard_map/ppermute | solution.py:266
  10.9 9.1 %collective-permute-start.4 = (bf16[64,1280]{1,0:T(8,128)(2,1)S(1)}, bf16[64,1280]{1,0:T(8,128)(2,1)S(1)}, u32[]{:S(2)}, u32[]{:S(2)}) collective-permute-start(bf16[64,1280]{1,0:T(8,128)(2,1)S(1)} %pad_maximum_fusion.4), channel_id=1, source_target_pairs={{0,1},{1,0},{2,3},{3,2},{4,5},{5,4},{6,7},{7,6},{8,9},{9,8},{10,11... | collective-permute-start | bytes 491528 | tf_op jit(solution)/shard_map/ppermute | solution.py:279
  14.5 32.2 %collective-permute-start.13 = (bf16[256,1280]{1,0:T(8,128)(2,1)S(1)}, bf16[256,1280]{1,0:T(8,128)(2,1)S(1)}, u32[]{:S(2)}, u32[]{:S(2)}) collective-permute-start(bf16[256,1280]{1,0:T(8,128)(2,1)S(1)} %pad_maximum_fusion), channel_id=1, source_target_pairs={{0,2},{1,3},{2,0},{3,1},{4,7},{5,6},{6,5},{7,4},{8,10},{9,11},{10,... | collective-permute-start | bytes 1966088 | tf_op jit(solution)/shard_map/ppermute | solution.py:275
  20.0 10.6 %collective-permute-start.5 = (bf16[128,1280]{1,0:T(8,128)(2,1)S(1)}, bf16[128,1280]{1,0:T(8,128)(2,1)S(1)}, u32[]{:S(2)}, u32[]{:S(2)}) collective-permute-start(bf16[128,1280]{1,0:T(8,128)(2,1)S(1)} %constant_dynamic-update-slice_fusion.refs_0_), channel_id=1, source_target_pairs={{0,8},{4,12},{8,0},{12,4},{16,24},{20,28},{24,16},{28,20},{1,9},{5... | collective-permute-start | bytes 983048 | tf_op jit(solution)/shard_map/ppermute | solution.py:285
  21.7 16.4 %collective-permute-start.6 = (bf16[128,1280]{1,0:T(8,128)(2,1)S(1)}, bf16[128,1280]{1,0:T(8,128)(2,1)S(1)}, u32[]{:S(2)}, u32[]{:S(2)}) collective-permute-start(bf16[128,1280]{1,0:T(8,128)(2,1)S(1)} %constant_dynamic-update-slice_fusion.refs_0_), channel_id=1, source_target_pairs={{0,16},{4,20},{8,24},{12,28},{16,0},{20,4},{24,8},{28,12},{1,17},{... | collective-permute-start | bytes 983048 | tf_op jit(solution)/shard_map/ppermute | solution.py:285
  23.2 14.8 %collective-permute-start.7 = (bf16[128,1280]{1,0:T(8,128)(2,1)S(1)}, bf16[128,1280]{1,0:T(8,128)(2,1)S(1)}, u32[]{:S(2)}, u32[]{:S(2)}) collective-permute-start(bf16[128,1280]{1,0:T(8,128)(2,1)S(1)} %constant_dynamic-update-slice_fusion.refs_0_), channel_id=1, source_target_pairs={{0,24},{4,28},{8,16},{12,20},{16,8},{20,12},{24,0},{28,4},{1,25},{... | collective-permute-start | bytes 983048 | tf_op jit(solution)/shard_map/ppermute | solution.py:285
  23.6 15.6 %collective-permute-start.1 = (bf16[256,512]{1,0:T(8,128)(2,1)S(1)}, bf16[256,512]{1,0:T(8,128)(2,1)S(1)}, u32[]{:S(2)}, u32[]{:S(2)}) collective-permute-start(bf16[256,512]{1,0:T(8,128)(2,1)S(1)} %pad_maximum_fusion.3), channel_id=1, source_target_pairs={{0,1},{1,0},{2,3},{3,2},{4,5},{5,4},{6,7},{7,6},{8,9},{9,8},{10,11... | collective-permute-start | bytes 786440 | tf_op jit(solution)/shard_map/ppermute | solution.py:280
  38.0 2.2 %copy-start = (bf16[1,128,256]{2,1,0:T(8,128)(2,1)S(1)}, bf16[1,128,256]{2,1,0:T(8,128)(2,1)}, u32[]{:S(2)}) copy-start(bf16[1,128,256]{2,1,0:T(8,128)(2,1)} %param.9) | copy-start | bytes 196612
  39.0 1.3 %collective-permute-start.8 = (bf16[4,32,128]{2,1,0:T(8,128)(2,1)S(1)}, bf16[4,32,128]{2,1,0:T(8,128)(2,1)S(1)}, u32[]{:S(2)}, u32[]{:S(2)}) collective-permute-start(bf16[4,32,128]{2,1,0:T(8,128)(2,1)S(1)} %get-tuple-element.25), channel_id=1, source_target_pairs={{0,4},{4,0},{8,12},{12,8},{16,20},{20,16},{24,28},{28,24},{1,5},{5... | collective-permute-start | bytes 98312 | tf_op jit(solution)/shard_map/ppermute | solution.py:291
  39.1 17.8 %collective-permute-start.12 = (bf16[128,1280]{1,0:T(8,128)(2,1)S(1)}, bf16[128,1280]{1,0:T(8,128)(2,1)S(1)}, u32[]{:S(2)}, u32[]{:S(2)}) collective-permute-start(bf16[128,1280]{1,0:T(8,128)(2,1)S(1)} %get-tuple-element.26.refs_5_), channel_id=1, source_target_pairs={{0,1},{1,0},{2,3},{3,2},{4,5},{5,4},{6,7},{7,6},{8,9},{9,8},{10,11... | collective-permute-start | bytes 983048 | tf_op jit(solution)/shard_map/ppermute | solution.py:292
  40.3 10.7 %copy-start.1 = (bf16[1,1280,256]{2,1,0:T(8,128)(2,1)S(1)}, bf16[1,1280,256]{2,1,0:T(8,128)(2,1)}, u32[]{:S(2)}) copy-start(bf16[1,1280,256]{2,1,0:T(8,128)(2,1)} %param.10) | copy-start | bytes 1966084
  47.5 9.4 %collective-permute-start.14 = (bf16[128,1280]{1,0:T(8,128)(2,1)}, bf16[128,1280]{1,0:T(8,128)(2,1)S(1)}, u32[]{:S(2)}, u32[]{:S(2)}) collective-permute-start(bf16[128,1280]{1,0:T(8,128)(2,1)} %get-tuple-element.58), channel_id=1, source_target_pairs={{0,4},{4,0},{8,12},{12,8},{16,20},{20,16},{24,28},{28,24},{1,5},{5... | collective-permute-start | bytes 983048 | tf_op jit(solution)/shard_map/ppermute | solution.py:296
  47.5 8.5 %collective-permute-start.10 = (bf16[256,128]{1,0:T(8,128)(2,1)S(1)}, bf16[256,128]{1,0:T(8,128)(2,1)S(1)}, u32[]{:S(2)}, u32[]{:S(2)}) collective-permute-start(bf16[256,128]{1,0:T(8,128)(2,1)S(1)} %shard_map.103.refs_0_), channel_id=1, source_target_pairs={{0,2},{1,3},{2,0},{3,1},{4,6},{5,7},{6,4},{7,5},{8,10},{9,11},{10,... | collective-permute-start | bytes 196616 | tf_op jit(solution)/shard_map/ppermute | solution.py:298
  48.6 7.3 %collective-permute-start.11 = (bf16[256,128]{1,0:T(8,128)(2,1)S(1)}, bf16[256,128]{1,0:T(8,128)(2,1)S(1)}, u32[]{:S(2)}, u32[]{:S(2)}) collective-permute-start(bf16[256,128]{1,0:T(8,128)(2,1)S(1)} %shard_map.103.refs_0_), channel_id=1, source_target_pairs={{0,3},{1,2},{2,1},{3,0},{4,7},{5,6},{6,5},{7,4},{8,11},{9,10},{10,... | collective-permute-start | bytes 196616 | tf_op jit(solution)/shard_map/ppermute | solution.py:298
  50.1 6.8 %collective-permute-start.9 = (bf16[256,128]{1,0:T(8,128)(2,1)S(1)}, bf16[256,128]{1,0:T(8,128)(2,1)S(1)}, u32[]{:S(2)}, u32[]{:S(2)}) collective-permute-start(bf16[256,128]{1,0:T(8,128)(2,1)S(1)} %shard_map.103.refs_0_), channel_id=1, source_target_pairs={{0,1},{1,0},{2,3},{3,2},{4,5},{5,4},{6,7},{7,6},{8,9},{9,8},{10,11... | collective-permute-start | bytes 196616 | tf_op jit(solution)/shard_map/ppermute | solution.py:298
  57.6 1.7 %collective-permute-start.15 = (bf16[4,32,1280]{2,1,0:T(8,128)(2,1)S(1)}, bf16[4,32,1280]{2,1,0:T(8,128)(2,1)S(1)}, u32[]{:S(2)}, u32[]{:S(2)}) collective-permute-start(bf16[4,32,1280]{2,1,0:T(8,128)(2,1)S(1)} %get-tuple-element.29), channel_id=1, source_target_pairs={{0,4},{4,0},{8,12},{12,8},{16,20},{20,16},{24,28},{28,24},{1,5},{5... | collective-permute-start | bytes 983048 | tf_op jit(solution)/shard_map/ppermute | solution.py:306
  59.3 5.9 %collective-permute-start.16 = (bf16[32,1280]{1,0:T(8,128)(2,1)S(1)}, bf16[32,1280]{1,0:T(8,128)(2,1)S(1)}, u32[]{:S(2)}, u32[]{:S(2)}) collective-permute-start(bf16[32,1280]{1,0:T(8,128)(2,1)S(1)} %get-tuple-element.31), channel_id=1, source_target_pairs={{0,8},{4,12},{8,0},{12,4},{16,24},{20,28},{24,16},{28,20},{1,9},{5... | collective-permute-start | bytes 245768 | tf_op jit(solution)/shard_map/ppermute | solution.py:319
  61.0 5.3 %collective-permute-start.17 = (bf16[32,1280]{1,0:T(8,128)(2,1)S(1)}, bf16[32,1280]{1,0:T(8,128)(2,1)S(1)}, u32[]{:S(2)}, u32[]{:S(2)}) collective-permute-start(bf16[32,1280]{1,0:T(8,128)(2,1)S(1)} %get-tuple-element.32), channel_id=1, source_target_pairs={{0,16},{4,20},{8,24},{12,28},{16,0},{20,4},{24,8},{28,12},{1,17},{... | collective-permute-start | bytes 245768 | tf_op jit(solution)/shard_map/ppermute | solution.py:319
  62.5 5.3 %collective-permute-start.18 = (bf16[32,1280]{1,0:T(8,128)(2,1)S(1)}, bf16[32,1280]{1,0:T(8,128)(2,1)S(1)}, u32[]{:S(2)}, u32[]{:S(2)}) collective-permute-start(bf16[32,1280]{1,0:T(8,128)(2,1)S(1)} %get-tuple-element.33), channel_id=1, source_target_pairs={{0,24},{4,28},{8,16},{12,20},{16,8},{20,12},{24,0},{28,4},{1,25},{... | collective-permute-start | bytes 245768 | tf_op jit(solution)/shard_map/ppermute | solution.py:319
  64.1 3.8 %copy-start.2 = (f32[1280,32]{0,1:T(8,128)S(1)}, f32[1280,32]{0,1:T(8,128)}, u32[]{:S(2)}) copy-start(f32[1280,32]{0,1:T(8,128)} %param.12) | copy-start | bytes 491524
  64.1 3.8 %copy-start.3 = (f32[1280,32]{0,1:T(8,128)S(1)}, f32[1280,32]{0,1:T(8,128)}, u32[]{:S(2)}) copy-start(f32[1280,32]{0,1:T(8,128)} %param.13) | copy-start | bytes 491524

commit v8 on v7

--- a/solution.py
+++ b/solution.py
@@ -173,24 +173,33 @@
     )(*operands, mine, other, cot)
 
 
-def adam_kernel(n_seq, n_chip, own_half, inverse, *refs):
-    dq_refs, state_refs = refs[:n_seq], refs[n_seq : 2 * n_seq]
-    first_ref, second_ref, first_out, second_out, delta_out = refs[2 * n_seq :]
+def adam_kernel(order, n_dq, n_chip, own_half, inverse, *refs):
+    n_seq = len(order)
+    dq_refs, state_refs = refs[:n_dq], refs[n_dq : n_dq + n_seq]
+    first_ref, second_ref, first_out, second_out, delta_out = refs[n_dq + n_seq :]
     share = first_ref.shape[2]
     core = lax.rem(lax.axis_index("island"), 2)
     half = core if own_half else 1 - core
-    left = []
+    rows = state_refs[0].shape[0]
+    left = [None] * n_seq
+    taken = 0
     for ref in dq_refs:
         pieces = []
         for j in range(n_chip):
             start = pl.multiple_of((2 * j + half) * share, share)
             pieces.append(ref[pl.ds(start, share), :])
-        left.append(jnp.concatenate(pieces, axis=0).astype(jnp.float32))
+        stack = jnp.concatenate(pieces, axis=0).astype(jnp.float32)
+        for at in range(ref.shape[1] // rows):
+            left[order[taken]] = stack[:, at * rows : (at + 1) * rows]
+            taken += 1
     for k in range(2, n_seq, 2):
         even, odd = left[k], left[k + 1]
         left[k], left[k + 1] = jnp.where(core == 0, even, odd), jnp.where(core == 0, odd, even)
     left = jnp.concatenate(left, axis=1).astype(jnp.bfloat16)
-    states = jnp.concatenate([ref[...] for ref in state_refs], axis=0)
+    states = [ref[...] for ref in state_refs[:2]]
+    for k in range(2, n_seq, 2):
+        states += [state_refs[k][:rows, :], state_refs[k + 1][rows:, :]]
+    states = jnp.concatenate(states, axis=0)
     gradient = jnp.dot(left, states, preferred_element_type=jnp.float32) * inverse
     for j in range(n_chip):
         grad = gradient[j * share : (j + 1) * share]
@@ -204,18 +213,17 @@
         delta_out[j] = delta.astype(jnp.bfloat16)
 
 
-def gradient_adam(dqueries, states, first, second, own_half, inverse):
-    n_seq = len(states)
+def gradient_adam(order, dqueries, states, first, second, own_half, inverse):
     n_chip, _, share, block = first.shape
     shape = jax.ShapeDtypeStruct((n_chip, share, block), jnp.bfloat16)
     operands = list(dqueries) + list(states) + [first, second]
     half = n_chip * share * block
     return pl.pallas_call(
-        functools.partial(adam_kernel, n_seq, n_chip, own_half, inverse),
+        functools.partial(adam_kernel, order, len(dqueries), n_chip, own_half, inverse),
         out_shape=(shape, shape, shape),
         compiler_params=PARAMS,
         cost_estimate=cost(
-            2 * half * n_seq * states[0].shape[0], sum(o.size for o in operands) + 3 * half, 2 * half
+            2 * half * len(order) * states[0].shape[0], sum(o.size for o in operands) + 3 * half, 2 * half
         ),
     )(*operands)
 
@@ -264,7 +272,6 @@
     held = jnp.concatenate([weight, lax.ppermute(weight, "seq", far_perm)], 0)
     kv = [key_vals[0].reshape(rows, 2 * cols)]
     kv.append(lax.ppermute(kv[0], "seq", far_perm))
-    held, partner_tokens = lax.optimization_barrier((held, partner_tokens))
 
     def feature_block(matrix, k):
         return lax.dynamic_slice(matrix, (0, jnp.bitwise_xor(seq, k) * block), (rows, block))
@@ -289,31 +296,36 @@
     )
     near, for_partner = lax.optimization_barrier((own_blocks[1], for_partner))
     other = lax.ppermute(for_partner, "island", swap)
-    gathered = [own_blocks[0], lax.ppermute(near, "seq", pair_perm(n_seq, 1))]
+    near = lax.ppermute(near, "seq", pair_perm(n_seq, 1))
     dquery = attention(kv, order, mine, other, cotangent[0])
-    _, far = lax.optimization_barrier((dquery, far))
+    dqueries = [dquery]
+    for bit in bits:
+        stack = jnp.concatenate(dqueries, axis=1)
+        dqueries.append(lax.ppermute(stack, "seq", pair_perm(n_seq, bit)))
+    _, near, far = lax.optimization_barrier((dqueries[1], near, far))
+    gathered = [own_blocks[0], near]
     for got in far:
-        gathered += [got[:rows], lax.ppermute(got[rows:], "island", swap)]
-    dqueries = [dquery] + [
-        lax.ppermute(dquery, "seq", pair_perm(n_seq, k)) for k in range(1, n_seq)
-    ]
-
+        gathered += [got, lax.ppermute(got, "island", swap)]
     first = first_moment[0].T.reshape(n_chip, 2, share, block)
     second = second_moment[0].T.reshape(n_chip, 2, share, block)
     first_other, second_other, delta_other = gradient_adam(
-        dqueries, gathered, first, second, False, inverse
+        order, dqueries, gathered, first, second, False, inverse
     )
     got = lax.ppermute(delta_other, "island", swap)
     first_own, second_own, delta_own = gradient_adam(
-        dqueries, gathered, first, second, True, inverse
-    )
-
+        order, dqueries, gathered, first, second, True, inverse
+    )
+
+    parts = pair_sum(delta_own, got)
     def whole(own, other):
         lower = jnp.where(core == 0, own, other)
         upper = jnp.where(core == 0, other, own)
         return jnp.stack([lower, upper], axis=1).reshape(cols, block).T[None]
 
-    parts = pair_sum(delta_own, got)
+    parts, held_moments = lax.optimization_barrier(
+        (parts, (first_own, first_other, second_own, second_other))
+    )
+    first_own, first_other, second_own, second_other = held_moments
     total = parts[0]
     for step in range(1, n_chip):
         total = total + lax.ppermute(

time: 68.9 us -> 95 us (1.38)
  waiting for transfers between devices: 31.9 us -> 60.1 us
  starting transfers between devices: 23.2 us -> 18.9 us
  Pallas kernels: 3.59 us -> 5.29 us
    ppermute x1, waiting for transfers between devices: 0.01 us -> 32.4 us  [on_device(): kv.append(lax.ppermute(kv[0], 'seq', far_perm))]
    ppermute x3, waiting for transfers between devices: 13.3 us -> 0.01 us  [on_device(): spread[step] = lax.ppermute(held, 'island', pair_perm(n_chip, step, 2))]
    ppermute x1, waiting for transfers between devices: 0.01 us -> 6.13 us  [on_device(): lax.ppermute(jnp.concatenate(kv, axis=0), 'seq', pair_perm(n_seq, bit))]
    ppermute x1, waiting for transfers between devices: 5.15 us -> 0.01 us  [on_device(): lax.ppermute(both, ('island', 'seq'), far_pairs(n_island, n_seq, k))]
    ppermute x5 -> x4, waiting for transfers between devices: 4.36 us -> 9.2 us  [the longest x2 9.2 us: on_device(): dqueries.append(lax.ppermute(stack, 'seq', pair_perm(n_seq, bit)))]
    ppermute x1, starting transfers between devices: 3.54 us -> 0.81 us  [on_device(): lax.ppermute(held, 'seq', pair_perm(n_seq, bit))]
    ppermute x1, waiting for transfers between devices: 2.41 us -> 4.86 us  [on_device(): held = jnp.concatenate([weight, lax.ppermute(weight, 'seq', far_perm)], 0)]
    ppermute x1, waiting for transfers between devices: 2.07 us -> 3.79 us  [on_device(): lax.ppermute(held, 'seq', pair_perm(n_seq, bit))]
  transfers between devices with their start and end apart: 19 -> 18, of which waited for: 11 -> 9; matrix products, arithmetic and copies ran while one was open for 12% -> 8% of each run, Pallas kernels for 4% -> 3%
where the time goes in v8:
time: 95 us; the launch traced here: 94.7 us
  waiting for transfers between devices  60.1 us (63%)
  starting transfers between devices  18.9 us (20%)
  local copies, waits for them, and re-layouts  6.94 us (7%)
  Pallas kernels  5.29 us (6%)
  other arithmetic  2.7 us (3%)
    ppermute x1, waiting for transfers between devices, on_device(): kv.append(lax.ppermute(kv[0], 'seq', far_perm))  32.4 us
    ppermute x2, waiting for transfers between devices, on_device(): dqueries.append(lax.ppermute(stack, 'seq', pair_perm(n_seq, bit)))  9.2 us
    ppermute x1, waiting for transfers between devices, on_device(): lax.ppermute(jnp.concatenate(kv, axis=0), 'seq', pair_perm(n_seq, bit))  6.13 us
    ppermute x1, waiting for transfers between devices, on_device(): held = jnp.concatenate([weight, lax.ppermute(weight, 'seq', far_perm)], 0)  4.86 us
    ppermute x1, waiting for transfers between devices, on_device(): lax.ppermute(held, 'seq', pair_perm(n_seq, bit))  3.79 us
    ppermute x1, starting transfers between devices, on_device(): held = jnp.concatenate([weight, lax.ppermute(weight, 'seq', far_perm)], 0)  3.67 us
    unnamed x21, local copies, waits for them, and re-layouts  3.66 us
    ppermute x3, starting transfers between devices, on_device(): lax.ppermute(parts[step], 'island', pair_perm(n_chip, step, 2))  3.55 us
  transfers between devices with their start and end apart: 18, of which 9 were waited for; matrix products, arithmetic and copies ran while one was open for 8% of the time, Pallas kernels for 3%

profile of v8, /device:TPU:0, one launch (start us, length us, event | category | flops | bytes accessed | tf_op | source)
XLA Modules:
  0.0 94.7 jit_solution(9316770776811496884)
XLA Ops:
  0.6 0.5 collective-permute-start.7
  1.1 0.9 convert_bitcast_fusion
  2.1 3.7 %collective-permute-start.2 = (bf16[32,1280]{1,0:T(8,128)(2,1)S(1)}, bf16[32,1280]{1,0:T(8,128)(2,1)S(1)}, u32[]{:S(2)}, u32[]{:S(2)}) collective-permute-start(bf16[32,1280]{1,0:T(8,128)(2,1)S(1)} %convert_bitcast_fusion), channel_id=1, source_target_pairs={{0,2},{1,3},{2,0},{3,1},{4,6},{5,7},{6,4},{7,5},{8,10},{9,11},{10,... | collective-permute-start | bytes 245768 | tf_op jit(solution)/shard_map/ppermute | solution.py:272
  5.7 4.9 %collective-permute-done.2 = bf16[32,1280]{1,0:T(8,128)(2,1)S(1)} collective-permute-done((bf16[32,1280]{1,0:T(8,128)(2,1)S(1)}, bf16[32,1280]{1,0:T(8,128)(2,1)S(1)}, u32[]{:S(2)}, u32[]{:S(2)}) %collective-permute-start.2) | collective-permute-done | bytes 81952 | tf_op jit(solution)/shard_map/ppermute | solution.py:272
  10.6 0.8 collective-permute-start.3
  11.4 1.5 %dynamic-slice_bitcast_fusion = (bf16[128,1280]{1,0:T(8,128)(2,1)S(1)}, bf16[128,1280]{1,0:T(8,128)(2,1)S(1)}, bf16[128,1280]{1,0:T(8,128)(2,1)S(1)}, bf16[128,1280]{1,0:T(8,128)(2,1)S(1)}, bf16[128,1280]{1,0:T(8,128)(2,1)S(1)}) fusion(bf16[1,128,5120]{2,1,0:T(8,128)(2,1)} %param.7, s32[]{:T(128)S(6)} %select_n.44, s32[]{:T(128)S(6)} %select_n.43, ...), kind=kLoop, calls=%fused_computation.8 | loop fusion | bytes 3276820 | tf_op jit(solution)/shard_map/dynamic_slice | solution.py:277
  12.9 3.8 %collective-permute-done.3 = bf16[64,1280]{1,0:T(8,128)(2,1)S(1)} collective-permute-done((bf16[64,1280]{1,0:T(8,128)(2,1)S(1)}, bf16[64,1280]{1,0:T(8,128)(2,1)S(1)}, u32[]{:S(2)}, u32[]{:S(2)}) %collective-permute-start.3) | collective-permute-done | bytes 163872 | tf_op jit(solution)/shard_map/ppermute | solution.py:286
  16.7 1.4 %collective-permute-start.4 = (bf16[128,1280]{1,0:T(8,128)(2,1)S(1)}, bf16[128,1280]{1,0:T(8,128)(2,1)S(1)}, u32[]{:S(2)}, u32[]{:S(2)}) collective-permute-start(bf16[128,1280]{1,0:T(8,128)(2,1)S(1)} %pad_maximum_fusion.3.refs_0_), channel_id=1, source_target_pairs={{0,8},{4,12},{8,0},{12,4},{16,24},{20,28},{24,16},{28,20},{1,9},{5... | collective-permute-start | bytes 983048 | tf_op jit(solution)/shard_map/ppermute | solution.py:292
  18.1 1.5 %collective-permute-start.5 = (bf16[128,1280]{1,0:T(8,128)(2,1)S(1)}, bf16[128,1280]{1,0:T(8,128)(2,1)S(1)}, u32[]{:S(2)}, u32[]{:S(2)}) collective-permute-start(bf16[128,1280]{1,0:T(8,128)(2,1)S(1)} %pad_maximum_fusion.3.refs_0_), channel_id=1, source_target_pairs={{0,16},{4,20},{8,24},{12,28},{16,0},{20,4},{24,8},{28,12},{1,17},{... | collective-permute-start | bytes 983048 | tf_op jit(solution)/shard_map/ppermute | solution.py:292
  19.6 0.6 collective-permute-start.6
  20.3 0.0 collective-permute-done.7
  20.3 0.1 constant_dynamic-slice_fusion
  20.4 0.0 copy-start.8
  20.5 2.6 %collective-permute-start.12 = (bf16[256,1280]{1,0:T(8,128)(2,1)S(1)}, bf16[256,1280]{1,0:T(8,128)(2,1)S(1)}, u32[]{:S(2)}, u32[]{:S(2)}) collective-permute-start(bf16[256,1280]{1,0:T(8,128)(2,1)S(1)} %pad_maximum_fusion), channel_id=1, source_target_pairs={{0,2},{1,3},{2,0},{3,1},{4,7},{5,6},{6,5},{7,4},{8,10},{9,11},{10,... | collective-permute-start | bytes 1966088 | tf_op jit(solution)/shard_map/ppermute | solution.py:282
  23.1 0.8 collective-permute-start
  23.9 32.4 %collective-permute-done.refs_2_.refs_3_ = bf16[128,512]{1,0:T(8,128)(2,1)S(1)} collective-permute-done((bf16[128,512]{1,0:T(8,128)(2,1)S(1)}, bf16[128,512]{1,0:T(8,128)(2,1)S(1)}, u32[]{:S(2)}, u32[]{:S(2)}) %collective-permute-start) | collective-permute-done | bytes 131104 | tf_op jit(solution)/shard_map/ppermute | solution.py:274
  56.4 0.1 collective-permute-start.1
  56.4 0.0 collective-permute-done.4.refs_1_
  56.5 0.0 collective-permute-done.5.refs_2_
  56.5 0.0 copy-start.4
  56.5 1.0 %shard_map.102 = (bf16[4,32,128]{2,1,0:T(8,128)(2,1)S(1)}, bf16[4,32,128]{2,1,0:T(8,128)(2,1)S(1)}) custom-call(bf16[128,1280]{1,0:T(8,128)(2,1)S(1)} %pad_maximum_fusion.3.refs_0_, bf16[128,1280]{1,0:T(8,128)(2,1)S(1)} %collective-permute-done.4.refs_1_, bf16[128,1280]{1,0:T(8,128)(2,1)S(1)} %collective-permute-done.5.refs_2_, ...), custom_call_target="tpu_custom_call" | custom-call | flops 335544320 | bytes 3932160 | tf_op jit(solution)/shard_map/pallas_call | solution.py:81
  57.5 0.0 copy-start.5
  57.5 2.1 %collective-permute-start.11 = (bf16[128,1280]{1,0:T(8,128)(2,1)S(1)}, bf16[128,1280]{1,0:T(8,128)(2,1)S(1)}, u32[]{:S(2)}, u32[]{:S(2)}) collective-permute-start(bf16[128,1280]{1,0:T(8,128)(2,1)S(1)} %get-tuple-element.31.refs_5_), channel_id=1, source_target_pairs={{0,1},{1,0},{2,3},{3,2},{4,5},{5,4},{6,7},{7,6},{8,9},{9,8},{10,11... | collective-permute-start | bytes 983048 | tf_op jit(solution)/shard_map/ppermute | solution.py:299
  59.5 6.1 %collective-permute-done.1.refs_4_.refs_5_ = bf16[256,512]{1,0:T(8,128)(2,1)S(1)} collective-permute-done((bf16[256,512]{1,0:T(8,128)(2,1)S(1)}, bf16[256,512]{1,0:T(8,128)(2,1)S(1)}, u32[]{:S(2)}, u32[]{:S(2)}) %collective-permute-start.1) | collective-permute-done | bytes 262176 | tf_op jit(solution)/shard_map/ppermute | solution.py:287
  65.7 1.2 %shard_map.103.refs_0_ = bf16[256,128]{1,0:T(8,128)(2,1)S(1)} custom-call(bf16[128,512]{1,0:T(8,128)(2,1)S(1)} %bitcast.57, bf16[128,512]{1,0:T(8,128)(2,1)S(1)} %bitcast.58, bf16[128,512]{1,0:T(8,128)(2,1)S(1)} %collective-permute-done.refs_2_.refs_3_, bf16[128,512]{1,0:T(8,128)(2,1)S(1)} %collective-permute-done.refs_2_.refs_3_, ...), custom_call_target="tpu_custom_call" | custom-call | flops 402653184 | bytes 786432 | tf_op jit(solution)/shard_map/pallas_call | solution.py:161
  66.9 1.2 %collective-permute-start.9 = (bf16[256,128]{1,0:T(8,128)(2,1)S(1)}, bf16[256,128]{1,0:T(8,128)(2,1)S(1)}, u32[]{:S(2)}, u32[]{:S(2)}) collective-permute-start(bf16[256,128]{1,0:T(8,128)(2,1)S(1)} %shard_map.103.refs_0_), channel_id=1, source_target_pairs={{0,2},{1,3},{2,0},{3,1},{4,6},{5,7},{6,4},{7,5},{8,10},{9,11},{10,... | collective-permute-start | bytes 196616 | tf_op jit(solution)/shard_map/ppermute | solution.py:304
  68.2 4.7 %collective-permute-done.9.refs_1_ = bf16[256,128]{1,0:T(8,128)(2,1)S(1)} collective-permute-done((bf16[256,128]{1,0:T(8,128)(2,1)S(1)}, bf16[256,128]{1,0:T(8,128)(2,1)S(1)}, u32[]{:S(2)}, u32[]{:S(2)}) %collective-permute-start.9) | collective-permute-done | bytes 65568 | tf_op jit(solution)/shard_map/ppermute | solution.py:304
  72.9 0.7 pad_maximum_fusion.6
  73.5 0.2 copy.13
  73.8 1.3 %copy.14 = bf16[256,1280]{1,0:T(8,128)(2,1)S(1)} copy(bf16[256,1280]{0,1:T(8,128)(2,1)} %bitcast.64) | data formatting | bytes 1310720 | tf_op jit(solution)/shard_map/transpose | solution.py:310
  75.1 4.5 %collective-permute-done.10.refs_2_ = bf16[256,256]{1,0:T(8,128)(2,1)S(1)} collective-permute-done((bf16[256,256]{1,0:T(8,128)(2,1)}, bf16[256,256]{1,0:T(8,128)(2,1)S(1)}, u32[]{:S(2)}, u32[]{:S(2)}) %collective-permute-start.10) | collective-permute-done | bytes 131104 | tf_op jit(solution)/shard_map/ppermute | solution.py:304
  79.7 1.4 %shard_map.105 = (bf16[4,32,1280]{2,1,0:T(8,128)(2,1)S(1)}, bf16[4,32,1280]{2,1,0:T(8,128)(2,1)S(1)}, bf16[4,32,1280]{2,1,0:T(8,128)(2,1)}) custom-call(bf16[256,128]{1,0:T(8,128)(2,1)S(1)} %shard_map.103.refs_0_, bf16[256,128]{1,0:T(8,128)(2,1)S(1)} %collective-permute-done.9.refs_1_, bf16[256,256]{1,0:T(8,128)(2,1)S(1)} %collective-permute-done.10.refs_2_, ...), custom_call_target="tpu_custom_call" | custom-call | flops 167772160 | bytes 4521984 | tf_op jit(solution)/shard_map/pallas_call | solution.py:221
  81.0 0.7 copy-done
  81.8 0.7 copy-done.2
  82.5 0.7 shard_map.104
  83.2 1.3 %collective-permute-done.14.got_ref = bf16[4,32,1280]{2,1,0:T(8,128)(2,1)} collective-permute-done((bf16[4,32,1280]{2,1,0:T(8,128)(2,1)}, bf16[4,32,1280]{2,1,0:T(8,128)(2,1)}, u32[]{:S(2)}, u32[]{:S(2)}) %collective-permute-start.14) | collective-permute-done | bytes 327712 | tf_op jit(solution)/shard_map/ppermute | solution.py:314
  84.5 1.0 %shard_map.106 = (f32[32,1280]{1,0:T(8,128)S(1)}, bf16[32,1280]{1,0:T(8,128)(2,1)S(1)}, bf16[32,1280]{1,0:T(8,128)(2,1)S(1)}, bf16[32,1280]{1,0:T(8,128)(2,1)S(1)}) custom-call(bf16[4,32,1280]{2,1,0:T(8,128)(2,1)S(1)} %get-tuple-element.34.same_ref, bf16[4,32,1280]{2,1,0:T(8,128)(2,1)} %collective-permute-done.14.got_ref), custom_call_target="tpu_custom_call" | custom-call | flops 163840 | bytes 983040 | tf_op jit(solution)/shard_map/pallas_call | solution.py:245
  85.5 1.6 %collective-permute-start.15 = (bf16[32,1280]{1,0:T(8,128)(2,1)S(1)}, bf16[32,1280]{1,0:T(8,128)(2,1)S(1)}, u32[]{:S(2)}, u32[]{:S(2)}) collective-permute-start(bf16[32,1280]{1,0:T(8,128)(2,1)S(1)} %get-tuple-element.45), channel_id=1, source_target_pairs={{0,8},{4,12},{8,0},{12,4},{16,24},{20,28},{24,16},{28,20},{1,9},{5... | collective-permute-start | bytes 245768 | tf_op jit(solution)/shard_map/ppermute | solution.py:331
  87.1 1.5 %collective-permute-start.16 = (bf16[32,1280]{1,0:T(8,128)(2,1)S(1)}, bf16[32,1280]{1,0:T(8,128)(2,1)S(1)}, u32[]{:S(2)}, u32[]{:S(2)}) collective-permute-start(bf16[32,1280]{1,0:T(8,128)(2,1)S(1)} %get-tuple-element.46), channel_id=1, source_target_pairs={{0,16},{4,20},{8,24},{12,28},{16,0},{20,4},{24,8},{28,12},{1,17},{... | collective-permute-start | bytes 245768 | tf_op jit(solution)/shard_map/ppermute | solution.py:331
  88.6 0.5 collective-permute-start.17
  89.1 0.1 select_bitcast_fusion.1
  89.2 0.1 pad_maximum_fusion.2
  89.2 0.1 pad_maximum_fusion.1
  89.4 1.1 %copy.18 = bf16[1,1280,256]{2,1,0:T(8,128)(2,1)} copy(bf16[1,1280,256]{1,2,0:T(8,128)(2,1)S(1)} %bitcast.60) | data formatting | bytes 1310720
  90.5 1.1 %copy.17 = bf16[1,1280,256]{2,1,0:T(8,128)(2,1)} copy(bf16[1,1280,256]{1,2,0:T(8,128)(2,1)S(1)} %bitcast.61) | data formatting | bytes 1310720
  91.6 0.8 collective-permute-done.16
  92.4 1.6 %collective-permute-done.17 = bf16[32,1280]{1,0:T(8,128)(2,1)S(1)} collective-permute-done((bf16[32,1280]{1,0:T(8,128)(2,1)S(1)}, bf16[32,1280]{1,0:T(8,128)(2,1)S(1)}, u32[]{:S(2)}, u32[]{:S(2)}) %collective-permute-start.17) | collective-permute-done | bytes 81952 | tf_op jit(solution)/shard_map/ppermute | solution.py:331
  94.0 0.8 fusion.1
  (30 shorter events, 0.2 us)
Async XLA Ops:
  0.6 19.7 %collective-permute-start.7 = (bf16[128,5120]{1,0:T(8,128)(2,1)}, bf16[128,5120]{1,0:T(8,128)(2,1)S(1)}, u32[]{:S(2)}, u32[]{:S(2)}) collective-permute-start(bf16[128,5120]{1,0:T(8,128)(2,1)} %bitcast.62), channel_id=1, source_target_pairs={{0,4},{4,0},{8,12},{12,8},{16,20},{20,16},{24,28},{28,24},{1,5},{5... | collective-permute-start | bytes 3932168 | tf_op jit(solution)/shard_map/ppermute | solution.py:270
  2.1 8.5 %collective-permute-start.2 = (bf16[32,1280]{1,0:T(8,128)(2,1)S(1)}, bf16[32,1280]{1,0:T(8,128)(2,1)S(1)}, u32[]{:S(2)}, u32[]{:S(2)}) collective-permute-start(bf16[32,1280]{1,0:T(8,128)(2,1)S(1)} %convert_bitcast_fusion), channel_id=1, source_target_pairs={{0,2},{1,3},{2,0},{3,1},{4,6},{5,7},{6,4},{7,5},{8,10},{9,11},{10,... | collective-permute-start | bytes 245768 | tf_op jit(solution)/shard_map/ppermute | solution.py:272
  10.6 6.1 %collective-permute-start.3 = (bf16[64,1280]{1,0:T(8,128)(2,1)S(1)}, bf16[64,1280]{1,0:T(8,128)(2,1)S(1)}, u32[]{:S(2)}, u32[]{:S(2)}) collective-permute-start(bf16[64,1280]{1,0:T(8,128)(2,1)S(1)} %pad_maximum_fusion.5), channel_id=1, source_target_pairs={{0,1},{1,0},{2,3},{3,2},{4,5},{5,4},{6,7},{7,6},{8,9},{9,8},{10,11... | collective-permute-start | bytes 491528 | tf_op jit(solution)/shard_map/ppermute | solution.py:286
  16.7 39.7 %collective-permute-start.4 = (bf16[128,1280]{1,0:T(8,128)(2,1)S(1)}, bf16[128,1280]{1,0:T(8,128)(2,1)S(1)}, u32[]{:S(2)}, u32[]{:S(2)}) collective-permute-start(bf16[128,1280]{1,0:T(8,128)(2,1)S(1)} %pad_maximum_fusion.3.refs_0_), channel_id=1, source_target_pairs={{0,8},{4,12},{8,0},{12,4},{16,24},{20,28},{24,16},{28,20},{1,9},{5... | collective-permute-start | bytes 983048 | tf_op jit(solution)/shard_map/ppermute | solution.py:292
  18.1 38.3 %collective-permute-start.5 = (bf16[128,1280]{1,0:T(8,128)(2,1)S(1)}, bf16[128,1280]{1,0:T(8,128)(2,1)S(1)}, u32[]{:S(2)}, u32[]{:S(2)}) collective-permute-start(bf16[128,1280]{1,0:T(8,128)(2,1)S(1)} %pad_maximum_fusion.3.refs_0_), channel_id=1, source_target_pairs={{0,16},{4,20},{8,24},{12,28},{16,0},{20,4},{24,8},{28,12},{1,17},{... | collective-permute-start | bytes 983048 | tf_op jit(solution)/shard_map/ppermute | solution.py:292
  19.6 36.8 %collective-permute-start.6 = (bf16[128,1280]{1,0:T(8,128)(2,1)S(1)}, bf16[128,1280]{1,0:T(8,128)(2,1)S(1)}, u32[]{:S(2)}, u32[]{:S(2)}) collective-permute-start(bf16[128,1280]{1,0:T(8,128)(2,1)S(1)} %pad_maximum_fusion.3.refs_0_), channel_id=1, source_target_pairs={{0,24},{4,28},{8,16},{12,20},{16,8},{20,12},{24,0},{28,4},{1,25},{... | collective-permute-start | bytes 983048 | tf_op jit(solution)/shard_map/ppermute | solution.py:292
  20.4 2.7 %copy-start.8 = (bf16[1,128,2,256]{3,2,1,0:T(2,128)(2,1)S(1)}, bf16[1,128,2,256]{3,2,1,0:T(2,128)(2,1)}, u32[]{:S(2)}) copy-start(bf16[1,128,2,256]{3,2,1,0:T(2,128)(2,1)} %param.8) | copy-start | bytes 393220
  20.5 52.4 %collective-permute-start.12 = (bf16[256,1280]{1,0:T(8,128)(2,1)S(1)}, bf16[256,1280]{1,0:T(8,128)(2,1)S(1)}, u32[]{:S(2)}, u32[]{:S(2)}) collective-permute-start(bf16[256,1280]{1,0:T(8,128)(2,1)S(1)} %pad_maximum_fusion), channel_id=1, source_target_pairs={{0,2},{1,3},{2,0},{3,1},{4,7},{5,6},{6,5},{7,4},{8,10},{9,11},{10,... | collective-permute-start | bytes 1966088 | tf_op jit(solution)/shard_map/ppermute | solution.py:282
  23.1 33.2 %collective-permute-start = (bf16[128,512]{1,0:T(8,128)(2,1)S(1)}, bf16[128,512]{1,0:T(8,128)(2,1)S(1)}, u32[]{:S(2)}, u32[]{:S(2)}) collective-permute-start(bf16[128,512]{1,0:T(8,128)(2,1)S(1)} %bitcast.55), channel_id=1, source_target_pairs={{0,2},{1,3},{2,0},{3,1},{4,6},{5,7},{6,4},{7,5},{8,10},{9,11},{10,... | collective-permute-start | bytes 393224 | tf_op jit(solution)/shard_map/ppermute | solution.py:274
  56.4 9.3 %collective-permute-start.1 = (bf16[256,512]{1,0:T(8,128)(2,1)S(1)}, bf16[256,512]{1,0:T(8,128)(2,1)S(1)}, u32[]{:S(2)}, u32[]{:S(2)}) collective-permute-start(bf16[256,512]{1,0:T(8,128)(2,1)S(1)} %pad_maximum_fusion.4), channel_id=1, source_target_pairs={{0,1},{1,0},{2,3},{3,2},{4,5},{5,4},{6,7},{7,6},{8,9},{9,8},{10,11... | collective-permute-start | bytes 786440 | tf_op jit(solution)/shard_map/ppermute | solution.py:287
  56.5 9.2 %copy-start.4 = (bf16[1,128,256]{2,1,0:T(8,128)(2,1)S(1)}, bf16[1,128,256]{2,1,0:T(8,128)(2,1)}, u32[]{:S(2)}) copy-start(bf16[1,128,256]{2,1,0:T(8,128)(2,1)} %param.9) | copy-start | bytes 196612
  57.5 16.1 %copy-start.5 = (bf16[1,1280,256]{2,1,0:T(8,128)(2,1)S(1)}, bf16[1,1280,256]{2,1,0:T(8,128)(2,1)}, u32[]{:S(2)}) copy-start(bf16[1,1280,256]{2,1,0:T(8,128)(2,1)} %param.10) | copy-start | bytes 1966084
  57.5 15.4 %collective-permute-start.11 = (bf16[128,1280]{1,0:T(8,128)(2,1)S(1)}, bf16[128,1280]{1,0:T(8,128)(2,1)S(1)}, u32[]{:S(2)}, u32[]{:S(2)}) collective-permute-start(bf16[128,1280]{1,0:T(8,128)(2,1)S(1)} %get-tuple-element.31.refs_5_), channel_id=1, source_target_pairs={{0,1},{1,0},{2,3},{3,2},{4,5},{5,4},{6,7},{7,6},{8,9},{9,8},{10,11... | collective-permute-start | bytes 983048 | tf_op jit(solution)/shard_map/ppermute | solution.py:299
  59.5 6.1 %collective-permute-start.8 = (bf16[4,32,128]{2,1,0:T(8,128)(2,1)S(1)}, bf16[4,32,128]{2,1,0:T(8,128)(2,1)S(1)}, u32[]{:S(2)}, u32[]{:S(2)}) collective-permute-start(bf16[4,32,128]{2,1,0:T(8,128)(2,1)S(1)} %get-tuple-element.30), channel_id=1, source_target_pairs={{0,4},{4,0},{8,12},{12,8},{16,20},{20,16},{24,28},{28,24},{1,5},{5... | collective-permute-start | bytes 98312 | tf_op jit(solution)/shard_map/ppermute | solution.py:298
  66.9 5.9 %collective-permute-start.9 = (bf16[256,128]{1,0:T(8,128)(2,1)S(1)}, bf16[256,128]{1,0:T(8,128)(2,1)S(1)}, u32[]{:S(2)}, u32[]{:S(2)}) collective-permute-start(bf16[256,128]{1,0:T(8,128)(2,1)S(1)} %shard_map.103.refs_0_), channel_id=1, source_target_pairs={{0,2},{1,3},{2,0},{3,1},{4,6},{5,7},{6,4},{7,5},{8,10},{9,11},{10,... | collective-permute-start | bytes 196616 | tf_op jit(solution)/shard_map/ppermute | solution.py:304
  72.9 6.8 %collective-permute-start.13 = (bf16[256,1280]{1,0:T(8,128)(2,1)S(1)}, bf16[256,1280]{1,0:T(8,128)(2,1)S(1)}, u32[]{:S(2)}, u32[]{:S(2)}) collective-permute-start(bf16[256,1280]{1,0:T(8,128)(2,1)S(1)} %collective-permute-done.12.refs_5_), channel_id=1, source_target_pairs={{0,4},{4,0},{8,12},{12,8},{16,20},{20,16},{24,28},{28,24},{1,5},{5... | collective-permute-start | bytes 1966088 | tf_op jit(solution)/shard_map/ppermute | solution.py:308
  73.5 6.1 %collective-permute-start.10 = (bf16[256,256]{1,0:T(8,128)(2,1)}, bf16[256,256]{1,0:T(8,128)(2,1)S(1)}, u32[]{:S(2)}, u32[]{:S(2)}) collective-permute-start(bf16[256,256]{1,0:T(8,128)(2,1)} %pad_maximum_fusion.6), channel_id=1, source_target_pairs={{0,1},{1,0},{2,3},{3,2},{4,5},{5,4},{6,7},{7,6},{8,9},{9,8},{10,11... | collective-permute-start | bytes 393224 | tf_op jit(solution)/shard_map/ppermute | solution.py:304
  81.0 0.7 copy-start
  81.8 0.7 copy-start.2
  82.5 2.0 %collective-permute-start.14 = (bf16[4,32,1280]{2,1,0:T(8,128)(2,1)}, bf16[4,32,1280]{2,1,0:T(8,128)(2,1)}, u32[]{:S(2)}, u32[]{:S(2)}) collective-permute-start(bf16[4,32,1280]{2,1,0:T(8,128)(2,1)} %get-tuple-element.35), channel_id=1, source_target_pairs={{0,4},{4,0},{8,12},{12,8},{16,20},{20,16},{24,28},{28,24},{1,5},{5... | collective-permute-start | bytes 983048 | tf_op jit(solution)/shard_map/ppermute | solution.py:314
  82.5 6.6 %copy-start.1 = (bf16[4,32,1280]{2,1,0:T(8,128)(2,1)S(1)}, bf16[4,32,1280]{2,1,0:T(8,128)(2,1)}, u32[]{:S(2)}) copy-start(bf16[4,32,1280]{2,1,0:T(8,128)(2,1)} %copy-done) | copy-start | bytes 983044
  82.5 6.6 %copy-start.3 = (bf16[4,32,1280]{2,1,0:T(8,128)(2,1)S(1)}, bf16[4,32,1280]{2,1,0:T(8,128)(2,1)}, u32[]{:S(2)}) copy-start(bf16[4,32,1280]{2,1,0:T(8,128)(2,1)} %copy-done.2) | copy-start | bytes 983044
  85.5 6.1 %collective-permute-start.15 = (bf16[32,1280]{1,0:T(8,128)(2,1)S(1)}, bf16[32,1280]{1,0:T(8,128)(2,1)S(1)}, u32[]{:S(2)}, u32[]{:S(2)}) collective-permute-start(bf16[32,1280]{1,0:T(8,128)(2,1)S(1)} %get-tuple-element.45), channel_id=1, source_target_pairs={{0,8},{4,12},{8,0},{12,4},{16,24},{20,28},{24,16},{28,20},{1,9},{5... | collective-permute-start | bytes 245768 | tf_op jit(solution)/shard_map/ppermute | solution.py:331
  87.1 5.3 %collective-permute-start.16 = (bf16[32,1280]{1,0:T(8,128)(2,1)S(1)}, bf16[32,1280]{1,0:T(8,128)(2,1)S(1)}, u32[]{:S(2)}, u32[]{:S(2)}) collective-permute-start(bf16[32,1280]{1,0:T(8,128)(2,1)S(1)} %get-tuple-element.46), channel_id=1, source_target_pairs={{0,16},{4,20},{8,24},{12,28},{16,0},{20,4},{24,8},{28,12},{1,17},{... | collective-permute-start | bytes 245768 | tf_op jit(solution)/shard_map/ppermute | solution.py:331
  88.6 5.3 %collective-permute-start.17 = (bf16[32,1280]{1,0:T(8,128)(2,1)S(1)}, bf16[32,1280]{1,0:T(8,128)(2,1)S(1)}, u32[]{:S(2)}, u32[]{:S(2)}) collective-permute-start(bf16[32,1280]{1,0:T(8,128)(2,1)S(1)} %get-tuple-element.47), channel_id=1, source_target_pairs={{0,24},{4,28},{8,16},{12,20},{16,8},{20,12},{24,0},{28,4},{1,25},{... | collective-permute-start | bytes 245768 | tf_op jit(solution)/shard_map/ppermute | solution.py:331
  90.4 3.5 %copy-start.6 = (f32[1280,32]{0,1:T(8,128)S(1)}, f32[1280,32]{0,1:T(8,128)}, u32[]{:S(2)}) copy-start(f32[1280,32]{0,1:T(8,128)} %param.12) | copy-start | bytes 491524
  90.4 3.5 %copy-start.7 = (f32[1280,32]{0,1:T(8,128)S(1)}, f32[1280,32]{0,1:T(8,128)}, u32[]{:S(2)}) copy-start(f32[1280,32]{0,1:T(8,128)} %param.13) | copy-start | bytes 491524

commit v9 on v8

--- a/solution.py
+++ b/solution.py
@@ -279,6 +279,7 @@
     far = []
     for k in range(2, n_seq, 2):
         both = jnp.concatenate([feature_block(m, k + core) for m in (tokens, partner_tokens)], 0)
+        both, kv = lax.optimization_barrier((both, kv))
         far.append(lax.ppermute(both, ("island", "seq"), far_pairs(n_island, n_seq, k)))
     own_blocks = [feature_block(tokens, k) for k in range(n_seq)]
     partner_blocks = [feature_block(partner_tokens, k) for k in range(n_seq)]
@@ -291,18 +292,19 @@
     for step in range(1, n_chip):
         spread[step] = lax.ppermute(held, "island", pair_perm(n_chip, step, 2))
 
+    near, kv = lax.optimization_barrier((own_blocks[1], kv))
+    near = lax.ppermute(near, "seq", pair_perm(n_seq, 1))
     mine, for_partner = half_queries(
         rounds, [spread], own_blocks, partner_blocks, share, inverse
     )
-    near, for_partner = lax.optimization_barrier((own_blocks[1], for_partner))
     other = lax.ppermute(for_partner, "island", swap)
-    near = lax.ppermute(near, "seq", pair_perm(n_seq, 1))
+    other, near = lax.optimization_barrier((other, near))
     dquery = attention(kv, order, mine, other, cotangent[0])
     dqueries = [dquery]
     for bit in bits:
         stack = jnp.concatenate(dqueries, axis=1)
         dqueries.append(lax.ppermute(stack, "seq", pair_perm(n_seq, bit)))
-    _, near, far = lax.optimization_barrier((dqueries[1], near, far))
+    _, far = lax.optimization_barrier((dqueries[1], far))
     gathered = [own_blocks[0], near]
     for got in far:
         gathered += [got, lax.ppermute(got, "island", swap)]

time: 95 us -> 75.4 us (0.79)
  waiting for transfers between devices: 60.1 us -> 35 us
  starting transfers between devices: 18.9 us -> 23.5 us
    ppermute x1, waiting for transfers between devices: 32.4 us -> 1.87 us  [on_device(): kv.append(lax.ppermute(kv[0], 'seq', far_perm))]
    ppermute x3, waiting for transfers between devices: 0.01 us -> 8.42 us  [on_device(): spread[step] = lax.ppermute(held, 'island', pair_perm(n_chip, step, 2))]
    ppermute x1, waiting for transfers between devices: 0.01 us -> 4.84 us  [on_device(): near = lax.ppermute(near, 'seq', pair_perm(n_seq, 1))]
    ppermute x1, waiting for transfers between devices: 3.79 us -> 0.01 us  [on_device(): lax.ppermute(held, 'seq', pair_perm(n_seq, bit))]
    ppermute x2, starting transfers between devices: 1.25 us -> 4.4 us  [on_device(): dqueries.append(lax.ppermute(stack, 'seq', pair_perm(n_seq, bit)))]
    ppermute x1, starting transfers between devices: 0.81 us -> 3.54 us  [on_device(): lax.ppermute(held, 'seq', pair_perm(n_seq, bit))]
    ppermute x1, waiting for transfers between devices: 4.86 us -> 2.41 us  [on_device(): held = jnp.concatenate([weight, lax.ppermute(weight, 'seq', far_perm)], 0)]
    ppermute x1, starting transfers between devices: 2.06 us -> 0.01 us  [on_device(): near = lax.ppermute(near, 'seq', pair_perm(n_seq, 1))]
  transfers between devices with their start and end apart: 18 -> 18, of which waited for: 9 -> 12; matrix products, arithmetic and copies ran while one was open for 8% -> 11% of each run, Pallas kernels for 3% -> 4%
where the time goes in v9:
time: 75.4 us; the launch traced here: 75.1 us
  waiting for transfers between devices  35 us (46%)
  starting transfers between devices  23.5 us (31%)
  local copies, waits for them, and re-layouts  7.84 us (10%)
  Pallas kernels  5.3 us (7%)
  other arithmetic  2.7 us (4%)
  between operations  0.8 us (1%)
    ppermute x3, waiting for transfers between devices, on_device(): spread[step] = lax.ppermute(held, 'island', pair_perm(n_chip, step, 2))  8.42 us
    ppermute x2, waiting for transfers between devices, on_device(): dqueries.append(lax.ppermute(stack, 'seq', pair_perm(n_seq, bit)))  7.25 us
    ppermute x1, waiting for transfers between devices, on_device(): lax.ppermute(jnp.concatenate(kv, axis=0), 'seq', pair_perm(n_seq, bit))  5.36 us
    ppermute x1, waiting for transfers between devices, on_device(): near = lax.ppermute(near, 'seq', pair_perm(n_seq, 1))  4.84 us
    unnamed x19, local copies, waits for them, and re-layouts  4.54 us
    ppermute x2, starting transfers between devices, on_device(): dqueries.append(lax.ppermute(stack, 'seq', pair_perm(n_seq, bit)))  4.4 us
    ppermute x1, starting transfers between devices, on_device(): held = jnp.concatenate([weight, lax.ppermute(weight, 'seq', far_perm)], 0)  3.67 us
    ppermute x3, starting transfers between devices, on_device(): lax.ppermute(parts[step], 'island', pair_perm(n_chip, step, 2))  3.55 us
  transfers between devices with their start and end apart: 18, of which 12 were waited for; matrix products, arithmetic and copies ran while one was open for 11% of the time, Pallas kernels for 4%

profile of v9, /device:TPU:0, one launch (start us, length us, event | category | flops | bytes accessed | tf_op | source)
XLA Modules:
  0.0 75.1 jit_solution(8700211662335915490)
XLA Ops:
  0.6 0.5 collective-permute-start
  1.1 0.9 %convert_bitcast_fusion = bf16[32,1280]{1,0:T(8,128)(2,1)S(1)} fusion(f32[1280,32]{0,1:T(8,128)} %param.12), kind=kLoop, calls=%fused_computation.21 | loop fusion | flops 40960 | bytes 245760 | tf_op jit(solution)/shard_map/convert_element_type | solution.py:271
  2.1 3.7 %collective-permute-start.3 = (bf16[32,1280]{1,0:T(8,128)(2,1)S(1)}, bf16[32,1280]{1,0:T(8,128)(2,1)S(1)}, u32[]{:S(2)}, u32[]{:S(2)}) collective-permute-start(bf16[32,1280]{1,0:T(8,128)(2,1)S(1)} %convert_bitcast_fusion), channel_id=1, source_target_pairs={{0,2},{1,3},{2,0},{3,1},{4,6},{5,7},{6,4},{7,5},{8,10},{9,11},{10,... | collective-permute-start | bytes 245768 | tf_op jit(solution)/shard_map/ppermute | solution.py:272
  5.7 0.9 %copy.19 = bf16[16,8,2,256]{3,1,2,0:T(8,128)(2,1)S(1)} copy(bf16[16,8,2,256]{3,2,1,0:T(2,128)(2,1)} %bitcast.65) | data formatting | bytes 262144
  6.7 0.1 collective-permute-start.1
  6.8 1.5 %dynamic-slice_bitcast_fusion = (bf16[128,1280]{1,0:T(8,128)(2,1)S(1)}, bf16[128,1280]{1,0:T(8,128)(2,1)S(1)}, bf16[128,1280]{1,0:T(8,128)(2,1)S(1)}, bf16[128,1280]{1,0:T(8,128)(2,1)S(1)}, bf16[128,1280]{1,0:T(8,128)(2,1)S(1)}) fusion(bf16[1,128,5120]{2,1,0:T(8,128)(2,1)} %param.7, s32[]{:T(128)S(6)} %select_n.44, s32[]{:T(128)S(6)} %select_n.42, ...), kind=kLoop, calls=%fused_computation.8 | loop fusion | bytes 3276820 | tf_op jit(solution)/shard_map/dynamic_slice | solution.py:277
  8.3 2.4 %collective-permute-done.3 = bf16[32,1280]{1,0:T(8,128)(2,1)S(1)} collective-permute-done((bf16[32,1280]{1,0:T(8,128)(2,1)S(1)}, bf16[32,1280]{1,0:T(8,128)(2,1)S(1)}, u32[]{:S(2)}, u32[]{:S(2)}) %collective-permute-start.3) | collective-permute-done | bytes 81952 | tf_op jit(solution)/shard_map/ppermute | solution.py:272
  10.7 3.5 %collective-permute-start.4 = (bf16[64,1280]{1,0:T(8,128)(2,1)S(1)}, bf16[64,1280]{1,0:T(8,128)(2,1)S(1)}, u32[]{:S(2)}, u32[]{:S(2)}) collective-permute-start(bf16[64,1280]{1,0:T(8,128)(2,1)S(1)} %pad_maximum_fusion.5), channel_id=1, source_target_pairs={{0,1},{1,0},{2,3},{3,2},{4,5},{5,4},{6,7},{7,6},{8,9},{9,8},{10,11... | collective-permute-start | bytes 491528 | tf_op jit(solution)/shard_map/ppermute | solution.py:287
  14.3 0.1 constant_dynamic-slice_fusion
  14.5 1.9 %collective-permute-done.1.refs_2_.refs_3_ = bf16[128,512]{1,0:T(8,128)(2,1)S(1)} collective-permute-done((bf16[128,512]{1,0:T(8,128)(2,1)S(1)}, bf16[128,512]{1,0:T(8,128)(2,1)S(1)}, u32[]{:S(2)}, u32[]{:S(2)}) %collective-permute-start.1) | collective-permute-done | bytes 131104 | tf_op jit(solution)/shard_map/ppermute | solution.py:274
  16.3 0.7 collective-permute-start.2
  17.1 3.4 %collective-permute-start.12 = (bf16[256,1280]{1,0:T(8,128)(2,1)S(1)}, bf16[256,1280]{1,0:T(8,128)(2,1)S(1)}, u32[]{:S(2)}, u32[]{:S(2)}) collective-permute-start(bf16[256,1280]{1,0:T(8,128)(2,1)S(1)} %pad_maximum_fusion), channel_id=1, source_target_pairs={{0,2},{1,3},{2,0},{3,1},{4,7},{5,6},{6,5},{7,4},{8,10},{9,11},{10,... | collective-permute-start | bytes 1966088 | tf_op jit(solution)/shard_map/ppermute | solution.py:283
  20.4 1.6 %collective-permute-start.5 = (bf16[128,1280]{1,0:T(8,128)(2,1)S(1)}, bf16[128,1280]{1,0:T(8,128)(2,1)S(1)}, u32[]{:S(2)}, u32[]{:S(2)}) collective-permute-start(bf16[128,1280]{1,0:T(8,128)(2,1)S(1)} %pad_maximum_fusion.3.refs_0_), channel_id=1, source_target_pairs={{0,8},{4,12},{8,0},{12,4},{16,24},{20,28},{24,16},{28,20},{1,9},{5... | collective-permute-start | bytes 983048 | tf_op jit(solution)/shard_map/ppermute | solution.py:293
  22.0 1.5 %collective-permute-start.6 = (bf16[128,1280]{1,0:T(8,128)(2,1)S(1)}, bf16[128,1280]{1,0:T(8,128)(2,1)S(1)}, u32[]{:S(2)}, u32[]{:S(2)}) collective-permute-start(bf16[128,1280]{1,0:T(8,128)(2,1)S(1)} %pad_maximum_fusion.3.refs_0_), channel_id=1, source_target_pairs={{0,16},{4,20},{8,24},{12,28},{16,0},{20,4},{24,8},{28,12},{1,17},{... | collective-permute-start | bytes 983048 | tf_op jit(solution)/shard_map/ppermute | solution.py:293
  23.5 0.5 collective-permute-start.7
  24.0 5.4 %collective-permute-done.2.refs_4_.refs_5_ = bf16[256,512]{1,0:T(8,128)(2,1)S(1)} collective-permute-done((bf16[256,512]{1,0:T(8,128)(2,1)S(1)}, bf16[256,512]{1,0:T(8,128)(2,1)S(1)}, u32[]{:S(2)}, u32[]{:S(2)}) %collective-permute-start.2) | collective-permute-done | bytes 262176 | tf_op jit(solution)/shard_map/ppermute | solution.py:288
  29.4 1.8 %collective-permute-done.5.refs_1_ = bf16[128,1280]{1,0:T(8,128)(2,1)S(1)} collective-permute-done((bf16[128,1280]{1,0:T(8,128)(2,1)S(1)}, bf16[128,1280]{1,0:T(8,128)(2,1)S(1)}, u32[]{:S(2)}, u32[]{:S(2)}) %collective-permute-start.5) | collective-permute-done | bytes 327712 | tf_op jit(solution)/shard_map/ppermute | solution.py:293
  31.2 6.6 %collective-permute-done.6.refs_2_ = bf16[128,1280]{1,0:T(8,128)(2,1)S(1)} collective-permute-done((bf16[128,1280]{1,0:T(8,128)(2,1)S(1)}, bf16[128,1280]{1,0:T(8,128)(2,1)S(1)}, u32[]{:S(2)}, u32[]{:S(2)}) %collective-permute-start.6) | collective-permute-done | bytes 327712 | tf_op jit(solution)/shard_map/ppermute | solution.py:293
  37.8 1.0 %shard_map.102 = (bf16[4,32,128]{2,1,0:T(8,128)(2,1)S(1)}, bf16[4,32,128]{2,1,0:T(8,128)(2,1)S(1)}) custom-call(bf16[128,1280]{1,0:T(8,128)(2,1)S(1)} %pad_maximum_fusion.3.refs_0_, bf16[128,1280]{1,0:T(8,128)(2,1)S(1)} %collective-permute-done.5.refs_1_, bf16[128,1280]{1,0:T(8,128)(2,1)S(1)} %collective-permute-done.6.refs_2_, ...), custom_call_target="tpu_custom_call" | custom-call | flops 335544320 | bytes 3932160 | tf_op jit(solution)/shard_map/pallas_call | solution.py:81
  38.8 0.0 copy-start.5
  38.8 0.1 collective-permute-start.8
  38.8 1.2 %collective-permute-done.8.refs_7_ = bf16[4,32,128]{2,1,0:T(8,128)(2,1)S(1)} collective-permute-done((bf16[4,32,128]{2,1,0:T(8,128)(2,1)S(1)}, bf16[4,32,128]{2,1,0:T(8,128)(2,1)S(1)}, u32[]{:S(2)}, u32[]{:S(2)}) %collective-permute-start.8) | collective-permute-done | bytes 32800 | tf_op jit(solution)/shard_map/ppermute | solution.py:300
  40.0 4.8 %collective-permute-done.9.refs_4_ = bf16[128,1280]{1,0:T(8,128)(2,1)S(1)} collective-permute-done((bf16[128,1280]{1,0:T(8,128)(2,1)S(1)}, bf16[128,1280]{1,0:T(8,128)(2,1)S(1)}, u32[]{:S(2)}, u32[]{:S(2)}) %collective-permute-start.9) | collective-permute-done | bytes 327712 | tf_op jit(solution)/shard_map/ppermute | solution.py:296
  44.9 1.2 %shard_map.103.refs_0_ = bf16[256,128]{1,0:T(8,128)(2,1)S(1)} custom-call(bf16[128,512]{1,0:T(8,128)(2,1)S(1)} %bitcast.57, bf16[128,512]{1,0:T(8,128)(2,1)S(1)} %bitcast.58, bf16[128,512]{1,0:T(8,128)(2,1)S(1)} %collective-permute-done.1.refs_2_.refs_3_, bf16[128,512]{1,0:T(8,128)(2,1)S(1)} %collective-permute-done.1.refs_2_.refs_3_, ...), custom_call_target="tpu_custom_call" | custom-call | flops 402653184 | bytes 786432 | tf_op jit(solution)/shard_map/pallas_call | solution.py:161
  46.1 3.9 %collective-permute-start.10 = (bf16[256,128]{1,0:T(8,128)(2,1)S(1)}, bf16[256,128]{1,0:T(8,128)(2,1)S(1)}, u32[]{:S(2)}, u32[]{:S(2)}) collective-permute-start(bf16[256,128]{1,0:T(8,128)(2,1)S(1)} %shard_map.103.refs_0_), channel_id=1, source_target_pairs={{0,2},{1,3},{2,0},{3,1},{4,6},{5,7},{6,4},{7,5},{8,10},{9,11},{10,... | collective-permute-start | bytes 196616 | tf_op jit(solution)/shard_map/ppermute | solution.py:306
  50.1 3.2 %collective-permute-done.10.refs_1_ = bf16[256,128]{1,0:T(8,128)(2,1)S(1)} collective-permute-done((bf16[256,128]{1,0:T(8,128)(2,1)S(1)}, bf16[256,128]{1,0:T(8,128)(2,1)S(1)}, u32[]{:S(2)}, u32[]{:S(2)}) %collective-permute-start.10) | collective-permute-done | bytes 65568 | tf_op jit(solution)/shard_map/ppermute | solution.py:306
  53.2 0.7 pad_maximum_fusion.6
  53.9 0.5 collective-permute-start.11
  54.4 0.2 copy.13
  54.6 1.3 %copy.14 = bf16[256,1280]{1,0:T(8,128)(2,1)S(1)} copy(bf16[256,1280]{0,1:T(8,128)(2,1)} %bitcast.64) | data formatting | bytes 1310720 | tf_op jit(solution)/shard_map/transpose | solution.py:312
  56.0 4.1 %collective-permute-done.11.refs_2_ = bf16[256,256]{1,0:T(8,128)(2,1)S(1)} collective-permute-done((bf16[256,256]{1,0:T(8,128)(2,1)}, bf16[256,256]{1,0:T(8,128)(2,1)S(1)}, u32[]{:S(2)}, u32[]{:S(2)}) %collective-permute-start.11) | collective-permute-done | bytes 131104 | tf_op jit(solution)/shard_map/ppermute | solution.py:306
  60.0 1.4 %shard_map.105 = (bf16[4,32,1280]{2,1,0:T(8,128)(2,1)S(1)}, bf16[4,32,1280]{2,1,0:T(8,128)(2,1)S(1)}, bf16[4,32,1280]{2,1,0:T(8,128)(2,1)}) custom-call(bf16[256,128]{1,0:T(8,128)(2,1)S(1)} %shard_map.103.refs_0_, bf16[256,128]{1,0:T(8,128)(2,1)S(1)} %collective-permute-done.10.refs_1_, bf16[256,256]{1,0:T(8,128)(2,1)S(1)} %collective-permute-done.11.refs_2_, ...), custom_call_target="tpu_custom_call" | custom-call | flops 167772160 | bytes 4521984 | tf_op jit(solution)/shard_map/pallas_call | solution.py:221
  61.4 0.7 copy-done
  62.2 0.7 copy-done.2
  62.9 0.7 shard_map.104
  63.6 1.3 %collective-permute-done.14.got_ref = bf16[4,32,1280]{2,1,0:T(8,128)(2,1)} collective-permute-done((bf16[4,32,1280]{2,1,0:T(8,128)(2,1)}, bf16[4,32,1280]{2,1,0:T(8,128)(2,1)}, u32[]{:S(2)}, u32[]{:S(2)}) %collective-permute-start.14) | collective-permute-done | bytes 327712 | tf_op jit(solution)/shard_map/ppermute | solution.py:316
  64.9 1.0 %shard_map.106 = (f32[32,1280]{1,0:T(8,128)S(1)}, bf16[32,1280]{1,0:T(8,128)(2,1)S(1)}, bf16[32,1280]{1,0:T(8,128)(2,1)S(1)}, bf16[32,1280]{1,0:T(8,128)(2,1)S(1)}) custom-call(bf16[4,32,1280]{2,1,0:T(8,128)(2,1)S(1)} %get-tuple-element.46.same_ref, bf16[4,32,1280]{2,1,0:T(8,128)(2,1)} %collective-permute-done.14.got_ref), custom_call_target="tpu_custom_call" | custom-call | flops 163840 | bytes 983040 | tf_op jit(solution)/shard_map/pallas_call | solution.py:245
  65.9 1.6 %collective-permute-start.15 = (bf16[32,1280]{1,0:T(8,128)(2,1)S(1)}, bf16[32,1280]{1,0:T(8,128)(2,1)S(1)}, u32[]{:S(2)}, u32[]{:S(2)}) collective-permute-start(bf16[32,1280]{1,0:T(8,128)(2,1)S(1)} %get-tuple-element.57), channel_id=1, source_target_pairs={{0,8},{4,12},{8,0},{12,4},{16,24},{20,28},{24,16},{28,20},{1,9},{5... | collective-permute-start | bytes 245768 | tf_op jit(solution)/shard_map/ppermute | solution.py:333
  67.5 1.5 %collective-permute-start.16 = (bf16[32,1280]{1,0:T(8,128)(2,1)S(1)}, bf16[32,1280]{1,0:T(8,128)(2,1)S(1)}, u32[]{:S(2)}, u32[]{:S(2)}) collective-permute-start(bf16[32,1280]{1,0:T(8,128)(2,1)S(1)} %get-tuple-element.58), channel_id=1, source_target_pairs={{0,16},{4,20},{8,24},{12,28},{16,0},{20,4},{24,8},{28,12},{1,17},{... | collective-permute-start | bytes 245768 | tf_op jit(solution)/shard_map/ppermute | solution.py:333
  69.0 0.5 collective-permute-start.17
  69.5 0.1 select_bitcast_fusion.1
  69.6 0.1 pad_maximum_fusion.2
  69.6 0.1 pad_maximum_fusion.1
  69.8 1.1 %copy.18 = bf16[1,1280,256]{2,1,0:T(8,128)(2,1)} copy(bf16[1,1280,256]{1,2,0:T(8,128)(2,1)S(1)} %bitcast.60) | data formatting | bytes 1310720
  70.9 1.1 %copy.17 = bf16[1,1280,256]{2,1,0:T(8,128)(2,1)} copy(bf16[1,1280,256]{1,2,0:T(8,128)(2,1)S(1)} %bitcast.61) | data formatting | bytes 1310720
  72.0 0.8 %collective-permute-done.16 = bf16[32,1280]{1,0:T(8,128)(2,1)S(1)} collective-permute-done((bf16[32,1280]{1,0:T(8,128)(2,1)S(1)}, bf16[32,1280]{1,0:T(8,128)(2,1)S(1)}, u32[]{:S(2)}, u32[]{:S(2)}) %collective-permute-start.16) | collective-permute-done | bytes 81952 | tf_op jit(solution)/shard_map/ppermute | solution.py:333
  72.7 1.6 %collective-permute-done.17 = bf16[32,1280]{1,0:T(8,128)(2,1)S(1)} collective-permute-done((bf16[32,1280]{1,0:T(8,128)(2,1)S(1)}, bf16[32,1280]{1,0:T(8,128)(2,1)S(1)}, u32[]{:S(2)}, u32[]{:S(2)}) %collective-permute-start.17) | collective-permute-done | bytes 81952 | tf_op jit(solution)/shard_map/ppermute | solution.py:333
  74.3 0.8 %fusion.1 = (f32[1280,32]{0,1:T(8,128)}, f32[1280,32]{0,1:T(8,128)}) fusion(f32[1280,32]{0,1:T(8,128)S(1)} %copy-done.6, bf16[32,1280]{1,0:T(8,128)(2,1)S(1)} %collective-permute-done.17, bf16[32,1280]{1,0:T(8,128)(2,1)S(1)} %collective-permute-done.16, f32[32,1280]{1,0:T(8,128)S(1)} %get-tuple-element.56, bf16[32,1280]{1,0:T(8,128)(2,1)S(1)} %collective-permute-done.15, ...), kind=kLoop, calls=%fused_computation.18 | loop fusion | flops 532480 | bytes 1064960 | tf_op jit(solution)/shard_map/sub | solution.py:338
  (28 shorter events, 0.2 us)
Async XLA Ops:
  0.6 13.6 %collective-permute-start = (bf16[128,5120]{1,0:T(8,128)(2,1)}, bf16[128,5120]{1,0:T(8,128)(2,1)S(1)}, u32[]{:S(2)}, u32[]{:S(2)}) collective-permute-start(bf16[128,5120]{1,0:T(8,128)(2,1)} %bitcast.62), channel_id=1, source_target_pairs={{0,4},{4,0},{8,12},{12,8},{16,20},{20,16},{24,28},{28,24},{1,5},{5... | collective-permute-start | bytes 3932168 | tf_op jit(solution)/shard_map/ppermute | solution.py:270
  2.1 8.6 %collective-permute-start.3 = (bf16[32,1280]{1,0:T(8,128)(2,1)S(1)}, bf16[32,1280]{1,0:T(8,128)(2,1)S(1)}, u32[]{:S(2)}, u32[]{:S(2)}) collective-permute-start(bf16[32,1280]{1,0:T(8,128)(2,1)S(1)} %convert_bitcast_fusion), channel_id=1, source_target_pairs={{0,2},{1,3},{2,0},{3,1},{4,6},{5,7},{6,4},{7,5},{8,10},{9,11},{10,... | collective-permute-start | bytes 245768 | tf_op jit(solution)/shard_map/ppermute | solution.py:272
  6.7 9.7 %collective-permute-start.1 = (bf16[128,512]{1,0:T(8,128)(2,1)S(1)}, bf16[128,512]{1,0:T(8,128)(2,1)S(1)}, u32[]{:S(2)}, u32[]{:S(2)}) collective-permute-start(bf16[128,512]{1,0:T(8,128)(2,1)S(1)} %bitcast.55), channel_id=1, source_target_pairs={{0,2},{1,3},{2,0},{3,1},{4,6},{5,7},{6,4},{7,5},{8,10},{9,11},{10,... | collective-permute-start | bytes 393224 | tf_op jit(solution)/shard_map/ppermute | solution.py:274
  10.7 9.7 %collective-permute-start.4 = (bf16[64,1280]{1,0:T(8,128)(2,1)S(1)}, bf16[64,1280]{1,0:T(8,128)(2,1)S(1)}, u32[]{:S(2)}, u32[]{:S(2)}) collective-permute-start(bf16[64,1280]{1,0:T(8,128)(2,1)S(1)} %pad_maximum_fusion.5), channel_id=1, source_target_pairs={{0,1},{1,0},{2,3},{3,2},{4,5},{5,4},{6,7},{7,6},{8,9},{9,8},{10,11... | collective-permute-start | bytes 491528 | tf_op jit(solution)/shard_map/ppermute | solution.py:287
  16.3 13.0 %collective-permute-start.2 = (bf16[256,512]{1,0:T(8,128)(2,1)S(1)}, bf16[256,512]{1,0:T(8,128)(2,1)S(1)}, u32[]{:S(2)}, u32[]{:S(2)}) collective-permute-start(bf16[256,512]{1,0:T(8,128)(2,1)S(1)} %pad_maximum_fusion.4), channel_id=1, source_target_pairs={{0,1},{1,0},{2,3},{3,2},{4,5},{5,4},{6,7},{7,6},{8,9},{9,8},{10,11... | collective-permute-start | bytes 786440 | tf_op jit(solution)/shard_map/ppermute | solution.py:288
  17.1 36.2 %collective-permute-start.12 = (bf16[256,1280]{1,0:T(8,128)(2,1)S(1)}, bf16[256,1280]{1,0:T(8,128)(2,1)S(1)}, u32[]{:S(2)}, u32[]{:S(2)}) collective-permute-start(bf16[256,1280]{1,0:T(8,128)(2,1)S(1)} %pad_maximum_fusion), channel_id=1, source_target_pairs={{0,2},{1,3},{2,0},{3,1},{4,7},{5,6},{6,5},{7,4},{8,10},{9,11},{10,... | collective-permute-start | bytes 1966088 | tf_op jit(solution)/shard_map/ppermute | solution.py:283
  20.4 10.7 %collective-permute-start.5 = (bf16[128,1280]{1,0:T(8,128)(2,1)S(1)}, bf16[128,1280]{1,0:T(8,128)(2,1)S(1)}, u32[]{:S(2)}, u32[]{:S(2)}) collective-permute-start(bf16[128,1280]{1,0:T(8,128)(2,1)S(1)} %pad_maximum_fusion.3.refs_0_), channel_id=1, source_target_pairs={{0,8},{4,12},{8,0},{12,4},{16,24},{20,28},{24,16},{28,20},{1,9},{5... | collective-permute-start | bytes 983048 | tf_op jit(solution)/shard_map/ppermute | solution.py:293
  22.0 15.8 %collective-permute-start.6 = (bf16[128,1280]{1,0:T(8,128)(2,1)S(1)}, bf16[128,1280]{1,0:T(8,128)(2,1)S(1)}, u32[]{:S(2)}, u32[]{:S(2)}) collective-permute-start(bf16[128,1280]{1,0:T(8,128)(2,1)S(1)} %pad_maximum_fusion.3.refs_0_), channel_id=1, source_target_pairs={{0,16},{4,20},{8,24},{12,28},{16,0},{20,4},{24,8},{28,12},{1,17},{... | collective-permute-start | bytes 983048 | tf_op jit(solution)/shard_map/ppermute | solution.py:293
  23.5 14.3 %collective-permute-start.7 = (bf16[128,1280]{1,0:T(8,128)(2,1)S(1)}, bf16[128,1280]{1,0:T(8,128)(2,1)S(1)}, u32[]{:S(2)}, u32[]{:S(2)}) collective-permute-start(bf16[128,1280]{1,0:T(8,128)(2,1)S(1)} %pad_maximum_fusion.3.refs_0_), channel_id=1, source_target_pairs={{0,24},{4,28},{8,16},{12,20},{16,8},{20,12},{24,0},{28,4},{1,25},{... | collective-permute-start | bytes 983048 | tf_op jit(solution)/shard_map/ppermute | solution.py:293
  29.4 15.5 %collective-permute-start.9 = (bf16[128,1280]{1,0:T(8,128)(2,1)S(1)}, bf16[128,1280]{1,0:T(8,128)(2,1)S(1)}, u32[]{:S(2)}, u32[]{:S(2)}) collective-permute-start(bf16[128,1280]{1,0:T(8,128)(2,1)S(1)} %get-tuple-element.41.refs_5_), channel_id=1, source_target_pairs={{0,1},{1,0},{2,3},{3,2},{4,5},{5,4},{6,7},{7,6},{8,9},{9,8},{10,11... | collective-permute-start | bytes 983048 | tf_op jit(solution)/shard_map/ppermute | solution.py:296
  37.8 7.1 %copy-start.4 = (bf16[1,128,256]{2,1,0:T(8,128)(2,1)S(1)}, bf16[1,128,256]{2,1,0:T(8,128)(2,1)}, u32[]{:S(2)}) copy-start(bf16[1,128,256]{2,1,0:T(8,128)(2,1)} %param.9) | copy-start | bytes 196612
  38.8 15.6 %copy-start.5 = (bf16[1,1280,256]{2,1,0:T(8,128)(2,1)S(1)}, bf16[1,1280,256]{2,1,0:T(8,128)(2,1)}, u32[]{:S(2)}) copy-start(bf16[1,1280,256]{2,1,0:T(8,128)(2,1)} %param.10) | copy-start | bytes 1966084
  38.8 1.3 %collective-permute-start.8 = (bf16[4,32,128]{2,1,0:T(8,128)(2,1)S(1)}, bf16[4,32,128]{2,1,0:T(8,128)(2,1)S(1)}, u32[]{:S(2)}, u32[]{:S(2)}) collective-permute-start(bf16[4,32,128]{2,1,0:T(8,128)(2,1)S(1)} %get-tuple-element.40), channel_id=1, source_target_pairs={{0,4},{4,0},{8,12},{12,8},{16,20},{20,16},{24,28},{28,24},{1,5},{5... | collective-permute-start | bytes 98312 | tf_op jit(solution)/shard_map/ppermute | solution.py:300
  46.1 7.1 %collective-permute-start.10 = (bf16[256,128]{1,0:T(8,128)(2,1)S(1)}, bf16[256,128]{1,0:T(8,128)(2,1)S(1)}, u32[]{:S(2)}, u32[]{:S(2)}) collective-permute-start(bf16[256,128]{1,0:T(8,128)(2,1)S(1)} %shard_map.103.refs_0_), channel_id=1, source_target_pairs={{0,2},{1,3},{2,0},{3,1},{4,6},{5,7},{6,4},{7,5},{8,10},{9,11},{10,... | collective-permute-start | bytes 196616 | tf_op jit(solution)/shard_map/ppermute | solution.py:306
  53.2 6.8 %collective-permute-start.13 = (bf16[256,1280]{1,0:T(8,128)(2,1)S(1)}, bf16[256,1280]{1,0:T(8,128)(2,1)S(1)}, u32[]{:S(2)}, u32[]{:S(2)}) collective-permute-start(bf16[256,1280]{1,0:T(8,128)(2,1)S(1)} %collective-permute-done.12.refs_5_), channel_id=1, source_target_pairs={{0,4},{4,0},{8,12},{12,8},{16,20},{20,16},{24,28},{28,24},{1,5},{5... | collective-permute-start | bytes 1966088 | tf_op jit(solution)/shard_map/ppermute | solution.py:310
  53.9 6.1 %collective-permute-start.11 = (bf16[256,256]{1,0:T(8,128)(2,1)}, bf16[256,256]{1,0:T(8,128)(2,1)S(1)}, u32[]{:S(2)}, u32[]{:S(2)}) collective-permute-start(bf16[256,256]{1,0:T(8,128)(2,1)} %pad_maximum_fusion.6), channel_id=1, source_target_pairs={{0,1},{1,0},{2,3},{3,2},{4,5},{5,4},{6,7},{7,6},{8,9},{9,8},{10,11... | collective-permute-start | bytes 393224 | tf_op jit(solution)/shard_map/ppermute | solution.py:306
  61.4 0.7 copy-start
  62.2 0.7 copy-start.2
  62.9 2.0 %collective-permute-start.14 = (bf16[4,32,1280]{2,1,0:T(8,128)(2,1)}, bf16[4,32,1280]{2,1,0:T(8,128)(2,1)}, u32[]{:S(2)}, u32[]{:S(2)}) collective-permute-start(bf16[4,32,1280]{2,1,0:T(8,128)(2,1)} %get-tuple-element.47), channel_id=1, source_target_pairs={{0,4},{4,0},{8,12},{12,8},{16,20},{20,16},{24,28},{28,24},{1,5},{5... | collective-permute-start | bytes 983048 | tf_op jit(solution)/shard_map/ppermute | solution.py:316
  62.9 6.6 %copy-start.1 = (bf16[4,32,1280]{2,1,0:T(8,128)(2,1)S(1)}, bf16[4,32,1280]{2,1,0:T(8,128)(2,1)}, u32[]{:S(2)}) copy-start(bf16[4,32,1280]{2,1,0:T(8,128)(2,1)} %copy-done) | copy-start | bytes 983044
  62.9 6.6 %copy-start.3 = (bf16[4,32,1280]{2,1,0:T(8,128)(2,1)S(1)}, bf16[4,32,1280]{2,1,0:T(8,128)(2,1)}, u32[]{:S(2)}) copy-start(bf16[4,32,1280]{2,1,0:T(8,128)(2,1)} %copy-done.2) | copy-start | bytes 983044
  65.9 6.1 %collective-permute-start.15 = (bf16[32,1280]{1,0:T(8,128)(2,1)S(1)}, bf16[32,1280]{1,0:T(8,128)(2,1)S(1)}, u32[]{:S(2)}, u32[]{:S(2)}) collective-permute-start(bf16[32,1280]{1,0:T(8,128)(2,1)S(1)} %get-tuple-element.57), channel_id=1, source_target_pairs={{0,8},{4,12},{8,0},{12,4},{16,24},{20,28},{24,16},{28,20},{1,9},{5... | collective-permute-start | bytes 245768 | tf_op jit(solution)/shard_map/ppermute | solution.py:333
  67.5 5.3 %collective-permute-start.16 = (bf16[32,1280]{1,0:T(8,128)(2,1)S(1)}, bf16[32,1280]{1,0:T(8,128)(2,1)S(1)}, u32[]{:S(2)}, u32[]{:S(2)}) collective-permute-start(bf16[32,1280]{1,0:T(8,128)(2,1)S(1)} %get-tuple-element.58), channel_id=1, source_target_pairs={{0,16},{4,20},{8,24},{12,28},{16,0},{20,4},{24,8},{28,12},{1,17},{... | collective-permute-start | bytes 245768 | tf_op jit(solution)/shard_map/ppermute | solution.py:333
  69.0 5.3 %collective-permute-start.17 = (bf16[32,1280]{1,0:T(8,128)(2,1)S(1)}, bf16[32,1280]{1,0:T(8,128)(2,1)S(1)}, u32[]{:S(2)}, u32[]{:S(2)}) collective-permute-start(bf16[32,1280]{1,0:T(8,128)(2,1)S(1)} %get-tuple-element.59), channel_id=1, source_target_pairs={{0,24},{4,28},{8,16},{12,20},{16,8},{20,12},{24,0},{28,4},{1,25},{... | collective-permute-start | bytes 245768 | tf_op jit(solution)/shard_map/ppermute | solution.py:333
  70.8 3.5 %copy-start.6 = (f32[1280,32]{0,1:T(8,128)S(1)}, f32[1280,32]{0,1:T(8,128)}, u32[]{:S(2)}) copy-start(f32[1280,32]{0,1:T(8,128)} %param.12) | copy-start | bytes 491524
  70.8 3.5 %copy-start.7 = (f32[1280,32]{0,1:T(8,128)S(1)}, f32[1280,32]{0,1:T(8,128)}, u32[]{:S(2)}) copy-start(f32[1280,32]{0,1:T(8,128)} %param.13) | copy-start | bytes 491524

commit v10 on v7

--- a/solution.py
+++ b/solution.py
@@ -18,7 +18,10 @@
 
 NT = (((1,), (1,)), ((), ()))
 TN = (((0,), (0,)), ((), ()))
-PARAMS = pltpu.CompilerParams(vmem_limit_bytes=48 * 1024 * 1024)
+
+
+def params(elements):
+    return pltpu.CompilerParams(vmem_limit_bytes=min(48, max(16, elements >> 18)) * 1024 * 1024)
 
 
 def cost(flops, elements, transcendentals=0):
@@ -81,7 +84,7 @@
     return pl.pallas_call(
         functools.partial(query_kernel, rounds, n_chip, inverse),
         out_shape=(shape, shape),
-        compiler_params=PARAMS,
+        compiler_params=params(sum(o.size for o in operands)),
         cost_estimate=cost(2 * macs, sum(o.size for o in operands)),
     )(*operands)
 
@@ -164,7 +167,7 @@
         in_specs=in_specs,
         out_specs=pl.BlockSpec((group, rows), lambda g: (g, 0)),
         out_shape=jax.ShapeDtypeStruct((cols, rows), jnp.bfloat16),
-        compiler_params=PARAMS,
+        compiler_params=params(8 * length * (group // HD) * rows),
         cost_estimate=cost(
             6 * length * cols * (group // HD) * rows,
             2 * length * cols + 4 * cols * rows,
@@ -190,7 +193,11 @@
         even, odd = left[k], left[k + 1]
         left[k], left[k + 1] = jnp.where(core == 0, even, odd), jnp.where(core == 0, odd, even)
     left = jnp.concatenate(left, axis=1).astype(jnp.bfloat16)
-    states = jnp.concatenate([ref[...] for ref in state_refs], axis=0)
+    rows = state_refs[0].shape[0]
+    states = [ref[...] for ref in state_refs[:2]]
+    for k in range(2, n_seq, 2):
+        states += [state_refs[k][:rows, :], state_refs[k + 1][rows:, :]]
+    states = jnp.concatenate(states, axis=0)
     gradient = jnp.dot(left, states, preferred_element_type=jnp.float32) * inverse
     for j in range(n_chip):
         grad = gradient[j * share : (j + 1) * share]
@@ -213,7 +220,7 @@
     return pl.pallas_call(
         functools.partial(adam_kernel, n_seq, n_chip, own_half, inverse),
         out_shape=(shape, shape, shape),
-        compiler_params=PARAMS,
+        compiler_params=params(sum(o.size for o in operands)),
         cost_estimate=cost(
             2 * half * n_seq * states[0].shape[0], sum(o.size for o in operands) + 3 * half, 2 * half
         ),
@@ -237,7 +244,7 @@
     return pl.pallas_call(
         functools.partial(pair_kernel, n_chip),
         out_shape=tuple(shapes),
-        compiler_params=PARAMS,
+        compiler_params=params(4 * same.size),
         cost_estimate=cost(same.size, 3 * same.size),
     )(same, got)
 
@@ -264,7 +271,6 @@
     held = jnp.concatenate([weight, lax.ppermute(weight, "seq", far_perm)], 0)
     kv = [key_vals[0].reshape(rows, 2 * cols)]
     kv.append(lax.ppermute(kv[0], "seq", far_perm))
-    held, partner_tokens = lax.optimization_barrier((held, partner_tokens))
 
     def feature_block(matrix, k):
         return lax.dynamic_slice(matrix, (0, jnp.bitwise_xor(seq, k) * block), (rows, block))
@@ -272,6 +278,7 @@
     far = []
     for k in range(2, n_seq, 2):
         both = jnp.concatenate([feature_block(m, k + core) for m in (tokens, partner_tokens)], 0)
+        both, kv = lax.optimization_barrier((both, kv))
         far.append(lax.ppermute(both, ("island", "seq"), far_pairs(n_island, n_seq, k)))
     own_blocks = [feature_block(tokens, k) for k in range(n_seq)]
     partner_blocks = [feature_block(partner_tokens, k) for k in range(n_seq)]
@@ -289,15 +296,16 @@
     )
     near, for_partner = lax.optimization_barrier((own_blocks[1], for_partner))
     other = lax.ppermute(for_partner, "island", swap)
-    gathered = [own_blocks[0], lax.ppermute(near, "seq", pair_perm(n_seq, 1))]
+    near = lax.ppermute(near, "seq", pair_perm(n_seq, 1))
     dquery = attention(kv, order, mine, other, cotangent[0])
-    _, far = lax.optimization_barrier((dquery, far))
-    for got in far:
-        gathered += [got[:rows], lax.ppermute(got[rows:], "island", swap)]
     dqueries = [dquery] + [
         lax.ppermute(dquery, "seq", pair_perm(n_seq, k)) for k in range(1, n_seq)
     ]
 
+    _, near, far = lax.optimization_barrier((dqueries[1:], near, far))
+    gathered = [own_blocks[0], near]
+    for got in far:
+        gathered += [got, lax.ppermute(got, "island", swap)]
     first = first_moment[0].T.reshape(n_chip, 2, share, block)
     second = second_moment[0].T.reshape(n_chip, 2, share, block)
     first_other, second_other, delta_other = gradient_adam(
@@ -308,12 +316,12 @@
         dqueries, gathered, first, second, True, inverse
     )
 
+    parts = pair_sum(delta_own, got)
     def whole(own, other):
         lower = jnp.where(core == 0, own, other)
         upper = jnp.where(core == 0, other, own)
         return jnp.stack([lower, upper], axis=1).reshape(cols, block).T[None]
 
-    parts = pair_sum(delta_own, got)
     total = parts[0]
     for step in range(1, n_chip):
         total = total + lax.ppermute(

time: 68.9 us -> 72.9 us (1.058)
  waiting for transfers between devices: 31.9 us -> 35.4 us
  starting transfers between devices: 23.2 us -> 24.4 us
  local copies, waits for them, and re-layouts: 7.19 us -> 6.37 us
    ppermute x1, waiting for transfers between devices: 0.01 us -> 6.56 us  [on_device(): lax.ppermute(jnp.concatenate(kv, axis=0), 'seq', pair_perm(n_seq, bit))]
    ppermute x1, waiting for transfers between devices: 5.15 us -> 0.01 us  [on_device(): lax.ppermute(both, ('island', 'seq'), far_pairs(n_island, n_seq, k))]
    ppermute x2, waiting for transfers between devices: 0.01 us -> 3.55 us  [the longest x1 3.04 us: on_device(): near = lax.ppermute(near, 'seq', pair_perm(n_seq, 1))]
    ppermute x3, waiting for transfers between devices: 13.3 us -> 10 us  [on_device(): spread[step] = lax.ppermute(held, 'island', pair_perm(n_chip, step, 2))]
    ppermute x1, waiting for transfers between devices: 2.07 us -> 4 us  [on_device(): lax.ppermute(held, 'seq', pair_perm(n_seq, bit))]
    ppermute x1, waiting for transfers between devices: 2.41 us -> 3.91 us  [on_device(): held = jnp.concatenate([weight, lax.ppermute(weight, 'seq', far_perm)], 0)]
    ppermute x3, starting transfers between devices: 3.49 us -> 4.91 us  [on_device(): lax.ppermute(dquery, 'seq', pair_perm(n_seq, k))]
    ppermute x3, waiting for transfers between devices: 4.36 us -> 3.02 us  [on_device(): lax.ppermute(dquery, 'seq', pair_perm(n_seq, k))]
  transfers between devices with their start and end apart: 19 -> 19, of which waited for: 11 -> 13; matrix products, arithmetic and copies ran while one was open for 12% -> 10% of each run, Pallas kernels for 4% -> 4%
where the time goes in v10:
time: 72.9 us; the launch traced here: 72.7 us
  waiting for transfers between devices  35.4 us (49%)
  starting transfers between devices  24.4 us (33%)
  local copies, waits for them, and re-layouts  6.37 us (9%)
  Pallas kernels  3.58 us (5%)
  other arithmetic  2.03 us (3%)
  between operations  0.82 us (1%)
    ppermute x3, waiting for transfers between devices, on_device(): spread[step] = lax.ppermute(held, 'island', pair_perm(n_chip, step, 2))  10 us
    ppermute x1, waiting for transfers between devices, on_device(): lax.ppermute(jnp.concatenate(kv, axis=0), 'seq', pair_perm(n_seq, bit))  6.56 us
    ppermute x3, starting transfers between devices, on_device(): lax.ppermute(dquery, 'seq', pair_perm(n_seq, k))  4.91 us
    ppermute x1, waiting for transfers between devices, on_device(): lax.ppermute(held, 'seq', pair_perm(n_seq, bit))  4 us
    ppermute x1, waiting for transfers between devices, on_device(): held = jnp.concatenate([weight, lax.ppermute(weight, 'seq', far_perm)], 0)  3.91 us
    ppermute x1, starting transfers between devices, on_device(): held = jnp.concatenate([weight, lax.ppermute(weight, 'seq', far_perm)], 0)  3.67 us
    ppermute x3, starting transfers between devices, on_device(): spread[step] = lax.ppermute(held, 'island', pair_perm(n_chip, step, 2))  3.55 us
    ppermute x3, starting transfers between devices, on_device(): lax.ppermute(parts[step], 'island', pair_perm(n_chip, step, 2))  3.55 us
  transfers between devices with their start and end apart: 19, of which 13 were waited for; matrix products, arithmetic and copies ran while one was open for 10% of the time, Pallas kernels for 4%

profile of v10, /device:TPU:0, one launch (start us, length us, event | category | flops | bytes accessed | tf_op | source)
XLA Modules:
  0.0 72.7 jit_solution(13494749770321372241)
XLA Ops:
  0.6 0.5 collective-permute-start
  1.1 0.9 %convert_bitcast_fusion = bf16[32,1280]{1,0:T(8,128)(2,1)S(1)} fusion(f32[1280,32]{0,1:T(8,128)} %param.12), kind=kLoop, calls=%fused_computation.20 | loop fusion | flops 40960 | bytes 245760 | tf_op jit(solution)/shard_map/convert_element_type | solution.py:270
  2.1 3.7 %collective-permute-start.3 = (bf16[32,1280]{1,0:T(8,128)(2,1)S(1)}, bf16[32,1280]{1,0:T(8,128)(2,1)S(1)}, u32[]{:S(2)}, u32[]{:S(2)}) collective-permute-start(bf16[32,1280]{1,0:T(8,128)(2,1)S(1)} %convert_bitcast_fusion), channel_id=1, source_target_pairs={{0,2},{1,3},{2,0},{3,1},{4,6},{5,7},{6,4},{7,5},{8,10},{9,11},{10,... | collective-permute-start | bytes 245768 | tf_op jit(solution)/shard_map/ppermute | solution.py:271
  5.7 0.9 %copy.19 = bf16[16,8,2,256]{3,1,2,0:T(8,128)(2,1)S(1)} copy(bf16[16,8,2,256]{3,2,1,0:T(2,128)(2,1)} %bitcast.65) | data formatting | bytes 262144
  6.7 0.1 collective-permute-start.1
  6.8 3.9 %collective-permute-done.3 = bf16[32,1280]{1,0:T(8,128)(2,1)S(1)} collective-permute-done((bf16[32,1280]{1,0:T(8,128)(2,1)S(1)}, bf16[32,1280]{1,0:T(8,128)(2,1)S(1)}, u32[]{:S(2)}, u32[]{:S(2)}) %collective-permute-start.3) | collective-permute-done | bytes 81952 | tf_op jit(solution)/shard_map/ppermute | solution.py:271
  10.7 3.5 %collective-permute-start.4 = (bf16[64,1280]{1,0:T(8,128)(2,1)S(1)}, bf16[64,1280]{1,0:T(8,128)(2,1)S(1)}, u32[]{:S(2)}, u32[]{:S(2)}) collective-permute-start(bf16[64,1280]{1,0:T(8,128)(2,1)S(1)} %pad_maximum_fusion.5), channel_id=1, source_target_pairs={{0,1},{1,0},{2,3},{3,2},{4,5},{5,4},{6,7},{7,6},{8,9},{9,8},{10,11... | collective-permute-start | bytes 491528 | tf_op jit(solution)/shard_map/ppermute | solution.py:286
  14.2 1.5 %dynamic-slice_bitcast_fusion = (bf16[128,1280]{1,0:T(8,128)(2,1)S(1)}, bf16[128,1280]{1,0:T(8,128)(2,1)S(1)}, bf16[128,1280]{1,0:T(8,128)(2,1)S(1)}, bf16[128,1280]{1,0:T(8,128)(2,1)S(1)}, bf16[128,1280]{1,0:T(8,128)(2,1)S(1)}) fusion(bf16[1,128,5120]{2,1,0:T(8,128)(2,1)} %param.7, s32[]{:T(128)S(6)} %select_n.44, s32[]{:T(128)S(6)} %select_n.42, ...), kind=kLoop, calls=%fused_computation.8 | loop fusion | bytes 3276820 | tf_op jit(solution)/shard_map/dynamic_slice | solution.py:276
  15.7 4.0 %collective-permute-done.4 = bf16[64,1280]{1,0:T(8,128)(2,1)S(1)} collective-permute-done((bf16[64,1280]{1,0:T(8,128)(2,1)S(1)}, bf16[64,1280]{1,0:T(8,128)(2,1)S(1)}, u32[]{:S(2)}, u32[]{:S(2)}) %collective-permute-start.4) | collective-permute-done | bytes 163872 | tf_op jit(solution)/shard_map/ppermute | solution.py:286
  19.8 1.6 %collective-permute-start.5 = (bf16[128,1280]{1,0:T(8,128)(2,1)S(1)}, bf16[128,1280]{1,0:T(8,128)(2,1)S(1)}, u32[]{:S(2)}, u32[]{:S(2)}) collective-permute-start(bf16[128,1280]{1,0:T(8,128)(2,1)S(1)} %pad_maximum_fusion.3.refs_0_), channel_id=1, source_target_pairs={{0,8},{4,12},{8,0},{12,4},{16,24},{20,28},{24,16},{28,20},{1,9},{5... | collective-permute-start | bytes 983048 | tf_op jit(solution)/shard_map/ppermute | solution.py:292
  21.4 1.5 %collective-permute-start.6 = (bf16[128,1280]{1,0:T(8,128)(2,1)S(1)}, bf16[128,1280]{1,0:T(8,128)(2,1)S(1)}, u32[]{:S(2)}, u32[]{:S(2)}) collective-permute-start(bf16[128,1280]{1,0:T(8,128)(2,1)S(1)} %pad_maximum_fusion.3.refs_0_), channel_id=1, source_target_pairs={{0,16},{4,20},{8,24},{12,28},{16,0},{20,4},{24,8},{28,12},{1,17},{... | collective-permute-start | bytes 983048 | tf_op jit(solution)/shard_map/ppermute | solution.py:292
  22.9 0.4 collective-permute-start.7
  23.3 0.1 constant_dynamic-slice_fusion
  23.5 2.4 %collective-permute-start.13 = (bf16[256,1280]{1,0:T(8,128)(2,1)S(1)}, bf16[256,1280]{1,0:T(8,128)(2,1)S(1)}, u32[]{:S(2)}, u32[]{:S(2)}) collective-permute-start(bf16[256,1280]{1,0:T(8,128)(2,1)S(1)} %pad_maximum_fusion), channel_id=1, source_target_pairs={{0,2},{1,3},{2,0},{3,1},{4,7},{5,6},{6,5},{7,4},{8,10},{9,11},{10,... | collective-permute-start | bytes 1966088 | tf_op jit(solution)/shard_map/ppermute | solution.py:282
  25.9 1.9 %collective-permute-start.2 = (bf16[256,512]{1,0:T(8,128)(2,1)S(1)}, bf16[256,512]{1,0:T(8,128)(2,1)S(1)}, u32[]{:S(2)}, u32[]{:S(2)}) collective-permute-start(bf16[256,512]{1,0:T(8,128)(2,1)S(1)} %pad_maximum_fusion.4), channel_id=1, source_target_pairs={{0,1},{1,0},{2,3},{3,2},{4,5},{5,4},{6,7},{7,6},{8,9},{9,8},{10,11... | collective-permute-start | bytes 786440 | tf_op jit(solution)/shard_map/ppermute | solution.py:287
  27.8 2.6 %collective-permute-done.5.refs_1_ = bf16[128,1280]{1,0:T(8,128)(2,1)S(1)} collective-permute-done((bf16[128,1280]{1,0:T(8,128)(2,1)S(1)}, bf16[128,1280]{1,0:T(8,128)(2,1)S(1)}, u32[]{:S(2)}, u32[]{:S(2)}) %collective-permute-start.5) | collective-permute-done | bytes 327712 | tf_op jit(solution)/shard_map/ppermute | solution.py:292
  30.4 7.4 %collective-permute-done.6.refs_2_ = bf16[128,1280]{1,0:T(8,128)(2,1)S(1)} collective-permute-done((bf16[128,1280]{1,0:T(8,128)(2,1)S(1)}, bf16[128,1280]{1,0:T(8,128)(2,1)S(1)}, u32[]{:S(2)}, u32[]{:S(2)}) %collective-permute-start.6) | collective-permute-done | bytes 327712 | tf_op jit(solution)/shard_map/ppermute | solution.py:292
  37.8 1.0 %shard_map.102 = (bf16[4,32,128]{2,1,0:T(8,128)(2,1)S(1)}, bf16[4,32,128]{2,1,0:T(8,128)(2,1)S(1)}) custom-call(bf16[128,1280]{1,0:T(8,128)(2,1)S(1)} %pad_maximum_fusion.3.refs_0_, bf16[128,1280]{1,0:T(8,128)(2,1)S(1)} %collective-permute-done.5.refs_1_, bf16[128,1280]{1,0:T(8,128)(2,1)S(1)} %collective-permute-done.6.refs_2_, ...), custom_call_target="tpu_custom_call" | custom-call | flops 335544320 | bytes 3932160 | tf_op jit(solution)/shard_map/pallas_call | solution.py:84
  38.8 0.0 copy-start.1
  38.8 0.1 collective-permute-start.12
  38.8 0.1 collective-permute-start.8
  38.9 1.2 %collective-permute-done.8.refs_7_ = bf16[4,32,128]{2,1,0:T(8,128)(2,1)S(1)} collective-permute-done((bf16[4,32,128]{2,1,0:T(8,128)(2,1)S(1)}, bf16[4,32,128]{2,1,0:T(8,128)(2,1)S(1)}, u32[]{:S(2)}, u32[]{:S(2)}) %collective-permute-start.8) | collective-permute-done | bytes 32800 | tf_op jit(solution)/shard_map/ppermute | solution.py:298
  40.1 6.6 %collective-permute-done.2.refs_4_.refs_5_ = bf16[256,512]{1,0:T(8,128)(2,1)S(1)} collective-permute-done((bf16[256,512]{1,0:T(8,128)(2,1)S(1)}, bf16[256,512]{1,0:T(8,128)(2,1)S(1)}, u32[]{:S(2)}, u32[]{:S(2)}) %collective-permute-start.2) | collective-permute-done | bytes 262176 | tf_op jit(solution)/shard_map/ppermute | solution.py:287
  46.7 1.2 %shard_map.103.refs_0_ = bf16[256,128]{1,0:T(8,128)(2,1)S(1)} custom-call(bf16[128,512]{1,0:T(8,128)(2,1)S(1)} %bitcast.57, bf16[128,512]{1,0:T(8,128)(2,1)S(1)} %bitcast.58, bf16[128,512]{1,0:T(8,128)(2,1)S(1)} %collective-permute-done.1.refs_2_.refs_3_, bf16[128,512]{1,0:T(8,128)(2,1)S(1)} %collective-permute-done.1.refs_2_.refs_3_, ...), custom_call_target="tpu_custom_call" | custom-call | flops 402653184 | bytes 786432 | tf_op jit(solution)/shard_map/pallas_call | solution.py:164
  47.9 2.4 %collective-permute-start.10 = (bf16[256,128]{1,0:T(8,128)(2,1)S(1)}, bf16[256,128]{1,0:T(8,128)(2,1)S(1)}, u32[]{:S(2)}, u32[]{:S(2)}) collective-permute-start(bf16[256,128]{1,0:T(8,128)(2,1)S(1)} %shard_map.103.refs_0_), channel_id=1, source_target_pairs={{0,2},{1,3},{2,0},{3,1},{4,6},{5,7},{6,4},{7,5},{8,10},{9,11},{10,... | collective-permute-start | bytes 196616 | tf_op jit(solution)/shard_map/ppermute | solution.py:302
  50.3 2.6 %collective-permute-start.11 = (bf16[256,128]{1,0:T(8,128)(2,1)S(1)}, bf16[256,128]{1,0:T(8,128)(2,1)S(1)}, u32[]{:S(2)}, u32[]{:S(2)}) collective-permute-start(bf16[256,128]{1,0:T(8,128)(2,1)S(1)} %shard_map.103.refs_0_), channel_id=1, source_target_pairs={{0,3},{1,2},{2,1},{3,0},{4,7},{5,6},{6,5},{7,4},{8,11},{9,10},{10,... | collective-permute-start | bytes 196616 | tf_op jit(solution)/shard_map/ppermute | solution.py:302
  52.8 3.0 %collective-permute-done.12.refs_5_ = bf16[128,1280]{1,0:T(8,128)(2,1)S(1)} collective-permute-done((bf16[128,1280]{1,0:T(8,128)(2,1)S(1)}, bf16[128,1280]{1,0:T(8,128)(2,1)S(1)}, u32[]{:S(2)}, u32[]{:S(2)}) %collective-permute-start.12) | collective-permute-done | bytes 327712 | tf_op jit(solution)/shard_map/ppermute | solution.py:299
  55.9 2.6 %collective-permute-done.10.refs_2_ = bf16[256,128]{1,0:T(8,128)(2,1)S(1)} collective-permute-done((bf16[256,128]{1,0:T(8,128)(2,1)S(1)}, bf16[256,128]{1,0:T(8,128)(2,1)S(1)}, u32[]{:S(2)}, u32[]{:S(2)}) %collective-permute-start.10) | collective-permute-done | bytes 65568 | tf_op jit(solution)/shard_map/ppermute | solution.py:302
  58.5 0.4 collective-permute-done.9.refs_1_
  58.9 0.2 copy.13
  59.2 1.3 %copy.14 = bf16[256,1280]{1,0:T(8,128)(2,1)S(1)} copy(bf16[256,1280]{0,1:T(8,128)(2,1)} %bitcast.64) | data formatting | bytes 1310720 | tf_op jit(solution)/shard_map/transpose | solution.py:310
  60.5 0.5 collective-permute-done.14.refs_7_
  61.0 0.7 shard_map.105
  61.7 0.2 collective-permute-start.15
  61.9 0.7 shard_map.104
  62.5 0.1 select_bitcast_fusion.1
  62.6 0.1 pad_maximum_fusion.2
  62.7 0.7 collective-permute-done.15.got_ref
  63.4 0.1 shard_map.106
  63.4 1.6 %collective-permute-start.16 = (bf16[32,1280]{1,0:T(8,128)(2,1)S(1)}, bf16[32,1280]{1,0:T(8,128)(2,1)S(1)}, u32[]{:S(2)}, u32[]{:S(2)}) collective-permute-start(bf16[32,1280]{1,0:T(8,128)(2,1)S(1)} %get-tuple-element.35), channel_id=1, source_target_pairs={{0,8},{4,12},{8,0},{12,4},{16,24},{20,28},{24,16},{28,20},{1,9},{5... | collective-permute-start | bytes 245768 | tf_op jit(solution)/shard_map/ppermute | solution.py:327
  65.0 1.5 %collective-permute-start.17 = (bf16[32,1280]{1,0:T(8,128)(2,1)S(1)}, bf16[32,1280]{1,0:T(8,128)(2,1)S(1)}, u32[]{:S(2)}, u32[]{:S(2)}) collective-permute-start(bf16[32,1280]{1,0:T(8,128)(2,1)S(1)} %get-tuple-element.36), channel_id=1, source_target_pairs={{0,16},{4,20},{8,24},{12,28},{16,0},{20,4},{24,8},{28,12},{1,17},{... | collective-permute-start | bytes 245768 | tf_op jit(solution)/shard_map/ppermute | solution.py:327
  66.5 0.5 collective-permute-start.18
  67.0 0.1 pad_maximum_fusion.1
  67.1 1.1 %copy.18 = bf16[1,1280,256]{2,1,0:T(8,128)(2,1)} copy(bf16[1,1280,256]{1,2,0:T(8,128)(2,1)S(1)} %bitcast.60) | data formatting | bytes 1310720
  68.2 1.1 %copy.17 = bf16[1,1280,256]{2,1,0:T(8,128)(2,1)} copy(bf16[1,1280,256]{1,2,0:T(8,128)(2,1)S(1)} %bitcast.61) | data formatting | bytes 1310720
  69.3 0.9 %collective-permute-done.17 = bf16[32,1280]{1,0:T(8,128)(2,1)S(1)} collective-permute-done((bf16[32,1280]{1,0:T(8,128)(2,1)S(1)}, bf16[32,1280]{1,0:T(8,128)(2,1)S(1)}, u32[]{:S(2)}, u32[]{:S(2)}) %collective-permute-start.17) | collective-permute-done | bytes 81952 | tf_op jit(solution)/shard_map/ppermute | solution.py:327
  70.3 1.6 %collective-permute-done.18 = bf16[32,1280]{1,0:T(8,128)(2,1)S(1)} collective-permute-done((bf16[32,1280]{1,0:T(8,128)(2,1)S(1)}, bf16[32,1280]{1,0:T(8,128)(2,1)S(1)}, u32[]{:S(2)}, u32[]{:S(2)}) %collective-permute-start.18) | collective-permute-done | bytes 81952 | tf_op jit(solution)/shard_map/ppermute | solution.py:327
  71.9 0.8 %fusion.1 = (f32[1280,32]{0,1:T(8,128)}, f32[1280,32]{0,1:T(8,128)}) fusion(f32[1280,32]{0,1:T(8,128)S(1)} %copy-done.2, bf16[32,1280]{1,0:T(8,128)(2,1)S(1)} %collective-permute-done.18, bf16[32,1280]{1,0:T(8,128)(2,1)S(1)} %collective-permute-done.17, f32[32,1280]{1,0:T(8,128)S(1)} %get-tuple-element.34, bf16[32,1280]{1,0:T(8,128)(2,1)S(1)} %collective-permute-done.16, ...), kind=kLoop, calls=%fused_computation.18 | loop fusion | flops 532480 | bytes 1064960 | tf_op jit(solution)/shard_map/sub | solution.py:332
  (21 shorter events, 0.2 us)
Async XLA Ops:
  0.6 22.7 %collective-permute-start = (bf16[128,5120]{1,0:T(8,128)(2,1)}, bf16[128,5120]{1,0:T(8,128)(2,1)S(1)}, u32[]{:S(2)}, u32[]{:S(2)}) collective-permute-start(bf16[128,5120]{1,0:T(8,128)(2,1)} %bitcast.62), channel_id=1, source_target_pairs={{0,4},{4,0},{8,12},{12,8},{16,20},{20,16},{24,28},{28,24},{1,5},{5... | collective-permute-start | bytes 3932168 | tf_op jit(solution)/shard_map/ppermute | solution.py:269
  2.1 8.6 %collective-permute-start.3 = (bf16[32,1280]{1,0:T(8,128)(2,1)S(1)}, bf16[32,1280]{1,0:T(8,128)(2,1)S(1)}, u32[]{:S(2)}, u32[]{:S(2)}) collective-permute-start(bf16[32,1280]{1,0:T(8,128)(2,1)S(1)} %convert_bitcast_fusion), channel_id=1, source_target_pairs={{0,2},{1,3},{2,0},{3,1},{4,6},{5,7},{6,4},{7,5},{8,10},{9,11},{10,... | collective-permute-start | bytes 245768 | tf_op jit(solution)/shard_map/ppermute | solution.py:271
  6.7 16.9 %collective-permute-start.1 = (bf16[128,512]{1,0:T(8,128)(2,1)S(1)}, bf16[128,512]{1,0:T(8,128)(2,1)S(1)}, u32[]{:S(2)}, u32[]{:S(2)}) collective-permute-start(bf16[128,512]{1,0:T(8,128)(2,1)S(1)} %bitcast.55), channel_id=1, source_target_pairs={{0,2},{1,3},{2,0},{3,1},{4,6},{5,7},{6,4},{7,5},{8,10},{9,11},{10,... | collective-permute-start | bytes 393224 | tf_op jit(solution)/shard_map/ppermute | solution.py:273
  10.7 9.0 %collective-permute-start.4 = (bf16[64,1280]{1,0:T(8,128)(2,1)S(1)}, bf16[64,1280]{1,0:T(8,128)(2,1)S(1)}, u32[]{:S(2)}, u32[]{:S(2)}) collective-permute-start(bf16[64,1280]{1,0:T(8,128)(2,1)S(1)} %pad_maximum_fusion.5), channel_id=1, source_target_pairs={{0,1},{1,0},{2,3},{3,2},{4,5},{5,4},{6,7},{7,6},{8,9},{9,8},{10,11... | collective-permute-start | bytes 491528 | tf_op jit(solution)/shard_map/ppermute | solution.py:286
  19.8 10.6 %collective-permute-start.5 = (bf16[128,1280]{1,0:T(8,128)(2,1)S(1)}, bf16[128,1280]{1,0:T(8,128)(2,1)S(1)}, u32[]{:S(2)}, u32[]{:S(2)}) collective-permute-start(bf16[128,1280]{1,0:T(8,128)(2,1)S(1)} %pad_maximum_fusion.3.refs_0_), channel_id=1, source_target_pairs={{0,8},{4,12},{8,0},{12,4},{16,24},{20,28},{24,16},{28,20},{1,9},{5... | collective-permute-start | bytes 983048 | tf_op jit(solution)/shard_map/ppermute | solution.py:292
  21.4 16.4 %collective-permute-start.6 = (bf16[128,1280]{1,0:T(8,128)(2,1)S(1)}, bf16[128,1280]{1,0:T(8,128)(2,1)S(1)}, u32[]{:S(2)}, u32[]{:S(2)}) collective-permute-start(bf16[128,1280]{1,0:T(8,128)(2,1)S(1)} %pad_maximum_fusion.3.refs_0_), channel_id=1, source_target_pairs={{0,16},{4,20},{8,24},{12,28},{16,0},{20,4},{24,8},{28,12},{1,17},{... | collective-permute-start | bytes 983048 | tf_op jit(solution)/shard_map/ppermute | solution.py:292
  22.9 14.9 %collective-permute-start.7 = (bf16[128,1280]{1,0:T(8,128)(2,1)S(1)}, bf16[128,1280]{1,0:T(8,128)(2,1)S(1)}, u32[]{:S(2)}, u32[]{:S(2)}) collective-permute-start(bf16[128,1280]{1,0:T(8,128)(2,1)S(1)} %pad_maximum_fusion.3.refs_0_), channel_id=1, source_target_pairs={{0,24},{4,28},{8,16},{12,20},{16,8},{20,12},{24,0},{28,4},{1,25},{... | collective-permute-start | bytes 983048 | tf_op jit(solution)/shard_map/ppermute | solution.py:292
  23.5 35.4 %collective-permute-start.13 = (bf16[256,1280]{1,0:T(8,128)(2,1)S(1)}, bf16[256,1280]{1,0:T(8,128)(2,1)S(1)}, u32[]{:S(2)}, u32[]{:S(2)}) collective-permute-start(bf16[256,1280]{1,0:T(8,128)(2,1)S(1)} %pad_maximum_fusion), channel_id=1, source_target_pairs={{0,2},{1,3},{2,0},{3,1},{4,7},{5,6},{6,5},{7,4},{8,10},{9,11},{10,... | collective-permute-start | bytes 1966088 | tf_op jit(solution)/shard_map/ppermute | solution.py:282
  25.9 20.8 %collective-permute-start.2 = (bf16[256,512]{1,0:T(8,128)(2,1)S(1)}, bf16[256,512]{1,0:T(8,128)(2,1)S(1)}, u32[]{:S(2)}, u32[]{:S(2)}) collective-permute-start(bf16[256,512]{1,0:T(8,128)(2,1)S(1)} %pad_maximum_fusion.4), channel_id=1, source_target_pairs={{0,1},{1,0},{2,3},{3,2},{4,5},{5,4},{6,7},{7,6},{8,9},{9,8},{10,11... | collective-permute-start | bytes 786440 | tf_op jit(solution)/shard_map/ppermute | solution.py:287
  37.8 8.9 %copy-start = (bf16[1,128,256]{2,1,0:T(8,128)(2,1)S(1)}, bf16[1,128,256]{2,1,0:T(8,128)(2,1)}, u32[]{:S(2)}) copy-start(bf16[1,128,256]{2,1,0:T(8,128)(2,1)} %param.9) | copy-start | bytes 196612
  38.8 20.2 %copy-start.1 = (bf16[1,1280,256]{2,1,0:T(8,128)(2,1)S(1)}, bf16[1,1280,256]{2,1,0:T(8,128)(2,1)}, u32[]{:S(2)}) copy-start(bf16[1,1280,256]{2,1,0:T(8,128)(2,1)} %param.10) | copy-start | bytes 1966084
  38.8 17.1 %collective-permute-start.12 = (bf16[128,1280]{1,0:T(8,128)(2,1)S(1)}, bf16[128,1280]{1,0:T(8,128)(2,1)S(1)}, u32[]{:S(2)}, u32[]{:S(2)}) collective-permute-start(bf16[128,1280]{1,0:T(8,128)(2,1)S(1)} %get-tuple-element.28.refs_5_), channel_id=1, source_target_pairs={{0,1},{1,0},{2,3},{3,2},{4,5},{5,4},{6,7},{7,6},{8,9},{9,8},{10,11... | collective-permute-start | bytes 983048 | tf_op jit(solution)/shard_map/ppermute | solution.py:299
  38.8 1.3 %collective-permute-start.8 = (bf16[4,32,128]{2,1,0:T(8,128)(2,1)S(1)}, bf16[4,32,128]{2,1,0:T(8,128)(2,1)S(1)}, u32[]{:S(2)}, u32[]{:S(2)}) collective-permute-start(bf16[4,32,128]{2,1,0:T(8,128)(2,1)S(1)} %get-tuple-element.27), channel_id=1, source_target_pairs={{0,4},{4,0},{8,12},{12,8},{16,20},{20,16},{24,28},{28,24},{1,5},{5... | collective-permute-start | bytes 98312 | tf_op jit(solution)/shard_map/ppermute | solution.py:298
  47.9 10.5 %collective-permute-start.10 = (bf16[256,128]{1,0:T(8,128)(2,1)S(1)}, bf16[256,128]{1,0:T(8,128)(2,1)S(1)}, u32[]{:S(2)}, u32[]{:S(2)}) collective-permute-start(bf16[256,128]{1,0:T(8,128)(2,1)S(1)} %shard_map.103.refs_0_), channel_id=1, source_target_pairs={{0,2},{1,3},{2,0},{3,1},{4,6},{5,7},{6,4},{7,5},{8,10},{9,11},{10,... | collective-permute-start | bytes 196616 | tf_op jit(solution)/shard_map/ppermute | solution.py:302
  50.3 8.2 %collective-permute-start.11 = (bf16[256,128]{1,0:T(8,128)(2,1)S(1)}, bf16[256,128]{1,0:T(8,128)(2,1)S(1)}, u32[]{:S(2)}, u32[]{:S(2)}) collective-permute-start(bf16[256,128]{1,0:T(8,128)(2,1)S(1)} %shard_map.103.refs_0_), channel_id=1, source_target_pairs={{0,3},{1,2},{2,1},{3,0},{4,7},{5,6},{6,5},{7,4},{8,11},{9,10},{10,... | collective-permute-start | bytes 196616 | tf_op jit(solution)/shard_map/ppermute | solution.py:302
  52.8 6.1 %collective-permute-start.9 = (bf16[256,128]{1,0:T(8,128)(2,1)S(1)}, bf16[256,128]{1,0:T(8,128)(2,1)S(1)}, u32[]{:S(2)}, u32[]{:S(2)}) collective-permute-start(bf16[256,128]{1,0:T(8,128)(2,1)S(1)} %shard_map.103.refs_0_), channel_id=1, source_target_pairs={{0,1},{1,0},{2,3},{3,2},{4,5},{5,4},{6,7},{7,6},{8,9},{9,8},{10,11... | collective-permute-start | bytes 196616 | tf_op jit(solution)/shard_map/ppermute | solution.py:302
  58.9 2.1 %collective-permute-start.14 = (bf16[256,1280]{1,0:T(8,128)(2,1)S(1)}, bf16[256,1280]{1,0:T(8,128)(2,1)S(1)}, u32[]{:S(2)}, u32[]{:S(2)}) collective-permute-start(bf16[256,1280]{1,0:T(8,128)(2,1)S(1)} %collective-permute-done.13.refs_6_), channel_id=1, source_target_pairs={{0,4},{4,0},{8,12},{12,8},{16,20},{20,16},{24,28},{28,24},{1,5},{5... | collective-permute-start | bytes 1966088 | tf_op jit(solution)/shard_map/ppermute | solution.py:308
  61.7 1.7 %collective-permute-start.15 = (bf16[4,32,1280]{2,1,0:T(8,128)(2,1)S(1)}, bf16[4,32,1280]{2,1,0:T(8,128)(2,1)S(1)}, u32[]{:S(2)}, u32[]{:S(2)}) collective-permute-start(bf16[4,32,1280]{2,1,0:T(8,128)(2,1)S(1)} %get-tuple-element.33), channel_id=1, source_target_pairs={{0,4},{4,0},{8,12},{12,8},{16,20},{20,16},{24,28},{28,24},{1,5},{5... | collective-permute-start | bytes 983048 | tf_op jit(solution)/shard_map/ppermute | solution.py:314
  63.4 5.9 %collective-permute-start.16 = (bf16[32,1280]{1,0:T(8,128)(2,1)S(1)}, bf16[32,1280]{1,0:T(8,128)(2,1)S(1)}, u32[]{:S(2)}, u32[]{:S(2)}) collective-permute-start(bf16[32,1280]{1,0:T(8,128)(2,1)S(1)} %get-tuple-element.35), channel_id=1, source_target_pairs={{0,8},{4,12},{8,0},{12,4},{16,24},{20,28},{24,16},{28,20},{1,9},{5... | collective-permute-start | bytes 245768 | tf_op jit(solution)/shard_map/ppermute | solution.py:327
  65.0 5.3 %collective-permute-start.17 = (bf16[32,1280]{1,0:T(8,128)(2,1)S(1)}, bf16[32,1280]{1,0:T(8,128)(2,1)S(1)}, u32[]{:S(2)}, u32[]{:S(2)}) collective-permute-start(bf16[32,1280]{1,0:T(8,128)(2,1)S(1)} %get-tuple-element.36), channel_id=1, source_target_pairs={{0,16},{4,20},{8,24},{12,28},{16,0},{20,4},{24,8},{28,12},{1,17},{... | collective-permute-start | bytes 245768 | tf_op jit(solution)/shard_map/ppermute | solution.py:327
  66.5 5.3 %collective-permute-start.18 = (bf16[32,1280]{1,0:T(8,128)(2,1)S(1)}, bf16[32,1280]{1,0:T(8,128)(2,1)S(1)}, u32[]{:S(2)}, u32[]{:S(2)}) collective-permute-start(bf16[32,1280]{1,0:T(8,128)(2,1)S(1)} %get-tuple-element.37), channel_id=1, source_target_pairs={{0,24},{4,28},{8,16},{12,20},{16,8},{20,12},{24,0},{28,4},{1,25},{... | collective-permute-start | bytes 245768 | tf_op jit(solution)/shard_map/ppermute | solution.py:327
  68.2 3.7 %copy-start.2 = (f32[1280,32]{0,1:T(8,128)S(1)}, f32[1280,32]{0,1:T(8,128)}, u32[]{:S(2)}) copy-start(f32[1280,32]{0,1:T(8,128)} %param.12) | copy-start | bytes 491524
  68.2 3.7 %copy-start.3 = (f32[1280,32]{0,1:T(8,128)S(1)}, f32[1280,32]{0,1:T(8,128)}, u32[]{:S(2)}) copy-start(f32[1280,32]{0,1:T(8,128)} %param.13) | copy-start | bytes 491524

commit v11 on v10

--- a/solution.py
+++ b/solution.py
@@ -294,7 +294,7 @@
     mine, for_partner = half_queries(
         rounds, [spread], own_blocks, partner_blocks, share, inverse
     )
-    near, for_partner = lax.optimization_barrier((own_blocks[1], for_partner))
+    near, kv = lax.optimization_barrier((own_blocks[1], kv))
     other = lax.ppermute(for_partner, "island", swap)
     near = lax.ppermute(near, "seq", pair_perm(n_seq, 1))
     dquery = attention(kv, order, mine, other, cotangent[0])

time: 72.9 us -> 68.1 us (0.934)
  waiting for transfers between devices: 35.4 us -> 32.2 us
  starting transfers between devices: 24.4 us -> 22.9 us
    ppermute x3, waiting for transfers between devices: 3.02 us -> 9.22 us  [on_device(): lax.ppermute(dquery, 'seq', pair_perm(n_seq, k))]
    ppermute x1, waiting for transfers between devices: 4 us -> 0.01 us  [on_device(): lax.ppermute(held, 'seq', pair_perm(n_seq, bit))]
    ppermute x1, waiting for transfers between devices: 3.04 us -> 0.01 us  [on_device(): near = lax.ppermute(near, 'seq', pair_perm(n_seq, 1))]
    ppermute x1, waiting for transfers between devices: 0.01 us -> 1.87 us  [on_device(): kv.append(lax.ppermute(kv[0], 'seq', far_perm))]
    ppermute x3, waiting for transfers between devices: 10 us -> 8.42 us  [on_device(): spread[step] = lax.ppermute(held, 'island', pair_perm(n_chip, step, 2))]
    ppermute x1, waiting for transfers between devices: 3.91 us -> 2.41 us  [on_device(): held = jnp.concatenate([weight, lax.ppermute(weight, 'seq', far_perm)], 0)]
    ppermute x3, starting transfers between devices: 4.91 us -> 3.55 us  [on_device(): lax.ppermute(dquery, 'seq', pair_perm(n_seq, k))]
    ppermute x1, waiting for transfers between devices: 6.56 us -> 5.36 us  [on_device(): lax.ppermute(jnp.concatenate(kv, axis=0), 'seq', pair_perm(n_seq, bit))]
  transfers between devices with their start and end apart: 19 -> 19, of which waited for: 13 -> 11; matrix products, arithmetic and copies ran while one was open for 10% -> 11% of each run, Pallas kernels for 4% -> 4%
where the time goes in v11:
time: 68.1 us; the launch traced here: 67.9 us
  waiting for transfers between devices  32.2 us (47%)
  starting transfers between devices  22.9 us (34%)
  local copies, waits for them, and re-layouts  6.39 us (9%)
  Pallas kernels  3.58 us (5%)
  other arithmetic  2.03 us (3%)
  between operations  0.83 us (1%)
    ppermute x3, waiting for transfers between devices, on_device(): lax.ppermute(dquery, 'seq', pair_perm(n_seq, k))  9.22 us
    ppermute x3, waiting for transfers between devices, on_device(): spread[step] = lax.ppermute(held, 'island', pair_perm(n_chip, step, 2))  8.42 us
    ppermute x1, waiting for transfers between devices, on_device(): lax.ppermute(jnp.concatenate(kv, axis=0), 'seq', pair_perm(n_seq, bit))  5.36 us
    ppermute x1, starting transfers between devices, on_device(): held = jnp.concatenate([weight, lax.ppermute(weight, 'seq', far_perm)], 0)  3.67 us
    ppermute x3, starting transfers between devices, on_device(): lax.ppermute(dquery, 'seq', pair_perm(n_seq, k))  3.55 us
    ppermute x3, starting transfers between devices, on_device(): spread[step] = lax.ppermute(held, 'island', pair_perm(n_chip, step, 2))  3.55 us
    ppermute x3, starting transfers between devices, on_device(): lax.ppermute(parts[step], 'island', pair_perm(n_chip, step, 2))  3.55 us
    ppermute x1, starting transfers between devices, on_device(): lax.ppermute(held, 'seq', pair_perm(n_seq, bit))  3.54 us
  transfers between devices with their start and end apart: 19, of which 11 were waited for; matrix products, arithmetic and copies ran while one was open for 11% of the time, Pallas kernels for 4%

profile of v11, /device:TPU:0, one launch (start us, length us, event | category | flops | bytes accessed | tf_op | source)
XLA Modules:
  0.0 67.9 jit_solution(14984921819116905624)
XLA Ops:
  0.6 0.5 collective-permute-start
  1.1 0.9 %convert_bitcast_fusion = bf16[32,1280]{1,0:T(8,128)(2,1)S(1)} fusion(f32[1280,32]{0,1:T(8,128)} %param.12), kind=kLoop, calls=%fused_computation.20 | loop fusion | flops 40960 | bytes 245760 | tf_op jit(solution)/shard_map/convert_element_type | solution.py:270
  2.1 3.7 %collective-permute-start.3 = (bf16[32,1280]{1,0:T(8,128)(2,1)S(1)}, bf16[32,1280]{1,0:T(8,128)(2,1)S(1)}, u32[]{:S(2)}, u32[]{:S(2)}) collective-permute-start(bf16[32,1280]{1,0:T(8,128)(2,1)S(1)} %convert_bitcast_fusion), channel_id=1, source_target_pairs={{0,2},{1,3},{2,0},{3,1},{4,6},{5,7},{6,4},{7,5},{8,10},{9,11},{10,... | collective-permute-start | bytes 245768 | tf_op jit(solution)/shard_map/ppermute | solution.py:271
  5.7 0.9 %copy.19 = bf16[16,8,2,256]{3,1,2,0:T(8,128)(2,1)S(1)} copy(bf16[16,8,2,256]{3,2,1,0:T(2,128)(2,1)} %bitcast.65) | data formatting | bytes 262144
  6.7 0.1 collective-permute-start.1
  6.8 1.5 %dynamic-slice_bitcast_fusion = (bf16[128,1280]{1,0:T(8,128)(2,1)S(1)}, bf16[128,1280]{1,0:T(8,128)(2,1)S(1)}, bf16[128,1280]{1,0:T(8,128)(2,1)S(1)}, bf16[128,1280]{1,0:T(8,128)(2,1)S(1)}, bf16[128,1280]{1,0:T(8,128)(2,1)S(1)}) fusion(bf16[1,128,5120]{2,1,0:T(8,128)(2,1)} %param.7, s32[]{:T(128)S(6)} %select_n.44, s32[]{:T(128)S(6)} %select_n.42, ...), kind=kLoop, calls=%fused_computation.8 | loop fusion | bytes 3276820 | tf_op jit(solution)/shard_map/dynamic_slice | solution.py:276
  8.3 2.4 %collective-permute-done.3 = bf16[32,1280]{1,0:T(8,128)(2,1)S(1)} collective-permute-done((bf16[32,1280]{1,0:T(8,128)(2,1)S(1)}, bf16[32,1280]{1,0:T(8,128)(2,1)S(1)}, u32[]{:S(2)}, u32[]{:S(2)}) %collective-permute-start.3) | collective-permute-done | bytes 81952 | tf_op jit(solution)/shard_map/ppermute | solution.py:271
  10.7 3.5 %collective-permute-start.4 = (bf16[64,1280]{1,0:T(8,128)(2,1)S(1)}, bf16[64,1280]{1,0:T(8,128)(2,1)S(1)}, u32[]{:S(2)}, u32[]{:S(2)}) collective-permute-start(bf16[64,1280]{1,0:T(8,128)(2,1)S(1)} %pad_maximum_fusion.5), channel_id=1, source_target_pairs={{0,1},{1,0},{2,3},{3,2},{4,5},{5,4},{6,7},{7,6},{8,9},{9,8},{10,11... | collective-permute-start | bytes 491528 | tf_op jit(solution)/shard_map/ppermute | solution.py:286
  14.2 0.0 collective-permute-done
  14.3 0.1 constant_dynamic-slice_fusion
  14.5 1.9 %collective-permute-done.1.refs_2_.refs_3_ = bf16[128,512]{1,0:T(8,128)(2,1)S(1)} collective-permute-done((bf16[128,512]{1,0:T(8,128)(2,1)S(1)}, bf16[128,512]{1,0:T(8,128)(2,1)S(1)}, u32[]{:S(2)}, u32[]{:S(2)}) %collective-permute-start.1) | collective-permute-done | bytes 131104 | tf_op jit(solution)/shard_map/ppermute | solution.py:273
  16.3 0.7 %collective-permute-start.2 = (bf16[256,512]{1,0:T(8,128)(2,1)S(1)}, bf16[256,512]{1,0:T(8,128)(2,1)S(1)}, u32[]{:S(2)}, u32[]{:S(2)}) collective-permute-start(bf16[256,512]{1,0:T(8,128)(2,1)S(1)} %pad_maximum_fusion.4), channel_id=1, source_target_pairs={{0,1},{1,0},{2,3},{3,2},{4,5},{5,4},{6,7},{7,6},{8,9},{9,8},{10,11... | collective-permute-start | bytes 786440 | tf_op jit(solution)/shard_map/ppermute | solution.py:287
  17.1 3.4 %collective-permute-start.13 = (bf16[256,1280]{1,0:T(8,128)(2,1)S(1)}, bf16[256,1280]{1,0:T(8,128)(2,1)S(1)}, u32[]{:S(2)}, u32[]{:S(2)}) collective-permute-start(bf16[256,1280]{1,0:T(8,128)(2,1)S(1)} %pad_maximum_fusion), channel_id=1, source_target_pairs={{0,2},{1,3},{2,0},{3,1},{4,7},{5,6},{6,5},{7,4},{8,10},{9,11},{10,... | collective-permute-start | bytes 1966088 | tf_op jit(solution)/shard_map/ppermute | solution.py:282
  20.4 1.6 %collective-permute-start.5 = (bf16[128,1280]{1,0:T(8,128)(2,1)S(1)}, bf16[128,1280]{1,0:T(8,128)(2,1)S(1)}, u32[]{:S(2)}, u32[]{:S(2)}) collective-permute-start(bf16[128,1280]{1,0:T(8,128)(2,1)S(1)} %pad_maximum_fusion.3.refs_0_), channel_id=1, source_target_pairs={{0,8},{4,12},{8,0},{12,4},{16,24},{20,28},{24,16},{28,20},{1,9},{5... | collective-permute-start | bytes 983048 | tf_op jit(solution)/shard_map/ppermute | solution.py:292
  22.0 1.5 %collective-permute-start.6 = (bf16[128,1280]{1,0:T(8,128)(2,1)S(1)}, bf16[128,1280]{1,0:T(8,128)(2,1)S(1)}, u32[]{:S(2)}, u32[]{:S(2)}) collective-permute-start(bf16[128,1280]{1,0:T(8,128)(2,1)S(1)} %pad_maximum_fusion.3.refs_0_), channel_id=1, source_target_pairs={{0,16},{4,20},{8,24},{12,28},{16,0},{20,4},{24,8},{28,12},{1,17},{... | collective-permute-start | bytes 983048 | tf_op jit(solution)/shard_map/ppermute | solution.py:292
  23.5 0.5 collective-permute-start.7
  24.0 5.4 %collective-permute-done.2.refs_4_.refs_5_ = bf16[256,512]{1,0:T(8,128)(2,1)S(1)} collective-permute-done((bf16[256,512]{1,0:T(8,128)(2,1)S(1)}, bf16[256,512]{1,0:T(8,128)(2,1)S(1)}, u32[]{:S(2)}, u32[]{:S(2)}) %collective-permute-start.2) | collective-permute-done | bytes 262176 | tf_op jit(solution)/shard_map/ppermute | solution.py:287
  29.4 1.8 %collective-permute-done.5.refs_1_ = bf16[128,1280]{1,0:T(8,128)(2,1)S(1)} collective-permute-done((bf16[128,1280]{1,0:T(8,128)(2,1)S(1)}, bf16[128,1280]{1,0:T(8,128)(2,1)S(1)}, u32[]{:S(2)}, u32[]{:S(2)}) %collective-permute-start.5) | collective-permute-done | bytes 327712 | tf_op jit(solution)/shard_map/ppermute | solution.py:292
  31.2 6.6 %collective-permute-done.6.refs_2_ = bf16[128,1280]{1,0:T(8,128)(2,1)S(1)} collective-permute-done((bf16[128,1280]{1,0:T(8,128)(2,1)S(1)}, bf16[128,1280]{1,0:T(8,128)(2,1)S(1)}, u32[]{:S(2)}, u32[]{:S(2)}) %collective-permute-start.6) | collective-permute-done | bytes 327712 | tf_op jit(solution)/shard_map/ppermute | solution.py:292
  37.8 1.0 %shard_map.102 = (bf16[4,32,128]{2,1,0:T(8,128)(2,1)S(1)}, bf16[4,32,128]{2,1,0:T(8,128)(2,1)S(1)}) custom-call(bf16[128,1280]{1,0:T(8,128)(2,1)S(1)} %pad_maximum_fusion.3.refs_0_, bf16[128,1280]{1,0:T(8,128)(2,1)S(1)} %collective-permute-done.5.refs_1_, bf16[128,1280]{1,0:T(8,128)(2,1)S(1)} %collective-permute-done.6.refs_2_, ...), custom_call_target="tpu_custom_call" | custom-call | flops 335544320 | bytes 3932160 | tf_op jit(solution)/shard_map/pallas_call | solution.py:84
  38.8 0.0 copy-start.1
  38.8 0.1 collective-permute-start.8
  38.8 1.2 %collective-permute-done.8.refs_7_ = bf16[4,32,128]{2,1,0:T(8,128)(2,1)S(1)} collective-permute-done((bf16[4,32,128]{2,1,0:T(8,128)(2,1)S(1)}, bf16[4,32,128]{2,1,0:T(8,128)(2,1)S(1)}, u32[]{:S(2)}, u32[]{:S(2)}) %collective-permute-start.8) | collective-permute-done | bytes 32800 | tf_op jit(solution)/shard_map/ppermute | solution.py:298
  40.0 1.2 %shard_map.103.refs_0_ = bf16[256,128]{1,0:T(8,128)(2,1)S(1)} custom-call(bf16[128,512]{1,0:T(8,128)(2,1)S(1)} %bitcast.57, bf16[128,512]{1,0:T(8,128)(2,1)S(1)} %bitcast.58, bf16[128,512]{1,0:T(8,128)(2,1)S(1)} %collective-permute-done.1.refs_2_.refs_3_, bf16[128,512]{1,0:T(8,128)(2,1)S(1)} %collective-permute-done.1.refs_2_.refs_3_, ...), custom_call_target="tpu_custom_call" | custom-call | flops 402653184 | bytes 786432 | tf_op jit(solution)/shard_map/pallas_call | solution.py:164
  41.3 1.8 %collective-permute-start.10 = (bf16[256,128]{1,0:T(8,128)(2,1)S(1)}, bf16[256,128]{1,0:T(8,128)(2,1)S(1)}, u32[]{:S(2)}, u32[]{:S(2)}) collective-permute-start(bf16[256,128]{1,0:T(8,128)(2,1)S(1)} %shard_map.103.refs_0_), channel_id=1, source_target_pairs={{0,2},{1,3},{2,0},{3,1},{4,6},{5,7},{6,4},{7,5},{8,10},{9,11},{10,... | collective-permute-start | bytes 196616 | tf_op jit(solution)/shard_map/ppermute | solution.py:302
  43.0 1.3 %collective-permute-start.11 = (bf16[256,128]{1,0:T(8,128)(2,1)S(1)}, bf16[256,128]{1,0:T(8,128)(2,1)S(1)}, u32[]{:S(2)}, u32[]{:S(2)}) collective-permute-start(bf16[256,128]{1,0:T(8,128)(2,1)S(1)} %shard_map.103.refs_0_), channel_id=1, source_target_pairs={{0,3},{1,2},{2,1},{3,0},{4,7},{5,6},{6,5},{7,4},{8,11},{9,10},{10,... | collective-permute-start | bytes 196616 | tf_op jit(solution)/shard_map/ppermute | solution.py:302
  44.4 0.5 collective-permute-start.9
  44.8 9.2 %collective-permute-done.10.refs_2_ = bf16[256,128]{1,0:T(8,128)(2,1)S(1)} collective-permute-done((bf16[256,128]{1,0:T(8,128)(2,1)S(1)}, bf16[256,128]{1,0:T(8,128)(2,1)S(1)}, u32[]{:S(2)}, u32[]{:S(2)}) %collective-permute-start.10) | collective-permute-done | bytes 65568 | tf_op jit(solution)/shard_map/ppermute | solution.py:302
  54.1 0.1 collective-permute-start.14
  54.2 0.2 copy.13
  54.4 1.3 %copy.14 = bf16[256,1280]{1,0:T(8,128)(2,1)S(1)} copy(bf16[256,1280]{0,1:T(8,128)(2,1)} %bitcast.64) | data formatting | bytes 1310720 | tf_op jit(solution)/shard_map/transpose | solution.py:310
  55.7 0.5 collective-permute-done.14.refs_7_
  56.2 0.7 shard_map.105
  56.9 0.2 collective-permute-start.15
  57.1 0.7 shard_map.104
  57.8 0.1 select_bitcast_fusion.1
  57.9 0.1 pad_maximum_fusion.2
  57.9 0.7 collective-permute-done.15.got_ref
  58.6 0.1 shard_map.106
  58.7 1.6 %collective-permute-start.16 = (bf16[32,1280]{1,0:T(8,128)(2,1)S(1)}, bf16[32,1280]{1,0:T(8,128)(2,1)S(1)}, u32[]{:S(2)}, u32[]{:S(2)}) collective-permute-start(bf16[32,1280]{1,0:T(8,128)(2,1)S(1)} %get-tuple-element.39), channel_id=1, source_target_pairs={{0,8},{4,12},{8,0},{12,4},{16,24},{20,28},{24,16},{28,20},{1,9},{5... | collective-permute-start | bytes 245768 | tf_op jit(solution)/shard_map/ppermute | solution.py:327
  60.2 1.5 %collective-permute-start.17 = (bf16[32,1280]{1,0:T(8,128)(2,1)S(1)}, bf16[32,1280]{1,0:T(8,128)(2,1)S(1)}, u32[]{:S(2)}, u32[]{:S(2)}) collective-permute-start(bf16[32,1280]{1,0:T(8,128)(2,1)S(1)} %get-tuple-element.40), channel_id=1, source_target_pairs={{0,16},{4,20},{8,24},{12,28},{16,0},{20,4},{24,8},{28,12},{1,17},{... | collective-permute-start | bytes 245768 | tf_op jit(solution)/shard_map/ppermute | solution.py:327
  61.8 0.5 collective-permute-start.18
  62.2 0.1 pad_maximum_fusion.1
  62.3 1.1 %copy.18 = bf16[1,1280,256]{2,1,0:T(8,128)(2,1)} copy(bf16[1,1280,256]{1,2,0:T(8,128)(2,1)S(1)} %bitcast.60) | data formatting | bytes 1310720
  63.5 1.1 %copy.17 = bf16[1,1280,256]{2,1,0:T(8,128)(2,1)} copy(bf16[1,1280,256]{1,2,0:T(8,128)(2,1)S(1)} %bitcast.61) | data formatting | bytes 1310720
  64.6 0.9 %collective-permute-done.17 = bf16[32,1280]{1,0:T(8,128)(2,1)S(1)} collective-permute-done((bf16[32,1280]{1,0:T(8,128)(2,1)S(1)}, bf16[32,1280]{1,0:T(8,128)(2,1)S(1)}, u32[]{:S(2)}, u32[]{:S(2)}) %collective-permute-start.17) | collective-permute-done | bytes 81952 | tf_op jit(solution)/shard_map/ppermute | solution.py:327
  65.5 1.6 %collective-permute-done.18 = bf16[32,1280]{1,0:T(8,128)(2,1)S(1)} collective-permute-done((bf16[32,1280]{1,0:T(8,128)(2,1)S(1)}, bf16[32,1280]{1,0:T(8,128)(2,1)S(1)}, u32[]{:S(2)}, u32[]{:S(2)}) %collective-permute-start.18) | collective-permute-done | bytes 81952 | tf_op jit(solution)/shard_map/ppermute | solution.py:327
  67.1 0.8 %fusion.1 = (f32[1280,32]{0,1:T(8,128)}, f32[1280,32]{0,1:T(8,128)}) fusion(f32[1280,32]{0,1:T(8,128)S(1)} %copy-done.2, bf16[32,1280]{1,0:T(8,128)(2,1)S(1)} %collective-permute-done.18, bf16[32,1280]{1,0:T(8,128)(2,1)S(1)} %collective-permute-done.17, f32[32,1280]{1,0:T(8,128)S(1)} %get-tuple-element.38, bf16[32,1280]{1,0:T(8,128)(2,1)S(1)} %collective-permute-done.16, ...), kind=kLoop, calls=%fused_computation.18 | loop fusion | flops 532480 | bytes 1064960 | tf_op jit(solution)/shard_map/sub | solution.py:332
  (21 shorter events, 0.2 us)
Async XLA Ops:
  0.6 13.6 %collective-permute-start = (bf16[128,5120]{1,0:T(8,128)(2,1)}, bf16[128,5120]{1,0:T(8,128)(2,1)S(1)}, u32[]{:S(2)}, u32[]{:S(2)}) collective-permute-start(bf16[128,5120]{1,0:T(8,128)(2,1)} %bitcast.62), channel_id=1, source_target_pairs={{0,4},{4,0},{8,12},{12,8},{16,20},{20,16},{24,28},{28,24},{1,5},{5... | collective-permute-start | bytes 3932168 | tf_op jit(solution)/shard_map/ppermute | solution.py:269
  2.1 8.6 %collective-permute-start.3 = (bf16[32,1280]{1,0:T(8,128)(2,1)S(1)}, bf16[32,1280]{1,0:T(8,128)(2,1)S(1)}, u32[]{:S(2)}, u32[]{:S(2)}) collective-permute-start(bf16[32,1280]{1,0:T(8,128)(2,1)S(1)} %convert_bitcast_fusion), channel_id=1, source_target_pairs={{0,2},{1,3},{2,0},{3,1},{4,6},{5,7},{6,4},{7,5},{8,10},{9,11},{10,... | collective-permute-start | bytes 245768 | tf_op jit(solution)/shard_map/ppermute | solution.py:271
  6.7 9.7 %collective-permute-start.1 = (bf16[128,512]{1,0:T(8,128)(2,1)S(1)}, bf16[128,512]{1,0:T(8,128)(2,1)S(1)}, u32[]{:S(2)}, u32[]{:S(2)}) collective-permute-start(bf16[128,512]{1,0:T(8,128)(2,1)S(1)} %bitcast.55), channel_id=1, source_target_pairs={{0,2},{1,3},{2,0},{3,1},{4,6},{5,7},{6,4},{7,5},{8,10},{9,11},{10,... | collective-permute-start | bytes 393224 | tf_op jit(solution)/shard_map/ppermute | solution.py:273
  10.7 9.7 %collective-permute-start.4 = (bf16[64,1280]{1,0:T(8,128)(2,1)S(1)}, bf16[64,1280]{1,0:T(8,128)(2,1)S(1)}, u32[]{:S(2)}, u32[]{:S(2)}) collective-permute-start(bf16[64,1280]{1,0:T(8,128)(2,1)S(1)} %pad_maximum_fusion.5), channel_id=1, source_target_pairs={{0,1},{1,0},{2,3},{3,2},{4,5},{5,4},{6,7},{7,6},{8,9},{9,8},{10,11... | collective-permute-start | bytes 491528 | tf_op jit(solution)/shard_map/ppermute | solution.py:286
  16.3 13.0 %collective-permute-start.2 = (bf16[256,512]{1,0:T(8,128)(2,1)S(1)}, bf16[256,512]{1,0:T(8,128)(2,1)S(1)}, u32[]{:S(2)}, u32[]{:S(2)}) collective-permute-start(bf16[256,512]{1,0:T(8,128)(2,1)S(1)} %pad_maximum_fusion.4), channel_id=1, source_target_pairs={{0,1},{1,0},{2,3},{3,2},{4,5},{5,4},{6,7},{7,6},{8,9},{9,8},{10,11... | collective-permute-start | bytes 786440 | tf_op jit(solution)/shard_map/ppermute | solution.py:287
  17.1 37.0 %collective-permute-start.13 = (bf16[256,1280]{1,0:T(8,128)(2,1)S(1)}, bf16[256,1280]{1,0:T(8,128)(2,1)S(1)}, u32[]{:S(2)}, u32[]{:S(2)}) collective-permute-start(bf16[256,1280]{1,0:T(8,128)(2,1)S(1)} %pad_maximum_fusion), channel_id=1, source_target_pairs={{0,2},{1,3},{2,0},{3,1},{4,7},{5,6},{6,5},{7,4},{8,10},{9,11},{10,... | collective-permute-start | bytes 1966088 | tf_op jit(solution)/shard_map/ppermute | solution.py:282
  20.4 10.7 %collective-permute-start.5 = (bf16[128,1280]{1,0:T(8,128)(2,1)S(1)}, bf16[128,1280]{1,0:T(8,128)(2,1)S(1)}, u32[]{:S(2)}, u32[]{:S(2)}) collective-permute-start(bf16[128,1280]{1,0:T(8,128)(2,1)S(1)} %pad_maximum_fusion.3.refs_0_), channel_id=1, source_target_pairs={{0,8},{4,12},{8,0},{12,4},{16,24},{20,28},{24,16},{28,20},{1,9},{5... | collective-permute-start | bytes 983048 | tf_op jit(solution)/shard_map/ppermute | solution.py:292
  22.0 15.8 %collective-permute-start.6 = (bf16[128,1280]{1,0:T(8,128)(2,1)S(1)}, bf16[128,1280]{1,0:T(8,128)(2,1)S(1)}, u32[]{:S(2)}, u32[]{:S(2)}) collective-permute-start(bf16[128,1280]{1,0:T(8,128)(2,1)S(1)} %pad_maximum_fusion.3.refs_0_), channel_id=1, source_target_pairs={{0,16},{4,20},{8,24},{12,28},{16,0},{20,4},{24,8},{28,12},{1,17},{... | collective-permute-start | bytes 983048 | tf_op jit(solution)/shard_map/ppermute | solution.py:292
  23.5 14.3 %collective-permute-start.7 = (bf16[128,1280]{1,0:T(8,128)(2,1)S(1)}, bf16[128,1280]{1,0:T(8,128)(2,1)S(1)}, u32[]{:S(2)}, u32[]{:S(2)}) collective-permute-start(bf16[128,1280]{1,0:T(8,128)(2,1)S(1)} %pad_maximum_fusion.3.refs_0_), channel_id=1, source_target_pairs={{0,24},{4,28},{8,16},{12,20},{16,8},{20,12},{24,0},{28,4},{1,25},{... | collective-permute-start | bytes 983048 | tf_op jit(solution)/shard_map/ppermute | solution.py:292
  29.4 24.7 %collective-permute-start.12 = (bf16[128,1280]{1,0:T(8,128)(2,1)S(1)}, bf16[128,1280]{1,0:T(8,128)(2,1)S(1)}, u32[]{:S(2)}, u32[]{:S(2)}) collective-permute-start(bf16[128,1280]{1,0:T(8,128)(2,1)S(1)} %get-tuple-element.32.refs_5_), channel_id=1, source_target_pairs={{0,1},{1,0},{2,3},{3,2},{4,5},{5,4},{6,7},{7,6},{8,9},{9,8},{10,11... | collective-permute-start | bytes 983048 | tf_op jit(solution)/shard_map/ppermute | solution.py:299
  37.8 2.3 %copy-start = (bf16[1,128,256]{2,1,0:T(8,128)(2,1)S(1)}, bf16[1,128,256]{2,1,0:T(8,128)(2,1)}, u32[]{:S(2)}) copy-start(bf16[1,128,256]{2,1,0:T(8,128)(2,1)} %param.9) | copy-start | bytes 196612
  38.8 15.4 %copy-start.1 = (bf16[1,1280,256]{2,1,0:T(8,128)(2,1)S(1)}, bf16[1,1280,256]{2,1,0:T(8,128)(2,1)}, u32[]{:S(2)}) copy-start(bf16[1,1280,256]{2,1,0:T(8,128)(2,1)} %param.10) | copy-start | bytes 1966084
  38.8 1.3 %collective-permute-start.8 = (bf16[4,32,128]{2,1,0:T(8,128)(2,1)S(1)}, bf16[4,32,128]{2,1,0:T(8,128)(2,1)S(1)}, u32[]{:S(2)}, u32[]{:S(2)}) collective-permute-start(bf16[4,32,128]{2,1,0:T(8,128)(2,1)S(1)} %get-tuple-element.31), channel_id=1, source_target_pairs={{0,4},{4,0},{8,12},{12,8},{16,20},{20,16},{24,28},{28,24},{1,5},{5... | collective-permute-start | bytes 98312 | tf_op jit(solution)/shard_map/ppermute | solution.py:298
  41.3 12.8 %collective-permute-start.10 = (bf16[256,128]{1,0:T(8,128)(2,1)S(1)}, bf16[256,128]{1,0:T(8,128)(2,1)S(1)}, u32[]{:S(2)}, u32[]{:S(2)}) collective-permute-start(bf16[256,128]{1,0:T(8,128)(2,1)S(1)} %shard_map.103.refs_0_), channel_id=1, source_target_pairs={{0,2},{1,3},{2,0},{3,1},{4,6},{5,7},{6,4},{7,5},{8,10},{9,11},{10,... | collective-permute-start | bytes 196616 | tf_op jit(solution)/shard_map/ppermute | solution.py:302
  43.0 11.0 %collective-permute-start.11 = (bf16[256,128]{1,0:T(8,128)(2,1)S(1)}, bf16[256,128]{1,0:T(8,128)(2,1)S(1)}, u32[]{:S(2)}, u32[]{:S(2)}) collective-permute-start(bf16[256,128]{1,0:T(8,128)(2,1)S(1)} %shard_map.103.refs_0_), channel_id=1, source_target_pairs={{0,3},{1,2},{2,1},{3,0},{4,7},{5,6},{6,5},{7,4},{8,11},{9,10},{10,... | collective-permute-start | bytes 196616 | tf_op jit(solution)/shard_map/ppermute | solution.py:302
  44.4 9.7 %collective-permute-start.9 = (bf16[256,128]{1,0:T(8,128)(2,1)S(1)}, bf16[256,128]{1,0:T(8,128)(2,1)S(1)}, u32[]{:S(2)}, u32[]{:S(2)}) collective-permute-start(bf16[256,128]{1,0:T(8,128)(2,1)S(1)} %shard_map.103.refs_0_), channel_id=1, source_target_pairs={{0,1},{1,0},{2,3},{3,2},{4,5},{5,4},{6,7},{7,6},{8,9},{9,8},{10,11... | collective-permute-start | bytes 196616 | tf_op jit(solution)/shard_map/ppermute | solution.py:302
  54.1 2.2 %collective-permute-start.14 = (bf16[256,1280]{1,0:T(8,128)(2,1)S(1)}, bf16[256,1280]{1,0:T(8,128)(2,1)S(1)}, u32[]{:S(2)}, u32[]{:S(2)}) collective-permute-start(bf16[256,1280]{1,0:T(8,128)(2,1)S(1)} %collective-permute-done.13.refs_6_), channel_id=1, source_target_pairs={{0,4},{4,0},{8,12},{12,8},{16,20},{20,16},{24,28},{28,24},{1,5},{5... | collective-permute-start | bytes 1966088 | tf_op jit(solution)/shard_map/ppermute | solution.py:308
  56.9 1.7 %collective-permute-start.15 = (bf16[4,32,1280]{2,1,0:T(8,128)(2,1)S(1)}, bf16[4,32,1280]{2,1,0:T(8,128)(2,1)S(1)}, u32[]{:S(2)}, u32[]{:S(2)}) collective-permute-start(bf16[4,32,1280]{2,1,0:T(8,128)(2,1)S(1)} %get-tuple-element.37), channel_id=1, source_target_pairs={{0,4},{4,0},{8,12},{12,8},{16,20},{20,16},{24,28},{28,24},{1,5},{5... | collective-permute-start | bytes 983048 | tf_op jit(solution)/shard_map/ppermute | solution.py:314
  58.7 5.9 %collective-permute-start.16 = (bf16[32,1280]{1,0:T(8,128)(2,1)S(1)}, bf16[32,1280]{1,0:T(8,128)(2,1)S(1)}, u32[]{:S(2)}, u32[]{:S(2)}) collective-permute-start(bf16[32,1280]{1,0:T(8,128)(2,1)S(1)} %get-tuple-element.39), channel_id=1, source_target_pairs={{0,8},{4,12},{8,0},{12,4},{16,24},{20,28},{24,16},{28,20},{1,9},{5... | collective-permute-start | bytes 245768 | tf_op jit(solution)/shard_map/ppermute | solution.py:327
  60.2 5.3 %collective-permute-start.17 = (bf16[32,1280]{1,0:T(8,128)(2,1)S(1)}, bf16[32,1280]{1,0:T(8,128)(2,1)S(1)}, u32[]{:S(2)}, u32[]{:S(2)}) collective-permute-start(bf16[32,1280]{1,0:T(8,128)(2,1)S(1)} %get-tuple-element.40), channel_id=1, source_target_pairs={{0,16},{4,20},{8,24},{12,28},{16,0},{20,4},{24,8},{28,12},{1,17},{... | collective-permute-start | bytes 245768 | tf_op jit(solution)/shard_map/ppermute | solution.py:327
  61.8 5.3 %collective-permute-start.18 = (bf16[32,1280]{1,0:T(8,128)(2,1)S(1)}, bf16[32,1280]{1,0:T(8,128)(2,1)S(1)}, u32[]{:S(2)}, u32[]{:S(2)}) collective-permute-start(bf16[32,1280]{1,0:T(8,128)(2,1)S(1)} %get-tuple-element.41), channel_id=1, source_target_pairs={{0,24},{4,28},{8,16},{12,20},{16,8},{20,12},{24,0},{28,4},{1,25},{... | collective-permute-start | bytes 245768 | tf_op jit(solution)/shard_map/ppermute | solution.py:327
  63.4 3.7 %copy-start.2 = (f32[1280,32]{0,1:T(8,128)S(1)}, f32[1280,32]{0,1:T(8,128)}, u32[]{:S(2)}) copy-start(f32[1280,32]{0,1:T(8,128)} %param.12) | copy-start | bytes 491524
  63.4 3.7 %copy-start.3 = (f32[1280,32]{0,1:T(8,128)S(1)}, f32[1280,32]{0,1:T(8,128)}, u32[]{:S(2)}) copy-start(f32[1280,32]{0,1:T(8,128)} %param.13) | copy-start | bytes 491524

commit v12 on v11

--- a/solution.py
+++ b/solution.py
@@ -278,36 +278,36 @@
     far = []
     for k in range(2, n_seq, 2):
         both = jnp.concatenate([feature_block(m, k + core) for m in (tokens, partner_tokens)], 0)
-        both, kv = lax.optimization_barrier((both, kv))
         far.append(lax.ppermute(both, ("island", "seq"), far_pairs(n_island, n_seq, k)))
     own_blocks = [feature_block(tokens, k) for k in range(n_seq)]
     partner_blocks = [feature_block(partner_tokens, k) for k in range(n_seq)]
+    near = lax.ppermute(own_blocks[1], "seq", pair_perm(n_seq, 1))
     for bit in bits[1:]:
         held = jnp.concatenate([held, lax.ppermute(held, "seq", pair_perm(n_seq, bit))], 0)
         kv.append(lax.ppermute(jnp.concatenate(kv, axis=0), "seq", pair_perm(n_seq, bit)))
 
     rounds = [order]
+    held, near = lax.optimization_barrier((held, near))
     spread = [held] + [None] * (n_chip - 1)
     for step in range(1, n_chip):
         spread[step] = lax.ppermute(held, "island", pair_perm(n_chip, step, 2))
 
+    first = first_moment[0].T.reshape(n_chip, 2, share, block)
+    second = second_moment[0].T.reshape(n_chip, 2, share, block)
+    spread, first, second = lax.optimization_barrier((spread, first, second))
     mine, for_partner = half_queries(
         rounds, [spread], own_blocks, partner_blocks, share, inverse
     )
-    near, kv = lax.optimization_barrier((own_blocks[1], kv))
     other = lax.ppermute(for_partner, "island", swap)
-    near = lax.ppermute(near, "seq", pair_perm(n_seq, 1))
     dquery = attention(kv, order, mine, other, cotangent[0])
     dqueries = [dquery] + [
         lax.ppermute(dquery, "seq", pair_perm(n_seq, k)) for k in range(1, n_seq)
     ]
 
-    _, near, far = lax.optimization_barrier((dqueries[1:], near, far))
+    _, far = lax.optimization_barrier((dqueries[1:], far))
     gathered = [own_blocks[0], near]
     for got in far:
         gathered += [got, lax.ppermute(got, "island", swap)]
-    first = first_moment[0].T.reshape(n_chip, 2, share, block)
-    second = second_moment[0].T.reshape(n_chip, 2, share, block)
     first_other, second_other, delta_other = gradient_adam(
         dqueries, gathered, first, second, False, inverse
     )
@@ -323,7 +323,7 @@
         return jnp.stack([lower, upper], axis=1).reshape(cols, block).T[None]
 
     total = parts[0]
-    for step in range(1, n_chip):
+    for step in reversed(range(1, n_chip)):
         total = total + lax.ppermute(
             parts[step], "island", pair_perm(n_chip, step, 2)
         ).astype(jnp.float32)

time: 68.1 us -> 82.4 us (1.21)
  starting transfers between devices: 22.9 us -> 30.7 us
  local copies, waits for them, and re-layouts: 6.39 us -> 13.6 us
  waiting for transfers between devices: 32.2 us -> 26.7 us
  Pallas kernels: 3.58 us -> 5.87 us
  other arithmetic: 2.03 us -> 4.31 us
    ppermute x3, starting transfers between devices: 3.55 us -> 10.2 us  [on_device(): lax.ppermute(dquery, 'seq', pair_perm(n_seq, k))]
    ppermute x1, waiting for transfers between devices: 5.36 us -> 0.01 us  [on_device(): lax.ppermute(jnp.concatenate(kv, axis=0), 'seq', pair_perm(n_seq, bit))]
    unnamed x11 -> x27, local copies, waits for them, and re-layouts: 3.09 us -> 7.96 us
    ppermute x1, waiting for transfers between devices: 0.01 us -> 4.64 us  [on_device(): lax.ppermute(held, 'seq', pair_perm(n_seq, bit))]
    ppermute x3, waiting for transfers between devices: 9.22 us -> 5.01 us  [on_device(): lax.ppermute(dquery, 'seq', pair_perm(n_seq, k))]
    ppermute x3, waiting for transfers between devices: 8.42 us -> 11 us  [on_device(): spread[step] = lax.ppermute(held, 'island', pair_perm(n_chip, step, 2))]
    dynamic_slice x2, local copies, waits for them, and re-layouts: 1.64 us -> 3.98 us  [feature_block(): lax.dynamic_slice(matrix, (0, jnp.bitwise_xor(seq, k) * block), (rows, bl...]
    ppermute x1, waiting for transfers between devices: 2.41 us -> 0.49 us  [on_device(): held = jnp.concatenate([weight, lax.ppermute(weight, 'seq', far_perm)], 0)]
  transfers between devices with their start and end apart: 19 -> 19, of which waited for: 11 -> 12; matrix products, arithmetic and copies ran while one was open for 11% -> 15% of each run, Pallas kernels for 4% -> 6%
where the time goes in v12:
time: 82.4 us; the launch traced here: 81.9 us
  starting transfers between devices  30.7 us (37%)
  waiting for transfers between devices  26.7 us (32%)
  local copies, waits for them, and re-layouts  13.6 us (17%)
  Pallas kernels  5.87 us (7%)
  other arithmetic  4.31 us (5%)
    ppermute x3, waiting for transfers between devices, on_device(): spread[step] = lax.ppermute(held, 'island', pair_perm(n_chip, step, 2))  11 us
    ppermute x3, starting transfers between devices, on_device(): lax.ppermute(dquery, 'seq', pair_perm(n_seq, k))  10.2 us
    unnamed x27, local copies, waits for them, and re-layouts  7.96 us
    ppermute x3, waiting for transfers between devices, on_device(): lax.ppermute(dquery, 'seq', pair_perm(n_seq, k))  5.01 us
    ppermute x1, waiting for transfers between devices, on_device(): lax.ppermute(held, 'seq', pair_perm(n_seq, bit))  4.64 us
    dynamic_slice x2, local copies, waits for them, and re-layouts, feature_block(): lax.dynamic_slice(matrix, (0, jnp.bitwise_xor(seq, k) * block), (rows, bl...  3.98 us
    ppermute x1, starting transfers between devices, on_device(): held = jnp.concatenate([weight, lax.ppermute(weight, 'seq', far_perm)], 0)  3.67 us
    ppermute x1, starting transfers between devices, on_device(): lax.ppermute(held, 'seq', pair_perm(n_seq, bit))  3.59 us
  transfers between devices with their start and end apart: 19, of which 12 were waited for; matrix products, arithmetic and copies ran while one was open for 15% of the time, Pallas kernels for 6%

profile of v12, /device:TPU:0, one launch (start us, length us, event | category | flops | bytes accessed | tf_op | source)
XLA Modules:
  0.0 81.9 jit_solution(619138424024164432)
XLA Ops:
  0.6 0.5 collective-permute-start.8
  1.1 0.9 %convert_bitcast_fusion = bf16[32,1280]{1,0:T(8,128)(2,1)S(1)} fusion(f32[1280,32]{0,1:T(8,128)} %param.12), kind=kLoop, calls=%fused_computation.20 | loop fusion | flops 40960 | bytes 245760 | tf_op jit(solution)/shard_map/convert_element_type | solution.py:270
  2.1 3.7 %collective-permute-start.2 = (bf16[32,1280]{1,0:T(8,128)(2,1)S(1)}, bf16[32,1280]{1,0:T(8,128)(2,1)S(1)}, u32[]{:S(2)}, u32[]{:S(2)}) collective-permute-start(bf16[32,1280]{1,0:T(8,128)(2,1)S(1)} %convert_bitcast_fusion), channel_id=1, source_target_pairs={{0,2},{1,3},{2,0},{3,1},{4,6},{5,7},{6,4},{7,5},{8,10},{9,11},{10,... | collective-permute-start | bytes 245768 | tf_op jit(solution)/shard_map/ppermute | solution.py:271
  5.7 0.9 %copy.19 = bf16[16,8,2,256]{3,1,2,0:T(8,128)(2,1)S(1)} copy(bf16[16,8,2,256]{3,2,1,0:T(2,128)(2,1)} %bitcast.65) | data formatting | bytes 262144
  6.8 1.5 %dynamic-slice_bitcast_fusion = (bf16[128,1280]{1,0:T(8,128)(2,1)S(1)}, bf16[128,1280]{1,0:T(8,128)(2,1)S(1)}, bf16[128,1280]{1,0:T(8,128)(2,1)S(1)}, bf16[128,1280]{1,0:T(8,128)(2,1)S(1)}, bf16[128,1280]{1,0:T(8,128)(2,1)S(1)}) fusion(bf16[1,128,5120]{2,1,0:T(8,128)(2,1)} %param.7, s32[]{:T(128)S(6)} %select_n.44, s32[]{:T(128)S(6)} %select_n.43, ...), kind=kLoop, calls=%fused_computation.8 | loop fusion | bytes 3276820 | tf_op jit(solution)/shard_map/dynamic_slice | solution.py:276
  8.3 1.9 %collective-permute-start.4 = (bf16[128,1280]{1,0:T(8,128)(2,1)S(1)}, bf16[128,1280]{1,0:T(8,128)(2,1)S(1)}, u32[]{:S(2)}, u32[]{:S(2)}) collective-permute-start(bf16[128,1280]{1,0:T(8,128)(2,1)S(1)} %get-tuple-element.56.refs_5_), channel_id=1, source_target_pairs={{0,1},{1,0},{2,3},{3,2},{4,5},{5,4},{6,7},{7,6},{8,9},{9,8},{10,11... | collective-permute-start | bytes 983048 | tf_op jit(solution)/shard_map/ppermute | solution.py:284
  10.2 0.5 collective-permute-done.2
  10.7 3.6 %collective-permute-start.3 = (bf16[64,1280]{1,0:T(8,128)(2,1)S(1)}, bf16[64,1280]{1,0:T(8,128)(2,1)S(1)}, u32[]{:S(2)}, u32[]{:S(2)}) collective-permute-start(bf16[64,1280]{1,0:T(8,128)(2,1)S(1)} %pad_maximum_fusion.5), channel_id=1, source_target_pairs={{0,1},{1,0},{2,3},{3,2},{4,5},{5,4},{6,7},{7,6},{8,9},{9,8},{10,11... | collective-permute-start | bytes 491528 | tf_op jit(solution)/shard_map/ppermute | solution.py:286
  14.3 2.5 %constant_dynamic-slice_fusion = (bf16[128,1280]{1,0:T(8,128)(2,1)S(1)}, bf16[128,1280]{1,0:T(8,128)(2,1)}, bf16[128,1280]{1,0:T(8,128)(2,1)}, bf16[128,1280]{1,0:T(8,128)(2,1)}, bf16[128,1280]{1,0:T(8,128)(2,1)}) fusion(bf16[128,5120]{1,0:T(8,128)(2,1)} %collective-permute-done.8, s32[]{:T(128)S(6)} %select_n.44, s32[]{:T(128)S(6)} %select_n.43, ...), kind=kLoop, calls=%fused_computation.21 | loop fusion | bytes 3276820 | tf_op jit(solution)/shard_map/dynamic_slice | solution.py:276
  16.8 0.9 %pad_maximum_fusion = bf16[256,1280]{1,0:T(8,128)(2,1)} fusion(bf16[128,1280]{1,0:T(8,128)(2,1)S(1)} %get-tuple-element.57, bf16[128,1280]{1,0:T(8,128)(2,1)S(1)} %get-tuple-element.52), kind=kLoop, calls=%fused_computation | loop fusion | flops 1310720 | bytes 1310720 | tf_op jit(solution)/shard_map/concatenate | solution.py:280
  17.7 3.4 %collective-permute-start.13 = (bf16[256,1280]{1,0:T(8,128)(2,1)}, bf16[256,1280]{1,0:T(8,128)(2,1)S(1)}, u32[]{:S(2)}, u32[]{:S(2)}) collective-permute-start(bf16[256,1280]{1,0:T(8,128)(2,1)} %pad_maximum_fusion), channel_id=1, source_target_pairs={{0,2},{1,3},{2,0},{3,1},{4,7},{5,6},{6,5},{7,4},{8,10},{9,11},{10,... | collective-permute-start | bytes 1966088 | tf_op jit(solution)/shard_map/ppermute | solution.py:281
  21.1 4.6 %collective-permute-done.3 = bf16[64,1280]{1,0:T(8,128)(2,1)S(1)} collective-permute-done((bf16[64,1280]{1,0:T(8,128)(2,1)S(1)}, bf16[64,1280]{1,0:T(8,128)(2,1)S(1)}, u32[]{:S(2)}, u32[]{:S(2)}) %collective-permute-start.3) | collective-permute-done | bytes 163872 | tf_op jit(solution)/shard_map/ppermute | solution.py:286
  25.7 0.7 pad_maximum_fusion.3.refs_0_
  26.5 2.5 %collective-permute-start.7 = (bf16[128,1280]{1,0:T(8,128)(2,1)}, bf16[128,1280]{1,0:T(8,128)(2,1)}, u32[]{:S(2)}, u32[]{:S(2)}) collective-permute-start(bf16[128,1280]{1,0:T(8,128)(2,1)} %pad_maximum_fusion.3.refs_0_), channel_id=1, source_target_pairs={{0,24},{4,28},{8,16},{12,20},{16,8},{20,12},{24,0},{28,4},{1,25},{... | collective-permute-start | bytes 983048 | tf_op jit(solution)/shard_map/ppermute | solution.py:293
  29.0 0.5 collective-permute-start.6
  29.6 0.4 collective-permute-start.5
  30.0 0.7 pad_maximum_fusion.4
  30.7 0.2 copy.13
  31.0 1.3 %copy.14 = bf16[256,1280]{1,0:T(8,128)(2,1)S(1)} copy(bf16[256,1280]{0,1:T(8,128)(2,1)} %bitcast.64) | data formatting | bytes 1310720 | tf_op jit(solution)/shard_map/transpose | solution.py:296
  32.3 6.1 %collective-permute-done.7.refs_3_ = bf16[128,1280]{1,0:T(8,128)(2,1)} collective-permute-done((bf16[128,1280]{1,0:T(8,128)(2,1)}, bf16[128,1280]{1,0:T(8,128)(2,1)}, u32[]{:S(2)}, u32[]{:S(2)}) %collective-permute-start.7) | collective-permute-done | bytes 327712 | tf_op jit(solution)/shard_map/ppermute | solution.py:293
  38.4 4.9 %collective-permute-done.6.refs_2_ = bf16[128,1280]{1,0:T(8,128)(2,1)} collective-permute-done((bf16[128,1280]{1,0:T(8,128)(2,1)}, bf16[128,1280]{1,0:T(8,128)(2,1)}, u32[]{:S(2)}, u32[]{:S(2)}) %collective-permute-start.6) | collective-permute-done | bytes 327712 | tf_op jit(solution)/shard_map/ppermute | solution.py:293
  43.3 1.0 %copy-done.1 = bf16[128,1280]{1,0:T(8,128)(2,1)S(1)} copy-done((bf16[128,1280]{1,0:T(8,128)(2,1)S(1)}, bf16[128,1280]{1,0:T(8,128)(2,1)}, u32[]{:S(2)}) %copy-start.1) | copy-done | bytes 327704
  44.3 1.0 %copy-done.2 = bf16[128,1280]{1,0:T(8,128)(2,1)S(1)} copy-done((bf16[128,1280]{1,0:T(8,128)(2,1)S(1)}, bf16[128,1280]{1,0:T(8,128)(2,1)}, u32[]{:S(2)}) %copy-start.2) | copy-done | bytes 327704
  45.2 1.0 %copy-done.3 = bf16[128,1280]{1,0:T(8,128)(2,1)S(1)} copy-done((bf16[128,1280]{1,0:T(8,128)(2,1)S(1)}, bf16[128,1280]{1,0:T(8,128)(2,1)}, u32[]{:S(2)}) %copy-start.3) | copy-done | bytes 327704
  46.2 1.0 %copy-done.4 = bf16[128,1280]{1,0:T(8,128)(2,1)S(1)} copy-done((bf16[128,1280]{1,0:T(8,128)(2,1)S(1)}, bf16[128,1280]{1,0:T(8,128)(2,1)}, u32[]{:S(2)}) %copy-start.4) | copy-done | bytes 327704
  47.2 1.0 %copy-done.5 = bf16[128,1280]{1,0:T(8,128)(2,1)S(1)} copy-done((bf16[128,1280]{1,0:T(8,128)(2,1)S(1)}, bf16[128,1280]{1,0:T(8,128)(2,1)}, u32[]{:S(2)}) %copy-start.5) | copy-done | bytes 327704
  48.2 2.3 %shard_map.102 = (bf16[4,32,128]{2,1,0:T(8,128)(2,1)S(1)}, bf16[4,32,128]{2,1,0:T(8,128)(2,1)S(1)}) custom-call(bf16[128,1280]{1,0:T(8,128)(2,1)} %pad_maximum_fusion.3.refs_0_, bf16[128,1280]{1,0:T(8,128)(2,1)} %collective-permute-done.5.refs_1_, bf16[128,1280]{1,0:T(8,128)(2,1)} %collective-permute-done.6.refs_2_, ...), custom_call_target="tpu_custom_call" | custom-call | flops 335544320 | bytes 3932160 | tf_op jit(solution)/shard_map/pallas_call | solution.py:84
  50.5 1.2 %collective-permute-done.9.refs_7_ = bf16[4,32,128]{2,1,0:T(8,128)(2,1)S(1)} collective-permute-done((bf16[4,32,128]{2,1,0:T(8,128)(2,1)S(1)}, bf16[4,32,128]{2,1,0:T(8,128)(2,1)S(1)}, u32[]{:S(2)}, u32[]{:S(2)}) %collective-permute-start.9) | collective-permute-done | bytes 32800 | tf_op jit(solution)/shard_map/ppermute | solution.py:301
  51.7 2.2 %shard_map.103.refs_0_ = bf16[256,128]{1,0:T(8,128)(2,1)S(1)} custom-call(bf16[128,512]{1,0:T(8,128)(2,1)S(1)} %bitcast.57, bf16[128,512]{1,0:T(8,128)(2,1)S(1)} %bitcast.58, bf16[128,512]{1,0:T(8,128)(2,1)S(1)} %copy-done.7, bf16[128,512]{1,0:T(8,128)(2,1)S(1)} %copy-done.7, bf16[256,512]{1,0:T(8,128)(2,1)} %collective-permute-done.1.refs_4_.refs_5_, ...), custom_call_target="tpu_custom_call" | custom-call | flops 402653184 | bytes 786432 | tf_op jit(solution)/shard_map/pallas_call | solution.py:164
  53.9 9.5 %collective-permute-start.12 = (bf16[256,128]{1,0:T(8,128)(2,1)S(1)}, bf16[256,128]{1,0:T(8,128)(2,1)S(1)}, u32[]{:S(2)}, u32[]{:S(2)}) collective-permute-start(bf16[256,128]{1,0:T(8,128)(2,1)S(1)} %shard_map.103.refs_0_), channel_id=1, source_target_pairs={{0,3},{1,2},{2,1},{3,0},{4,7},{5,6},{6,5},{7,4},{8,11},{9,10},{10,... | collective-permute-start | bytes 196616 | tf_op jit(solution)/shard_map/ppermute | solution.py:304
  63.5 0.6 collective-permute-start.10
  64.1 2.2 %collective-permute-done.12.refs_3_ = bf16[256,128]{1,0:T(8,128)(2,1)S(1)} collective-permute-done((bf16[256,128]{1,0:T(8,128)(2,1)S(1)}, bf16[256,128]{1,0:T(8,128)(2,1)S(1)}, u32[]{:S(2)}, u32[]{:S(2)}) %collective-permute-start.12) | collective-permute-done | bytes 65568 | tf_op jit(solution)/shard_map/ppermute | solution.py:304
  66.4 2.5 %collective-permute-done.11.refs_2_ = bf16[256,128]{1,0:T(8,128)(2,1)S(1)} collective-permute-done((bf16[256,128]{1,0:T(8,128)(2,1)S(1)}, bf16[256,128]{1,0:T(8,128)(2,1)S(1)}, u32[]{:S(2)}, u32[]{:S(2)}) %collective-permute-start.11) | collective-permute-done | bytes 65568 | tf_op jit(solution)/shard_map/ppermute | solution.py:304
  68.8 0.3 collective-permute-done.10.refs_1_
  69.1 2.1 %collective-permute-done.14.refs_7_ = bf16[256,1280]{1,0:T(8,128)(2,1)S(1)} collective-permute-done((bf16[256,1280]{1,0:T(8,128)(2,1)S(1)}, bf16[256,1280]{1,0:T(8,128)(2,1)S(1)}, u32[]{:S(2)}, u32[]{:S(2)}) %collective-permute-start.14) | collective-permute-done | bytes 655392 | tf_op jit(solution)/shard_map/ppermute | solution.py:310
  71.2 0.7 shard_map.105
  71.9 0.2 collective-permute-start.15
  72.1 0.7 shard_map.104
  72.8 0.1 select_bitcast_fusion.1
  72.9 0.7 collective-permute-done.15.got_ref
  73.7 1.7 %collective-permute-start.16 = (bf16[32,1280]{1,0:T(8,128)(2,1)S(1)}, bf16[32,1280]{1,0:T(8,128)(2,1)S(1)}, u32[]{:S(2)}, u32[]{:S(2)}) collective-permute-start(bf16[32,1280]{1,0:T(8,128)(2,1)S(1)} %get-tuple-element.39), channel_id=1, source_target_pairs={{0,24},{4,28},{8,16},{12,20},{16,8},{20,12},{24,0},{28,4},{1,25},{... | collective-permute-start | bytes 245768 | tf_op jit(solution)/shard_map/ppermute | solution.py:327
  75.4 1.3 %collective-permute-start.17 = (bf16[32,1280]{1,0:T(8,128)(2,1)S(1)}, bf16[32,1280]{1,0:T(8,128)(2,1)S(1)}, u32[]{:S(2)}, u32[]{:S(2)}) collective-permute-start(bf16[32,1280]{1,0:T(8,128)(2,1)S(1)} %get-tuple-element.40), channel_id=1, source_target_pairs={{0,16},{4,20},{8,24},{12,28},{16,0},{20,4},{24,8},{28,12},{1,17},{... | collective-permute-start | bytes 245768 | tf_op jit(solution)/shard_map/ppermute | solution.py:327
  76.7 0.5 collective-permute-start.18
  77.4 1.1 %copy.18 = bf16[1,1280,256]{2,1,0:T(8,128)(2,1)} copy(bf16[1,1280,256]{1,2,0:T(8,128)(2,1)S(1)} %bitcast.60) | data formatting | bytes 1310720
  78.5 1.1 %copy.17 = bf16[1,1280,256]{2,1,0:T(8,128)(2,1)} copy(bf16[1,1280,256]{1,2,0:T(8,128)(2,1)S(1)} %bitcast.61) | data formatting | bytes 1310720
  79.6 1.3 %collective-permute-done.17 = bf16[32,1280]{1,0:T(8,128)(2,1)S(1)} collective-permute-done((bf16[32,1280]{1,0:T(8,128)(2,1)S(1)}, bf16[32,1280]{1,0:T(8,128)(2,1)S(1)}, u32[]{:S(2)}, u32[]{:S(2)}) %collective-permute-start.17) | collective-permute-done | bytes 81952 | tf_op jit(solution)/shard_map/ppermute | solution.py:327
  80.9 0.2 collective-permute-done.18
  81.1 0.8 fusion.1
  (37 shorter events, 0.5 us)
Async XLA Ops:
  0.6 13.7 %collective-permute-start.8 = (bf16[128,5120]{1,0:T(8,128)(2,1)}, bf16[128,5120]{1,0:T(8,128)(2,1)}, u32[]{:S(2)}, u32[]{:S(2)}) collective-permute-start(bf16[128,5120]{1,0:T(8,128)(2,1)} %bitcast.62), channel_id=1, source_target_pairs={{0,4},{4,0},{8,12},{12,8},{16,20},{20,16},{24,28},{28,24},{1,5},{5... | collective-permute-start | bytes 3932168 | tf_op jit(solution)/shard_map/ppermute | solution.py:269
  2.1 8.6 %collective-permute-start.2 = (bf16[32,1280]{1,0:T(8,128)(2,1)S(1)}, bf16[32,1280]{1,0:T(8,128)(2,1)S(1)}, u32[]{:S(2)}, u32[]{:S(2)}) collective-permute-start(bf16[32,1280]{1,0:T(8,128)(2,1)S(1)} %convert_bitcast_fusion), channel_id=1, source_target_pairs={{0,2},{1,3},{2,0},{3,1},{4,6},{5,7},{6,4},{7,5},{8,10},{9,11},{10,... | collective-permute-start | bytes 245768 | tf_op jit(solution)/shard_map/ppermute | solution.py:271
  6.7 23.3 %collective-permute-start = (bf16[128,512]{1,0:T(8,128)(2,1)S(1)}, bf16[128,512]{1,0:T(8,128)(2,1)S(1)}, u32[]{:S(2)}, u32[]{:S(2)}) collective-permute-start(bf16[128,512]{1,0:T(8,128)(2,1)S(1)} %bitcast.55), channel_id=1, source_target_pairs={{0,2},{1,3},{2,0},{3,1},{4,6},{5,7},{6,4},{7,5},{8,10},{9,11},{10,... | collective-permute-start | bytes 393224 | tf_op jit(solution)/shard_map/ppermute | solution.py:273
  8.3 8.5 %copy-start = (bf16[128,1280]{1,0:T(8,128)(2,1)}, bf16[128,1280]{1,0:T(8,128)(2,1)S(1)}, u32[]{:S(2)}) copy-start(bf16[128,1280]{1,0:T(8,128)(2,1)S(1)} %get-tuple-element.56.refs_5_) | copy-start | bytes 983044
  8.3 18.2 %collective-permute-start.4 = (bf16[128,1280]{1,0:T(8,128)(2,1)S(1)}, bf16[128,1280]{1,0:T(8,128)(2,1)S(1)}, u32[]{:S(2)}, u32[]{:S(2)}) collective-permute-start(bf16[128,1280]{1,0:T(8,128)(2,1)S(1)} %get-tuple-element.56.refs_5_), channel_id=1, source_target_pairs={{0,1},{1,0},{2,3},{3,2},{4,5},{5,4},{6,7},{7,6},{8,9},{9,8},{10,11... | collective-permute-start | bytes 983048 | tf_op jit(solution)/shard_map/ppermute | solution.py:284
  10.7 15.0 %collective-permute-start.3 = (bf16[64,1280]{1,0:T(8,128)(2,1)S(1)}, bf16[64,1280]{1,0:T(8,128)(2,1)S(1)}, u32[]{:S(2)}, u32[]{:S(2)}) collective-permute-start(bf16[64,1280]{1,0:T(8,128)(2,1)S(1)} %pad_maximum_fusion.5), channel_id=1, source_target_pairs={{0,1},{1,0},{2,3},{3,2},{4,5},{5,4},{6,7},{7,6},{8,9},{9,8},{10,11... | collective-permute-start | bytes 491528 | tf_op jit(solution)/shard_map/ppermute | solution.py:286
  16.8 14.0 %copy-start.9 = (bf16[1,1280,256]{2,1,0:T(8,128)(2,1)S(1)}, bf16[1,1280,256]{2,1,0:T(8,128)(2,1)}, u32[]{:S(2)}) copy-start(bf16[1,1280,256]{2,1,0:T(8,128)(2,1)} %param.10) | copy-start | bytes 1966084
  17.7 51.5 %collective-permute-start.13 = (bf16[256,1280]{1,0:T(8,128)(2,1)}, bf16[256,1280]{1,0:T(8,128)(2,1)S(1)}, u32[]{:S(2)}, u32[]{:S(2)}) collective-permute-start(bf16[256,1280]{1,0:T(8,128)(2,1)} %pad_maximum_fusion), channel_id=1, source_target_pairs={{0,2},{1,3},{2,0},{3,1},{4,7},{5,6},{6,5},{7,4},{8,10},{9,11},{10,... | collective-permute-start | bytes 1966088 | tf_op jit(solution)/shard_map/ppermute | solution.py:281
  26.5 11.9 %collective-permute-start.7 = (bf16[128,1280]{1,0:T(8,128)(2,1)}, bf16[128,1280]{1,0:T(8,128)(2,1)}, u32[]{:S(2)}, u32[]{:S(2)}) collective-permute-start(bf16[128,1280]{1,0:T(8,128)(2,1)} %pad_maximum_fusion.3.refs_0_), channel_id=1, source_target_pairs={{0,24},{4,28},{8,16},{12,20},{16,8},{20,12},{24,0},{28,4},{1,25},{... | collective-permute-start | bytes 983048 | tf_op jit(solution)/shard_map/ppermute | solution.py:293
  29.0 14.2 %collective-permute-start.6 = (bf16[128,1280]{1,0:T(8,128)(2,1)}, bf16[128,1280]{1,0:T(8,128)(2,1)}, u32[]{:S(2)}, u32[]{:S(2)}) collective-permute-start(bf16[128,1280]{1,0:T(8,128)(2,1)} %pad_maximum_fusion.3.refs_0_), channel_id=1, source_target_pairs={{0,16},{4,20},{8,24},{12,28},{16,0},{20,4},{24,8},{28,12},{1,17},{... | collective-permute-start | bytes 983048 | tf_op jit(solution)/shard_map/ppermute | solution.py:293
  29.6 13.7 %collective-permute-start.5 = (bf16[128,1280]{1,0:T(8,128)(2,1)}, bf16[128,1280]{1,0:T(8,128)(2,1)}, u32[]{:S(2)}, u32[]{:S(2)}) collective-permute-start(bf16[128,1280]{1,0:T(8,128)(2,1)} %pad_maximum_fusion.3.refs_0_), channel_id=1, source_target_pairs={{0,8},{4,12},{8,0},{12,4},{16,24},{20,28},{24,16},{28,20},{1,9},{5... | collective-permute-start | bytes 983048 | tf_op jit(solution)/shard_map/ppermute | solution.py:293
  30.0 0.7 copy-start.6
  30.7 19.8 %collective-permute-start.1 = (bf16[256,512]{1,0:T(8,128)(2,1)}, bf16[256,512]{1,0:T(8,128)(2,1)}, u32[]{:S(2)}, u32[]{:S(2)}) collective-permute-start(bf16[256,512]{1,0:T(8,128)(2,1)} %pad_maximum_fusion.4), channel_id=1, source_target_pairs={{0,1},{1,0},{2,3},{3,2},{4,5},{5,4},{6,7},{7,6},{8,9},{9,8},{10,11... | collective-permute-start | bytes 786440 | tf_op jit(solution)/shard_map/ppermute | solution.py:287
  43.3 1.0 %copy-start.1 = (bf16[128,1280]{1,0:T(8,128)(2,1)S(1)}, bf16[128,1280]{1,0:T(8,128)(2,1)}, u32[]{:S(2)}) copy-start(bf16[128,1280]{1,0:T(8,128)(2,1)} %copy-done) | copy-start | bytes 983044
  44.3 1.0 %copy-start.2 = (bf16[128,1280]{1,0:T(8,128)(2,1)S(1)}, bf16[128,1280]{1,0:T(8,128)(2,1)}, u32[]{:S(2)}) copy-start(bf16[128,1280]{1,0:T(8,128)(2,1)} %get-tuple-element.58.refs_11_) | copy-start | bytes 983044
  45.2 1.0 %copy-start.3 = (bf16[128,1280]{1,0:T(8,128)(2,1)S(1)}, bf16[128,1280]{1,0:T(8,128)(2,1)}, u32[]{:S(2)}) copy-start(bf16[128,1280]{1,0:T(8,128)(2,1)} %get-tuple-element.59.refs_10_) | copy-start | bytes 983044
  46.2 1.0 %copy-start.4 = (bf16[128,1280]{1,0:T(8,128)(2,1)S(1)}, bf16[128,1280]{1,0:T(8,128)(2,1)}, u32[]{:S(2)}) copy-start(bf16[128,1280]{1,0:T(8,128)(2,1)} %get-tuple-element.60.refs_9_) | copy-start | bytes 983044
  47.2 1.0 %copy-start.5 = (bf16[128,1280]{1,0:T(8,128)(2,1)S(1)}, bf16[128,1280]{1,0:T(8,128)(2,1)}, u32[]{:S(2)}) copy-start(bf16[128,1280]{1,0:T(8,128)(2,1)} %get-tuple-element.61.refs_8_) | copy-start | bytes 983044
  48.2 3.6 %copy-start.7 = (bf16[128,512]{1,0:T(8,128)(2,1)S(1)}, bf16[128,512]{1,0:T(8,128)(2,1)}, u32[]{:S(2)}) copy-start(bf16[128,512]{1,0:T(8,128)(2,1)} %copy-done.6) | copy-start | bytes 393220
  48.2 3.6 %copy-start.8 = (bf16[1,128,256]{2,1,0:T(8,128)(2,1)S(1)}, bf16[1,128,256]{2,1,0:T(8,128)(2,1)}, u32[]{:S(2)}) copy-start(bf16[1,128,256]{2,1,0:T(8,128)(2,1)} %param.9) | copy-start | bytes 196612
  50.5 1.3 %collective-permute-start.9 = (bf16[4,32,128]{2,1,0:T(8,128)(2,1)S(1)}, bf16[4,32,128]{2,1,0:T(8,128)(2,1)S(1)}, u32[]{:S(2)}, u32[]{:S(2)}) collective-permute-start(bf16[4,32,128]{2,1,0:T(8,128)(2,1)S(1)} %get-tuple-element.31), channel_id=1, source_target_pairs={{0,4},{4,0},{8,12},{12,8},{16,20},{20,16},{24,28},{28,24},{1,5},{5... | collective-permute-start | bytes 98312 | tf_op jit(solution)/shard_map/ppermute | solution.py:301
  53.9 12.4 %collective-permute-start.12 = (bf16[256,128]{1,0:T(8,128)(2,1)S(1)}, bf16[256,128]{1,0:T(8,128)(2,1)S(1)}, u32[]{:S(2)}, u32[]{:S(2)}) collective-permute-start(bf16[256,128]{1,0:T(8,128)(2,1)S(1)} %shard_map.103.refs_0_), channel_id=1, source_target_pairs={{0,3},{1,2},{2,1},{3,0},{4,7},{5,6},{6,5},{7,4},{8,11},{9,10},{10,... | collective-permute-start | bytes 196616 | tf_op jit(solution)/shard_map/ppermute | solution.py:304
  63.5 5.3 %collective-permute-start.11 = (bf16[256,128]{1,0:T(8,128)(2,1)S(1)}, bf16[256,128]{1,0:T(8,128)(2,1)S(1)}, u32[]{:S(2)}, u32[]{:S(2)}) collective-permute-start(bf16[256,128]{1,0:T(8,128)(2,1)S(1)} %shard_map.103.refs_0_), channel_id=1, source_target_pairs={{0,2},{1,3},{2,0},{3,1},{4,6},{5,7},{6,4},{7,5},{8,10},{9,11},{10,... | collective-permute-start | bytes 196616 | tf_op jit(solution)/shard_map/ppermute | solution.py:304
  63.5 5.7 %collective-permute-start.10 = (bf16[256,128]{1,0:T(8,128)(2,1)S(1)}, bf16[256,128]{1,0:T(8,128)(2,1)S(1)}, u32[]{:S(2)}, u32[]{:S(2)}) collective-permute-start(bf16[256,128]{1,0:T(8,128)(2,1)S(1)} %shard_map.103.refs_0_), channel_id=1, source_target_pairs={{0,1},{1,0},{2,3},{3,2},{4,5},{5,4},{6,7},{7,6},{8,9},{9,8},{10,11... | collective-permute-start | bytes 196616 | tf_op jit(solution)/shard_map/ppermute | solution.py:304
  69.1 2.1 %collective-permute-start.14 = (bf16[256,1280]{1,0:T(8,128)(2,1)S(1)}, bf16[256,1280]{1,0:T(8,128)(2,1)S(1)}, u32[]{:S(2)}, u32[]{:S(2)}) collective-permute-start(bf16[256,1280]{1,0:T(8,128)(2,1)S(1)} %collective-permute-done.13.refs_6_), channel_id=1, source_target_pairs={{0,4},{4,0},{8,12},{12,8},{16,20},{20,16},{24,28},{28,24},{1,5},{5... | collective-permute-start | bytes 1966088 | tf_op jit(solution)/shard_map/ppermute | solution.py:310
  71.9 1.7 %collective-permute-start.15 = (bf16[4,32,1280]{2,1,0:T(8,128)(2,1)S(1)}, bf16[4,32,1280]{2,1,0:T(8,128)(2,1)S(1)}, u32[]{:S(2)}, u32[]{:S(2)}) collective-permute-start(bf16[4,32,1280]{2,1,0:T(8,128)(2,1)S(1)} %get-tuple-element.37), channel_id=1, source_target_pairs={{0,4},{4,0},{8,12},{12,8},{16,20},{20,16},{24,28},{28,24},{1,5},{5... | collective-permute-start | bytes 983048 | tf_op jit(solution)/shard_map/ppermute | solution.py:314
  73.7 5.9 %collective-permute-start.16 = (bf16[32,1280]{1,0:T(8,128)(2,1)S(1)}, bf16[32,1280]{1,0:T(8,128)(2,1)S(1)}, u32[]{:S(2)}, u32[]{:S(2)}) collective-permute-start(bf16[32,1280]{1,0:T(8,128)(2,1)S(1)} %get-tuple-element.39), channel_id=1, source_target_pairs={{0,24},{4,28},{8,16},{12,20},{16,8},{20,12},{24,0},{28,4},{1,25},{... | collective-permute-start | bytes 245768 | tf_op jit(solution)/shard_map/ppermute | solution.py:327
  75.4 5.5 %collective-permute-start.17 = (bf16[32,1280]{1,0:T(8,128)(2,1)S(1)}, bf16[32,1280]{1,0:T(8,128)(2,1)S(1)}, u32[]{:S(2)}, u32[]{:S(2)}) collective-permute-start(bf16[32,1280]{1,0:T(8,128)(2,1)S(1)} %get-tuple-element.40), channel_id=1, source_target_pairs={{0,16},{4,20},{8,24},{12,28},{16,0},{20,4},{24,8},{28,12},{1,17},{... | collective-permute-start | bytes 245768 | tf_op jit(solution)/shard_map/ppermute | solution.py:327
  76.7 4.4 %collective-permute-start.18 = (bf16[32,1280]{1,0:T(8,128)(2,1)S(1)}, bf16[32,1280]{1,0:T(8,128)(2,1)S(1)}, u32[]{:S(2)}, u32[]{:S(2)}) collective-permute-start(bf16[32,1280]{1,0:T(8,128)(2,1)S(1)} %get-tuple-element.41), channel_id=1, source_target_pairs={{0,8},{4,12},{8,0},{12,4},{16,24},{20,28},{24,16},{28,20},{1,9},{5... | collective-permute-start | bytes 245768 | tf_op jit(solution)/shard_map/ppermute | solution.py:327
  78.4 2.7 %copy-start.10 = (f32[1280,32]{0,1:T(8,128)S(1)}, f32[1280,32]{0,1:T(8,128)}, u32[]{:S(2)}) copy-start(f32[1280,32]{0,1:T(8,128)} %param.12) | copy-start | bytes 491524
  78.4 2.7 %copy-start.11 = (f32[1280,32]{0,1:T(8,128)S(1)}, f32[1280,32]{0,1:T(8,128)}, u32[]{:S(2)}) copy-start(f32[1280,32]{0,1:T(8,128)} %param.13) | copy-start | bytes 491524

commit v13 on v12

--- a/solution.py
+++ b/solution.py
@@ -292,9 +292,6 @@
     for step in range(1, n_chip):
         spread[step] = lax.ppermute(held, "island", pair_perm(n_chip, step, 2))
 
-    first = first_moment[0].T.reshape(n_chip, 2, share, block)
-    second = second_moment[0].T.reshape(n_chip, 2, share, block)
-    spread, first, second = lax.optimization_barrier((spread, first, second))
     mine, for_partner = half_queries(
         rounds, [spread], own_blocks, partner_blocks, share, inverse
     )
@@ -308,6 +305,8 @@
     gathered = [own_blocks[0], near]
     for got in far:
         gathered += [got, lax.ppermute(got, "island", swap)]
+    first = first_moment[0].T.reshape(n_chip, 2, share, block)
+    second = second_moment[0].T.reshape(n_chip, 2, share, block)
     first_other, second_other, delta_other = gradient_adam(
         dqueries, gathered, first, second, False, inverse
     )

time: 82.4 us -> 72 us (0.87)
  waiting for transfers between devices: 26.7 us -> 37.3 us
  starting transfers between devices: 30.7 us -> 22.5 us
  local copies, waits for them, and re-layouts: 13.6 us -> 5.51 us
  Pallas kernels: 5.87 us -> 3.59 us
  other arithmetic: 4.31 us -> 2.03 us
    ppermute x1, waiting for transfers between devices: 4.64 us -> 13.6 us  [on_device(): lax.ppermute(held, 'seq', pair_perm(n_seq, bit))]
    unnamed x27 -> x13, local copies, waits for them, and re-layouts: 7.96 us -> 2.19 us
    ppermute x3, starting transfers between devices: 10.2 us -> 4.44 us  [on_device(): lax.ppermute(dquery, 'seq', pair_perm(n_seq, k))]
    ppermute x3, waiting for transfers between devices: 11 us -> 14.3 us  [on_device(): spread[step] = lax.ppermute(held, 'island', pair_perm(n_chip, step, 2))]
    ppermute x1, starting transfers between devices: 3.59 us -> 0.82 us  [on_device(): lax.ppermute(held, 'seq', pair_perm(n_seq, bit))]
    dynamic_slice x2, local copies, waits for them, and re-layouts: 3.98 us -> 1.66 us  [feature_block(): lax.dynamic_slice(matrix, (0, jnp.bitwise_xor(seq, k) * block), (rows, bl...]
    ppermute x1, waiting for transfers between devices: 2.1 us -> 0.5 us  [on_device(): gathered += [got, lax.ppermute(got, 'island', swap)]]
    pallas_call x1, Pallas kernels: 2.28 us -> 0.97 us  [half_queries(): pl.pallas_call(functools.partial(query_kernel, rounds, n_chip, inverse),...]
  transfers between devices with their start and end apart: 19 -> 19, of which waited for: 12 -> 11; matrix products, arithmetic and copies ran while one was open for 15% -> 9% of each run, Pallas kernels for 6% -> 4%
where the time goes in v13:
time: 72 us; the launch traced here: 71.8 us
  waiting for transfers between devices  37.3 us (52%)
  starting transfers between devices  22.5 us (31%)
  local copies, waits for them, and re-layouts  5.51 us (8%)
  Pallas kernels  3.59 us (5%)
  other arithmetic  2.03 us (3%)
  between operations  0.82 us (1%)
    ppermute x3, waiting for transfers between devices, on_device(): spread[step] = lax.ppermute(held, 'island', pair_perm(n_chip, step, 2))  14.3 us
    ppermute x1, waiting for transfers between devices, on_device(): lax.ppermute(held, 'seq', pair_perm(n_seq, bit))  13.6 us
    ppermute x3, starting transfers between devices, on_device(): lax.ppermute(dquery, 'seq', pair_perm(n_seq, k))  4.44 us
    ppermute x3, waiting for transfers between devices, on_device(): lax.ppermute(dquery, 'seq', pair_perm(n_seq, k))  4.27 us
    ppermute x1, starting transfers between devices, on_device(): held = jnp.concatenate([weight, lax.ppermute(weight, 'seq', far_perm)], 0)  3.67 us
    ppermute x3, starting transfers between devices, on_device(): spread[step] = lax.ppermute(held, 'island', pair_perm(n_chip, step, 2))  3.65 us
    ppermute x3, starting transfers between devices, on_device(): lax.ppermute(parts[step], 'island', pair_perm(n_chip, step, 2))  3.55 us
    ppermute x1, starting transfers between devices, on_device(): lax.ppermute(both, ('island', 'seq'), far_pairs(n_island, n_seq, k))  3.5 us
  transfers between devices with their start and end apart: 19, of which 11 were waited for; matrix products, arithmetic and copies ran while one was open for 9% of the time, Pallas kernels for 4%

profile of v13, /device:TPU:0, one launch (start us, length us, event | category | flops | bytes accessed | tf_op | source)
XLA Modules:
  0.0 71.8 jit_solution(11240755595590545108)
XLA Ops:
  0.6 0.5 collective-permute-start.8
  1.1 0.9 %convert_bitcast_fusion = bf16[32,1280]{1,0:T(8,128)(2,1)S(1)} fusion(f32[1280,32]{0,1:T(8,128)} %param.12), kind=kLoop, calls=%fused_computation.20 | loop fusion | flops 40960 | bytes 245760 | tf_op jit(solution)/shard_map/convert_element_type | solution.py:270
  2.1 3.7 %collective-permute-start.2 = (bf16[32,1280]{1,0:T(8,128)(2,1)S(1)}, bf16[32,1280]{1,0:T(8,128)(2,1)S(1)}, u32[]{:S(2)}, u32[]{:S(2)}) collective-permute-start(bf16[32,1280]{1,0:T(8,128)(2,1)S(1)} %convert_bitcast_fusion), channel_id=1, source_target_pairs={{0,2},{1,3},{2,0},{3,1},{4,6},{5,7},{6,4},{7,5},{8,10},{9,11},{10,... | collective-permute-start | bytes 245768 | tf_op jit(solution)/shard_map/ppermute | solution.py:271
  5.7 1.5 %dynamic-slice_bitcast_fusion = (bf16[128,1280]{1,0:T(8,128)(2,1)S(1)}, bf16[128,1280]{1,0:T(8,128)(2,1)S(1)}, bf16[128,1280]{1,0:T(8,128)(2,1)S(1)}, bf16[128,1280]{1,0:T(8,128)(2,1)S(1)}, bf16[128,1280]{1,0:T(8,128)(2,1)S(1)}) fusion(bf16[1,128,5120]{2,1,0:T(8,128)(2,1)} %param.7, s32[]{:T(128)S(6)} %select_n.44, s32[]{:T(128)S(6)} %select_n.43, ...), kind=kLoop, calls=%fused_computation.8 | loop fusion | bytes 3276820 | tf_op jit(solution)/shard_map/dynamic_slice | solution.py:276
  7.3 1.6 %collective-permute-start.4 = (bf16[128,1280]{1,0:T(8,128)(2,1)S(1)}, bf16[128,1280]{1,0:T(8,128)(2,1)S(1)}, u32[]{:S(2)}, u32[]{:S(2)}) collective-permute-start(bf16[128,1280]{1,0:T(8,128)(2,1)S(1)} %get-tuple-element.44.refs_5_), channel_id=1, source_target_pairs={{0,1},{1,0},{2,3},{3,2},{4,5},{5,4},{6,7},{7,6},{8,9},{9,8},{10,11... | collective-permute-start | bytes 983048 | tf_op jit(solution)/shard_map/ppermute | solution.py:284
  8.9 0.4 collective-permute-start
  9.3 1.3 %collective-permute-done.2 = bf16[32,1280]{1,0:T(8,128)(2,1)S(1)} collective-permute-done((bf16[32,1280]{1,0:T(8,128)(2,1)S(1)}, bf16[32,1280]{1,0:T(8,128)(2,1)S(1)}, u32[]{:S(2)}, u32[]{:S(2)}) %collective-permute-start.2) | collective-permute-done | bytes 81952 | tf_op jit(solution)/shard_map/ppermute | solution.py:271
  10.7 0.8 %collective-permute-start.3 = (bf16[64,1280]{1,0:T(8,128)(2,1)S(1)}, bf16[64,1280]{1,0:T(8,128)(2,1)S(1)}, u32[]{:S(2)}, u32[]{:S(2)}) collective-permute-start(bf16[64,1280]{1,0:T(8,128)(2,1)S(1)} %pad_maximum_fusion.5), channel_id=1, source_target_pairs={{0,1},{1,0},{2,3},{3,2},{4,5},{5,4},{6,7},{7,6},{8,9},{9,8},{10,11... | collective-permute-start | bytes 491528 | tf_op jit(solution)/shard_map/ppermute | solution.py:286
  11.5 0.1 constant_dynamic-slice_fusion
  11.7 3.5 %collective-permute-start.13 = (bf16[256,1280]{1,0:T(8,128)(2,1)S(1)}, bf16[256,1280]{1,0:T(8,128)(2,1)S(1)}, u32[]{:S(2)}, u32[]{:S(2)}) collective-permute-start(bf16[256,1280]{1,0:T(8,128)(2,1)S(1)} %pad_maximum_fusion), channel_id=1, source_target_pairs={{0,2},{1,3},{2,0},{3,1},{4,7},{5,6},{6,5},{7,4},{8,10},{9,11},{10,... | collective-permute-start | bytes 1966088 | tf_op jit(solution)/shard_map/ppermute | solution.py:281
  15.2 13.6 %collective-permute-done.3 = bf16[64,1280]{1,0:T(8,128)(2,1)S(1)} collective-permute-done((bf16[64,1280]{1,0:T(8,128)(2,1)S(1)}, bf16[64,1280]{1,0:T(8,128)(2,1)S(1)}, u32[]{:S(2)}, u32[]{:S(2)}) %collective-permute-start.3) | collective-permute-done | bytes 163872 | tf_op jit(solution)/shard_map/ppermute | solution.py:286
  28.8 0.0 collective-permute-done.4.refs_5_
  28.8 2.1 %collective-permute-start.5 = (bf16[128,1280]{1,0:T(8,128)(2,1)S(1)}, bf16[128,1280]{1,0:T(8,128)(2,1)S(1)}, u32[]{:S(2)}, u32[]{:S(2)}) collective-permute-start(bf16[128,1280]{1,0:T(8,128)(2,1)S(1)} %pad_maximum_fusion.3.refs_0_), channel_id=1, source_target_pairs={{0,8},{4,12},{8,0},{12,4},{16,24},{20,28},{24,16},{28,20},{1,9},{5... | collective-permute-start | bytes 983048 | tf_op jit(solution)/shard_map/ppermute | solution.py:293
  30.9 1.5 %collective-permute-start.6 = (bf16[128,1280]{1,0:T(8,128)(2,1)S(1)}, bf16[128,1280]{1,0:T(8,128)(2,1)S(1)}, u32[]{:S(2)}, u32[]{:S(2)}) collective-permute-start(bf16[128,1280]{1,0:T(8,128)(2,1)S(1)} %pad_maximum_fusion.3.refs_0_), channel_id=1, source_target_pairs={{0,16},{4,20},{8,24},{12,28},{16,0},{20,4},{24,8},{28,12},{1,17},{... | collective-permute-start | bytes 983048 | tf_op jit(solution)/shard_map/ppermute | solution.py:293
  32.4 0.0 collective-permute-start.7
  32.5 0.0 collective-permute-done.refs_2_.refs_3_
  32.5 0.1 collective-permute-start.1
  32.6 6.9 %collective-permute-done.5.refs_1_ = bf16[128,1280]{1,0:T(8,128)(2,1)S(1)} collective-permute-done((bf16[128,1280]{1,0:T(8,128)(2,1)S(1)}, bf16[128,1280]{1,0:T(8,128)(2,1)S(1)}, u32[]{:S(2)}, u32[]{:S(2)}) %collective-permute-start.5) | collective-permute-done | bytes 327712 | tf_op jit(solution)/shard_map/ppermute | solution.py:293
  39.5 7.4 %collective-permute-done.6.refs_2_ = bf16[128,1280]{1,0:T(8,128)(2,1)S(1)} collective-permute-done((bf16[128,1280]{1,0:T(8,128)(2,1)S(1)}, bf16[128,1280]{1,0:T(8,128)(2,1)S(1)}, u32[]{:S(2)}, u32[]{:S(2)}) %collective-permute-start.6) | collective-permute-done | bytes 327712 | tf_op jit(solution)/shard_map/ppermute | solution.py:293
  46.9 1.0 %shard_map.102 = (bf16[4,32,128]{2,1,0:T(8,128)(2,1)S(1)}, bf16[4,32,128]{2,1,0:T(8,128)(2,1)S(1)}) custom-call(bf16[128,1280]{1,0:T(8,128)(2,1)S(1)} %pad_maximum_fusion.3.refs_0_, bf16[128,1280]{1,0:T(8,128)(2,1)S(1)} %collective-permute-done.5.refs_1_, bf16[128,1280]{1,0:T(8,128)(2,1)S(1)} %collective-permute-done.6.refs_2_, ...), custom_call_target="tpu_custom_call" | custom-call | flops 335544320 | bytes 3932160 | tf_op jit(solution)/shard_map/pallas_call | solution.py:84
  47.9 0.0 copy-start.1
  47.9 0.1 collective-permute-start.9
  48.0 1.2 %collective-permute-done.9.refs_7_ = bf16[4,32,128]{2,1,0:T(8,128)(2,1)S(1)} collective-permute-done((bf16[4,32,128]{2,1,0:T(8,128)(2,1)S(1)}, bf16[4,32,128]{2,1,0:T(8,128)(2,1)S(1)}, u32[]{:S(2)}, u32[]{:S(2)}) %collective-permute-start.9) | collective-permute-done | bytes 32800 | tf_op jit(solution)/shard_map/ppermute | solution.py:298
  49.2 1.2 %shard_map.103.refs_0_ = bf16[256,128]{1,0:T(8,128)(2,1)S(1)} custom-call(bf16[128,512]{1,0:T(8,128)(2,1)S(1)} %bitcast.57, bf16[128,512]{1,0:T(8,128)(2,1)S(1)} %bitcast.58, bf16[128,512]{1,0:T(8,128)(2,1)S(1)} %collective-permute-done.refs_2_.refs_3_, bf16[128,512]{1,0:T(8,128)(2,1)S(1)} %collective-permute-done.refs_2_.refs_3_, ...), custom_call_target="tpu_custom_call" | custom-call | flops 402653184 | bytes 786432 | tf_op jit(solution)/shard_map/pallas_call | solution.py:164
  50.4 0.1 collective-permute-start.10
  50.5 2.2 %collective-permute-start.11 = (bf16[256,128]{1,0:T(8,128)(2,1)S(1)}, bf16[256,128]{1,0:T(8,128)(2,1)S(1)}, u32[]{:S(2)}, u32[]{:S(2)}) collective-permute-start(bf16[256,128]{1,0:T(8,128)(2,1)S(1)} %shard_map.103.refs_0_), channel_id=1, source_target_pairs={{0,2},{1,3},{2,0},{3,1},{4,6},{5,7},{6,4},{7,5},{8,10},{9,11},{10,... | collective-permute-start | bytes 196616 | tf_op jit(solution)/shard_map/ppermute | solution.py:301
  52.7 2.2 %collective-permute-start.12 = (bf16[256,128]{1,0:T(8,128)(2,1)S(1)}, bf16[256,128]{1,0:T(8,128)(2,1)S(1)}, u32[]{:S(2)}, u32[]{:S(2)}) collective-permute-start(bf16[256,128]{1,0:T(8,128)(2,1)S(1)} %shard_map.103.refs_0_), channel_id=1, source_target_pairs={{0,3},{1,2},{2,1},{3,0},{4,7},{5,6},{6,5},{7,4},{8,11},{9,10},{10,... | collective-permute-start | bytes 196616 | tf_op jit(solution)/shard_map/ppermute | solution.py:301
  54.9 0.8 %collective-permute-done.10.refs_1_ = bf16[256,128]{1,0:T(8,128)(2,1)S(1)} collective-permute-done((bf16[256,128]{1,0:T(8,128)(2,1)S(1)}, bf16[256,128]{1,0:T(8,128)(2,1)S(1)}, u32[]{:S(2)}, u32[]{:S(2)}) %collective-permute-start.10) | collective-permute-done | bytes 65568 | tf_op jit(solution)/shard_map/ppermute | solution.py:301
  55.7 3.5 %collective-permute-done.11.refs_2_ = bf16[256,128]{1,0:T(8,128)(2,1)S(1)} collective-permute-done((bf16[256,128]{1,0:T(8,128)(2,1)S(1)}, bf16[256,128]{1,0:T(8,128)(2,1)S(1)}, u32[]{:S(2)}, u32[]{:S(2)}) %collective-permute-start.11) | collective-permute-done | bytes 65568 | tf_op jit(solution)/shard_map/ppermute | solution.py:301
  59.2 0.2 copy.13
  59.4 1.3 %copy.14 = bf16[256,1280]{1,0:T(8,128)(2,1)S(1)} copy(bf16[256,1280]{0,1:T(8,128)(2,1)} %bitcast.64) | data formatting | bytes 1310720 | tf_op jit(solution)/shard_map/transpose | solution.py:309
  60.7 0.5 collective-permute-done.14.refs_7_
  61.2 0.7 shard_map.105
  61.9 0.2 collective-permute-start.15
  62.1 0.7 shard_map.104
  62.8 0.1 select_bitcast_fusion.1
  62.9 0.1 pad_maximum_fusion.2
  62.9 0.7 collective-permute-done.15.got_ref
  63.6 0.1 shard_map.106
  63.7 1.5 %collective-permute-start.16 = (bf16[32,1280]{1,0:T(8,128)(2,1)S(1)}, bf16[32,1280]{1,0:T(8,128)(2,1)S(1)}, u32[]{:S(2)}, u32[]{:S(2)}) collective-permute-start(bf16[32,1280]{1,0:T(8,128)(2,1)S(1)} %get-tuple-element.27), channel_id=1, source_target_pairs={{0,24},{4,28},{8,16},{12,20},{16,8},{20,12},{24,0},{28,4},{1,25},{... | collective-permute-start | bytes 245768 | tf_op jit(solution)/shard_map/ppermute | solution.py:326
  65.2 1.2 %collective-permute-start.17 = (bf16[32,1280]{1,0:T(8,128)(2,1)S(1)}, bf16[32,1280]{1,0:T(8,128)(2,1)S(1)}, u32[]{:S(2)}, u32[]{:S(2)}) collective-permute-start(bf16[32,1280]{1,0:T(8,128)(2,1)S(1)} %get-tuple-element.28), channel_id=1, source_target_pairs={{0,16},{4,20},{8,24},{12,28},{16,0},{20,4},{24,8},{28,12},{1,17},{... | collective-permute-start | bytes 245768 | tf_op jit(solution)/shard_map/ppermute | solution.py:326
  66.4 0.8 %collective-permute-start.18 = (bf16[32,1280]{1,0:T(8,128)(2,1)S(1)}, bf16[32,1280]{1,0:T(8,128)(2,1)S(1)}, u32[]{:S(2)}, u32[]{:S(2)}) collective-permute-start(bf16[32,1280]{1,0:T(8,128)(2,1)S(1)} %get-tuple-element.29), channel_id=1, source_target_pairs={{0,8},{4,12},{8,0},{12,4},{16,24},{20,28},{24,16},{28,20},{1,9},{5... | collective-permute-start | bytes 245768 | tf_op jit(solution)/shard_map/ppermute | solution.py:326
  67.2 0.1 pad_maximum_fusion.1
  67.3 1.1 %copy.18 = bf16[1,1280,256]{2,1,0:T(8,128)(2,1)} copy(bf16[1,1280,256]{1,2,0:T(8,128)(2,1)S(1)} %bitcast.60) | data formatting | bytes 1310720
  68.5 1.1 %copy.17 = bf16[1,1280,256]{2,1,0:T(8,128)(2,1)} copy(bf16[1,1280,256]{1,2,0:T(8,128)(2,1)S(1)} %bitcast.61) | data formatting | bytes 1310720
  69.6 1.3 %collective-permute-done.17 = bf16[32,1280]{1,0:T(8,128)(2,1)S(1)} collective-permute-done((bf16[32,1280]{1,0:T(8,128)(2,1)S(1)}, bf16[32,1280]{1,0:T(8,128)(2,1)S(1)}, u32[]{:S(2)}, u32[]{:S(2)}) %collective-permute-start.17) | collective-permute-done | bytes 81952 | tf_op jit(solution)/shard_map/ppermute | solution.py:326
  70.9 0.1 collective-permute-done.18
  71.0 0.8 %fusion.1 = (f32[1280,32]{0,1:T(8,128)}, f32[1280,32]{0,1:T(8,128)}) fusion(f32[1280,32]{0,1:T(8,128)S(1)} %copy-done.2, bf16[32,1280]{1,0:T(8,128)(2,1)S(1)} %collective-permute-done.18, bf16[32,1280]{1,0:T(8,128)(2,1)S(1)} %collective-permute-done.17, f32[32,1280]{1,0:T(8,128)S(1)} %get-tuple-element.26, bf16[32,1280]{1,0:T(8,128)(2,1)S(1)} %collective-permute-done.16, ...), kind=kLoop, calls=%fused_computation.18 | loop fusion | flops 532480 | bytes 1064960 | tf_op jit(solution)/shard_map/sub | solution.py:331
  (23 shorter events, 0.2 us)
Async XLA Ops:
  0.6 10.9 %collective-permute-start.8 = (bf16[128,5120]{1,0:T(8,128)(2,1)}, bf16[128,5120]{1,0:T(8,128)(2,1)S(1)}, u32[]{:S(2)}, u32[]{:S(2)}) collective-permute-start(bf16[128,5120]{1,0:T(8,128)(2,1)} %bitcast.62), channel_id=1, source_target_pairs={{0,4},{4,0},{8,12},{12,8},{16,20},{20,16},{24,28},{28,24},{1,5},{5... | collective-permute-start | bytes 3932168 | tf_op jit(solution)/shard_map/ppermute | solution.py:269
  2.1 8.6 %collective-permute-start.2 = (bf16[32,1280]{1,0:T(8,128)(2,1)S(1)}, bf16[32,1280]{1,0:T(8,128)(2,1)S(1)}, u32[]{:S(2)}, u32[]{:S(2)}) collective-permute-start(bf16[32,1280]{1,0:T(8,128)(2,1)S(1)} %convert_bitcast_fusion), channel_id=1, source_target_pairs={{0,2},{1,3},{2,0},{3,1},{4,6},{5,7},{6,4},{7,5},{8,10},{9,11},{10,... | collective-permute-start | bytes 245768 | tf_op jit(solution)/shard_map/ppermute | solution.py:271
  5.7 3.2 %copy-start.4 = (bf16[1,128,2,256]{3,2,1,0:T(2,128)(2,1)S(1)}, bf16[1,128,2,256]{3,2,1,0:T(2,128)(2,1)}, u32[]{:S(2)}) copy-start(bf16[1,128,2,256]{3,2,1,0:T(2,128)(2,1)} %param.8) | copy-start | bytes 393220
  7.3 21.5 %collective-permute-start.4 = (bf16[128,1280]{1,0:T(8,128)(2,1)S(1)}, bf16[128,1280]{1,0:T(8,128)(2,1)S(1)}, u32[]{:S(2)}, u32[]{:S(2)}) collective-permute-start(bf16[128,1280]{1,0:T(8,128)(2,1)S(1)} %get-tuple-element.44.refs_5_), channel_id=1, source_target_pairs={{0,1},{1,0},{2,3},{3,2},{4,5},{5,4},{6,7},{7,6},{8,9},{9,8},{10,11... | collective-permute-start | bytes 983048 | tf_op jit(solution)/shard_map/ppermute | solution.py:284
  8.9 23.5 %collective-permute-start = (bf16[128,512]{1,0:T(8,128)(2,1)S(1)}, bf16[128,512]{1,0:T(8,128)(2,1)S(1)}, u32[]{:S(2)}, u32[]{:S(2)}) collective-permute-start(bf16[128,512]{1,0:T(8,128)(2,1)S(1)} %bitcast.55), channel_id=1, source_target_pairs={{0,2},{1,3},{2,0},{3,1},{4,6},{5,7},{6,4},{7,5},{8,10},{9,11},{10,... | collective-permute-start | bytes 393224 | tf_op jit(solution)/shard_map/ppermute | solution.py:273
  10.7 18.1 %collective-permute-start.3 = (bf16[64,1280]{1,0:T(8,128)(2,1)S(1)}, bf16[64,1280]{1,0:T(8,128)(2,1)S(1)}, u32[]{:S(2)}, u32[]{:S(2)}) collective-permute-start(bf16[64,1280]{1,0:T(8,128)(2,1)S(1)} %pad_maximum_fusion.5), channel_id=1, source_target_pairs={{0,1},{1,0},{2,3},{3,2},{4,5},{5,4},{6,7},{7,6},{8,9},{9,8},{10,11... | collective-permute-start | bytes 491528 | tf_op jit(solution)/shard_map/ppermute | solution.py:286
  11.7 47.4 %collective-permute-start.13 = (bf16[256,1280]{1,0:T(8,128)(2,1)S(1)}, bf16[256,1280]{1,0:T(8,128)(2,1)S(1)}, u32[]{:S(2)}, u32[]{:S(2)}) collective-permute-start(bf16[256,1280]{1,0:T(8,128)(2,1)S(1)} %pad_maximum_fusion), channel_id=1, source_target_pairs={{0,2},{1,3},{2,0},{3,1},{4,7},{5,6},{6,5},{7,4},{8,10},{9,11},{10,... | collective-permute-start | bytes 1966088 | tf_op jit(solution)/shard_map/ppermute | solution.py:281
  28.8 10.7 %collective-permute-start.5 = (bf16[128,1280]{1,0:T(8,128)(2,1)S(1)}, bf16[128,1280]{1,0:T(8,128)(2,1)S(1)}, u32[]{:S(2)}, u32[]{:S(2)}) collective-permute-start(bf16[128,1280]{1,0:T(8,128)(2,1)S(1)} %pad_maximum_fusion.3.refs_0_), channel_id=1, source_target_pairs={{0,8},{4,12},{8,0},{12,4},{16,24},{20,28},{24,16},{28,20},{1,9},{5... | collective-permute-start | bytes 983048 | tf_op jit(solution)/shard_map/ppermute | solution.py:293
  30.9 16.0 %collective-permute-start.6 = (bf16[128,1280]{1,0:T(8,128)(2,1)S(1)}, bf16[128,1280]{1,0:T(8,128)(2,1)S(1)}, u32[]{:S(2)}, u32[]{:S(2)}) collective-permute-start(bf16[128,1280]{1,0:T(8,128)(2,1)S(1)} %pad_maximum_fusion.3.refs_0_), channel_id=1, source_target_pairs={{0,16},{4,20},{8,24},{12,28},{16,0},{20,4},{24,8},{28,12},{1,17},{... | collective-permute-start | bytes 983048 | tf_op jit(solution)/shard_map/ppermute | solution.py:293
  32.4 14.5 %collective-permute-start.7 = (bf16[128,1280]{1,0:T(8,128)(2,1)S(1)}, bf16[128,1280]{1,0:T(8,128)(2,1)S(1)}, u32[]{:S(2)}, u32[]{:S(2)}) collective-permute-start(bf16[128,1280]{1,0:T(8,128)(2,1)S(1)} %pad_maximum_fusion.3.refs_0_), channel_id=1, source_target_pairs={{0,24},{4,28},{8,16},{12,20},{16,8},{20,12},{24,0},{28,4},{1,25},{... | collective-permute-start | bytes 983048 | tf_op jit(solution)/shard_map/ppermute | solution.py:293
  32.5 15.5 %collective-permute-start.1 = (bf16[256,512]{1,0:T(8,128)(2,1)S(1)}, bf16[256,512]{1,0:T(8,128)(2,1)S(1)}, u32[]{:S(2)}, u32[]{:S(2)}) collective-permute-start(bf16[256,512]{1,0:T(8,128)(2,1)S(1)} %pad_maximum_fusion.4), channel_id=1, source_target_pairs={{0,1},{1,0},{2,3},{3,2},{4,5},{5,4},{6,7},{7,6},{8,9},{9,8},{10,11... | collective-permute-start | bytes 786440 | tf_op jit(solution)/shard_map/ppermute | solution.py:287
  46.9 2.3 %copy-start = (bf16[1,128,256]{2,1,0:T(8,128)(2,1)S(1)}, bf16[1,128,256]{2,1,0:T(8,128)(2,1)}, u32[]{:S(2)}) copy-start(bf16[1,128,256]{2,1,0:T(8,128)(2,1)} %param.9) | copy-start | bytes 196612
  47.9 11.3 %copy-start.1 = (bf16[1,1280,256]{2,1,0:T(8,128)(2,1)S(1)}, bf16[1,1280,256]{2,1,0:T(8,128)(2,1)}, u32[]{:S(2)}) copy-start(bf16[1,1280,256]{2,1,0:T(8,128)(2,1)} %param.10) | copy-start | bytes 1966084
  47.9 1.3 %collective-permute-start.9 = (bf16[4,32,128]{2,1,0:T(8,128)(2,1)S(1)}, bf16[4,32,128]{2,1,0:T(8,128)(2,1)S(1)}, u32[]{:S(2)}, u32[]{:S(2)}) collective-permute-start(bf16[4,32,128]{2,1,0:T(8,128)(2,1)S(1)} %get-tuple-element.21), channel_id=1, source_target_pairs={{0,4},{4,0},{8,12},{12,8},{16,20},{20,16},{24,28},{28,24},{1,5},{5... | collective-permute-start | bytes 98312 | tf_op jit(solution)/shard_map/ppermute | solution.py:298
  50.4 5.2 %collective-permute-start.10 = (bf16[256,128]{1,0:T(8,128)(2,1)S(1)}, bf16[256,128]{1,0:T(8,128)(2,1)S(1)}, u32[]{:S(2)}, u32[]{:S(2)}) collective-permute-start(bf16[256,128]{1,0:T(8,128)(2,1)S(1)} %shard_map.103.refs_0_), channel_id=1, source_target_pairs={{0,1},{1,0},{2,3},{3,2},{4,5},{5,4},{6,7},{7,6},{8,9},{9,8},{10,11... | collective-permute-start | bytes 196616 | tf_op jit(solution)/shard_map/ppermute | solution.py:301
  50.5 8.6 %collective-permute-start.11 = (bf16[256,128]{1,0:T(8,128)(2,1)S(1)}, bf16[256,128]{1,0:T(8,128)(2,1)S(1)}, u32[]{:S(2)}, u32[]{:S(2)}) collective-permute-start(bf16[256,128]{1,0:T(8,128)(2,1)S(1)} %shard_map.103.refs_0_), channel_id=1, source_target_pairs={{0,2},{1,3},{2,0},{3,1},{4,6},{5,7},{6,4},{7,5},{8,10},{9,11},{10,... | collective-permute-start | bytes 196616 | tf_op jit(solution)/shard_map/ppermute | solution.py:301
  52.7 6.4 %collective-permute-start.12 = (bf16[256,128]{1,0:T(8,128)(2,1)S(1)}, bf16[256,128]{1,0:T(8,128)(2,1)S(1)}, u32[]{:S(2)}, u32[]{:S(2)}) collective-permute-start(bf16[256,128]{1,0:T(8,128)(2,1)S(1)} %shard_map.103.refs_0_), channel_id=1, source_target_pairs={{0,3},{1,2},{2,1},{3,0},{4,7},{5,6},{6,5},{7,4},{8,11},{9,10},{10,... | collective-permute-start | bytes 196616 | tf_op jit(solution)/shard_map/ppermute | solution.py:301
  59.1 2.1 %collective-permute-start.14 = (bf16[256,1280]{1,0:T(8,128)(2,1)S(1)}, bf16[256,1280]{1,0:T(8,128)(2,1)S(1)}, u32[]{:S(2)}, u32[]{:S(2)}) collective-permute-start(bf16[256,1280]{1,0:T(8,128)(2,1)S(1)} %collective-permute-done.13.refs_6_), channel_id=1, source_target_pairs={{0,4},{4,0},{8,12},{12,8},{16,20},{20,16},{24,28},{28,24},{1,5},{5... | collective-permute-start | bytes 1966088 | tf_op jit(solution)/shard_map/ppermute | solution.py:307
  61.9 1.7 %collective-permute-start.15 = (bf16[4,32,1280]{2,1,0:T(8,128)(2,1)S(1)}, bf16[4,32,1280]{2,1,0:T(8,128)(2,1)S(1)}, u32[]{:S(2)}, u32[]{:S(2)}) collective-permute-start(bf16[4,32,1280]{2,1,0:T(8,128)(2,1)S(1)} %get-tuple-element.25), channel_id=1, source_target_pairs={{0,4},{4,0},{8,12},{12,8},{16,20},{20,16},{24,28},{28,24},{1,5},{5... | collective-permute-start | bytes 983048 | tf_op jit(solution)/shard_map/ppermute | solution.py:313
  63.7 5.9 %collective-permute-start.16 = (bf16[32,1280]{1,0:T(8,128)(2,1)S(1)}, bf16[32,1280]{1,0:T(8,128)(2,1)S(1)}, u32[]{:S(2)}, u32[]{:S(2)}) collective-permute-start(bf16[32,1280]{1,0:T(8,128)(2,1)S(1)} %get-tuple-element.27), channel_id=1, source_target_pairs={{0,24},{4,28},{8,16},{12,20},{16,8},{20,12},{24,0},{28,4},{1,25},{... | collective-permute-start | bytes 245768 | tf_op jit(solution)/shard_map/ppermute | solution.py:326
  65.2 5.7 %collective-permute-start.17 = (bf16[32,1280]{1,0:T(8,128)(2,1)S(1)}, bf16[32,1280]{1,0:T(8,128)(2,1)S(1)}, u32[]{:S(2)}, u32[]{:S(2)}) collective-permute-start(bf16[32,1280]{1,0:T(8,128)(2,1)S(1)} %get-tuple-element.28), channel_id=1, source_target_pairs={{0,16},{4,20},{8,24},{12,28},{16,0},{20,4},{24,8},{28,12},{1,17},{... | collective-permute-start | bytes 245768 | tf_op jit(solution)/shard_map/ppermute | solution.py:326
  66.4 4.6 %collective-permute-start.18 = (bf16[32,1280]{1,0:T(8,128)(2,1)S(1)}, bf16[32,1280]{1,0:T(8,128)(2,1)S(1)}, u32[]{:S(2)}, u32[]{:S(2)}) collective-permute-start(bf16[32,1280]{1,0:T(8,128)(2,1)S(1)} %get-tuple-element.29), channel_id=1, source_target_pairs={{0,8},{4,12},{8,0},{12,4},{16,24},{20,28},{24,16},{28,20},{1,9},{5... | collective-permute-start | bytes 245768 | tf_op jit(solution)/shard_map/ppermute | solution.py:326
  68.4 2.6 %copy-start.2 = (f32[1280,32]{0,1:T(8,128)S(1)}, f32[1280,32]{0,1:T(8,128)}, u32[]{:S(2)}) copy-start(f32[1280,32]{0,1:T(8,128)} %param.12) | copy-start | bytes 491524
  68.4 2.6 %copy-start.3 = (f32[1280,32]{0,1:T(8,128)S(1)}, f32[1280,32]{0,1:T(8,128)}, u32[]{:S(2)}) copy-start(f32[1280,32]{0,1:T(8,128)} %param.13) | copy-start | bytes 491524

commit v14 on v11

--- a/solution.py
+++ b/solution.py
@@ -268,8 +268,10 @@
     far_perm = pair_perm(n_seq, bits[0])
     partner_tokens = lax.ppermute(tokens, "island", swap)
     weight = anchor.T.astype(jnp.bfloat16)
+    own_kv = key_vals[0].reshape(rows, 2 * cols)
+    weight, own_kv = lax.optimization_barrier((weight, own_kv))
+    kv = [own_kv]
     held = jnp.concatenate([weight, lax.ppermute(weight, "seq", far_perm)], 0)
-    kv = [key_vals[0].reshape(rows, 2 * cols)]
     kv.append(lax.ppermute(kv[0], "seq", far_perm))
 
     def feature_block(matrix, k):
@@ -323,7 +325,7 @@
         return jnp.stack([lower, upper], axis=1).reshape(cols, block).T[None]
 
     total = parts[0]
-    for step in range(1, n_chip):
+    for step in reversed(range(1, n_chip)):
         total = total + lax.ppermute(
             parts[step], "island", pair_perm(n_chip, step, 2)
         ).astype(jnp.float32)

time: 68.1 us -> 68.1 us (level)
  starting transfers between devices: 22.9 us -> 20 us
  waiting for transfers between devices: 32.2 us -> 35 us
    ppermute x1, waiting for transfers between devices: 2.41 us -> 6.28 us  [on_device(): held = jnp.concatenate([weight, lax.ppermute(weight, 'seq', far_perm)], 0)]
    ppermute x1, starting transfers between devices: 3.54 us -> 0.65 us  [on_device(): lax.ppermute(held, 'seq', pair_perm(n_seq, bit))]
    ppermute x3, waiting for transfers between devices: 2.54 us -> 1.57 us  [on_device(): lax.ppermute(parts[step], 'island', pair_perm(n_chip, step, 2))]
    unnamed x11 -> x13, local copies, waits for them, and re-layouts: 3.09 us -> 3.1 us
  transfers between devices with their start and end apart: 19 -> 19, of which waited for: 11 -> 12; matrix products, arithmetic and copies ran while one was open for 11% -> 11% of each run, Pallas kernels for 4% -> 4%
where the time goes in v14:
time: 68.1 us; the launch traced here: 67.9 us
  waiting for transfers between devices  35 us (51%)
  starting transfers between devices  20 us (29%)
  local copies, waits for them, and re-layouts  6.41 us (9%)
  Pallas kernels  3.59 us (5%)
  other arithmetic  2.01 us (3%)
  between operations  0.81 us (1%)
    ppermute x3, waiting for transfers between devices, on_device(): lax.ppermute(dquery, 'seq', pair_perm(n_seq, k))  9.36 us
    ppermute x3, waiting for transfers between devices, on_device(): spread[step] = lax.ppermute(held, 'island', pair_perm(n_chip, step, 2))  8.31 us
    ppermute x1, waiting for transfers between devices, on_device(): held = jnp.concatenate([weight, lax.ppermute(weight, 'seq', far_perm)], 0)  6.28 us
    ppermute x1, waiting for transfers between devices, on_device(): lax.ppermute(jnp.concatenate(kv, axis=0), 'seq', pair_perm(n_seq, bit))  5.2 us
    ppermute x1, starting transfers between devices, on_device(): held = jnp.concatenate([weight, lax.ppermute(weight, 'seq', far_perm)], 0)  3.67 us
    ppermute x3, starting transfers between devices, on_device(): lax.ppermute(dquery, 'seq', pair_perm(n_seq, k))  3.55 us
    ppermute x3, starting transfers between devices, on_device(): lax.ppermute(parts[step], 'island', pair_perm(n_chip, step, 2))  3.55 us
    ppermute x3, starting transfers between devices, on_device(): spread[step] = lax.ppermute(held, 'island', pair_perm(n_chip, step, 2))  3.55 us
  transfers between devices with their start and end apart: 19, of which 12 were waited for; matrix products, arithmetic and copies ran while one was open for 11% of the time, Pallas kernels for 4%

profile of v14, /device:TPU:0, one launch (start us, length us, event | category | flops | bytes accessed | tf_op | source)
XLA Modules:
  0.0 67.9 jit_solution(13932036414778366956)
XLA Ops:
  0.6 0.5 collective-permute-start
  1.1 0.9 %copy.19 = bf16[16,8,2,256]{3,1,2,0:T(8,128)(2,1)S(1)} copy(bf16[16,8,2,256]{3,2,1,0:T(2,128)(2,1)} %bitcast.65) | data formatting | bytes 262144
  2.1 0.9 %convert_bitcast_fusion = bf16[32,1280]{1,0:T(8,128)(2,1)S(1)} fusion(f32[1280,32]{0,1:T(8,128)} %param.12), kind=kLoop, calls=%fused_computation.19 | loop fusion | flops 40960 | bytes 245760 | tf_op jit(solution)/shard_map/convert_element_type | solution.py:270
  3.0 3.7 %collective-permute-start.3 = (bf16[32,1280]{1,0:T(8,128)(2,1)S(1)}, bf16[32,1280]{1,0:T(8,128)(2,1)S(1)}, u32[]{:S(2)}, u32[]{:S(2)}) collective-permute-start(bf16[32,1280]{1,0:T(8,128)(2,1)S(1)} %convert_bitcast_fusion), channel_id=1, source_target_pairs={{0,2},{1,3},{2,0},{3,1},{4,6},{5,7},{6,4},{7,5},{8,10},{9,11},{10,... | collective-permute-start | bytes 245768 | tf_op jit(solution)/shard_map/ppermute | solution.py:274
  6.7 0.1 collective-permute-start.1
  6.7 1.5 %dynamic-slice_bitcast_fusion = (bf16[128,1280]{1,0:T(8,128)(2,1)S(1)}, bf16[128,1280]{1,0:T(8,128)(2,1)S(1)}, bf16[128,1280]{1,0:T(8,128)(2,1)S(1)}, bf16[128,1280]{1,0:T(8,128)(2,1)S(1)}, bf16[128,1280]{1,0:T(8,128)(2,1)S(1)}) fusion(bf16[1,128,5120]{2,1,0:T(8,128)(2,1)} %param.7, s32[]{:T(128)S(6)} %select_n.44, s32[]{:T(128)S(6)} %select_n.42, ...), kind=kLoop, calls=%fused_computation.7 | loop fusion | bytes 3276820 | tf_op jit(solution)/shard_map/dynamic_slice | solution.py:278
  8.2 6.3 %collective-permute-done.3 = bf16[32,1280]{1,0:T(8,128)(2,1)S(1)} collective-permute-done((bf16[32,1280]{1,0:T(8,128)(2,1)S(1)}, bf16[32,1280]{1,0:T(8,128)(2,1)S(1)}, u32[]{:S(2)}, u32[]{:S(2)}) %collective-permute-start.3) | collective-permute-done | bytes 81952 | tf_op jit(solution)/shard_map/ppermute | solution.py:274
  14.5 0.6 collective-permute-start.4
  15.2 0.2 constant_dynamic-slice_fusion
  15.4 1.8 %collective-permute-done.1.refs_2_.refs_3_ = bf16[128,512]{1,0:T(8,128)(2,1)S(1)} collective-permute-done((bf16[128,512]{1,0:T(8,128)(2,1)S(1)}, bf16[128,512]{1,0:T(8,128)(2,1)S(1)}, u32[]{:S(2)}, u32[]{:S(2)}) %collective-permute-start.1) | collective-permute-done | bytes 131104 | tf_op jit(solution)/shard_map/ppermute | solution.py:275
  17.3 0.7 %collective-permute-start.2 = (bf16[256,512]{1,0:T(8,128)(2,1)S(1)}, bf16[256,512]{1,0:T(8,128)(2,1)S(1)}, u32[]{:S(2)}, u32[]{:S(2)}) collective-permute-start(bf16[256,512]{1,0:T(8,128)(2,1)S(1)} %pad_maximum_fusion.3), channel_id=1, source_target_pairs={{0,1},{1,0},{2,3},{3,2},{4,5},{5,4},{6,7},{7,6},{8,9},{9,8},{10,11... | collective-permute-start | bytes 786440 | tf_op jit(solution)/shard_map/ppermute | solution.py:289
  18.0 3.4 %collective-permute-start.13 = (bf16[256,1280]{1,0:T(8,128)(2,1)S(1)}, bf16[256,1280]{1,0:T(8,128)(2,1)S(1)}, u32[]{:S(2)}, u32[]{:S(2)}) collective-permute-start(bf16[256,1280]{1,0:T(8,128)(2,1)S(1)} %pad_maximum_fusion), channel_id=1, source_target_pairs={{0,2},{1,3},{2,0},{3,1},{4,7},{5,6},{6,5},{7,4},{8,10},{9,11},{10,... | collective-permute-start | bytes 1966088 | tf_op jit(solution)/shard_map/ppermute | solution.py:284
  21.4 0.1 collective-permute-done.4
  21.5 1.9 %collective-permute-start.5 = (bf16[128,1280]{1,0:T(8,128)(2,1)S(1)}, bf16[128,1280]{1,0:T(8,128)(2,1)S(1)}, u32[]{:S(2)}, u32[]{:S(2)}) collective-permute-start(bf16[128,1280]{1,0:T(8,128)(2,1)S(1)} %constant_dynamic-update-slice_fusion.refs_0_), channel_id=1, source_target_pairs={{0,8},{4,12},{8,0},{12,4},{16,24},{20,28},{24,16},{28,20},{1,9},{5... | collective-permute-start | bytes 983048 | tf_op jit(solution)/shard_map/ppermute | solution.py:294
  23.4 1.5 %collective-permute-start.6 = (bf16[128,1280]{1,0:T(8,128)(2,1)S(1)}, bf16[128,1280]{1,0:T(8,128)(2,1)S(1)}, u32[]{:S(2)}, u32[]{:S(2)}) collective-permute-start(bf16[128,1280]{1,0:T(8,128)(2,1)S(1)} %constant_dynamic-update-slice_fusion.refs_0_), channel_id=1, source_target_pairs={{0,16},{4,20},{8,24},{12,28},{16,0},{20,4},{24,8},{28,12},{1,17},{... | collective-permute-start | bytes 983048 | tf_op jit(solution)/shard_map/ppermute | solution.py:294
  24.9 0.2 collective-permute-start.7
  25.1 5.2 %collective-permute-done.2.refs_4_.refs_5_ = bf16[256,512]{1,0:T(8,128)(2,1)S(1)} collective-permute-done((bf16[256,512]{1,0:T(8,128)(2,1)S(1)}, bf16[256,512]{1,0:T(8,128)(2,1)S(1)}, u32[]{:S(2)}, u32[]{:S(2)}) %collective-permute-start.2) | collective-permute-done | bytes 262176 | tf_op jit(solution)/shard_map/ppermute | solution.py:289
  30.3 2.0 %collective-permute-done.5.refs_1_ = bf16[128,1280]{1,0:T(8,128)(2,1)S(1)} collective-permute-done((bf16[128,1280]{1,0:T(8,128)(2,1)S(1)}, bf16[128,1280]{1,0:T(8,128)(2,1)S(1)}, u32[]{:S(2)}, u32[]{:S(2)}) %collective-permute-start.5) | collective-permute-done | bytes 327712 | tf_op jit(solution)/shard_map/ppermute | solution.py:294
  32.2 6.3 %collective-permute-done.6.refs_2_ = bf16[128,1280]{1,0:T(8,128)(2,1)S(1)} collective-permute-done((bf16[128,1280]{1,0:T(8,128)(2,1)S(1)}, bf16[128,1280]{1,0:T(8,128)(2,1)S(1)}, u32[]{:S(2)}, u32[]{:S(2)}) %collective-permute-start.6) | collective-permute-done | bytes 327712 | tf_op jit(solution)/shard_map/ppermute | solution.py:294
  38.6 1.0 %shard_map.102 = (bf16[4,32,128]{2,1,0:T(8,128)(2,1)S(1)}, bf16[4,32,128]{2,1,0:T(8,128)(2,1)S(1)}) custom-call(bf16[128,1280]{1,0:T(8,128)(2,1)S(1)} %constant_dynamic-update-slice_fusion.refs_0_, bf16[128,1280]{1,0:T(8,128)(2,1)S(1)} %collective-permute-done.5.refs_1_, bf16[128,1280]{1,0:T(8,128)(2,1)S(1)} %collective-permute-done.6.refs_2_, ...), custom_call_target="tpu_custom_call" | custom-call | flops 335544320 | bytes 3932160 | tf_op jit(solution)/shard_map/pallas_call | solution.py:84
  39.6 0.0 copy-start.1
  39.6 0.1 collective-permute-start.8
  39.6 1.2 %collective-permute-done.8.refs_7_ = bf16[4,32,128]{2,1,0:T(8,128)(2,1)S(1)} collective-permute-done((bf16[4,32,128]{2,1,0:T(8,128)(2,1)S(1)}, bf16[4,32,128]{2,1,0:T(8,128)(2,1)S(1)}, u32[]{:S(2)}, u32[]{:S(2)}) %collective-permute-start.8) | collective-permute-done | bytes 32800 | tf_op jit(solution)/shard_map/ppermute | solution.py:300
  40.8 1.2 %shard_map.103.refs_0_ = bf16[256,128]{1,0:T(8,128)(2,1)S(1)} custom-call(bf16[128,512]{1,0:T(8,128)(2,1)S(1)} %bitcast.57, bf16[128,512]{1,0:T(8,128)(2,1)S(1)} %bitcast.58, bf16[128,512]{1,0:T(8,128)(2,1)S(1)} %collective-permute-done.1.refs_2_.refs_3_, bf16[128,512]{1,0:T(8,128)(2,1)S(1)} %collective-permute-done.1.refs_2_.refs_3_, ...), custom_call_target="tpu_custom_call" | custom-call | flops 402653184 | bytes 786432 | tf_op jit(solution)/shard_map/pallas_call | solution.py:164
  42.1 1.9 %collective-permute-start.10 = (bf16[256,128]{1,0:T(8,128)(2,1)S(1)}, bf16[256,128]{1,0:T(8,128)(2,1)S(1)}, u32[]{:S(2)}, u32[]{:S(2)}) collective-permute-start(bf16[256,128]{1,0:T(8,128)(2,1)S(1)} %shard_map.103.refs_0_), channel_id=1, source_target_pairs={{0,2},{1,3},{2,0},{3,1},{4,6},{5,7},{6,4},{7,5},{8,10},{9,11},{10,... | collective-permute-start | bytes 196616 | tf_op jit(solution)/shard_map/ppermute | solution.py:304
  44.0 1.3 %collective-permute-start.11 = (bf16[256,128]{1,0:T(8,128)(2,1)S(1)}, bf16[256,128]{1,0:T(8,128)(2,1)S(1)}, u32[]{:S(2)}, u32[]{:S(2)}) collective-permute-start(bf16[256,128]{1,0:T(8,128)(2,1)S(1)} %shard_map.103.refs_0_), channel_id=1, source_target_pairs={{0,3},{1,2},{2,1},{3,0},{4,7},{5,6},{6,5},{7,4},{8,11},{9,10},{10,... | collective-permute-start | bytes 196616 | tf_op jit(solution)/shard_map/ppermute | solution.py:304
  45.3 0.4 collective-permute-start.9
  45.6 9.4 %collective-permute-done.10.refs_2_ = bf16[256,128]{1,0:T(8,128)(2,1)S(1)} collective-permute-done((bf16[256,128]{1,0:T(8,128)(2,1)S(1)}, bf16[256,128]{1,0:T(8,128)(2,1)S(1)}, u32[]{:S(2)}, u32[]{:S(2)}) %collective-permute-start.10) | collective-permute-done | bytes 65568 | tf_op jit(solution)/shard_map/ppermute | solution.py:304
  55.0 0.1 collective-permute-start.14
  55.1 0.2 copy.13
  55.4 1.3 %copy.14 = bf16[256,1280]{1,0:T(8,128)(2,1)S(1)} copy(bf16[256,1280]{0,1:T(8,128)(2,1)} %bitcast.64) | data formatting | bytes 1310720 | tf_op jit(solution)/shard_map/transpose | solution.py:312
  56.7 0.5 collective-permute-done.14.refs_7_
  57.2 0.7 shard_map.105
  57.8 0.2 collective-permute-start.15
  58.0 0.7 shard_map.104
  58.7 0.1 select_bitcast_fusion.1
  58.8 0.1 pad_maximum_fusion.2
  58.9 0.7 collective-permute-done.15.got_ref
  59.5 0.1 shard_map.106
  59.6 2.5 %collective-permute-start.16 = (bf16[32,1280]{1,0:T(8,128)(2,1)S(1)}, bf16[32,1280]{1,0:T(8,128)(2,1)S(1)}, u32[]{:S(2)}, u32[]{:S(2)}) collective-permute-start(bf16[32,1280]{1,0:T(8,128)(2,1)S(1)} %get-tuple-element.43), channel_id=1, source_target_pairs={{0,24},{4,28},{8,16},{12,20},{16,8},{20,12},{24,0},{28,4},{1,25},{... | collective-permute-start | bytes 245768 | tf_op jit(solution)/shard_map/ppermute | solution.py:329
  62.1 0.5 collective-permute-start.17
  62.6 0.6 collective-permute-start.18
  63.2 0.1 pad_maximum_fusion.1
  63.3 1.1 %copy.18 = bf16[1,1280,256]{2,1,0:T(8,128)(2,1)} copy(bf16[1,1280,256]{1,2,0:T(8,128)(2,1)S(1)} %bitcast.60) | data formatting | bytes 1310720
  64.4 1.1 %copy.17 = bf16[1,1280,256]{2,1,0:T(8,128)(2,1)} copy(bf16[1,1280,256]{1,2,0:T(8,128)(2,1)S(1)} %bitcast.61) | data formatting | bytes 1310720
  65.5 1.3 %collective-permute-done.17 = bf16[32,1280]{1,0:T(8,128)(2,1)S(1)} collective-permute-done((bf16[32,1280]{1,0:T(8,128)(2,1)S(1)}, bf16[32,1280]{1,0:T(8,128)(2,1)S(1)}, u32[]{:S(2)}, u32[]{:S(2)}) %collective-permute-start.17) | collective-permute-done | bytes 81952 | tf_op jit(solution)/shard_map/ppermute | solution.py:329
  66.8 0.2 collective-permute-done.18
  67.1 0.8 %fusion.1 = (f32[1280,32]{0,1:T(8,128)}, f32[1280,32]{0,1:T(8,128)}) fusion(f32[1280,32]{0,1:T(8,128)S(1)} %copy-done.2, bf16[32,1280]{1,0:T(8,128)(2,1)S(1)} %collective-permute-done.18, bf16[32,1280]{1,0:T(8,128)(2,1)S(1)} %collective-permute-done.17, f32[32,1280]{1,0:T(8,128)S(1)} %get-tuple-element.42, bf16[32,1280]{1,0:T(8,128)(2,1)S(1)} %collective-permute-done.16, ...), kind=kLoop, calls=%fused_computation.17 | loop fusion | flops 532480 | bytes 1064960 | tf_op jit(solution)/shard_map/sub | solution.py:334
  (23 shorter events, 0.2 us)
Async XLA Ops:
  0.6 14.6 %collective-permute-start = (bf16[128,5120]{1,0:T(8,128)(2,1)}, bf16[128,5120]{1,0:T(8,128)(2,1)S(1)}, u32[]{:S(2)}, u32[]{:S(2)}) collective-permute-start(bf16[128,5120]{1,0:T(8,128)(2,1)} %bitcast.62), channel_id=1, source_target_pairs={{0,4},{4,0},{8,12},{12,8},{16,20},{20,16},{24,28},{28,24},{1,5},{5... | collective-permute-start | bytes 3932168 | tf_op jit(solution)/shard_map/ppermute | solution.py:269
  3.0 11.5 %collective-permute-start.3 = (bf16[32,1280]{1,0:T(8,128)(2,1)S(1)}, bf16[32,1280]{1,0:T(8,128)(2,1)S(1)}, u32[]{:S(2)}, u32[]{:S(2)}) collective-permute-start(bf16[32,1280]{1,0:T(8,128)(2,1)S(1)} %convert_bitcast_fusion), channel_id=1, source_target_pairs={{0,2},{1,3},{2,0},{3,1},{4,6},{5,7},{6,4},{7,5},{8,10},{9,11},{10,... | collective-permute-start | bytes 245768 | tf_op jit(solution)/shard_map/ppermute | solution.py:274
  6.7 10.6 %collective-permute-start.1 = (bf16[128,512]{1,0:T(8,128)(2,1)S(1)}, bf16[128,512]{1,0:T(8,128)(2,1)S(1)}, u32[]{:S(2)}, u32[]{:S(2)}) collective-permute-start(bf16[128,512]{1,0:T(8,128)(2,1)S(1)} %bitcast.55), channel_id=1, source_target_pairs={{0,2},{1,3},{2,0},{3,1},{4,6},{5,7},{6,4},{7,5},{8,10},{9,11},{10,... | collective-permute-start | bytes 393224 | tf_op jit(solution)/shard_map/ppermute | solution.py:275
  14.5 7.0 %collective-permute-start.4 = (bf16[64,1280]{1,0:T(8,128)(2,1)S(1)}, bf16[64,1280]{1,0:T(8,128)(2,1)S(1)}, u32[]{:S(2)}, u32[]{:S(2)}) collective-permute-start(bf16[64,1280]{1,0:T(8,128)(2,1)S(1)} %pad_maximum_fusion.4), channel_id=1, source_target_pairs={{0,1},{1,0},{2,3},{3,2},{4,5},{5,4},{6,7},{7,6},{8,9},{9,8},{10,11... | collective-permute-start | bytes 491528 | tf_op jit(solution)/shard_map/ppermute | solution.py:288
  17.3 13.0 %collective-permute-start.2 = (bf16[256,512]{1,0:T(8,128)(2,1)S(1)}, bf16[256,512]{1,0:T(8,128)(2,1)S(1)}, u32[]{:S(2)}, u32[]{:S(2)}) collective-permute-start(bf16[256,512]{1,0:T(8,128)(2,1)S(1)} %pad_maximum_fusion.3), channel_id=1, source_target_pairs={{0,1},{1,0},{2,3},{3,2},{4,5},{5,4},{6,7},{7,6},{8,9},{9,8},{10,11... | collective-permute-start | bytes 786440 | tf_op jit(solution)/shard_map/ppermute | solution.py:289
  18.0 37.0 %collective-permute-start.13 = (bf16[256,1280]{1,0:T(8,128)(2,1)S(1)}, bf16[256,1280]{1,0:T(8,128)(2,1)S(1)}, u32[]{:S(2)}, u32[]{:S(2)}) collective-permute-start(bf16[256,1280]{1,0:T(8,128)(2,1)S(1)} %pad_maximum_fusion), channel_id=1, source_target_pairs={{0,2},{1,3},{2,0},{3,1},{4,7},{5,6},{6,5},{7,4},{8,10},{9,11},{10,... | collective-permute-start | bytes 1966088 | tf_op jit(solution)/shard_map/ppermute | solution.py:284
  21.5 10.7 %collective-permute-start.5 = (bf16[128,1280]{1,0:T(8,128)(2,1)S(1)}, bf16[128,1280]{1,0:T(8,128)(2,1)S(1)}, u32[]{:S(2)}, u32[]{:S(2)}) collective-permute-start(bf16[128,1280]{1,0:T(8,128)(2,1)S(1)} %constant_dynamic-update-slice_fusion.refs_0_), channel_id=1, source_target_pairs={{0,8},{4,12},{8,0},{12,4},{16,24},{20,28},{24,16},{28,20},{1,9},{5... | collective-permute-start | bytes 983048 | tf_op jit(solution)/shard_map/ppermute | solution.py:294
  23.4 15.2 %collective-permute-start.6 = (bf16[128,1280]{1,0:T(8,128)(2,1)S(1)}, bf16[128,1280]{1,0:T(8,128)(2,1)S(1)}, u32[]{:S(2)}, u32[]{:S(2)}) collective-permute-start(bf16[128,1280]{1,0:T(8,128)(2,1)S(1)} %constant_dynamic-update-slice_fusion.refs_0_), channel_id=1, source_target_pairs={{0,16},{4,20},{8,24},{12,28},{16,0},{20,4},{24,8},{28,12},{1,17},{... | collective-permute-start | bytes 983048 | tf_op jit(solution)/shard_map/ppermute | solution.py:294
  24.9 13.7 %collective-permute-start.7 = (bf16[128,1280]{1,0:T(8,128)(2,1)S(1)}, bf16[128,1280]{1,0:T(8,128)(2,1)S(1)}, u32[]{:S(2)}, u32[]{:S(2)}) collective-permute-start(bf16[128,1280]{1,0:T(8,128)(2,1)S(1)} %constant_dynamic-update-slice_fusion.refs_0_), channel_id=1, source_target_pairs={{0,24},{4,28},{8,16},{12,20},{16,8},{20,12},{24,0},{28,4},{1,25},{... | collective-permute-start | bytes 983048 | tf_op jit(solution)/shard_map/ppermute | solution.py:294
  30.3 24.7 %collective-permute-start.12 = (bf16[128,1280]{1,0:T(8,128)(2,1)S(1)}, bf16[128,1280]{1,0:T(8,128)(2,1)S(1)}, u32[]{:S(2)}, u32[]{:S(2)}) collective-permute-start(bf16[128,1280]{1,0:T(8,128)(2,1)S(1)} %get-tuple-element.36.refs_5_), channel_id=1, source_target_pairs={{0,1},{1,0},{2,3},{3,2},{4,5},{5,4},{6,7},{7,6},{8,9},{9,8},{10,11... | collective-permute-start | bytes 983048 | tf_op jit(solution)/shard_map/ppermute | solution.py:301
  38.6 2.3 %copy-start = (bf16[1,128,256]{2,1,0:T(8,128)(2,1)S(1)}, bf16[1,128,256]{2,1,0:T(8,128)(2,1)}, u32[]{:S(2)}) copy-start(bf16[1,128,256]{2,1,0:T(8,128)(2,1)} %param.9) | copy-start | bytes 196612
  39.6 15.6 %copy-start.1 = (bf16[1,1280,256]{2,1,0:T(8,128)(2,1)S(1)}, bf16[1,1280,256]{2,1,0:T(8,128)(2,1)}, u32[]{:S(2)}) copy-start(bf16[1,1280,256]{2,1,0:T(8,128)(2,1)} %param.10) | copy-start | bytes 1966084
  39.6 1.3 %collective-permute-start.8 = (bf16[4,32,128]{2,1,0:T(8,128)(2,1)S(1)}, bf16[4,32,128]{2,1,0:T(8,128)(2,1)S(1)}, u32[]{:S(2)}, u32[]{:S(2)}) collective-permute-start(bf16[4,32,128]{2,1,0:T(8,128)(2,1)S(1)} %get-tuple-element.35), channel_id=1, source_target_pairs={{0,4},{4,0},{8,12},{12,8},{16,20},{20,16},{24,28},{28,24},{1,5},{5... | collective-permute-start | bytes 98312 | tf_op jit(solution)/shard_map/ppermute | solution.py:300
  42.1 12.9 %collective-permute-start.10 = (bf16[256,128]{1,0:T(8,128)(2,1)S(1)}, bf16[256,128]{1,0:T(8,128)(2,1)S(1)}, u32[]{:S(2)}, u32[]{:S(2)}) collective-permute-start(bf16[256,128]{1,0:T(8,128)(2,1)S(1)} %shard_map.103.refs_0_), channel_id=1, source_target_pairs={{0,2},{1,3},{2,0},{3,1},{4,6},{5,7},{6,4},{7,5},{8,10},{9,11},{10,... | collective-permute-start | bytes 196616 | tf_op jit(solution)/shard_map/ppermute | solution.py:304
  44.0 11.0 %collective-permute-start.11 = (bf16[256,128]{1,0:T(8,128)(2,1)S(1)}, bf16[256,128]{1,0:T(8,128)(2,1)S(1)}, u32[]{:S(2)}, u32[]{:S(2)}) collective-permute-start(bf16[256,128]{1,0:T(8,128)(2,1)S(1)} %shard_map.103.refs_0_), channel_id=1, source_target_pairs={{0,3},{1,2},{2,1},{3,0},{4,7},{5,6},{6,5},{7,4},{8,11},{9,10},{10,... | collective-permute-start | bytes 196616 | tf_op jit(solution)/shard_map/ppermute | solution.py:304
  45.3 9.7 %collective-permute-start.9 = (bf16[256,128]{1,0:T(8,128)(2,1)S(1)}, bf16[256,128]{1,0:T(8,128)(2,1)S(1)}, u32[]{:S(2)}, u32[]{:S(2)}) collective-permute-start(bf16[256,128]{1,0:T(8,128)(2,1)S(1)} %shard_map.103.refs_0_), channel_id=1, source_target_pairs={{0,1},{1,0},{2,3},{3,2},{4,5},{5,4},{6,7},{7,6},{8,9},{9,8},{10,11... | collective-permute-start | bytes 196616 | tf_op jit(solution)/shard_map/ppermute | solution.py:304
  55.0 2.2 %collective-permute-start.14 = (bf16[256,1280]{1,0:T(8,128)(2,1)S(1)}, bf16[256,1280]{1,0:T(8,128)(2,1)S(1)}, u32[]{:S(2)}, u32[]{:S(2)}) collective-permute-start(bf16[256,1280]{1,0:T(8,128)(2,1)S(1)} %collective-permute-done.13.refs_6_), channel_id=1, source_target_pairs={{0,4},{4,0},{8,12},{12,8},{16,20},{20,16},{24,28},{28,24},{1,5},{5... | collective-permute-start | bytes 1966088 | tf_op jit(solution)/shard_map/ppermute | solution.py:310
  57.8 1.7 %collective-permute-start.15 = (bf16[4,32,1280]{2,1,0:T(8,128)(2,1)S(1)}, bf16[4,32,1280]{2,1,0:T(8,128)(2,1)S(1)}, u32[]{:S(2)}, u32[]{:S(2)}) collective-permute-start(bf16[4,32,1280]{2,1,0:T(8,128)(2,1)S(1)} %get-tuple-element.41), channel_id=1, source_target_pairs={{0,4},{4,0},{8,12},{12,8},{16,20},{20,16},{24,28},{28,24},{1,5},{5... | collective-permute-start | bytes 983048 | tf_op jit(solution)/shard_map/ppermute | solution.py:316
  59.6 5.9 %collective-permute-start.16 = (bf16[32,1280]{1,0:T(8,128)(2,1)S(1)}, bf16[32,1280]{1,0:T(8,128)(2,1)S(1)}, u32[]{:S(2)}, u32[]{:S(2)}) collective-permute-start(bf16[32,1280]{1,0:T(8,128)(2,1)S(1)} %get-tuple-element.43), channel_id=1, source_target_pairs={{0,24},{4,28},{8,16},{12,20},{16,8},{20,12},{24,0},{28,4},{1,25},{... | collective-permute-start | bytes 245768 | tf_op jit(solution)/shard_map/ppermute | solution.py:329
  62.1 4.7 %collective-permute-start.17 = (bf16[32,1280]{1,0:T(8,128)(2,1)S(1)}, bf16[32,1280]{1,0:T(8,128)(2,1)S(1)}, u32[]{:S(2)}, u32[]{:S(2)}) collective-permute-start(bf16[32,1280]{1,0:T(8,128)(2,1)S(1)} %get-tuple-element.44), channel_id=1, source_target_pairs={{0,16},{4,20},{8,24},{12,28},{16,0},{20,4},{24,8},{28,12},{1,17},{... | collective-permute-start | bytes 245768 | tf_op jit(solution)/shard_map/ppermute | solution.py:329
  62.6 4.4 %collective-permute-start.18 = (bf16[32,1280]{1,0:T(8,128)(2,1)S(1)}, bf16[32,1280]{1,0:T(8,128)(2,1)S(1)}, u32[]{:S(2)}, u32[]{:S(2)}) collective-permute-start(bf16[32,1280]{1,0:T(8,128)(2,1)S(1)} %get-tuple-element.45), channel_id=1, source_target_pairs={{0,8},{4,12},{8,0},{12,4},{16,24},{20,28},{24,16},{28,20},{1,9},{5... | collective-permute-start | bytes 245768 | tf_op jit(solution)/shard_map/ppermute | solution.py:329
  64.4 2.7 %copy-start.2 = (f32[1280,32]{0,1:T(8,128)S(1)}, f32[1280,32]{0,1:T(8,128)}, u32[]{:S(2)}) copy-start(f32[1280,32]{0,1:T(8,128)} %param.12) | copy-start | bytes 491524
  64.4 2.7 %copy-start.3 = (f32[1280,32]{0,1:T(8,128)S(1)}, f32[1280,32]{0,1:T(8,128)}, u32[]{:S(2)}) copy-start(f32[1280,32]{0,1:T(8,128)} %param.13) | copy-start | bytes 491524

commit v15 on v11

--- a/solution.py
+++ b/solution.py
@@ -196,7 +196,7 @@
     rows = state_refs[0].shape[0]
     states = [ref[...] for ref in state_refs[:2]]
     for k in range(2, n_seq, 2):
-        states += [state_refs[k][:rows, :], state_refs[k + 1][rows:, :]]
+        states += [state_refs[k][...], state_refs[k + 1][...]]
     states = jnp.concatenate(states, axis=0)
     gradient = jnp.dot(left, states, preferred_element_type=jnp.float32) * inverse
     for j in range(n_chip):
@@ -275,11 +275,12 @@
     def feature_block(matrix, k):
         return lax.dynamic_slice(matrix, (0, jnp.bitwise_xor(seq, k) * block), (rows, block))
 
-    far = []
+    far, far_partner = [], []
     for k in range(2, n_seq, 2):
-        both = jnp.concatenate([feature_block(m, k + core) for m in (tokens, partner_tokens)], 0)
-        both, kv = lax.optimization_barrier((both, kv))
-        far.append(lax.ppermute(both, ("island", "seq"), far_pairs(n_island, n_seq, k)))
+        piece, kv = lax.optimization_barrier((feature_block(partner_tokens, k + core), kv))
+        pairs = far_pairs(n_island, n_seq, k)
+        far_partner.append(lax.ppermute(piece, ("island", "seq"), pairs))
+        far.append(lax.ppermute(feature_block(tokens, k + core), ("island", "seq"), pairs))
     own_blocks = [feature_block(tokens, k) for k in range(n_seq)]
     partner_blocks = [feature_block(partner_tokens, k) for k in range(n_seq)]
     for bit in bits[1:]:
@@ -297,15 +298,16 @@
     near, kv = lax.optimization_barrier((own_blocks[1], kv))
     other = lax.ppermute(for_partner, "island", swap)
     near = lax.ppermute(near, "seq", pair_perm(n_seq, 1))
+    far_partner = [lax.ppermute(piece, "island", swap) for piece in far_partner]
+    other, far_partner = lax.optimization_barrier((other, far_partner))
     dquery = attention(kv, order, mine, other, cotangent[0])
     dqueries = [dquery] + [
         lax.ppermute(dquery, "seq", pair_perm(n_seq, k)) for k in range(1, n_seq)
     ]
 
-    _, near, far = lax.optimization_barrier((dqueries[1:], near, far))
     gathered = [own_blocks[0], near]
-    for got in far:
-        gathered += [got, lax.ppermute(got, "island", swap)]
+    for got, swapped in zip(far, far_partner):
+        gathered += [got, swapped]
     first = first_moment[0].T.reshape(n_chip, 2, share, block)
     second = second_moment[0].T.reshape(n_chip, 2, share, block)
     first_other, second_other, delta_other = gradient_adam(
@@ -323,7 +325,7 @@
         return jnp.stack([lower, upper], axis=1).reshape(cols, block).T[None]
 
     total = parts[0]
-    for step in range(1, n_chip):
+    for step in reversed(range(1, n_chip)):
         total = total + lax.ppermute(
             parts[step], "island", pair_perm(n_chip, step, 2)
         ).astype(jnp.float32)

time: 68.1 us -> 68.4 us (level)
  starting transfers between devices: 22.9 us -> 25.7 us
  waiting for transfers between devices: 32.2 us -> 30.4 us
    ppermute x2 -> x3, waiting for transfers between devices: 0.49 us -> 12.7 us  [the longest x1 9.14 us: on_device(): far_partner.append(lax.ppermute(piece, ('island', 'seq'), pairs))]
    ppermute x3, waiting for transfers between devices: 8.42 us -> 0.01 us  [on_device(): spread[step] = lax.ppermute(held, 'island', pair_perm(n_chip, step, 2))]
    ppermute x3, waiting for transfers between devices: 9.22 us -> 2.59 us  [on_device(): lax.ppermute(dquery, 'seq', pair_perm(n_seq, k))]
    ppermute x1, waiting for transfers between devices: 5.36 us -> 1.29 us  [on_device(): lax.ppermute(jnp.concatenate(kv, axis=0), 'seq', pair_perm(n_seq, bit))]
    ppermute x1, waiting for transfers between devices: 0.01 us -> 2.48 us  [on_device(): near = lax.ppermute(near, 'seq', pair_perm(n_seq, 1))]
    ppermute x1, starting transfers between devices: 0.01 us -> 2.48 us  [on_device(): near = lax.ppermute(near, 'seq', pair_perm(n_seq, 1))]
    ppermute x1, waiting for transfers between devices: 0.01 us -> 1.87 us  [on_device(): lax.ppermute(held, 'seq', pair_perm(n_seq, bit))]
    ppermute x1, waiting for transfers between devices: 2.41 us -> 3.92 us  [on_device(): held = jnp.concatenate([weight, lax.ppermute(weight, 'seq', far_perm)], 0)]
  transfers between devices with their start and end apart: 19 -> 20, of which waited for: 11 -> 13; matrix products, arithmetic and copies ran while one was open for 11% -> 10% of each run, Pallas kernels for 4% -> 4%
where the time goes in v15:
time: 68.4 us; the launch traced here: 68.2 us
  waiting for transfers between devices  30.4 us (44%)
  starting transfers between devices  25.7 us (38%)
  local copies, waits for them, and re-layouts  5.77 us (8%)
  Pallas kernels  3.6 us (5%)
  other arithmetic  1.99 us (3%)
  between operations  0.8 us (1%)
    ppermute x1, waiting for transfers between devices, on_device(): far_partner.append(lax.ppermute(piece, ('island', 'seq'), pairs))  9.14 us
    ppermute x3, starting transfers between devices, on_device(): lax.ppermute(dquery, 'seq', pair_perm(n_seq, k))  4.45 us
    ppermute x1, waiting for transfers between devices, on_device(): held = jnp.concatenate([weight, lax.ppermute(weight, 'seq', far_perm)], 0)  3.92 us
    ppermute x1, starting transfers between devices, on_device(): held = jnp.concatenate([weight, lax.ppermute(weight, 'seq', far_perm)], 0)  3.67 us
    ppermute x1, waiting for transfers between devices, on_device(): lax.ppermute(feature_block(tokens, k + core), ('island', 'seq'), pairs)  3.59 us
    ppermute x3, starting transfers between devices, on_device(): lax.ppermute(parts[step], 'island', pair_perm(n_chip, step, 2))  3.55 us
    ppermute x3, starting transfers between devices, on_device(): spread[step] = lax.ppermute(held, 'island', pair_perm(n_chip, step, 2))  3.55 us
    ppermute x1, starting transfers between devices, on_device(): lax.ppermute(held, 'seq', pair_perm(n_seq, bit))  3.54 us
  transfers between devices with their start and end apart: 20, of which 13 were waited for; matrix products, arithmetic and copies ran while one was open for 10% of the time, Pallas kernels for 4%

profile of v15, /device:TPU:0, one launch (start us, length us, event | category | flops | bytes accessed | tf_op | source)
XLA Modules:
  0.0 68.2 jit_solution(780650588286606218)
XLA Ops:
  0.6 0.5 collective-permute-start
  1.1 0.9 %convert_bitcast_fusion = bf16[32,1280]{1,0:T(8,128)(2,1)S(1)} fusion(f32[1280,32]{0,1:T(8,128)} %param.12), kind=kLoop, calls=%fused_computation.19 | loop fusion | flops 40960 | bytes 245760 | tf_op jit(solution)/shard_map/convert_element_type | solution.py:270
  2.1 3.7 %collective-permute-start.3 = (bf16[32,1280]{1,0:T(8,128)(2,1)S(1)}, bf16[32,1280]{1,0:T(8,128)(2,1)S(1)}, u32[]{:S(2)}, u32[]{:S(2)}) collective-permute-start(bf16[32,1280]{1,0:T(8,128)(2,1)S(1)} %convert_bitcast_fusion), channel_id=1, source_target_pairs={{0,2},{1,3},{2,0},{3,1},{4,6},{5,7},{6,4},{7,5},{8,10},{9,11},{10,... | collective-permute-start | bytes 245768 | tf_op jit(solution)/shard_map/ppermute | solution.py:271
  5.7 0.9 %copy.19 = bf16[16,8,2,256]{3,1,2,0:T(8,128)(2,1)S(1)} copy(bf16[16,8,2,256]{3,2,1,0:T(2,128)(2,1)} %bitcast.65) | data formatting | bytes 262144
  6.7 0.1 collective-permute-start.1
  6.8 3.9 %collective-permute-done.3 = bf16[32,1280]{1,0:T(8,128)(2,1)S(1)} collective-permute-done((bf16[32,1280]{1,0:T(8,128)(2,1)S(1)}, bf16[32,1280]{1,0:T(8,128)(2,1)S(1)}, u32[]{:S(2)}, u32[]{:S(2)}) %collective-permute-start.3) | collective-permute-done | bytes 81952 | tf_op jit(solution)/shard_map/ppermute | solution.py:271
  10.7 3.5 %collective-permute-start.4 = (bf16[64,1280]{1,0:T(8,128)(2,1)S(1)}, bf16[64,1280]{1,0:T(8,128)(2,1)S(1)}, u32[]{:S(2)}, u32[]{:S(2)}) collective-permute-start(bf16[64,1280]{1,0:T(8,128)(2,1)S(1)} %pad_maximum_fusion.4), channel_id=1, source_target_pairs={{0,1},{1,0},{2,3},{3,2},{4,5},{5,4},{6,7},{7,6},{8,9},{9,8},{10,11... | collective-permute-start | bytes 491528 | tf_op jit(solution)/shard_map/ppermute | solution.py:287
  14.3 0.1 constant_dynamic-slice_fusion
  14.4 1.9 %collective-permute-done.1.refs_2_.refs_3_ = bf16[128,512]{1,0:T(8,128)(2,1)S(1)} collective-permute-done((bf16[128,512]{1,0:T(8,128)(2,1)S(1)}, bf16[128,512]{1,0:T(8,128)(2,1)S(1)}, u32[]{:S(2)}, u32[]{:S(2)}) %collective-permute-start.1) | collective-permute-done | bytes 131104 | tf_op jit(solution)/shard_map/ppermute | solution.py:273
  16.3 1.5 %collective-permute-start.9 = (bf16[128,1280]{1,0:T(8,128)(2,1)S(1)}, bf16[128,1280]{1,0:T(8,128)(2,1)S(1)}, u32[]{:S(2)}, u32[]{:S(2)}) collective-permute-start(bf16[128,1280]{1,0:T(8,128)(2,1)S(1)} %get-tuple-element.32), channel_id=1, source_target_pairs={{0,2},{1,3},{2,0},{3,1},{4,7},{5,6},{6,5},{7,4},{8,10},{9,11},{10,... | collective-permute-start | bytes 983048 | tf_op jit(solution)/shard_map/ppermute | solution.py:282
  17.9 1.9 %collective-permute-done.4 = bf16[64,1280]{1,0:T(8,128)(2,1)S(1)} collective-permute-done((bf16[64,1280]{1,0:T(8,128)(2,1)S(1)}, bf16[64,1280]{1,0:T(8,128)(2,1)S(1)}, u32[]{:S(2)}, u32[]{:S(2)}) %collective-permute-start.4) | collective-permute-done | bytes 163872 | tf_op jit(solution)/shard_map/ppermute | solution.py:287
  19.8 1.6 %collective-permute-start.5 = (bf16[128,1280]{1,0:T(8,128)(2,1)S(1)}, bf16[128,1280]{1,0:T(8,128)(2,1)S(1)}, u32[]{:S(2)}, u32[]{:S(2)}) collective-permute-start(bf16[128,1280]{1,0:T(8,128)(2,1)S(1)} %pad_maximum_fusion.2.refs_0_), channel_id=1, source_target_pairs={{0,8},{4,12},{8,0},{12,4},{16,24},{20,28},{24,16},{28,20},{1,9},{5... | collective-permute-start | bytes 983048 | tf_op jit(solution)/shard_map/ppermute | solution.py:293
  21.4 1.5 %collective-permute-start.6 = (bf16[128,1280]{1,0:T(8,128)(2,1)S(1)}, bf16[128,1280]{1,0:T(8,128)(2,1)S(1)}, u32[]{:S(2)}, u32[]{:S(2)}) collective-permute-start(bf16[128,1280]{1,0:T(8,128)(2,1)S(1)} %pad_maximum_fusion.2.refs_0_), channel_id=1, source_target_pairs={{0,16},{4,20},{8,24},{12,28},{16,0},{20,4},{24,8},{28,12},{1,17},{... | collective-permute-start | bytes 983048 | tf_op jit(solution)/shard_map/ppermute | solution.py:293
  22.9 0.4 collective-permute-start.7
  23.3 0.7 %collective-permute-start.2 = (bf16[256,512]{1,0:T(8,128)(2,1)S(1)}, bf16[256,512]{1,0:T(8,128)(2,1)S(1)}, u32[]{:S(2)}, u32[]{:S(2)}) collective-permute-start(bf16[256,512]{1,0:T(8,128)(2,1)S(1)} %pad_maximum_fusion.3), channel_id=1, source_target_pairs={{0,1},{1,0},{2,3},{3,2},{4,5},{5,4},{6,7},{7,6},{8,9},{9,8},{10,11... | collective-permute-start | bytes 786440 | tf_op jit(solution)/shard_map/ppermute | solution.py:288
  24.1 9.1 %collective-permute-done.9 = bf16[128,1280]{1,0:T(8,128)(2,1)S(1)} collective-permute-done((bf16[128,1280]{1,0:T(8,128)(2,1)S(1)}, bf16[128,1280]{1,0:T(8,128)(2,1)S(1)}, u32[]{:S(2)}, u32[]{:S(2)}) %collective-permute-start.9) | collective-permute-done | bytes 327712 | tf_op jit(solution)/shard_map/ppermute | solution.py:282
  33.2 0.9 %dynamic-slice_bitcast_fusion = (bf16[128,1280]{1,0:T(8,128)(2,1)}, bf16[128,1280]{1,0:T(8,128)(2,1)S(1)}, bf16[128,1280]{1,0:T(8,128)(2,1)S(1)}, bf16[128,1280]{1,0:T(8,128)(2,1)S(1)}, bf16[128,1280]{1,0:T(8,128)(2,1)S(1)}) fusion(bf16[1,128,5120]{2,1,0:T(8,128)(2,1)S(1)} %copy-done.1, s32[]{:T(128)S(6)} %select_n.41, s32[]{:T(128)S(6)} %select_n.43, ...), kind=kLoop, calls=%fused_computation.7 | loop fusion | bytes 3276820 | tf_op jit(solution)/shard_map/dynamic_slice | solution.py:276
  34.1 1.3 %collective-permute-done.2.refs_4_.refs_5_ = bf16[256,512]{1,0:T(8,128)(2,1)S(1)} collective-permute-done((bf16[256,512]{1,0:T(8,128)(2,1)S(1)}, bf16[256,512]{1,0:T(8,128)(2,1)S(1)}, u32[]{:S(2)}, u32[]{:S(2)}) %collective-permute-start.2) | collective-permute-done | bytes 262176 | tf_op jit(solution)/shard_map/ppermute | solution.py:288
  35.4 1.5 %collective-permute-start.15 = (bf16[128,1280]{1,0:T(8,128)(2,1)}, bf16[128,1280]{1,0:T(8,128)(2,1)S(1)}, u32[]{:S(2)}, u32[]{:S(2)}) collective-permute-start(bf16[128,1280]{1,0:T(8,128)(2,1)} %get-tuple-element.52), channel_id=1, source_target_pairs={{0,2},{1,3},{2,0},{3,1},{4,7},{5,6},{6,5},{7,4},{8,10},{9,11},{10,... | collective-permute-start | bytes 983048 | tf_op jit(solution)/shard_map/ppermute | solution.py:283
  36.8 2.5 %collective-permute-start.14 = (bf16[128,1280]{1,0:T(8,128)(2,1)S(1)}, bf16[128,1280]{1,0:T(8,128)(2,1)S(1)}, u32[]{:S(2)}, u32[]{:S(2)}) collective-permute-start(bf16[128,1280]{1,0:T(8,128)(2,1)S(1)} %get-tuple-element.34.refs_5_), channel_id=1, source_target_pairs={{0,1},{1,0},{2,3},{3,2},{4,5},{5,4},{6,7},{7,6},{8,9},{9,8},{10,11... | collective-permute-start | bytes 983048 | tf_op jit(solution)/shard_map/ppermute | solution.py:300
  39.3 1.0 %shard_map.102 = (bf16[4,32,128]{2,1,0:T(8,128)(2,1)S(1)}, bf16[4,32,128]{2,1,0:T(8,128)(2,1)S(1)}) custom-call(bf16[128,1280]{1,0:T(8,128)(2,1)S(1)} %pad_maximum_fusion.2.refs_0_, bf16[128,1280]{1,0:T(8,128)(2,1)S(1)} %collective-permute-done.5.refs_1_, bf16[128,1280]{1,0:T(8,128)(2,1)S(1)} %collective-permute-done.6.refs_2_, ...), custom_call_target="tpu_custom_call" | custom-call | flops 335544320 | bytes 3932160 | tf_op jit(solution)/shard_map/pallas_call | solution.py:84
  40.3 0.1 collective-permute-start.8
  40.4 1.2 %collective-permute-done.8.refs_7_ = bf16[4,32,128]{2,1,0:T(8,128)(2,1)S(1)} collective-permute-done((bf16[4,32,128]{2,1,0:T(8,128)(2,1)S(1)}, bf16[4,32,128]{2,1,0:T(8,128)(2,1)S(1)}, u32[]{:S(2)}, u32[]{:S(2)}) %collective-permute-start.8) | collective-permute-done | bytes 32800 | tf_op jit(solution)/shard_map/ppermute | solution.py:299
  41.6 1.2 %shard_map.103.refs_0_ = bf16[256,128]{1,0:T(8,128)(2,1)S(1)} custom-call(bf16[128,512]{1,0:T(8,128)(2,1)S(1)} %bitcast.57, bf16[128,512]{1,0:T(8,128)(2,1)S(1)} %bitcast.58, bf16[128,512]{1,0:T(8,128)(2,1)S(1)} %collective-permute-done.1.refs_2_.refs_3_, bf16[128,512]{1,0:T(8,128)(2,1)S(1)} %collective-permute-done.1.refs_2_.refs_3_, ...), custom_call_target="tpu_custom_call" | custom-call | flops 402653184 | bytes 786432 | tf_op jit(solution)/shard_map/pallas_call | solution.py:164
  42.8 0.1 collective-permute-start.11
  42.9 1.7 %collective-permute-start.12 = (bf16[256,128]{1,0:T(8,128)(2,1)S(1)}, bf16[256,128]{1,0:T(8,128)(2,1)S(1)}, u32[]{:S(2)}, u32[]{:S(2)}) collective-permute-start(bf16[256,128]{1,0:T(8,128)(2,1)S(1)} %shard_map.103.refs_0_), channel_id=1, source_target_pairs={{0,2},{1,3},{2,0},{3,1},{4,6},{5,7},{6,4},{7,5},{8,10},{9,11},{10,... | collective-permute-start | bytes 196616 | tf_op jit(solution)/shard_map/ppermute | solution.py:305
  44.6 2.7 %collective-permute-start.13 = (bf16[256,128]{1,0:T(8,128)(2,1)S(1)}, bf16[256,128]{1,0:T(8,128)(2,1)S(1)}, u32[]{:S(2)}, u32[]{:S(2)}) collective-permute-start(bf16[256,128]{1,0:T(8,128)(2,1)S(1)} %shard_map.103.refs_0_), channel_id=1, source_target_pairs={{0,3},{1,2},{2,1},{3,0},{4,7},{5,6},{6,5},{7,4},{8,11},{9,10},{10,... | collective-permute-start | bytes 196616 | tf_op jit(solution)/shard_map/ppermute | solution.py:305
  47.3 0.2 copy.13
  47.5 1.3 %copy.14 = bf16[256,1280]{1,0:T(8,128)(2,1)S(1)} copy(bf16[256,1280]{0,1:T(8,128)(2,1)} %bitcast.64) | data formatting | bytes 1310720 | tf_op jit(solution)/shard_map/transpose | solution.py:312
  48.9 3.6 %collective-permute-done.15.refs_6_ = bf16[128,1280]{1,0:T(8,128)(2,1)S(1)} collective-permute-done((bf16[128,1280]{1,0:T(8,128)(2,1)}, bf16[128,1280]{1,0:T(8,128)(2,1)S(1)}, u32[]{:S(2)}, u32[]{:S(2)}) %collective-permute-start.15) | collective-permute-done | bytes 327712 | tf_op jit(solution)/shard_map/ppermute | solution.py:283
  52.5 2.5 %collective-permute-done.14.refs_5_ = bf16[128,1280]{1,0:T(8,128)(2,1)S(1)} collective-permute-done((bf16[128,1280]{1,0:T(8,128)(2,1)S(1)}, bf16[128,1280]{1,0:T(8,128)(2,1)S(1)}, u32[]{:S(2)}, u32[]{:S(2)}) %collective-permute-start.14) | collective-permute-done | bytes 327712 | tf_op jit(solution)/shard_map/ppermute | solution.py:300
  55.0 1.9 %collective-permute-done.11.refs_1_ = bf16[256,128]{1,0:T(8,128)(2,1)S(1)} collective-permute-done((bf16[256,128]{1,0:T(8,128)(2,1)S(1)}, bf16[256,128]{1,0:T(8,128)(2,1)S(1)}, u32[]{:S(2)}, u32[]{:S(2)}) %collective-permute-start.11) | collective-permute-done | bytes 65568 | tf_op jit(solution)/shard_map/ppermute | solution.py:305
  56.9 0.7 %collective-permute-done.13.refs_3_ = bf16[256,128]{1,0:T(8,128)(2,1)S(1)} collective-permute-done((bf16[256,128]{1,0:T(8,128)(2,1)S(1)}, bf16[256,128]{1,0:T(8,128)(2,1)S(1)}, u32[]{:S(2)}, u32[]{:S(2)}) %collective-permute-start.13) | collective-permute-done | bytes 65568 | tf_op jit(solution)/shard_map/ppermute | solution.py:305
  57.5 0.7 shard_map.105
  58.2 0.1 collective-permute-start.16
  58.3 0.7 shard_map.104
  59.0 0.1 select_bitcast_fusion.1
  59.1 0.1 pad_maximum_fusion.1
  59.1 0.8 %collective-permute-done.16.got_ref = bf16[4,32,1280]{2,1,0:T(8,128)(2,1)S(1)} collective-permute-done((bf16[4,32,1280]{2,1,0:T(8,128)(2,1)S(1)}, bf16[4,32,1280]{2,1,0:T(8,128)(2,1)S(1)}, u32[]{:S(2)}, u32[]{:S(2)}) %collective-permute-start.16) | collective-permute-done | bytes 327712 | tf_op jit(solution)/shard_map/ppermute | solution.py:316
  59.9 0.1 shard_map.106
  60.0 2.5 %collective-permute-start.17 = (bf16[32,1280]{1,0:T(8,128)(2,1)S(1)}, bf16[32,1280]{1,0:T(8,128)(2,1)S(1)}, u32[]{:S(2)}, u32[]{:S(2)}) collective-permute-start(bf16[32,1280]{1,0:T(8,128)(2,1)S(1)} %get-tuple-element.39), channel_id=1, source_target_pairs={{0,24},{4,28},{8,16},{12,20},{16,8},{20,12},{24,0},{28,4},{1,25},{... | collective-permute-start | bytes 245768 | tf_op jit(solution)/shard_map/ppermute | solution.py:329
  62.5 0.5 collective-permute-start.18
  63.0 0.5 collective-permute-start.19
  63.7 1.1 %copy.18 = bf16[1,1280,256]{2,1,0:T(8,128)(2,1)} copy(bf16[1,1280,256]{1,2,0:T(8,128)(2,1)S(1)} %bitcast.60) | data formatting | bytes 1310720
  64.8 1.1 %copy.17 = bf16[1,1280,256]{2,1,0:T(8,128)(2,1)} copy(bf16[1,1280,256]{1,2,0:T(8,128)(2,1)S(1)} %bitcast.61) | data formatting | bytes 1310720
  65.9 1.3 %collective-permute-done.18 = bf16[32,1280]{1,0:T(8,128)(2,1)S(1)} collective-permute-done((bf16[32,1280]{1,0:T(8,128)(2,1)S(1)}, bf16[32,1280]{1,0:T(8,128)(2,1)S(1)}, u32[]{:S(2)}, u32[]{:S(2)}) %collective-permute-start.18) | collective-permute-done | bytes 81952 | tf_op jit(solution)/shard_map/ppermute | solution.py:329
  67.2 0.3 collective-permute-done.19
  67.4 0.8 %fusion.1 = (f32[1280,32]{0,1:T(8,128)}, f32[1280,32]{0,1:T(8,128)}) fusion(f32[1280,32]{0,1:T(8,128)S(1)} %copy-done.3, bf16[32,1280]{1,0:T(8,128)(2,1)S(1)} %collective-permute-done.19, bf16[32,1280]{1,0:T(8,128)(2,1)S(1)} %collective-permute-done.18, f32[32,1280]{1,0:T(8,128)S(1)} %get-tuple-element.38, bf16[32,1280]{1,0:T(8,128)(2,1)S(1)} %collective-permute-done.17, ...), kind=kLoop, calls=%fused_computation.17 | loop fusion | flops 532480 | bytes 1064960 | tf_op jit(solution)/shard_map/sub | solution.py:334
  (24 shorter events, 0.2 us)
Async XLA Ops:
  0.6 13.6 %collective-permute-start = (bf16[128,5120]{1,0:T(8,128)(2,1)}, bf16[128,5120]{1,0:T(8,128)(2,1)S(1)}, u32[]{:S(2)}, u32[]{:S(2)}) collective-permute-start(bf16[128,5120]{1,0:T(8,128)(2,1)} %bitcast.62), channel_id=1, source_target_pairs={{0,4},{4,0},{8,12},{12,8},{16,20},{20,16},{24,28},{28,24},{1,5},{5... | collective-permute-start | bytes 3932168 | tf_op jit(solution)/shard_map/ppermute | solution.py:269
  2.1 8.6 %collective-permute-start.3 = (bf16[32,1280]{1,0:T(8,128)(2,1)S(1)}, bf16[32,1280]{1,0:T(8,128)(2,1)S(1)}, u32[]{:S(2)}, u32[]{:S(2)}) collective-permute-start(bf16[32,1280]{1,0:T(8,128)(2,1)S(1)} %convert_bitcast_fusion), channel_id=1, source_target_pairs={{0,2},{1,3},{2,0},{3,1},{4,6},{5,7},{6,4},{7,5},{8,10},{9,11},{10,... | collective-permute-start | bytes 245768 | tf_op jit(solution)/shard_map/ppermute | solution.py:271
  6.7 9.7 %collective-permute-start.1 = (bf16[128,512]{1,0:T(8,128)(2,1)S(1)}, bf16[128,512]{1,0:T(8,128)(2,1)S(1)}, u32[]{:S(2)}, u32[]{:S(2)}) collective-permute-start(bf16[128,512]{1,0:T(8,128)(2,1)S(1)} %bitcast.55), channel_id=1, source_target_pairs={{0,2},{1,3},{2,0},{3,1},{4,6},{5,7},{6,4},{7,5},{8,10},{9,11},{10,... | collective-permute-start | bytes 393224 | tf_op jit(solution)/shard_map/ppermute | solution.py:273
  10.7 9.0 %collective-permute-start.4 = (bf16[64,1280]{1,0:T(8,128)(2,1)S(1)}, bf16[64,1280]{1,0:T(8,128)(2,1)S(1)}, u32[]{:S(2)}, u32[]{:S(2)}) collective-permute-start(bf16[64,1280]{1,0:T(8,128)(2,1)S(1)} %pad_maximum_fusion.4), channel_id=1, source_target_pairs={{0,1},{1,0},{2,3},{3,2},{4,5},{5,4},{6,7},{7,6},{8,9},{9,8},{10,11... | collective-permute-start | bytes 491528 | tf_op jit(solution)/shard_map/ppermute | solution.py:287
  14.3 18.9 %copy-start.1 = (bf16[1,128,5120]{2,1,0:T(8,128)(2,1)S(1)}, bf16[1,128,5120]{2,1,0:T(8,128)(2,1)}, u32[]{:S(2)}) copy-start(bf16[1,128,5120]{2,1,0:T(8,128)(2,1)} %param.7) | copy-start | bytes 3932164
  16.3 16.9 %collective-permute-start.9 = (bf16[128,1280]{1,0:T(8,128)(2,1)S(1)}, bf16[128,1280]{1,0:T(8,128)(2,1)S(1)}, u32[]{:S(2)}, u32[]{:S(2)}) collective-permute-start(bf16[128,1280]{1,0:T(8,128)(2,1)S(1)} %get-tuple-element.32), channel_id=1, source_target_pairs={{0,2},{1,3},{2,0},{3,1},{4,7},{5,6},{6,5},{7,4},{8,10},{9,11},{10,... | collective-permute-start | bytes 983048 | tf_op jit(solution)/shard_map/ppermute | solution.py:282
  19.8 17.1 %collective-permute-start.5 = (bf16[128,1280]{1,0:T(8,128)(2,1)S(1)}, bf16[128,1280]{1,0:T(8,128)(2,1)S(1)}, u32[]{:S(2)}, u32[]{:S(2)}) collective-permute-start(bf16[128,1280]{1,0:T(8,128)(2,1)S(1)} %pad_maximum_fusion.2.refs_0_), channel_id=1, source_target_pairs={{0,8},{4,12},{8,0},{12,4},{16,24},{20,28},{24,16},{28,20},{1,9},{5... | collective-permute-start | bytes 983048 | tf_op jit(solution)/shard_map/ppermute | solution.py:293
  21.4 18.0 %collective-permute-start.6 = (bf16[128,1280]{1,0:T(8,128)(2,1)S(1)}, bf16[128,1280]{1,0:T(8,128)(2,1)S(1)}, u32[]{:S(2)}, u32[]{:S(2)}) collective-permute-start(bf16[128,1280]{1,0:T(8,128)(2,1)S(1)} %pad_maximum_fusion.2.refs_0_), channel_id=1, source_target_pairs={{0,16},{4,20},{8,24},{12,28},{16,0},{20,4},{24,8},{28,12},{1,17},{... | collective-permute-start | bytes 983048 | tf_op jit(solution)/shard_map/ppermute | solution.py:293
  22.9 16.4 %collective-permute-start.7 = (bf16[128,1280]{1,0:T(8,128)(2,1)S(1)}, bf16[128,1280]{1,0:T(8,128)(2,1)S(1)}, u32[]{:S(2)}, u32[]{:S(2)}) collective-permute-start(bf16[128,1280]{1,0:T(8,128)(2,1)S(1)} %pad_maximum_fusion.2.refs_0_), channel_id=1, source_target_pairs={{0,24},{4,28},{8,16},{12,20},{16,8},{20,12},{24,0},{28,4},{1,25},{... | collective-permute-start | bytes 983048 | tf_op jit(solution)/shard_map/ppermute | solution.py:293
  23.3 12.0 %collective-permute-start.2 = (bf16[256,512]{1,0:T(8,128)(2,1)S(1)}, bf16[256,512]{1,0:T(8,128)(2,1)S(1)}, u32[]{:S(2)}, u32[]{:S(2)}) collective-permute-start(bf16[256,512]{1,0:T(8,128)(2,1)S(1)} %pad_maximum_fusion.3), channel_id=1, source_target_pairs={{0,1},{1,0},{2,3},{3,2},{4,5},{5,4},{6,7},{7,6},{8,9},{9,8},{10,11... | collective-permute-start | bytes 786440 | tf_op jit(solution)/shard_map/ppermute | solution.py:288
  33.2 8.4 %collective-permute-start.10 = (bf16[128,1280]{1,0:T(8,128)(2,1)S(1)}, bf16[128,1280]{1,0:T(8,128)(2,1)S(1)}, u32[]{:S(2)}, u32[]{:S(2)}) collective-permute-start(bf16[128,1280]{1,0:T(8,128)(2,1)S(1)} %collective-permute-done.9), channel_id=1, source_target_pairs={{0,4},{4,0},{8,12},{12,8},{16,20},{20,16},{24,28},{28,24},{1,5},{5... | collective-permute-start | bytes 983048 | tf_op jit(solution)/shard_map/ppermute | solution.py:301
  35.4 17.1 %collective-permute-start.15 = (bf16[128,1280]{1,0:T(8,128)(2,1)}, bf16[128,1280]{1,0:T(8,128)(2,1)S(1)}, u32[]{:S(2)}, u32[]{:S(2)}) collective-permute-start(bf16[128,1280]{1,0:T(8,128)(2,1)} %get-tuple-element.52), channel_id=1, source_target_pairs={{0,2},{1,3},{2,0},{3,1},{4,7},{5,6},{6,5},{7,4},{8,10},{9,11},{10,... | collective-permute-start | bytes 983048 | tf_op jit(solution)/shard_map/ppermute | solution.py:283
  36.8 18.1 %collective-permute-start.14 = (bf16[128,1280]{1,0:T(8,128)(2,1)S(1)}, bf16[128,1280]{1,0:T(8,128)(2,1)S(1)}, u32[]{:S(2)}, u32[]{:S(2)}) collective-permute-start(bf16[128,1280]{1,0:T(8,128)(2,1)S(1)} %get-tuple-element.34.refs_5_), channel_id=1, source_target_pairs={{0,1},{1,0},{2,3},{3,2},{4,5},{5,4},{6,7},{7,6},{8,9},{9,8},{10,11... | collective-permute-start | bytes 983048 | tf_op jit(solution)/shard_map/ppermute | solution.py:300
  39.3 2.3 %copy-start = (bf16[1,128,256]{2,1,0:T(8,128)(2,1)S(1)}, bf16[1,128,256]{2,1,0:T(8,128)(2,1)}, u32[]{:S(2)}) copy-start(bf16[1,128,256]{2,1,0:T(8,128)(2,1)} %param.9) | copy-start | bytes 196612
  40.3 7.0 %copy-start.2 = (bf16[1,1280,256]{2,1,0:T(8,128)(2,1)S(1)}, bf16[1,1280,256]{2,1,0:T(8,128)(2,1)}, u32[]{:S(2)}) copy-start(bf16[1,1280,256]{2,1,0:T(8,128)(2,1)} %param.10) | copy-start | bytes 1966084
  40.3 1.3 %collective-permute-start.8 = (bf16[4,32,128]{2,1,0:T(8,128)(2,1)S(1)}, bf16[4,32,128]{2,1,0:T(8,128)(2,1)S(1)}, u32[]{:S(2)}, u32[]{:S(2)}) collective-permute-start(bf16[4,32,128]{2,1,0:T(8,128)(2,1)S(1)} %get-tuple-element.31), channel_id=1, source_target_pairs={{0,4},{4,0},{8,12},{12,8},{16,20},{20,16},{24,28},{28,24},{1,5},{5... | collective-permute-start | bytes 98312 | tf_op jit(solution)/shard_map/ppermute | solution.py:299
  42.8 14.0 %collective-permute-start.11 = (bf16[256,128]{1,0:T(8,128)(2,1)S(1)}, bf16[256,128]{1,0:T(8,128)(2,1)S(1)}, u32[]{:S(2)}, u32[]{:S(2)}) collective-permute-start(bf16[256,128]{1,0:T(8,128)(2,1)S(1)} %shard_map.103.refs_0_), channel_id=1, source_target_pairs={{0,1},{1,0},{2,3},{3,2},{4,5},{5,4},{6,7},{7,6},{8,9},{9,8},{10,11... | collective-permute-start | bytes 196616 | tf_op jit(solution)/shard_map/ppermute | solution.py:305
  42.9 13.9 %collective-permute-start.12 = (bf16[256,128]{1,0:T(8,128)(2,1)S(1)}, bf16[256,128]{1,0:T(8,128)(2,1)S(1)}, u32[]{:S(2)}, u32[]{:S(2)}) collective-permute-start(bf16[256,128]{1,0:T(8,128)(2,1)S(1)} %shard_map.103.refs_0_), channel_id=1, source_target_pairs={{0,2},{1,3},{2,0},{3,1},{4,6},{5,7},{6,4},{7,5},{8,10},{9,11},{10,... | collective-permute-start | bytes 196616 | tf_op jit(solution)/shard_map/ppermute | solution.py:305
  44.6 12.9 %collective-permute-start.13 = (bf16[256,128]{1,0:T(8,128)(2,1)S(1)}, bf16[256,128]{1,0:T(8,128)(2,1)S(1)}, u32[]{:S(2)}, u32[]{:S(2)}) collective-permute-start(bf16[256,128]{1,0:T(8,128)(2,1)S(1)} %shard_map.103.refs_0_), channel_id=1, source_target_pairs={{0,3},{1,2},{2,1},{3,0},{4,7},{5,6},{6,5},{7,4},{8,11},{9,10},{10,... | collective-permute-start | bytes 196616 | tf_op jit(solution)/shard_map/ppermute | solution.py:305
  58.2 1.7 %collective-permute-start.16 = (bf16[4,32,1280]{2,1,0:T(8,128)(2,1)S(1)}, bf16[4,32,1280]{2,1,0:T(8,128)(2,1)S(1)}, u32[]{:S(2)}, u32[]{:S(2)}) collective-permute-start(bf16[4,32,1280]{2,1,0:T(8,128)(2,1)S(1)} %get-tuple-element.37), channel_id=1, source_target_pairs={{0,4},{4,0},{8,12},{12,8},{16,20},{20,16},{24,28},{28,24},{1,5},{5... | collective-permute-start | bytes 983048 | tf_op jit(solution)/shard_map/ppermute | solution.py:316
  60.0 5.9 %collective-permute-start.17 = (bf16[32,1280]{1,0:T(8,128)(2,1)S(1)}, bf16[32,1280]{1,0:T(8,128)(2,1)S(1)}, u32[]{:S(2)}, u32[]{:S(2)}) collective-permute-start(bf16[32,1280]{1,0:T(8,128)(2,1)S(1)} %get-tuple-element.39), channel_id=1, source_target_pairs={{0,24},{4,28},{8,16},{12,20},{16,8},{20,12},{24,0},{28,4},{1,25},{... | collective-permute-start | bytes 245768 | tf_op jit(solution)/shard_map/ppermute | solution.py:329
  62.5 4.7 %collective-permute-start.18 = (bf16[32,1280]{1,0:T(8,128)(2,1)S(1)}, bf16[32,1280]{1,0:T(8,128)(2,1)S(1)}, u32[]{:S(2)}, u32[]{:S(2)}) collective-permute-start(bf16[32,1280]{1,0:T(8,128)(2,1)S(1)} %get-tuple-element.40), channel_id=1, source_target_pairs={{0,16},{4,20},{8,24},{12,28},{16,0},{20,4},{24,8},{28,12},{1,17},{... | collective-permute-start | bytes 245768 | tf_op jit(solution)/shard_map/ppermute | solution.py:329
  63.0 4.4 %collective-permute-start.19 = (bf16[32,1280]{1,0:T(8,128)(2,1)S(1)}, bf16[32,1280]{1,0:T(8,128)(2,1)S(1)}, u32[]{:S(2)}, u32[]{:S(2)}) collective-permute-start(bf16[32,1280]{1,0:T(8,128)(2,1)S(1)} %get-tuple-element.41), channel_id=1, source_target_pairs={{0,8},{4,12},{8,0},{12,4},{16,24},{20,28},{24,16},{28,20},{1,9},{5... | collective-permute-start | bytes 245768 | tf_op jit(solution)/shard_map/ppermute | solution.py:329
  64.7 2.7 %copy-start.3 = (f32[1280,32]{0,1:T(8,128)S(1)}, f32[1280,32]{0,1:T(8,128)}, u32[]{:S(2)}) copy-start(f32[1280,32]{0,1:T(8,128)} %param.12) | copy-start | bytes 491524
  64.7 2.7 %copy-start.4 = (f32[1280,32]{0,1:T(8,128)S(1)}, f32[1280,32]{0,1:T(8,128)}, u32[]{:S(2)}) copy-start(f32[1280,32]{0,1:T(8,128)} %param.13) | copy-start | bytes 491524

commit v16 on v11

--- a/solution.py
+++ b/solution.py
@@ -323,7 +323,7 @@
         return jnp.stack([lower, upper], axis=1).reshape(cols, block).T[None]
 
     total = parts[0]
-    for step in range(1, n_chip):
+    for step in reversed(range(1, n_chip)):
         total = total + lax.ppermute(
             parts[step], "island", pair_perm(n_chip, step, 2)
         ).astype(jnp.float32)

time: 68.1 us -> 67.2 us (0.987)
  waiting for transfers between devices: 32.2 us -> 31.2 us
    ppermute x3, waiting for transfers between devices: 2.54 us -> 1.58 us  [on_device(): lax.ppermute(parts[step], 'island', pair_perm(n_chip, step, 2))]
where the time goes in v16:
time: 67.2 us; the launch traced here: 66.9 us
  waiting for transfers between devices  31.2 us (46%)
  starting transfers between devices  22.9 us (34%)
  local copies, waits for them, and re-layouts  6.39 us (10%)
  Pallas kernels  3.58 us (5%)
  other arithmetic  2.03 us (3%)
  between operations  0.83 us (1%)
    ppermute x3, waiting for transfers between devices, on_device(): lax.ppermute(dquery, 'seq', pair_perm(n_seq, k))  9.22 us
    ppermute x3, waiting for transfers between devices, on_device(): spread[step] = lax.ppermute(held, 'island', pair_perm(n_chip, step, 2))  8.42 us
    ppermute x1, waiting for transfers between devices, on_device(): lax.ppermute(jnp.concatenate(kv, axis=0), 'seq', pair_perm(n_seq, bit))  5.36 us
    ppermute x1, starting transfers between devices, on_device(): held = jnp.concatenate([weight, lax.ppermute(weight, 'seq', far_perm)], 0)  3.67 us
    ppermute x3, starting transfers between devices, on_device(): lax.ppermute(dquery, 'seq', pair_perm(n_seq, k))  3.55 us
    ppermute x3, starting transfers between devices, on_device(): lax.ppermute(parts[step], 'island', pair_perm(n_chip, step, 2))  3.55 us
    ppermute x3, starting transfers between devices, on_device(): spread[step] = lax.ppermute(held, 'island', pair_perm(n_chip, step, 2))  3.55 us
    ppermute x1, starting transfers between devices, on_device(): lax.ppermute(held, 'seq', pair_perm(n_seq, bit))  3.54 us
  transfers between devices with their start and end apart: 19, of which 11 were waited for; matrix products, arithmetic and copies ran while one was open for 11% of the time, Pallas kernels for 4%

profile of v16, /device:TPU:0, one launch (start us, length us, event | category | flops | bytes accessed | tf_op | source)
XLA Modules:
  0.0 66.9 jit_solution(5630790059956571170)
XLA Ops:
  0.6 0.5 collective-permute-start
  1.1 0.9 %convert_bitcast_fusion = bf16[32,1280]{1,0:T(8,128)(2,1)S(1)} fusion(f32[1280,32]{0,1:T(8,128)} %param.12), kind=kLoop, calls=%fused_computation.20 | loop fusion | flops 40960 | bytes 245760 | tf_op jit(solution)/shard_map/convert_element_type | solution.py:270
  2.1 3.7 %collective-permute-start.3 = (bf16[32,1280]{1,0:T(8,128)(2,1)S(1)}, bf16[32,1280]{1,0:T(8,128)(2,1)S(1)}, u32[]{:S(2)}, u32[]{:S(2)}) collective-permute-start(bf16[32,1280]{1,0:T(8,128)(2,1)S(1)} %convert_bitcast_fusion), channel_id=1, source_target_pairs={{0,2},{1,3},{2,0},{3,1},{4,6},{5,7},{6,4},{7,5},{8,10},{9,11},{10,... | collective-permute-start | bytes 245768 | tf_op jit(solution)/shard_map/ppermute | solution.py:271
  5.7 0.9 %copy.19 = bf16[16,8,2,256]{3,1,2,0:T(8,128)(2,1)S(1)} copy(bf16[16,8,2,256]{3,2,1,0:T(2,128)(2,1)} %bitcast.65) | data formatting | bytes 262144
  6.7 0.1 collective-permute-start.1
  6.8 1.5 %dynamic-slice_bitcast_fusion = (bf16[128,1280]{1,0:T(8,128)(2,1)S(1)}, bf16[128,1280]{1,0:T(8,128)(2,1)S(1)}, bf16[128,1280]{1,0:T(8,128)(2,1)S(1)}, bf16[128,1280]{1,0:T(8,128)(2,1)S(1)}, bf16[128,1280]{1,0:T(8,128)(2,1)S(1)}) fusion(bf16[1,128,5120]{2,1,0:T(8,128)(2,1)} %param.7, s32[]{:T(128)S(6)} %select_n.44, s32[]{:T(128)S(6)} %select_n.42, ...), kind=kLoop, calls=%fused_computation.8 | loop fusion | bytes 3276820 | tf_op jit(solution)/shard_map/dynamic_slice | solution.py:276
  8.3 2.4 %collective-permute-done.3 = bf16[32,1280]{1,0:T(8,128)(2,1)S(1)} collective-permute-done((bf16[32,1280]{1,0:T(8,128)(2,1)S(1)}, bf16[32,1280]{1,0:T(8,128)(2,1)S(1)}, u32[]{:S(2)}, u32[]{:S(2)}) %collective-permute-start.3) | collective-permute-done | bytes 81952 | tf_op jit(solution)/shard_map/ppermute | solution.py:271
  10.7 3.5 %collective-permute-start.4 = (bf16[64,1280]{1,0:T(8,128)(2,1)S(1)}, bf16[64,1280]{1,0:T(8,128)(2,1)S(1)}, u32[]{:S(2)}, u32[]{:S(2)}) collective-permute-start(bf16[64,1280]{1,0:T(8,128)(2,1)S(1)} %pad_maximum_fusion.5), channel_id=1, source_target_pairs={{0,1},{1,0},{2,3},{3,2},{4,5},{5,4},{6,7},{7,6},{8,9},{9,8},{10,11... | collective-permute-start | bytes 491528 | tf_op jit(solution)/shard_map/ppermute | solution.py:286
  14.2 0.0 collective-permute-done
  14.3 0.1 constant_dynamic-slice_fusion
  14.5 1.9 %collective-permute-done.1.refs_2_.refs_3_ = bf16[128,512]{1,0:T(8,128)(2,1)S(1)} collective-permute-done((bf16[128,512]{1,0:T(8,128)(2,1)S(1)}, bf16[128,512]{1,0:T(8,128)(2,1)S(1)}, u32[]{:S(2)}, u32[]{:S(2)}) %collective-permute-start.1) | collective-permute-done | bytes 131104 | tf_op jit(solution)/shard_map/ppermute | solution.py:273
  16.3 0.7 %collective-permute-start.2 = (bf16[256,512]{1,0:T(8,128)(2,1)S(1)}, bf16[256,512]{1,0:T(8,128)(2,1)S(1)}, u32[]{:S(2)}, u32[]{:S(2)}) collective-permute-start(bf16[256,512]{1,0:T(8,128)(2,1)S(1)} %pad_maximum_fusion.4), channel_id=1, source_target_pairs={{0,1},{1,0},{2,3},{3,2},{4,5},{5,4},{6,7},{7,6},{8,9},{9,8},{10,11... | collective-permute-start | bytes 786440 | tf_op jit(solution)/shard_map/ppermute | solution.py:287
  17.1 3.4 %collective-permute-start.13 = (bf16[256,1280]{1,0:T(8,128)(2,1)S(1)}, bf16[256,1280]{1,0:T(8,128)(2,1)S(1)}, u32[]{:S(2)}, u32[]{:S(2)}) collective-permute-start(bf16[256,1280]{1,0:T(8,128)(2,1)S(1)} %pad_maximum_fusion), channel_id=1, source_target_pairs={{0,2},{1,3},{2,0},{3,1},{4,7},{5,6},{6,5},{7,4},{8,10},{9,11},{10,... | collective-permute-start | bytes 1966088 | tf_op jit(solution)/shard_map/ppermute | solution.py:282
  20.4 1.6 %collective-permute-start.5 = (bf16[128,1280]{1,0:T(8,128)(2,1)S(1)}, bf16[128,1280]{1,0:T(8,128)(2,1)S(1)}, u32[]{:S(2)}, u32[]{:S(2)}) collective-permute-start(bf16[128,1280]{1,0:T(8,128)(2,1)S(1)} %pad_maximum_fusion.3.refs_0_), channel_id=1, source_target_pairs={{0,8},{4,12},{8,0},{12,4},{16,24},{20,28},{24,16},{28,20},{1,9},{5... | collective-permute-start | bytes 983048 | tf_op jit(solution)/shard_map/ppermute | solution.py:292
  22.0 1.5 %collective-permute-start.6 = (bf16[128,1280]{1,0:T(8,128)(2,1)S(1)}, bf16[128,1280]{1,0:T(8,128)(2,1)S(1)}, u32[]{:S(2)}, u32[]{:S(2)}) collective-permute-start(bf16[128,1280]{1,0:T(8,128)(2,1)S(1)} %pad_maximum_fusion.3.refs_0_), channel_id=1, source_target_pairs={{0,16},{4,20},{8,24},{12,28},{16,0},{20,4},{24,8},{28,12},{1,17},{... | collective-permute-start | bytes 983048 | tf_op jit(solution)/shard_map/ppermute | solution.py:292
  23.5 0.5 collective-permute-start.7
  24.0 5.4 %collective-permute-done.2.refs_4_.refs_5_ = bf16[256,512]{1,0:T(8,128)(2,1)S(1)} collective-permute-done((bf16[256,512]{1,0:T(8,128)(2,1)S(1)}, bf16[256,512]{1,0:T(8,128)(2,1)S(1)}, u32[]{:S(2)}, u32[]{:S(2)}) %collective-permute-start.2) | collective-permute-done | bytes 262176 | tf_op jit(solution)/shard_map/ppermute | solution.py:287
  29.4 1.8 %collective-permute-done.5.refs_1_ = bf16[128,1280]{1,0:T(8,128)(2,1)S(1)} collective-permute-done((bf16[128,1280]{1,0:T(8,128)(2,1)S(1)}, bf16[128,1280]{1,0:T(8,128)(2,1)S(1)}, u32[]{:S(2)}, u32[]{:S(2)}) %collective-permute-start.5) | collective-permute-done | bytes 327712 | tf_op jit(solution)/shard_map/ppermute | solution.py:292
  31.2 6.6 %collective-permute-done.6.refs_2_ = bf16[128,1280]{1,0:T(8,128)(2,1)S(1)} collective-permute-done((bf16[128,1280]{1,0:T(8,128)(2,1)S(1)}, bf16[128,1280]{1,0:T(8,128)(2,1)S(1)}, u32[]{:S(2)}, u32[]{:S(2)}) %collective-permute-start.6) | collective-permute-done | bytes 327712 | tf_op jit(solution)/shard_map/ppermute | solution.py:292
  37.8 1.0 %shard_map.102 = (bf16[4,32,128]{2,1,0:T(8,128)(2,1)S(1)}, bf16[4,32,128]{2,1,0:T(8,128)(2,1)S(1)}) custom-call(bf16[128,1280]{1,0:T(8,128)(2,1)S(1)} %pad_maximum_fusion.3.refs_0_, bf16[128,1280]{1,0:T(8,128)(2,1)S(1)} %collective-permute-done.5.refs_1_, bf16[128,1280]{1,0:T(8,128)(2,1)S(1)} %collective-permute-done.6.refs_2_, ...), custom_call_target="tpu_custom_call" | custom-call | flops 335544320 | bytes 3932160 | tf_op jit(solution)/shard_map/pallas_call | solution.py:84
  38.8 0.0 copy-start.1
  38.8 0.1 collective-permute-start.8
  38.8 1.2 %collective-permute-done.8.refs_7_ = bf16[4,32,128]{2,1,0:T(8,128)(2,1)S(1)} collective-permute-done((bf16[4,32,128]{2,1,0:T(8,128)(2,1)S(1)}, bf16[4,32,128]{2,1,0:T(8,128)(2,1)S(1)}, u32[]{:S(2)}, u32[]{:S(2)}) %collective-permute-start.8) | collective-permute-done | bytes 32800 | tf_op jit(solution)/shard_map/ppermute | solution.py:298
  40.0 1.2 %shard_map.103.refs_0_ = bf16[256,128]{1,0:T(8,128)(2,1)S(1)} custom-call(bf16[128,512]{1,0:T(8,128)(2,1)S(1)} %bitcast.57, bf16[128,512]{1,0:T(8,128)(2,1)S(1)} %bitcast.58, bf16[128,512]{1,0:T(8,128)(2,1)S(1)} %collective-permute-done.1.refs_2_.refs_3_, bf16[128,512]{1,0:T(8,128)(2,1)S(1)} %collective-permute-done.1.refs_2_.refs_3_, ...), custom_call_target="tpu_custom_call" | custom-call | flops 402653184 | bytes 786432 | tf_op jit(solution)/shard_map/pallas_call | solution.py:164
  41.3 1.8 %collective-permute-start.10 = (bf16[256,128]{1,0:T(8,128)(2,1)S(1)}, bf16[256,128]{1,0:T(8,128)(2,1)S(1)}, u32[]{:S(2)}, u32[]{:S(2)}) collective-permute-start(bf16[256,128]{1,0:T(8,128)(2,1)S(1)} %shard_map.103.refs_0_), channel_id=1, source_target_pairs={{0,2},{1,3},{2,0},{3,1},{4,6},{5,7},{6,4},{7,5},{8,10},{9,11},{10,... | collective-permute-start | bytes 196616 | tf_op jit(solution)/shard_map/ppermute | solution.py:302
  43.0 1.3 %collective-permute-start.11 = (bf16[256,128]{1,0:T(8,128)(2,1)S(1)}, bf16[256,128]{1,0:T(8,128)(2,1)S(1)}, u32[]{:S(2)}, u32[]{:S(2)}) collective-permute-start(bf16[256,128]{1,0:T(8,128)(2,1)S(1)} %shard_map.103.refs_0_), channel_id=1, source_target_pairs={{0,3},{1,2},{2,1},{3,0},{4,7},{5,6},{6,5},{7,4},{8,11},{9,10},{10,... | collective-permute-start | bytes 196616 | tf_op jit(solution)/shard_map/ppermute | solution.py:302
  44.4 0.5 collective-permute-start.9
  44.8 9.2 %collective-permute-done.10.refs_2_ = bf16[256,128]{1,0:T(8,128)(2,1)S(1)} collective-permute-done((bf16[256,128]{1,0:T(8,128)(2,1)S(1)}, bf16[256,128]{1,0:T(8,128)(2,1)S(1)}, u32[]{:S(2)}, u32[]{:S(2)}) %collective-permute-start.10) | collective-permute-done | bytes 65568 | tf_op jit(solution)/shard_map/ppermute | solution.py:302
  54.1 0.1 collective-permute-start.14
  54.2 0.2 copy.13
  54.4 1.3 %copy.14 = bf16[256,1280]{1,0:T(8,128)(2,1)S(1)} copy(bf16[256,1280]{0,1:T(8,128)(2,1)} %bitcast.64) | data formatting | bytes 1310720 | tf_op jit(solution)/shard_map/transpose | solution.py:310
  55.7 0.5 collective-permute-done.14.refs_7_
  56.2 0.7 shard_map.105
  56.9 0.2 collective-permute-start.15
  57.1 0.7 shard_map.104
  57.8 0.1 select_bitcast_fusion.1
  57.9 0.1 pad_maximum_fusion.2
  57.9 0.7 %collective-permute-done.15.got_ref = bf16[4,32,1280]{2,1,0:T(8,128)(2,1)S(1)} collective-permute-done((bf16[4,32,1280]{2,1,0:T(8,128)(2,1)S(1)}, bf16[4,32,1280]{2,1,0:T(8,128)(2,1)S(1)}, u32[]{:S(2)}, u32[]{:S(2)}) %collective-permute-start.15) | collective-permute-done | bytes 327712 | tf_op jit(solution)/shard_map/ppermute | solution.py:314
  58.6 0.1 shard_map.106
  58.7 2.5 %collective-permute-start.16 = (bf16[32,1280]{1,0:T(8,128)(2,1)S(1)}, bf16[32,1280]{1,0:T(8,128)(2,1)S(1)}, u32[]{:S(2)}, u32[]{:S(2)}) collective-permute-start(bf16[32,1280]{1,0:T(8,128)(2,1)S(1)} %get-tuple-element.39), channel_id=1, source_target_pairs={{0,24},{4,28},{8,16},{12,20},{16,8},{20,12},{24,0},{28,4},{1,25},{... | collective-permute-start | bytes 245768 | tf_op jit(solution)/shard_map/ppermute | solution.py:327
  61.2 0.5 collective-permute-start.17
  61.7 0.5 collective-permute-start.18
  62.2 0.1 pad_maximum_fusion.1
  62.4 1.1 %copy.18 = bf16[1,1280,256]{2,1,0:T(8,128)(2,1)} copy(bf16[1,1280,256]{1,2,0:T(8,128)(2,1)S(1)} %bitcast.60) | data formatting | bytes 1310720
  63.5 1.1 %copy.17 = bf16[1,1280,256]{2,1,0:T(8,128)(2,1)} copy(bf16[1,1280,256]{1,2,0:T(8,128)(2,1)S(1)} %bitcast.61) | data formatting | bytes 1310720
  64.6 1.3 %collective-permute-done.17 = bf16[32,1280]{1,0:T(8,128)(2,1)S(1)} collective-permute-done((bf16[32,1280]{1,0:T(8,128)(2,1)S(1)}, bf16[32,1280]{1,0:T(8,128)(2,1)S(1)}, u32[]{:S(2)}, u32[]{:S(2)}) %collective-permute-start.17) | collective-permute-done | bytes 81952 | tf_op jit(solution)/shard_map/ppermute | solution.py:327
  65.9 0.3 collective-permute-done.18
  66.1 0.8 %fusion.1 = (f32[1280,32]{0,1:T(8,128)}, f32[1280,32]{0,1:T(8,128)}) fusion(f32[1280,32]{0,1:T(8,128)S(1)} %copy-done.2, bf16[32,1280]{1,0:T(8,128)(2,1)S(1)} %collective-permute-done.18, bf16[32,1280]{1,0:T(8,128)(2,1)S(1)} %collective-permute-done.17, f32[32,1280]{1,0:T(8,128)S(1)} %get-tuple-element.38, bf16[32,1280]{1,0:T(8,128)(2,1)S(1)} %collective-permute-done.16, ...), kind=kLoop, calls=%fused_computation.18 | loop fusion | flops 532480 | bytes 1064960 | tf_op jit(solution)/shard_map/sub | solution.py:332
  (21 shorter events, 0.2 us)
Async XLA Ops:
  0.6 13.6 %collective-permute-start = (bf16[128,5120]{1,0:T(8,128)(2,1)}, bf16[128,5120]{1,0:T(8,128)(2,1)S(1)}, u32[]{:S(2)}, u32[]{:S(2)}) collective-permute-start(bf16[128,5120]{1,0:T(8,128)(2,1)} %bitcast.62), channel_id=1, source_target_pairs={{0,4},{4,0},{8,12},{12,8},{16,20},{20,16},{24,28},{28,24},{1,5},{5... | collective-permute-start | bytes 3932168 | tf_op jit(solution)/shard_map/ppermute | solution.py:269
  2.1 8.6 %collective-permute-start.3 = (bf16[32,1280]{1,0:T(8,128)(2,1)S(1)}, bf16[32,1280]{1,0:T(8,128)(2,1)S(1)}, u32[]{:S(2)}, u32[]{:S(2)}) collective-permute-start(bf16[32,1280]{1,0:T(8,128)(2,1)S(1)} %convert_bitcast_fusion), channel_id=1, source_target_pairs={{0,2},{1,3},{2,0},{3,1},{4,6},{5,7},{6,4},{7,5},{8,10},{9,11},{10,... | collective-permute-start | bytes 245768 | tf_op jit(solution)/shard_map/ppermute | solution.py:271
  6.7 9.7 %collective-permute-start.1 = (bf16[128,512]{1,0:T(8,128)(2,1)S(1)}, bf16[128,512]{1,0:T(8,128)(2,1)S(1)}, u32[]{:S(2)}, u32[]{:S(2)}) collective-permute-start(bf16[128,512]{1,0:T(8,128)(2,1)S(1)} %bitcast.55), channel_id=1, source_target_pairs={{0,2},{1,3},{2,0},{3,1},{4,6},{5,7},{6,4},{7,5},{8,10},{9,11},{10,... | collective-permute-start | bytes 393224 | tf_op jit(solution)/shard_map/ppermute | solution.py:273
  10.7 9.7 %collective-permute-start.4 = (bf16[64,1280]{1,0:T(8,128)(2,1)S(1)}, bf16[64,1280]{1,0:T(8,128)(2,1)S(1)}, u32[]{:S(2)}, u32[]{:S(2)}) collective-permute-start(bf16[64,1280]{1,0:T(8,128)(2,1)S(1)} %pad_maximum_fusion.5), channel_id=1, source_target_pairs={{0,1},{1,0},{2,3},{3,2},{4,5},{5,4},{6,7},{7,6},{8,9},{9,8},{10,11... | collective-permute-start | bytes 491528 | tf_op jit(solution)/shard_map/ppermute | solution.py:286
  16.3 13.0 %collective-permute-start.2 = (bf16[256,512]{1,0:T(8,128)(2,1)S(1)}, bf16[256,512]{1,0:T(8,128)(2,1)S(1)}, u32[]{:S(2)}, u32[]{:S(2)}) collective-permute-start(bf16[256,512]{1,0:T(8,128)(2,1)S(1)} %pad_maximum_fusion.4), channel_id=1, source_target_pairs={{0,1},{1,0},{2,3},{3,2},{4,5},{5,4},{6,7},{7,6},{8,9},{9,8},{10,11... | collective-permute-start | bytes 786440 | tf_op jit(solution)/shard_map/ppermute | solution.py:287
  17.1 37.0 %collective-permute-start.13 = (bf16[256,1280]{1,0:T(8,128)(2,1)S(1)}, bf16[256,1280]{1,0:T(8,128)(2,1)S(1)}, u32[]{:S(2)}, u32[]{:S(2)}) collective-permute-start(bf16[256,1280]{1,0:T(8,128)(2,1)S(1)} %pad_maximum_fusion), channel_id=1, source_target_pairs={{0,2},{1,3},{2,0},{3,1},{4,7},{5,6},{6,5},{7,4},{8,10},{9,11},{10,... | collective-permute-start | bytes 1966088 | tf_op jit(solution)/shard_map/ppermute | solution.py:282
  20.4 10.7 %collective-permute-start.5 = (bf16[128,1280]{1,0:T(8,128)(2,1)S(1)}, bf16[128,1280]{1,0:T(8,128)(2,1)S(1)}, u32[]{:S(2)}, u32[]{:S(2)}) collective-permute-start(bf16[128,1280]{1,0:T(8,128)(2,1)S(1)} %pad_maximum_fusion.3.refs_0_), channel_id=1, source_target_pairs={{0,8},{4,12},{8,0},{12,4},{16,24},{20,28},{24,16},{28,20},{1,9},{5... | collective-permute-start | bytes 983048 | tf_op jit(solution)/shard_map/ppermute | solution.py:292
  22.0 15.8 %collective-permute-start.6 = (bf16[128,1280]{1,0:T(8,128)(2,1)S(1)}, bf16[128,1280]{1,0:T(8,128)(2,1)S(1)}, u32[]{:S(2)}, u32[]{:S(2)}) collective-permute-start(bf16[128,1280]{1,0:T(8,128)(2,1)S(1)} %pad_maximum_fusion.3.refs_0_), channel_id=1, source_target_pairs={{0,16},{4,20},{8,24},{12,28},{16,0},{20,4},{24,8},{28,12},{1,17},{... | collective-permute-start | bytes 983048 | tf_op jit(solution)/shard_map/ppermute | solution.py:292
  23.5 14.3 %collective-permute-start.7 = (bf16[128,1280]{1,0:T(8,128)(2,1)S(1)}, bf16[128,1280]{1,0:T(8,128)(2,1)S(1)}, u32[]{:S(2)}, u32[]{:S(2)}) collective-permute-start(bf16[128,1280]{1,0:T(8,128)(2,1)S(1)} %pad_maximum_fusion.3.refs_0_), channel_id=1, source_target_pairs={{0,24},{4,28},{8,16},{12,20},{16,8},{20,12},{24,0},{28,4},{1,25},{... | collective-permute-start | bytes 983048 | tf_op jit(solution)/shard_map/ppermute | solution.py:292
  29.4 24.7 %collective-permute-start.12 = (bf16[128,1280]{1,0:T(8,128)(2,1)S(1)}, bf16[128,1280]{1,0:T(8,128)(2,1)S(1)}, u32[]{:S(2)}, u32[]{:S(2)}) collective-permute-start(bf16[128,1280]{1,0:T(8,128)(2,1)S(1)} %get-tuple-element.32.refs_5_), channel_id=1, source_target_pairs={{0,1},{1,0},{2,3},{3,2},{4,5},{5,4},{6,7},{7,6},{8,9},{9,8},{10,11... | collective-permute-start | bytes 983048 | tf_op jit(solution)/shard_map/ppermute | solution.py:299
  37.8 2.3 %copy-start = (bf16[1,128,256]{2,1,0:T(8,128)(2,1)S(1)}, bf16[1,128,256]{2,1,0:T(8,128)(2,1)}, u32[]{:S(2)}) copy-start(bf16[1,128,256]{2,1,0:T(8,128)(2,1)} %param.9) | copy-start | bytes 196612
  38.8 15.4 %copy-start.1 = (bf16[1,1280,256]{2,1,0:T(8,128)(2,1)S(1)}, bf16[1,1280,256]{2,1,0:T(8,128)(2,1)}, u32[]{:S(2)}) copy-start(bf16[1,1280,256]{2,1,0:T(8,128)(2,1)} %param.10) | copy-start | bytes 1966084
  38.8 1.3 %collective-permute-start.8 = (bf16[4,32,128]{2,1,0:T(8,128)(2,1)S(1)}, bf16[4,32,128]{2,1,0:T(8,128)(2,1)S(1)}, u32[]{:S(2)}, u32[]{:S(2)}) collective-permute-start(bf16[4,32,128]{2,1,0:T(8,128)(2,1)S(1)} %get-tuple-element.31), channel_id=1, source_target_pairs={{0,4},{4,0},{8,12},{12,8},{16,20},{20,16},{24,28},{28,24},{1,5},{5... | collective-permute-start | bytes 98312 | tf_op jit(solution)/shard_map/ppermute | solution.py:298
  41.3 12.8 %collective-permute-start.10 = (bf16[256,128]{1,0:T(8,128)(2,1)S(1)}, bf16[256,128]{1,0:T(8,128)(2,1)S(1)}, u32[]{:S(2)}, u32[]{:S(2)}) collective-permute-start(bf16[256,128]{1,0:T(8,128)(2,1)S(1)} %shard_map.103.refs_0_), channel_id=1, source_target_pairs={{0,2},{1,3},{2,0},{3,1},{4,6},{5,7},{6,4},{7,5},{8,10},{9,11},{10,... | collective-permute-start | bytes 196616 | tf_op jit(solution)/shard_map/ppermute | solution.py:302
  43.0 11.0 %collective-permute-start.11 = (bf16[256,128]{1,0:T(8,128)(2,1)S(1)}, bf16[256,128]{1,0:T(8,128)(2,1)S(1)}, u32[]{:S(2)}, u32[]{:S(2)}) collective-permute-start(bf16[256,128]{1,0:T(8,128)(2,1)S(1)} %shard_map.103.refs_0_), channel_id=1, source_target_pairs={{0,3},{1,2},{2,1},{3,0},{4,7},{5,6},{6,5},{7,4},{8,11},{9,10},{10,... | collective-permute-start | bytes 196616 | tf_op jit(solution)/shard_map/ppermute | solution.py:302
  44.4 9.7 %collective-permute-start.9 = (bf16[256,128]{1,0:T(8,128)(2,1)S(1)}, bf16[256,128]{1,0:T(8,128)(2,1)S(1)}, u32[]{:S(2)}, u32[]{:S(2)}) collective-permute-start(bf16[256,128]{1,0:T(8,128)(2,1)S(1)} %shard_map.103.refs_0_), channel_id=1, source_target_pairs={{0,1},{1,0},{2,3},{3,2},{4,5},{5,4},{6,7},{7,6},{8,9},{9,8},{10,11... | collective-permute-start | bytes 196616 | tf_op jit(solution)/shard_map/ppermute | solution.py:302
  54.1 2.2 %collective-permute-start.14 = (bf16[256,1280]{1,0:T(8,128)(2,1)S(1)}, bf16[256,1280]{1,0:T(8,128)(2,1)S(1)}, u32[]{:S(2)}, u32[]{:S(2)}) collective-permute-start(bf16[256,1280]{1,0:T(8,128)(2,1)S(1)} %collective-permute-done.13.refs_6_), channel_id=1, source_target_pairs={{0,4},{4,0},{8,12},{12,8},{16,20},{20,16},{24,28},{28,24},{1,5},{5... | collective-permute-start | bytes 1966088 | tf_op jit(solution)/shard_map/ppermute | solution.py:308
  56.9 1.7 %collective-permute-start.15 = (bf16[4,32,1280]{2,1,0:T(8,128)(2,1)S(1)}, bf16[4,32,1280]{2,1,0:T(8,128)(2,1)S(1)}, u32[]{:S(2)}, u32[]{:S(2)}) collective-permute-start(bf16[4,32,1280]{2,1,0:T(8,128)(2,1)S(1)} %get-tuple-element.37), channel_id=1, source_target_pairs={{0,4},{4,0},{8,12},{12,8},{16,20},{20,16},{24,28},{28,24},{1,5},{5... | collective-permute-start | bytes 983048 | tf_op jit(solution)/shard_map/ppermute | solution.py:314
  58.7 5.9 %collective-permute-start.16 = (bf16[32,1280]{1,0:T(8,128)(2,1)S(1)}, bf16[32,1280]{1,0:T(8,128)(2,1)S(1)}, u32[]{:S(2)}, u32[]{:S(2)}) collective-permute-start(bf16[32,1280]{1,0:T(8,128)(2,1)S(1)} %get-tuple-element.39), channel_id=1, source_target_pairs={{0,24},{4,28},{8,16},{12,20},{16,8},{20,12},{24,0},{28,4},{1,25},{... | collective-permute-start | bytes 245768 | tf_op jit(solution)/shard_map/ppermute | solution.py:327
  61.2 4.7 %collective-permute-start.17 = (bf16[32,1280]{1,0:T(8,128)(2,1)S(1)}, bf16[32,1280]{1,0:T(8,128)(2,1)S(1)}, u32[]{:S(2)}, u32[]{:S(2)}) collective-permute-start(bf16[32,1280]{1,0:T(8,128)(2,1)S(1)} %get-tuple-element.40), channel_id=1, source_target_pairs={{0,16},{4,20},{8,24},{12,28},{16,0},{20,4},{24,8},{28,12},{1,17},{... | collective-permute-start | bytes 245768 | tf_op jit(solution)/shard_map/ppermute | solution.py:327
  61.7 4.4 %collective-permute-start.18 = (bf16[32,1280]{1,0:T(8,128)(2,1)S(1)}, bf16[32,1280]{1,0:T(8,128)(2,1)S(1)}, u32[]{:S(2)}, u32[]{:S(2)}) collective-permute-start(bf16[32,1280]{1,0:T(8,128)(2,1)S(1)} %get-tuple-element.41), channel_id=1, source_target_pairs={{0,8},{4,12},{8,0},{12,4},{16,24},{20,28},{24,16},{28,20},{1,9},{5... | collective-permute-start | bytes 245768 | tf_op jit(solution)/shard_map/ppermute | solution.py:327
  63.4 2.7 %copy-start.2 = (f32[1280,32]{0,1:T(8,128)S(1)}, f32[1280,32]{0,1:T(8,128)}, u32[]{:S(2)}) copy-start(f32[1280,32]{0,1:T(8,128)} %param.12) | copy-start | bytes 491524
  63.4 2.7 %copy-start.3 = (f32[1280,32]{0,1:T(8,128)S(1)}, f32[1280,32]{0,1:T(8,128)}, u32[]{:S(2)}) copy-start(f32[1280,32]{0,1:T(8,128)} %param.13) | copy-start | bytes 491524

commit v17 on v16

--- a/solution.py
+++ b/solution.py
@@ -288,7 +288,7 @@
 
     rounds = [order]
     spread = [held] + [None] * (n_chip - 1)
-    for step in range(1, n_chip):
+    for step in reversed(range(1, n_chip)):
         spread[step] = lax.ppermute(held, "island", pair_perm(n_chip, step, 2))
 
     mine, for_partner = half_queries(

time: 67.2 us -> 67.2 us (level)
  no operation moved by 1% of the time
where the time goes in v17:
time: 67.2 us; the launch traced here: 66.9 us
  waiting for transfers between devices  31.2 us (46%)
  starting transfers between devices  22.9 us (34%)
  local copies, waits for them, and re-layouts  6.39 us (10%)
  Pallas kernels  3.58 us (5%)
  other arithmetic  2.03 us (3%)
  between operations  0.83 us (1%)
    ppermute x3, waiting for transfers between devices, on_device(): lax.ppermute(dquery, 'seq', pair_perm(n_seq, k))  9.22 us
    ppermute x3, waiting for transfers between devices, on_device(): spread[step] = lax.ppermute(held, 'island', pair_perm(n_chip, step, 2))  8.42 us
    ppermute x1, waiting for transfers between devices, on_device(): lax.ppermute(jnp.concatenate(kv, axis=0), 'seq', pair_perm(n_seq, bit))  5.36 us
    ppermute x1, starting transfers between devices, on_device(): held = jnp.concatenate([weight, lax.ppermute(weight, 'seq', far_perm)], 0)  3.67 us
    ppermute x3, starting transfers between devices, on_device(): lax.ppermute(dquery, 'seq', pair_perm(n_seq, k))  3.55 us
    ppermute x3, starting transfers between devices, on_device(): lax.ppermute(parts[step], 'island', pair_perm(n_chip, step, 2))  3.55 us
    ppermute x3, starting transfers between devices, on_device(): spread[step] = lax.ppermute(held, 'island', pair_perm(n_chip, step, 2))  3.55 us
    ppermute x1, starting transfers between devices, on_device(): lax.ppermute(held, 'seq', pair_perm(n_seq, bit))  3.54 us
  transfers between devices with their start and end apart: 19, of which 11 were waited for; matrix products, arithmetic and copies ran while one was open for 11% of the time, Pallas kernels for 4%

profile of v17, /device:TPU:0, one launch (start us, length us, event | category | flops | bytes accessed | tf_op | source)
XLA Modules:
  0.0 66.9 jit_solution(5630790059956571170)
XLA Ops:
  0.6 0.5 collective-permute-start
  1.1 0.9 %convert_bitcast_fusion = bf16[32,1280]{1,0:T(8,128)(2,1)S(1)} fusion(f32[1280,32]{0,1:T(8,128)} %param.12), kind=kLoop, calls=%fused_computation.20 | loop fusion | flops 40960 | bytes 245760 | tf_op jit(solution)/shard_map/convert_element_type | solution.py:270
  2.1 3.7 %collective-permute-start.3 = (bf16[32,1280]{1,0:T(8,128)(2,1)S(1)}, bf16[32,1280]{1,0:T(8,128)(2,1)S(1)}, u32[]{:S(2)}, u32[]{:S(2)}) collective-permute-start(bf16[32,1280]{1,0:T(8,128)(2,1)S(1)} %convert_bitcast_fusion), channel_id=1, source_target_pairs={{0,2},{1,3},{2,0},{3,1},{4,6},{5,7},{6,4},{7,5},{8,10},{9,11},{10,... | collective-permute-start | bytes 245768 | tf_op jit(solution)/shard_map/ppermute | solution.py:271
  5.7 0.9 %copy.19 = bf16[16,8,2,256]{3,1,2,0:T(8,128)(2,1)S(1)} copy(bf16[16,8,2,256]{3,2,1,0:T(2,128)(2,1)} %bitcast.65) | data formatting | bytes 262144
  6.7 0.1 collective-permute-start.1
  6.8 1.5 %dynamic-slice_bitcast_fusion = (bf16[128,1280]{1,0:T(8,128)(2,1)S(1)}, bf16[128,1280]{1,0:T(8,128)(2,1)S(1)}, bf16[128,1280]{1,0:T(8,128)(2,1)S(1)}, bf16[128,1280]{1,0:T(8,128)(2,1)S(1)}, bf16[128,1280]{1,0:T(8,128)(2,1)S(1)}) fusion(bf16[1,128,5120]{2,1,0:T(8,128)(2,1)} %param.7, s32[]{:T(128)S(6)} %select_n.44, s32[]{:T(128)S(6)} %select_n.42, ...), kind=kLoop, calls=%fused_computation.8 | loop fusion | bytes 3276820 | tf_op jit(solution)/shard_map/dynamic_slice | solution.py:276
  8.3 2.4 %collective-permute-done.3 = bf16[32,1280]{1,0:T(8,128)(2,1)S(1)} collective-permute-done((bf16[32,1280]{1,0:T(8,128)(2,1)S(1)}, bf16[32,1280]{1,0:T(8,128)(2,1)S(1)}, u32[]{:S(2)}, u32[]{:S(2)}) %collective-permute-start.3) | collective-permute-done | bytes 81952 | tf_op jit(solution)/shard_map/ppermute | solution.py:271
  10.7 3.5 %collective-permute-start.4 = (bf16[64,1280]{1,0:T(8,128)(2,1)S(1)}, bf16[64,1280]{1,0:T(8,128)(2,1)S(1)}, u32[]{:S(2)}, u32[]{:S(2)}) collective-permute-start(bf16[64,1280]{1,0:T(8,128)(2,1)S(1)} %pad_maximum_fusion.5), channel_id=1, source_target_pairs={{0,1},{1,0},{2,3},{3,2},{4,5},{5,4},{6,7},{7,6},{8,9},{9,8},{10,11... | collective-permute-start | bytes 491528 | tf_op jit(solution)/shard_map/ppermute | solution.py:286
  14.2 0.0 collective-permute-done
  14.3 0.1 constant_dynamic-slice_fusion
  14.5 1.9 %collective-permute-done.1.refs_2_.refs_3_ = bf16[128,512]{1,0:T(8,128)(2,1)S(1)} collective-permute-done((bf16[128,512]{1,0:T(8,128)(2,1)S(1)}, bf16[128,512]{1,0:T(8,128)(2,1)S(1)}, u32[]{:S(2)}, u32[]{:S(2)}) %collective-permute-start.1) | collective-permute-done | bytes 131104 | tf_op jit(solution)/shard_map/ppermute | solution.py:273
  16.3 0.7 %collective-permute-start.2 = (bf16[256,512]{1,0:T(8,128)(2,1)S(1)}, bf16[256,512]{1,0:T(8,128)(2,1)S(1)}, u32[]{:S(2)}, u32[]{:S(2)}) collective-permute-start(bf16[256,512]{1,0:T(8,128)(2,1)S(1)} %pad_maximum_fusion.4), channel_id=1, source_target_pairs={{0,1},{1,0},{2,3},{3,2},{4,5},{5,4},{6,7},{7,6},{8,9},{9,8},{10,11... | collective-permute-start | bytes 786440 | tf_op jit(solution)/shard_map/ppermute | solution.py:287
  17.1 3.4 %collective-permute-start.13 = (bf16[256,1280]{1,0:T(8,128)(2,1)S(1)}, bf16[256,1280]{1,0:T(8,128)(2,1)S(1)}, u32[]{:S(2)}, u32[]{:S(2)}) collective-permute-start(bf16[256,1280]{1,0:T(8,128)(2,1)S(1)} %pad_maximum_fusion), channel_id=1, source_target_pairs={{0,2},{1,3},{2,0},{3,1},{4,7},{5,6},{6,5},{7,4},{8,10},{9,11},{10,... | collective-permute-start | bytes 1966088 | tf_op jit(solution)/shard_map/ppermute | solution.py:282
  20.4 1.6 %collective-permute-start.5 = (bf16[128,1280]{1,0:T(8,128)(2,1)S(1)}, bf16[128,1280]{1,0:T(8,128)(2,1)S(1)}, u32[]{:S(2)}, u32[]{:S(2)}) collective-permute-start(bf16[128,1280]{1,0:T(8,128)(2,1)S(1)} %pad_maximum_fusion.3.refs_0_), channel_id=1, source_target_pairs={{0,8},{4,12},{8,0},{12,4},{16,24},{20,28},{24,16},{28,20},{1,9},{5... | collective-permute-start | bytes 983048 | tf_op jit(solution)/shard_map/ppermute | solution.py:292
  22.0 1.5 %collective-permute-start.6 = (bf16[128,1280]{1,0:T(8,128)(2,1)S(1)}, bf16[128,1280]{1,0:T(8,128)(2,1)S(1)}, u32[]{:S(2)}, u32[]{:S(2)}) collective-permute-start(bf16[128,1280]{1,0:T(8,128)(2,1)S(1)} %pad_maximum_fusion.3.refs_0_), channel_id=1, source_target_pairs={{0,16},{4,20},{8,24},{12,28},{16,0},{20,4},{24,8},{28,12},{1,17},{... | collective-permute-start | bytes 983048 | tf_op jit(solution)/shard_map/ppermute | solution.py:292
  23.5 0.5 collective-permute-start.7
  24.0 5.4 %collective-permute-done.2.refs_4_.refs_5_ = bf16[256,512]{1,0:T(8,128)(2,1)S(1)} collective-permute-done((bf16[256,512]{1,0:T(8,128)(2,1)S(1)}, bf16[256,512]{1,0:T(8,128)(2,1)S(1)}, u32[]{:S(2)}, u32[]{:S(2)}) %collective-permute-start.2) | collective-permute-done | bytes 262176 | tf_op jit(solution)/shard_map/ppermute | solution.py:287
  29.4 1.8 %collective-permute-done.5.refs_1_ = bf16[128,1280]{1,0:T(8,128)(2,1)S(1)} collective-permute-done((bf16[128,1280]{1,0:T(8,128)(2,1)S(1)}, bf16[128,1280]{1,0:T(8,128)(2,1)S(1)}, u32[]{:S(2)}, u32[]{:S(2)}) %collective-permute-start.5) | collective-permute-done | bytes 327712 | tf_op jit(solution)/shard_map/ppermute | solution.py:292
  31.2 6.6 %collective-permute-done.6.refs_2_ = bf16[128,1280]{1,0:T(8,128)(2,1)S(1)} collective-permute-done((bf16[128,1280]{1,0:T(8,128)(2,1)S(1)}, bf16[128,1280]{1,0:T(8,128)(2,1)S(1)}, u32[]{:S(2)}, u32[]{:S(2)}) %collective-permute-start.6) | collective-permute-done | bytes 327712 | tf_op jit(solution)/shard_map/ppermute | solution.py:292
  37.8 1.0 %shard_map.102 = (bf16[4,32,128]{2,1,0:T(8,128)(2,1)S(1)}, bf16[4,32,128]{2,1,0:T(8,128)(2,1)S(1)}) custom-call(bf16[128,1280]{1,0:T(8,128)(2,1)S(1)} %pad_maximum_fusion.3.refs_0_, bf16[128,1280]{1,0:T(8,128)(2,1)S(1)} %collective-permute-done.5.refs_1_, bf16[128,1280]{1,0:T(8,128)(2,1)S(1)} %collective-permute-done.6.refs_2_, ...), custom_call_target="tpu_custom_call" | custom-call | flops 335544320 | bytes 3932160 | tf_op jit(solution)/shard_map/pallas_call | solution.py:84
  38.8 0.0 copy-start.1
  38.8 0.1 collective-permute-start.8
  38.8 1.2 %collective-permute-done.8.refs_7_ = bf16[4,32,128]{2,1,0:T(8,128)(2,1)S(1)} collective-permute-done((bf16[4,32,128]{2,1,0:T(8,128)(2,1)S(1)}, bf16[4,32,128]{2,1,0:T(8,128)(2,1)S(1)}, u32[]{:S(2)}, u32[]{:S(2)}) %collective-permute-start.8) | collective-permute-done | bytes 32800 | tf_op jit(solution)/shard_map/ppermute | solution.py:298
  40.0 1.2 %shard_map.103.refs_0_ = bf16[256,128]{1,0:T(8,128)(2,1)S(1)} custom-call(bf16[128,512]{1,0:T(8,128)(2,1)S(1)} %bitcast.57, bf16[128,512]{1,0:T(8,128)(2,1)S(1)} %bitcast.58, bf16[128,512]{1,0:T(8,128)(2,1)S(1)} %collective-permute-done.1.refs_2_.refs_3_, bf16[128,512]{1,0:T(8,128)(2,1)S(1)} %collective-permute-done.1.refs_2_.refs_3_, ...), custom_call_target="tpu_custom_call" | custom-call | flops 402653184 | bytes 786432 | tf_op jit(solution)/shard_map/pallas_call | solution.py:164
  41.3 1.8 %collective-permute-start.10 = (bf16[256,128]{1,0:T(8,128)(2,1)S(1)}, bf16[256,128]{1,0:T(8,128)(2,1)S(1)}, u32[]{:S(2)}, u32[]{:S(2)}) collective-permute-start(bf16[256,128]{1,0:T(8,128)(2,1)S(1)} %shard_map.103.refs_0_), channel_id=1, source_target_pairs={{0,2},{1,3},{2,0},{3,1},{4,6},{5,7},{6,4},{7,5},{8,10},{9,11},{10,... | collective-permute-start | bytes 196616 | tf_op jit(solution)/shard_map/ppermute | solution.py:302
  43.0 1.3 %collective-permute-start.11 = (bf16[256,128]{1,0:T(8,128)(2,1)S(1)}, bf16[256,128]{1,0:T(8,128)(2,1)S(1)}, u32[]{:S(2)}, u32[]{:S(2)}) collective-permute-start(bf16[256,128]{1,0:T(8,128)(2,1)S(1)} %shard_map.103.refs_0_), channel_id=1, source_target_pairs={{0,3},{1,2},{2,1},{3,0},{4,7},{5,6},{6,5},{7,4},{8,11},{9,10},{10,... | collective-permute-start | bytes 196616 | tf_op jit(solution)/shard_map/ppermute | solution.py:302
  44.4 0.5 collective-permute-start.9
  44.8 9.2 %collective-permute-done.10.refs_2_ = bf16[256,128]{1,0:T(8,128)(2,1)S(1)} collective-permute-done((bf16[256,128]{1,0:T(8,128)(2,1)S(1)}, bf16[256,128]{1,0:T(8,128)(2,1)S(1)}, u32[]{:S(2)}, u32[]{:S(2)}) %collective-permute-start.10) | collective-permute-done | bytes 65568 | tf_op jit(solution)/shard_map/ppermute | solution.py:302
  54.1 0.1 collective-permute-start.14
  54.2 0.2 copy.13
  54.4 1.3 %copy.14 = bf16[256,1280]{1,0:T(8,128)(2,1)S(1)} copy(bf16[256,1280]{0,1:T(8,128)(2,1)} %bitcast.64) | data formatting | bytes 1310720 | tf_op jit(solution)/shard_map/transpose | solution.py:310
  55.7 0.5 collective-permute-done.14.refs_7_
  56.2 0.7 shard_map.105
  56.9 0.2 collective-permute-start.15
  57.1 0.7 shard_map.104
  57.8 0.1 select_bitcast_fusion.1
  57.9 0.1 pad_maximum_fusion.2
  57.9 0.7 %collective-permute-done.15.got_ref = bf16[4,32,1280]{2,1,0:T(8,128)(2,1)S(1)} collective-permute-done((bf16[4,32,1280]{2,1,0:T(8,128)(2,1)S(1)}, bf16[4,32,1280]{2,1,0:T(8,128)(2,1)S(1)}, u32[]{:S(2)}, u32[]{:S(2)}) %collective-permute-start.15) | collective-permute-done | bytes 327712 | tf_op jit(solution)/shard_map/ppermute | solution.py:314
  58.6 0.1 shard_map.106
  58.7 2.5 %collective-permute-start.16 = (bf16[32,1280]{1,0:T(8,128)(2,1)S(1)}, bf16[32,1280]{1,0:T(8,128)(2,1)S(1)}, u32[]{:S(2)}, u32[]{:S(2)}) collective-permute-start(bf16[32,1280]{1,0:T(8,128)(2,1)S(1)} %get-tuple-element.39), channel_id=1, source_target_pairs={{0,24},{4,28},{8,16},{12,20},{16,8},{20,12},{24,0},{28,4},{1,25},{... | collective-permute-start | bytes 245768 | tf_op jit(solution)/shard_map/ppermute | solution.py:327
  61.2 0.5 collective-permute-start.17
  61.7 0.5 collective-permute-start.18
  62.2 0.1 pad_maximum_fusion.1
  62.4 1.1 %copy.18 = bf16[1,1280,256]{2,1,0:T(8,128)(2,1)} copy(bf16[1,1280,256]{1,2,0:T(8,128)(2,1)S(1)} %bitcast.60) | data formatting | bytes 1310720
  63.5 1.1 %copy.17 = bf16[1,1280,256]{2,1,0:T(8,128)(2,1)} copy(bf16[1,1280,256]{1,2,0:T(8,128)(2,1)S(1)} %bitcast.61) | data formatting | bytes 1310720
  64.6 1.3 %collective-permute-done.17 = bf16[32,1280]{1,0:T(8,128)(2,1)S(1)} collective-permute-done((bf16[32,1280]{1,0:T(8,128)(2,1)S(1)}, bf16[32,1280]{1,0:T(8,128)(2,1)S(1)}, u32[]{:S(2)}, u32[]{:S(2)}) %collective-permute-start.17) | collective-permute-done | bytes 81952 | tf_op jit(solution)/shard_map/ppermute | solution.py:327
  65.9 0.3 collective-permute-done.18
  66.1 0.8 %fusion.1 = (f32[1280,32]{0,1:T(8,128)}, f32[1280,32]{0,1:T(8,128)}) fusion(f32[1280,32]{0,1:T(8,128)S(1)} %copy-done.2, bf16[32,1280]{1,0:T(8,128)(2,1)S(1)} %collective-permute-done.18, bf16[32,1280]{1,0:T(8,128)(2,1)S(1)} %collective-permute-done.17, f32[32,1280]{1,0:T(8,128)S(1)} %get-tuple-element.38, bf16[32,1280]{1,0:T(8,128)(2,1)S(1)} %collective-permute-done.16, ...), kind=kLoop, calls=%fused_computation.18 | loop fusion | flops 532480 | bytes 1064960 | tf_op jit(solution)/shard_map/sub | solution.py:332
  (21 shorter events, 0.2 us)
Async XLA Ops:
  0.6 13.6 %collective-permute-start = (bf16[128,5120]{1,0:T(8,128)(2,1)}, bf16[128,5120]{1,0:T(8,128)(2,1)S(1)}, u32[]{:S(2)}, u32[]{:S(2)}) collective-permute-start(bf16[128,5120]{1,0:T(8,128)(2,1)} %bitcast.62), channel_id=1, source_target_pairs={{0,4},{4,0},{8,12},{12,8},{16,20},{20,16},{24,28},{28,24},{1,5},{5... | collective-permute-start | bytes 3932168 | tf_op jit(solution)/shard_map/ppermute | solution.py:269
  2.1 8.6 %collective-permute-start.3 = (bf16[32,1280]{1,0:T(8,128)(2,1)S(1)}, bf16[32,1280]{1,0:T(8,128)(2,1)S(1)}, u32[]{:S(2)}, u32[]{:S(2)}) collective-permute-start(bf16[32,1280]{1,0:T(8,128)(2,1)S(1)} %convert_bitcast_fusion), channel_id=1, source_target_pairs={{0,2},{1,3},{2,0},{3,1},{4,6},{5,7},{6,4},{7,5},{8,10},{9,11},{10,... | collective-permute-start | bytes 245768 | tf_op jit(solution)/shard_map/ppermute | solution.py:271
  6.7 9.7 %collective-permute-start.1 = (bf16[128,512]{1,0:T(8,128)(2,1)S(1)}, bf16[128,512]{1,0:T(8,128)(2,1)S(1)}, u32[]{:S(2)}, u32[]{:S(2)}) collective-permute-start(bf16[128,512]{1,0:T(8,128)(2,1)S(1)} %bitcast.55), channel_id=1, source_target_pairs={{0,2},{1,3},{2,0},{3,1},{4,6},{5,7},{6,4},{7,5},{8,10},{9,11},{10,... | collective-permute-start | bytes 393224 | tf_op jit(solution)/shard_map/ppermute | solution.py:273
  10.7 9.7 %collective-permute-start.4 = (bf16[64,1280]{1,0:T(8,128)(2,1)S(1)}, bf16[64,1280]{1,0:T(8,128)(2,1)S(1)}, u32[]{:S(2)}, u32[]{:S(2)}) collective-permute-start(bf16[64,1280]{1,0:T(8,128)(2,1)S(1)} %pad_maximum_fusion.5), channel_id=1, source_target_pairs={{0,1},{1,0},{2,3},{3,2},{4,5},{5,4},{6,7},{7,6},{8,9},{9,8},{10,11... | collective-permute-start | bytes 491528 | tf_op jit(solution)/shard_map/ppermute | solution.py:286
  16.3 13.0 %collective-permute-start.2 = (bf16[256,512]{1,0:T(8,128)(2,1)S(1)}, bf16[256,512]{1,0:T(8,128)(2,1)S(1)}, u32[]{:S(2)}, u32[]{:S(2)}) collective-permute-start(bf16[256,512]{1,0:T(8,128)(2,1)S(1)} %pad_maximum_fusion.4), channel_id=1, source_target_pairs={{0,1},{1,0},{2,3},{3,2},{4,5},{5,4},{6,7},{7,6},{8,9},{9,8},{10,11... | collective-permute-start | bytes 786440 | tf_op jit(solution)/shard_map/ppermute | solution.py:287
  17.1 37.0 %collective-permute-start.13 = (bf16[256,1280]{1,0:T(8,128)(2,1)S(1)}, bf16[256,1280]{1,0:T(8,128)(2,1)S(1)}, u32[]{:S(2)}, u32[]{:S(2)}) collective-permute-start(bf16[256,1280]{1,0:T(8,128)(2,1)S(1)} %pad_maximum_fusion), channel_id=1, source_target_pairs={{0,2},{1,3},{2,0},{3,1},{4,7},{5,6},{6,5},{7,4},{8,10},{9,11},{10,... | collective-permute-start | bytes 1966088 | tf_op jit(solution)/shard_map/ppermute | solution.py:282
  20.4 10.7 %collective-permute-start.5 = (bf16[128,1280]{1,0:T(8,128)(2,1)S(1)}, bf16[128,1280]{1,0:T(8,128)(2,1)S(1)}, u32[]{:S(2)}, u32[]{:S(2)}) collective-permute-start(bf16[128,1280]{1,0:T(8,128)(2,1)S(1)} %pad_maximum_fusion.3.refs_0_), channel_id=1, source_target_pairs={{0,8},{4,12},{8,0},{12,4},{16,24},{20,28},{24,16},{28,20},{1,9},{5... | collective-permute-start | bytes 983048 | tf_op jit(solution)/shard_map/ppermute | solution.py:292
  22.0 15.8 %collective-permute-start.6 = (bf16[128,1280]{1,0:T(8,128)(2,1)S(1)}, bf16[128,1280]{1,0:T(8,128)(2,1)S(1)}, u32[]{:S(2)}, u32[]{:S(2)}) collective-permute-start(bf16[128,1280]{1,0:T(8,128)(2,1)S(1)} %pad_maximum_fusion.3.refs_0_), channel_id=1, source_target_pairs={{0,16},{4,20},{8,24},{12,28},{16,0},{20,4},{24,8},{28,12},{1,17},{... | collective-permute-start | bytes 983048 | tf_op jit(solution)/shard_map/ppermute | solution.py:292
  23.5 14.3 %collective-permute-start.7 = (bf16[128,1280]{1,0:T(8,128)(2,1)S(1)}, bf16[128,1280]{1,0:T(8,128)(2,1)S(1)}, u32[]{:S(2)}, u32[]{:S(2)}) collective-permute-start(bf16[128,1280]{1,0:T(8,128)(2,1)S(1)} %pad_maximum_fusion.3.refs_0_), channel_id=1, source_target_pairs={{0,24},{4,28},{8,16},{12,20},{16,8},{20,12},{24,0},{28,4},{1,25},{... | collective-permute-start | bytes 983048 | tf_op jit(solution)/shard_map/ppermute | solution.py:292
  29.4 24.7 %collective-permute-start.12 = (bf16[128,1280]{1,0:T(8,128)(2,1)S(1)}, bf16[128,1280]{1,0:T(8,128)(2,1)S(1)}, u32[]{:S(2)}, u32[]{:S(2)}) collective-permute-start(bf16[128,1280]{1,0:T(8,128)(2,1)S(1)} %get-tuple-element.32.refs_5_), channel_id=1, source_target_pairs={{0,1},{1,0},{2,3},{3,2},{4,5},{5,4},{6,7},{7,6},{8,9},{9,8},{10,11... | collective-permute-start | bytes 983048 | tf_op jit(solution)/shard_map/ppermute | solution.py:299
  37.8 2.3 %copy-start = (bf16[1,128,256]{2,1,0:T(8,128)(2,1)S(1)}, bf16[1,128,256]{2,1,0:T(8,128)(2,1)}, u32[]{:S(2)}) copy-start(bf16[1,128,256]{2,1,0:T(8,128)(2,1)} %param.9) | copy-start | bytes 196612
  38.8 15.4 %copy-start.1 = (bf16[1,1280,256]{2,1,0:T(8,128)(2,1)S(1)}, bf16[1,1280,256]{2,1,0:T(8,128)(2,1)}, u32[]{:S(2)}) copy-start(bf16[1,1280,256]{2,1,0:T(8,128)(2,1)} %param.10) | copy-start | bytes 1966084
  38.8 1.3 %collective-permute-start.8 = (bf16[4,32,128]{2,1,0:T(8,128)(2,1)S(1)}, bf16[4,32,128]{2,1,0:T(8,128)(2,1)S(1)}, u32[]{:S(2)}, u32[]{:S(2)}) collective-permute-start(bf16[4,32,128]{2,1,0:T(8,128)(2,1)S(1)} %get-tuple-element.31), channel_id=1, source_target_pairs={{0,4},{4,0},{8,12},{12,8},{16,20},{20,16},{24,28},{28,24},{1,5},{5... | collective-permute-start | bytes 98312 | tf_op jit(solution)/shard_map/ppermute | solution.py:298
  41.3 12.8 %collective-permute-start.10 = (bf16[256,128]{1,0:T(8,128)(2,1)S(1)}, bf16[256,128]{1,0:T(8,128)(2,1)S(1)}, u32[]{:S(2)}, u32[]{:S(2)}) collective-permute-start(bf16[256,128]{1,0:T(8,128)(2,1)S(1)} %shard_map.103.refs_0_), channel_id=1, source_target_pairs={{0,2},{1,3},{2,0},{3,1},{4,6},{5,7},{6,4},{7,5},{8,10},{9,11},{10,... | collective-permute-start | bytes 196616 | tf_op jit(solution)/shard_map/ppermute | solution.py:302
  43.0 11.0 %collective-permute-start.11 = (bf16[256,128]{1,0:T(8,128)(2,1)S(1)}, bf16[256,128]{1,0:T(8,128)(2,1)S(1)}, u32[]{:S(2)}, u32[]{:S(2)}) collective-permute-start(bf16[256,128]{1,0:T(8,128)(2,1)S(1)} %shard_map.103.refs_0_), channel_id=1, source_target_pairs={{0,3},{1,2},{2,1},{3,0},{4,7},{5,6},{6,5},{7,4},{8,11},{9,10},{10,... | collective-permute-start | bytes 196616 | tf_op jit(solution)/shard_map/ppermute | solution.py:302
  44.4 9.7 %collective-permute-start.9 = (bf16[256,128]{1,0:T(8,128)(2,1)S(1)}, bf16[256,128]{1,0:T(8,128)(2,1)S(1)}, u32[]{:S(2)}, u32[]{:S(2)}) collective-permute-start(bf16[256,128]{1,0:T(8,128)(2,1)S(1)} %shard_map.103.refs_0_), channel_id=1, source_target_pairs={{0,1},{1,0},{2,3},{3,2},{4,5},{5,4},{6,7},{7,6},{8,9},{9,8},{10,11... | collective-permute-start | bytes 196616 | tf_op jit(solution)/shard_map/ppermute | solution.py:302
  54.1 2.2 %collective-permute-start.14 = (bf16[256,1280]{1,0:T(8,128)(2,1)S(1)}, bf16[256,1280]{1,0:T(8,128)(2,1)S(1)}, u32[]{:S(2)}, u32[]{:S(2)}) collective-permute-start(bf16[256,1280]{1,0:T(8,128)(2,1)S(1)} %collective-permute-done.13.refs_6_), channel_id=1, source_target_pairs={{0,4},{4,0},{8,12},{12,8},{16,20},{20,16},{24,28},{28,24},{1,5},{5... | collective-permute-start | bytes 1966088 | tf_op jit(solution)/shard_map/ppermute | solution.py:308
  56.9 1.7 %collective-permute-start.15 = (bf16[4,32,1280]{2,1,0:T(8,128)(2,1)S(1)}, bf16[4,32,1280]{2,1,0:T(8,128)(2,1)S(1)}, u32[]{:S(2)}, u32[]{:S(2)}) collective-permute-start(bf16[4,32,1280]{2,1,0:T(8,128)(2,1)S(1)} %get-tuple-element.37), channel_id=1, source_target_pairs={{0,4},{4,0},{8,12},{12,8},{16,20},{20,16},{24,28},{28,24},{1,5},{5... | collective-permute-start | bytes 983048 | tf_op jit(solution)/shard_map/ppermute | solution.py:314
  58.7 5.9 %collective-permute-start.16 = (bf16[32,1280]{1,0:T(8,128)(2,1)S(1)}, bf16[32,1280]{1,0:T(8,128)(2,1)S(1)}, u32[]{:S(2)}, u32[]{:S(2)}) collective-permute-start(bf16[32,1280]{1,0:T(8,128)(2,1)S(1)} %get-tuple-element.39), channel_id=1, source_target_pairs={{0,24},{4,28},{8,16},{12,20},{16,8},{20,12},{24,0},{28,4},{1,25},{... | collective-permute-start | bytes 245768 | tf_op jit(solution)/shard_map/ppermute | solution.py:327
  61.2 4.7 %collective-permute-start.17 = (bf16[32,1280]{1,0:T(8,128)(2,1)S(1)}, bf16[32,1280]{1,0:T(8,128)(2,1)S(1)}, u32[]{:S(2)}, u32[]{:S(2)}) collective-permute-start(bf16[32,1280]{1,0:T(8,128)(2,1)S(1)} %get-tuple-element.40), channel_id=1, source_target_pairs={{0,16},{4,20},{8,24},{12,28},{16,0},{20,4},{24,8},{28,12},{1,17},{... | collective-permute-start | bytes 245768 | tf_op jit(solution)/shard_map/ppermute | solution.py:327
  61.7 4.4 %collective-permute-start.18 = (bf16[32,1280]{1,0:T(8,128)(2,1)S(1)}, bf16[32,1280]{1,0:T(8,128)(2,1)S(1)}, u32[]{:S(2)}, u32[]{:S(2)}) collective-permute-start(bf16[32,1280]{1,0:T(8,128)(2,1)S(1)} %get-tuple-element.41), channel_id=1, source_target_pairs={{0,8},{4,12},{8,0},{12,4},{16,24},{20,28},{24,16},{28,20},{1,9},{5... | collective-permute-start | bytes 245768 | tf_op jit(solution)/shard_map/ppermute | solution.py:327
  63.4 2.7 %copy-start.2 = (f32[1280,32]{0,1:T(8,128)S(1)}, f32[1280,32]{0,1:T(8,128)}, u32[]{:S(2)}) copy-start(f32[1280,32]{0,1:T(8,128)} %param.12) | copy-start | bytes 491524
  63.4 2.7 %copy-start.3 = (f32[1280,32]{0,1:T(8,128)S(1)}, f32[1280,32]{0,1:T(8,128)}, u32[]{:S(2)}) copy-start(f32[1280,32]{0,1:T(8,128)} %param.13) | copy-start | bytes 491524
